TPU v7x, 128 devices: a whole 4x4x4 slice. The times are simulated.
128 devices in a mesh: seq: 16 (over x, z), rep: 8 (over y, core).
Axes of the slice: x: 4, y: 4, z: 4, core: 2. Of those that a mesh axis runs over, the one named last changes fastest.
Arguments:
- residual_in: bfloat16 [8192, 5120], P('seq', 'rep'), may hold values from -3 to 3
- queries: bfloat16 [8192, 5120], P('seq'), may hold values from -36 to 36
- keys: bfloat16 [8192, 5120], P('seq'), may hold values from -36 to 36
- values: bfloat16 [8192, 5120], P('seq'), may hold values from -6 to 6
- w_out: bfloat16 [5120, 5120], P(None, 'rep'), may hold values from -0.078125 to 0.078125
- gate_scale: float32 [5120], P('rep'), may hold values from 0.5 to 2
- tile_mask: int32 [40, 64, 64], replicated, may hold values from 0 to 1, as said below
Outputs:
- block_out: bfloat16 [8192, 5120], P('seq', 'rep')
Inputs may be any that keep to these rules, and one draw needn't show every extreme that they name: Every diagonal entry tile_mask[h, a, a] is 1 and each head's mask is symmetric.
All inputs are finite; a program needn't handle non-finite values.
Results may differ from a plain program's by a relative error of at most 0.0037.
Values may be sent and summed in bfloat16 or wider, within the bound.
No kernel may reach another device: no remote copies, remote signals or barrier semaphores. Data moves between devices by JAX's collectives and lax.ppermute only.
A program may use at most 192 MiB of HBM per device.

v0:
```python
import functools

import jax
import jax.numpy as jnp
from jax import lax
from jax.experimental import pallas as pl
from jax.experimental.pallas import tpu as pltpu
from jax.sharding import Mesh
from jax.sharding import PartitionSpec as P

TILE = 128
HEADS = 40
PLANES = 4
PLANE_HEADS = HEADS // PLANES
CHIPS = 16
HALF = 256
GROUP = 4
UNROLL = 8
ITEMS = 256
LOG2E = 1.4426950408889634
TOKENS_AXES = ("x", "z")
LOW = -1e30


def head_plan(work):
    ids = jnp.arange(HEADS)
    ahead = (work[None, :] > work[:, None]) | ((work[None, :] == work[:, None]) & (ids[None, :] < ids[:, None]))
    rank = jnp.sum(ahead.astype(jnp.int32), axis=1)
    row, col = rank // PLANES, rank % PLANES
    plane = jnp.where(row % 2 == 1, PLANES - 1 - col, col)
    place = plane * PLANE_HEADS + row
    hit = (place[None, :] == ids[:, None]).astype(jnp.int32)
    head_at = jnp.sum(hit * ids[None, :], axis=1)
    work_at = jnp.sum(hit * work[None, :], axis=1)
    return head_at, work_at


def chip_plan(work_at):
    extra = CHIPS - PLANE_HEADS
    quota = (work_at[:, None].astype(jnp.float32) / jnp.arange(1, extra + 1).astype(jnp.float32)[None, :]).reshape(-1)
    ids = jnp.arange(quota.shape[0])
    ahead = (quota[None, :] > quota[:, None]) | ((quota[None, :] == quota[:, None]) & (ids[None, :] < ids[:, None]))
    won = (jnp.sum(ahead.astype(jnp.int32), axis=1) < extra).astype(jnp.int32)
    chips = 1 + jnp.sum(won.reshape(PLANE_HEADS, extra), axis=1)
    slots = jnp.arange(PLANE_HEADS)
    first = jnp.sum(jnp.where(slots[None, :] < slots[:, None], chips[None, :], 0), axis=1)
    return chips, first


def pack_kernel(heads, q_ref, k_ref, v_ref, out_ref, held, turned, sem_in, sem_out):
    rows = pl.ds(pl.multiple_of(heads[CHIPS] * HALF, HALF), HALF)
    loads, stores = [], []
    for t in range(CHIPS):
        cols = pl.ds(pl.multiple_of(heads[t] * TILE, TILE), TILE)
        for j, ref in enumerate((k_ref, v_ref, q_ref)):
            loads.append(pltpu.make_async_copy(ref.at[rows, cols], held.at[t, j], sem_in.at[t, j]))
            loads[-1].start()
    for t in range(CHIPS):
        for j in range(3):
            loads[3 * t + j].wait()
            source = held.at[t, j]
            if j == 1:
                for sub in range(2):
                    part = pl.ds(sub * TILE, TILE)
                    turned[t, part, :] = held[t, 1, part, :].T
                source = turned.at[t]
            stores.append(pltpu.make_async_copy(source, out_ref.at[t, j], sem_out.at[t, j]))
            stores[-1].start()
    for store in stores:
        store.wait()


def pack(queries, keys, values, chip_heads, core):
    scalars = jnp.concatenate([chip_heads, core[None]]).astype(jnp.int32)
    hbm = pl.BlockSpec(memory_space=pl.ANY)
    return pl.pallas_call(
        pack_kernel,
        in_specs=[pl.BlockSpec(memory_space=pltpu.SMEM)] + [hbm] * 3,
        out_specs=hbm,
        out_shape=jax.ShapeDtypeStruct((CHIPS, 3, HALF, TILE), jnp.bfloat16),
        scratch_shapes=[
            pltpu.VMEM((CHIPS, 3, HALF, TILE), jnp.bfloat16),
            pltpu.VMEM((CHIPS, HALF, TILE), jnp.bfloat16),
            pltpu.SemaphoreType.DMA((CHIPS, 3)),
            pltpu.SemaphoreType.DMA((CHIPS, 3)),
        ],
        compiler_params=pltpu.CompilerParams(vmem_limit_bytes=16 * 2**20),
    )(scalars, queries, keys, values)


def attend_kernel(scale, meta, q_of, k_of, valid_of, own_ref, other_ref, out_ref, kv_s, q_s, acc_s, max_s, sum_s, sems):
    core, sub = meta[0], meta[2]
    loads = [
        pltpu.make_async_copy(own_ref.at[:, pl.ds(0, 4)], kv_s.at[core], sems.at[0]),
        pltpu.make_async_copy(other_ref.at[:, pl.ds(0, 4)], kv_s.at[1 - core], sems.at[1]),
        pltpu.make_async_copy(own_ref.at[:, pl.ds(4 + sub, 1)], q_s, sems.at[2]),
    ]
    for load in loads:
        load.start()
    acc_s[...] = jnp.zeros_like(acc_s)
    sum_s[...] = jnp.zeros_like(sum_s)
    max_s[...] = jnp.full_like(max_s, LOW)
    for load in loads:
        load.wait()

    def body(step, _):
        parts = []
        for u in range(UNROLL):
            e = step * UNROLL + u
            t = q_of[e]
            kid = [k_of[e * GROUP + g] for g in range(GROUP)]
            valid = valid_of[e]
            keys = jnp.concatenate([kv_s[i // 64, i % 64 // 4, i % 4] for i in kid], axis=0)
            scores = lax.dot_general(keys, q_s[t, 0], (((1,), (1,)), ((), ())), preferred_element_type=jnp.float32)
            top = jnp.max(scores, axis=0, keepdims=True) * scale
            weights = []
            total = jnp.zeros((1, TILE), jnp.float32)
            for g in range(GROUP):
                shift = top + jnp.where(g < valid, 0.0, -LOW)
                w = jnp.exp2(scores[g * TILE : (g + 1) * TILE] * scale - shift)
                total = total + jnp.sum(w, axis=0, keepdims=True)
                weights.append(w.astype(jnp.bfloat16))
            vals = jnp.concatenate([kv_s[i // 64, i % 64 // 4, i % 4 + 2] for i in kid], axis=1)
            part = jnp.dot(vals, jnp.concatenate(weights, axis=0), preferred_element_type=jnp.float32)
            parts.append((t, top, total, part))
        for t, top, total, part in parts:
            old = max_s[t]
            new = jnp.maximum(old, top)
            a = jnp.exp2(old - new)
            b = jnp.exp2(top - new)
            max_s[t] = new
            sum_s[t] = sum_s[t] * a + total * b
            acc_s[t] = acc_s[t] * a + part * b
        return 0

    lax.fori_loop(0, meta[1], body, 0)

    def finish(t, _):
        inverse = 1.0 / jnp.maximum(sum_s[t], 1e-30)
        out_ref[t] = (acc_s[t] * inverse).astype(jnp.bfloat16)
        return 0

    lax.fori_loop(0, CHIPS, finish, 0)


def attend(meta, q_of, k_of, valid_of, own, other):
    smem = pl.BlockSpec(memory_space=pltpu.SMEM)
    hbm = pl.BlockSpec(memory_space=pl.ANY)
    return pl.pallas_call(
        functools.partial(attend_kernel, TILE**-0.5 * LOG2E),
        in_specs=[smem] * 4 + [hbm] * 2,
        out_specs=pl.BlockSpec(memory_space=pltpu.VMEM),
        out_shape=jax.ShapeDtypeStruct((CHIPS, TILE, TILE), jnp.bfloat16),
        scratch_shapes=[
            pltpu.VMEM((2, CHIPS, 4, TILE, TILE), jnp.bfloat16),
            pltpu.VMEM((CHIPS, 1, TILE, TILE), jnp.bfloat16),
            pltpu.VMEM((CHIPS, TILE, TILE), jnp.float32),
            pltpu.VMEM((CHIPS, 1, TILE), jnp.float32),
            pltpu.VMEM((CHIPS, 1, TILE), jnp.float32),
            pltpu.SemaphoreType.DMA((3,)),
        ],
        compiler_params=pltpu.CompilerParams(vmem_limit_bytes=40 * 2**20),
    )(meta, q_of, k_of, valid_of, own, other)


def item_lists(allowed, mine):
    tiles = allowed.shape[1]
    count = jnp.sum(allowed, axis=1) * mine
    groups = (count + GROUP - 1) // GROUP
    slots = jnp.arange(groups.shape[0])
    end = jnp.sum(jnp.where(slots[None, :] <= slots[:, None], groups[None, :], 0), axis=1)
    steps = (end[-1] + UNROLL - 1) // UNROLL
    key_ids = jnp.arange(tiles)
    before = jnp.sum(allowed[:, None, :] * (key_ids[None, :] < key_ids[:, None])[None].astype(jnp.int32), axis=2)
    held_at = (key_ids // 2 % 2) * 64 + key_ids // 4 * 4 + key_ids % 2
    listed = jnp.sum(
        jnp.where((before[:, :, None] == key_ids[None, None, :]) & (allowed[:, :, None] > 0), held_at[None, :, None], 0),
        axis=1,
    )
    item = jnp.arange(ITEMS)
    real = (item < end[-1]).astype(jnp.int32)
    held = jnp.maximum(jnp.minimum(item, end[-1] - 1), 0)
    q_of = jnp.minimum(jnp.sum((end[None, :] <= held[:, None]).astype(jnp.int32), axis=1), CHIPS - 1)
    pick = (q_of[:, None] == slots[None, :]).astype(jnp.int32)
    start = GROUP * (held - jnp.sum(pick * (end - groups)[None, :], axis=1))
    left = jnp.sum(pick * count[None, :], axis=1) - start
    rows = jnp.dot(pick.astype(jnp.float32), listed.astype(jnp.float32))
    offset = jnp.arange(GROUP)
    where = start[:, None] + jnp.where(offset[None, :] < left[:, None], offset[None, :], 0)
    k_of = jnp.sum(jnp.where(where[:, :, None] == key_ids[None, None, :], rows[:, None, :], 0.0), axis=2)
    valid = jnp.minimum(left, GROUP) * real
    return steps, q_of, k_of.astype(jnp.int32).reshape(-1), valid


def select_kernel(source, got_ref, out_ref):
    for i in range(PLANE_HEADS):
        out_ref[:, pl.ds(i * TILE, TILE)] = got_ref[source[i]].T


def select(source, got):
    vmem = pl.BlockSpec(memory_space=pltpu.VMEM)
    return pl.pallas_call(
        select_kernel,
        in_specs=[pl.BlockSpec(memory_space=pltpu.SMEM), vmem],
        out_specs=vmem,
        out_shape=jax.ShapeDtypeStruct((TILE, PLANE_HEADS * TILE), jnp.bfloat16),
    )(source, got)


def exchange(block):
    return lax.all_to_all(block, TOKENS_AXES, split_axis=0, concat_axis=0, tiled=True)


def along_y(block, step):
    return lax.ppermute(block, "y", [(i, (i + step) % PLANES) for i in range(PLANES)])


def swap(block):
    return lax.ppermute(block, "c", [(0, 1), (1, 0)])


def shards(residual_in, queries, keys, values, w_out, gate_scale, tile_mask):
    chip = lax.axis_index("x") * 4 + lax.axis_index("z")
    plane = lax.axis_index("y")
    core = lax.axis_index("c")
    tile_work = jnp.sum(tile_mask, axis=2)
    head_at, work_at = head_plan(jnp.sum(tile_work, axis=1))
    plane_heads = lax.dynamic_slice_in_dim(head_at, plane * PLANE_HEADS, PLANE_HEADS)
    chips, first = chip_plan(lax.dynamic_slice_in_dim(work_at, plane * PLANE_HEADS, PLANE_HEADS))
    chip_ids = jnp.arange(CHIPS)
    on_chip = (first[None, :] <= chip_ids[:, None]) & (chip_ids[:, None] < (first + chips)[None, :])
    chip_heads = jnp.sum(jnp.where(on_chip, plane_heads[None, :], 0), axis=1)
    got = exchange(pack(queries, keys, values, chip_heads, core)).reshape(CHIPS, 6, TILE, TILE)

    half_work = lax.dynamic_index_in_dim(tile_work.reshape(HEADS, CHIPS, 2, 2), core, 2, keepdims=False)
    half_work = jnp.take(half_work.reshape(HEADS, 2 * CHIPS), plane_heads, axis=0, mode="clip")
    tile_ids = jnp.arange(2 * CHIPS)
    done = jnp.sum(
        jnp.where((tile_ids[None, :] < tile_ids[:, None])[None], half_work[:, None, :], 0), axis=2
    )
    total = jnp.sum(half_work, axis=1, keepdims=True)
    owner = first[:, None] + ((2 * done + half_work) * chips[:, None]) // (2 * total)
    my_slot = jnp.sum(jnp.where(on_chip[chip], jnp.arange(PLANE_HEADS), 0))
    my_head = chip_heads[chip]
    mine_tiles = (owner[my_slot] == chip).astype(jnp.int32).reshape(CHIPS, 2)
    allowed = lax.dynamic_index_in_dim(tile_mask, my_head, 0, keepdims=False)
    allowed = lax.dynamic_index_in_dim(allowed.reshape(CHIPS, 2, 2, 4 * CHIPS), core, 1, keepdims=False)
    source = lax.dynamic_slice_in_dim(owner, 2 * chip, 2, 1)

    w_heads = w_out.reshape(HEADS, TILE, w_out.shape[1])
    weights = []
    for ahead in (0, 3, 1, 2):
        w_order = lax.dynamic_slice_in_dim(head_at, (plane + ahead) % PLANES * PLANE_HEADS, PLANE_HEADS)
        weights.append(jnp.take(w_heads, w_order, axis=0, mode="clip").reshape(PLANE_HEADS * TILE, -1))
    lists = [item_lists(allowed[:, sub], mine_tiles[:, sub]) for sub in range(2)]
    got, lists, weights = lax.optimization_barrier((got, lists, weights))
    got_other = swap(got)

    halves = []
    for sub in range(2):
        steps, q_of, k_of, valid = lists[sub]
        meta = jnp.stack([core, steps, jnp.int32(sub)]).astype(jnp.int32)
        attended = attend(meta, q_of, k_of, valid, got, got_other)
        own = select(source[:, sub], exchange(attended))
        blocks = [own, along_y(own, 1), along_y(own, 3), along_y(own, 2)]
        total = jnp.zeros((2 * TILE, w_out.shape[1]), jnp.float32)
        for k, block in enumerate(blocks):
            both = jnp.concatenate([block, swap(block)], axis=0)
            total = total + jnp.dot(both, weights[k], preferred_element_type=jnp.float32)
        halves.append(total.reshape(2, TILE, -1))
    mine, theirs = (jnp.concatenate([halves[0][i], halves[1][i]], axis=0) for i in range(2))
    low = jnp.where(core == 0, mine, theirs)
    high = jnp.where(core == 0, theirs, mine)
    projected = jnp.concatenate([low, high], axis=0)
    return (residual_in.astype(jnp.float32) + gate_scale * projected).astype(jnp.bfloat16)


def solution(mesh):
    fine = Mesh(mesh.devices.reshape(4, 4, 4, 2), ("x", "z", "y", "c"))
    seq, rep = TOKENS_AXES, ("y", "c")
    in_specs = (
        P(seq, rep),
        P(seq, None),
        P(seq, None),
        P(seq, None),
        P(None, rep),
        P(rep),
        P(),
    )
    return jax.shard_map(shards, mesh=fine, in_specs=in_specs, out_specs=P(seq, rep), check_vma=False)
```

profile of v0, /device:TPU:1, one launch (start us, length us, event | category | flops | bytes accessed | tf_op | source)
XLA Modules:
  0.0 157.9 jit_solution(9370505845305581173)
XLA Ops:
  0.0 2.8 %fusion.72 = (s32[40,64]{1,0:T(8,128)S(1)}, s32[40]{0:T(128)S(1)}) fusion(s32[40,64,64]{2,1,0:T(8,128)} %param.13), kind=kLoop, calls=%fused_computation.196 | loop fusion | flops 325080 | bytes 665760 | tf_op jit(solution)/shard_map/reduce_sum | solution.py:226
  4.2 2.5 %copy-done.3 = bf16[512,5120]{1,0:T(8,128)(2,1)S(1)} copy-done((bf16[512,5120]{1,0:T(8,128)(2,1)S(1)}, bf16[512,5120]{1,0:T(8,128)(2,1)}, u32[]{:S(2)}) %copy-start.3) | copy-done | bytes 5242904
  6.7 2.5 %copy-done.4 = bf16[512,5120]{1,0:T(8,128)(2,1)S(1)} copy-done((bf16[512,5120]{1,0:T(8,128)(2,1)S(1)}, bf16[512,5120]{1,0:T(8,128)(2,1)}, u32[]{:S(2)}) %copy-start.4) | copy-done | bytes 5242904
  9.2 2.5 %copy-done.5 = bf16[512,5120]{1,0:T(8,128)(2,1)S(1)} copy-done((bf16[512,5120]{1,0:T(8,128)(2,1)S(1)}, bf16[512,5120]{1,0:T(8,128)(2,1)}, u32[]{:S(2)}) %copy-start.5) | copy-done | bytes 5242904
  11.7 7.6 %shard_map.73 = bf16[16,3,256,128]{3,2,1,0:T(8,128)(2,1)S(1)} custom-call(s32[17]{0:T(128)S(1)} %pad_add_fusion.heads, bf16[512,5120]{1,0:T(8,128)(2,1)S(1)} %copy-done.3, bf16[512,5120]{1,0:T(8,128)(2,1)S(1)} %copy-done.4, bf16[512,5120]{1,0:T(8,128)(2,1)S(1)} %copy-done.5), custom_call_target="tpu_custom_call" | custom-call | tf_op jit(solution)/shard_map/pallas_call | solution.py:76
  21.0 8.4 %all-to-all-start = ((bf16[16,3,256,128]{3,2,1,0:T(8,128)(2,1)}), bf16[16,3,256,128]{3,2,1,0:T(8,128)(2,1)S(1)}, u32[]{:S(2)}, u32[]{:S(2)}) async-start(bf16[16,3,256,128]{3,2,1,0:T(8,128)(2,1)} %copy-done.2), calls=%async_computation | async-start | bytes 6291456 | tf_op jit(solution)/shard_map/all_to_all | solution.py:211
  44.7 4.9 %gather_fusion.2 = bf16[10,128,640]{2,1,0:T(8,128)(2,1)} fusion(bf16[40,128,640]{2,1,0:T(8,128)(2,1)} %bitcast.45, s32[1024]{0:T(1024)S(1)} %get-tuple-element.83), kind=kCustom, calls=%fused_computation.2 | custom fusion | bytes 3276840 | tf_op jit(solution)/shard_map/jit(_take)/gather | solution.py:254
  49.6 4.9 %gather_fusion.4 = bf16[10,128,640]{2,1,0:T(8,128)(2,1)} fusion(bf16[40,128,640]{2,1,0:T(8,128)(2,1)} %bitcast.46, s32[1024]{0:T(1024)S(1)} %get-tuple-element.81), kind=kCustom, calls=%fused_computation.4 | custom fusion | bytes 3276840 | tf_op jit(solution)/shard_map/jit(_take)/gather | solution.py:254
  54.5 5.0 %gather_fusion.1 = bf16[10,128,640]{2,1,0:T(8,128)(2,1)} fusion(bf16[40,128,640]{2,1,0:T(8,128)(2,1)} %bitcast.47, s32[1024]{0:T(1024)S(1)} %get-tuple-element.84), kind=kCustom, calls=%fused_computation.1 | custom fusion | bytes 3276840 | tf_op jit(solution)/shard_map/jit(_take)/gather | solution.py:254
  59.5 4.9 %gather_fusion.3 = bf16[10,128,640]{2,1,0:T(8,128)(2,1)} fusion(bf16[40,128,640]{2,1,0:T(8,128)(2,1)} %bitcast.48, s32[1024]{0:T(1024)S(1)} %get-tuple-element.82), kind=kCustom, calls=%fused_computation.3 | custom fusion | bytes 3276840 | tf_op jit(solution)/shard_map/jit(_take)/gather | solution.py:254
  64.3 5.3 %all-to-all-done = bf16[16,3,256,128]{3,2,1,0:T(8,128)(2,1)S(1)} async-done(((bf16[16,3,256,128]{3,2,1,0:T(8,128)(2,1)}), bf16[16,3,256,128]{3,2,1,0:T(8,128)(2,1)S(1)}, u32[]{:S(2)}, u32[]{:S(2)}) %all-to-all-start) | async-done | bytes 3145760 | tf_op jit(solution)/shard_map/all_to_all | solution.py:211
  69.7 3.1 %collective-permute-start = (bf16[16,6,128,128]{3,2,1,0:T(8,128)(2,1)S(1)}, bf16[16,6,128,128]{3,2,1,0:T(8,128)(2,1)S(1)}, u32[]{:S(2)}, u32[]{:S(2)}) collective-permute-start(bf16[16,6,128,128]{3,2,1,0:T(8,128)(2,1)S(1)} %bitcast.38), channel_id=1, source_target_pairs={{0,1},{1,0},{2,3},{3,2},{4,5},{5,4},{6,7},{7,6},{8,9},{9,8},{10,11... | collective-permute-start | bytes 9437192 | tf_op jit(solution)/shard_map/ppermute | solution.py:219
  72.9 5.2 %collective-permute-done.other_ref = bf16[16,6,128,128]{3,2,1,0:T(8,128)(2,1)S(1)} collective-permute-done((bf16[16,6,128,128]{3,2,1,0:T(8,128)(2,1)S(1)}, bf16[16,6,128,128]{3,2,1,0:T(8,128)(2,1)S(1)}, u32[]{:S(2)}, u32[]{:S(2)}) %collective-permute-start) | collective-permute-done | bytes 3145760 | tf_op jit(solution)/shard_map/ppermute | solution.py:219
  78.1 6.7 %shard_map.76 = bf16[16,128,128]{2,1,0:T(8,128)(2,1)S(1)} custom-call(s32[3]{0:T(128)S(1)} %pad_add_fusion.2.meta, s32[256]{0:T(256)S(1)} %broadcast_minimum_fusion.q_of, s32[1024]{0:T(1024)S(1)} %convert_element_type.110.k_of, s32[256]{0:T(256)S(1)} %get-tuple-element.30.valid_of, bf16[16,6,128,128]{3,2,1,0:T(8,128)(2,1)S(1)} %bitcast.39, ...), custom_call_target="tpu_custom_call" | custom-call | tf_op jit(solution)/shard_map/pallas_call | solution.py:149
  87.3 7.6 %all-to-all-start.2 = ((bf16[16,128,128]{2,1,0:T(8,128)(2,1)}), bf16[16,128,128]{2,1,0:T(8,128)(2,1)}, u32[]{:S(2)}, u32[]{:S(2)}) async-start(bf16[16,128,128]{2,1,0:T(8,128)(2,1)} %copy-done.7), calls=%async_computation.2 | async-start | bytes 1048576 | tf_op jit(solution)/shard_map/all_to_all | solution.py:211
  96.9 10.8 %shard_map.74 = bf16[16,128,128]{2,1,0:T(8,128)(2,1)S(1)} custom-call(s32[3]{0:T(128)S(1)} %pad_add_fusion.1.meta, s32[256]{0:T(256)S(1)} %broadcast_minimum_fusion.1.q_of, s32[1024]{0:T(1024)S(1)} %convert_element_type.104.k_of, s32[256]{0:T(256)S(1)} %get-tuple-element.21.valid_of, bf16[16,6,128,128]{3,2,1,0:T(8,128)(2,1)S(1)} %bitcast.40, ...), custom_call_target="tpu_custom_call" | custom-call | tf_op jit(solution)/shard_map/pallas_call | solution.py:149
  108.5 5.2 %all-to-all-start.1 = ((bf16[16,128,128]{2,1,0:T(8,128)(2,1)}), bf16[16,128,128]{2,1,0:T(8,128)(2,1)S(1)}, u32[]{:S(2)}, u32[]{:S(2)}) async-start(bf16[16,128,128]{2,1,0:T(8,128)(2,1)} %copy-done.6), calls=%async_computation.1 | async-start | bytes 1048576 | tf_op jit(solution)/shard_map/all_to_all | solution.py:211
  114.5 1.9 %shard_map.77 = bf16[128,1280]{1,0:T(8,128)(2,1)} custom-call(s32[10]{0:T(128)} %get-tuple-element.38.source, bf16[16,128,128]{2,1,0:T(8,128)(2,1)} %all-to-all-done.2.got_ref), custom_call_target="tpu_custom_call" | custom-call | tf_op jit(solution)/shard_map/pallas_call | solution.py:202
  116.4 3.3 %collective-permute-start.13 = (bf16[128,1280]{1,0:T(8,128)(2,1)}, bf16[128,1280]{1,0:T(8,128)(2,1)S(1)}, u32[]{:S(2)}, u32[]{:S(2)}) collective-permute-start(bf16[128,1280]{1,0:T(8,128)(2,1)} %shard_map.77), channel_id=1, source_target_pairs={{0,4},{2,6},{4,0},{6,2},{1,5},{3,7},{5,1},{7,3},{8,12},{10,14},{12... | collective-permute-start | bytes 983048 | tf_op jit(solution)/shard_map/ppermute | solution.py:215
  121.2 3.1 %collective-permute-start.8 = (bf16[128,1280]{1,0:T(8,128)(2,1)}, bf16[128,1280]{1,0:T(8,128)(2,1)S(1)}, u32[]{:S(2)}, u32[]{:S(2)}) collective-permute-start(bf16[128,1280]{1,0:T(8,128)(2,1)} %shard_map.77), channel_id=1, source_target_pairs={{0,1},{1,0},{2,3},{3,2},{4,5},{5,4},{6,7},{7,6},{8,9},{9,8},{10,11... | collective-permute-start | bytes 983048 | tf_op jit(solution)/shard_map/ppermute | solution.py:219
  128.9 3.3 %collective-permute-start.6 = (bf16[128,1280]{1,0:T(8,128)(2,1)}, bf16[128,1280]{1,0:T(8,128)(2,1)S(1)}, u32[]{:S(2)}, u32[]{:S(2)}) collective-permute-start(bf16[128,1280]{1,0:T(8,128)(2,1)} %shard_map.75), channel_id=1, source_target_pairs={{0,4},{2,6},{4,0},{6,2},{1,5},{3,7},{5,1},{7,3},{8,12},{10,14},{12... | collective-permute-start | bytes 983048 | tf_op jit(solution)/shard_map/ppermute | solution.py:215
  132.2 3.2 %collective-permute-done.11 = bf16[128,1280]{1,0:T(8,128)(2,1)S(1)} collective-permute-done((bf16[128,1280]{1,0:T(8,128)(2,1)}, bf16[128,1280]{1,0:T(8,128)(2,1)S(1)}, u32[]{:S(2)}, u32[]{:S(2)}) %collective-permute-start.11) | collective-permute-done | bytes 327712 | tf_op jit(solution)/shard_map/ppermute | solution.py:215
  135.5 3.8 %collective-permute-start.4 = (bf16[128,1280]{1,0:T(8,128)(2,1)}, bf16[128,1280]{1,0:T(8,128)(2,1)S(1)}, u32[]{:S(2)}, u32[]{:S(2)}) collective-permute-start(bf16[128,1280]{1,0:T(8,128)(2,1)} %shard_map.75), channel_id=1, source_target_pairs={{0,6},{2,0},{4,2},{6,4},{1,7},{3,1},{5,3},{7,5},{8,14},{10,8},{12,... | collective-permute-start | bytes 983048 | tf_op jit(solution)/shard_map/ppermute | solution.py:215
  144.3 4.1 %collective-permute-done.4 = bf16[128,1280]{1,0:T(8,128)(2,1)S(1)} collective-permute-done((bf16[128,1280]{1,0:T(8,128)(2,1)}, bf16[128,1280]{1,0:T(8,128)(2,1)S(1)}, u32[]{:S(2)}, u32[]{:S(2)}) %collective-permute-start.4) | collective-permute-done | bytes 327712 | tf_op jit(solution)/shard_map/ppermute | solution.py:215
  (142 shorter events, 38.6 us)
Async XLA Ops:
  4.2 2.5 %copy-start.3 = (bf16[512,5120]{1,0:T(8,128)(2,1)S(1)}, bf16[512,5120]{1,0:T(8,128)(2,1)}, u32[]{:S(2)}) copy-start(bf16[512,5120]{1,0:T(8,128)(2,1)} %q_ref.1) | copy-start | bytes 15728644
  6.7 2.5 %copy-start.4 = (bf16[512,5120]{1,0:T(8,128)(2,1)S(1)}, bf16[512,5120]{1,0:T(8,128)(2,1)}, u32[]{:S(2)}) copy-start(bf16[512,5120]{1,0:T(8,128)(2,1)} %k_ref.1) | copy-start | bytes 15728644
  21.0 48.7 %all-to-all-start = ((bf16[16,3,256,128]{3,2,1,0:T(8,128)(2,1)}), bf16[16,3,256,128]{3,2,1,0:T(8,128)(2,1)S(1)}, u32[]{:S(2)}, u32[]{:S(2)}) async-start(bf16[16,3,256,128]{3,2,1,0:T(8,128)(2,1)} %copy-done.2), calls=%async_computation | async-start | bytes 6291456 | tf_op jit(solution)/shard_map/all_to_all | solution.py:211
  69.7 8.4 %collective-permute-start = (bf16[16,6,128,128]{3,2,1,0:T(8,128)(2,1)S(1)}, bf16[16,6,128,128]{3,2,1,0:T(8,128)(2,1)S(1)}, u32[]{:S(2)}, u32[]{:S(2)}) collective-permute-start(bf16[16,6,128,128]{3,2,1,0:T(8,128)(2,1)S(1)} %bitcast.38), channel_id=1, source_target_pairs={{0,1},{1,0},{2,3},{3,2},{4,5},{5,4},{6,7},{7,6},{8,9},{9,8},{10,11... | collective-permute-start | bytes 9437192 | tf_op jit(solution)/shard_map/ppermute | solution.py:219
  87.3 21.2 %all-to-all-start.2 = ((bf16[16,128,128]{2,1,0:T(8,128)(2,1)}), bf16[16,128,128]{2,1,0:T(8,128)(2,1)}, u32[]{:S(2)}, u32[]{:S(2)}) async-start(bf16[16,128,128]{2,1,0:T(8,128)(2,1)} %copy-done.7), calls=%async_computation.2 | async-start | bytes 1048576 | tf_op jit(solution)/shard_map/all_to_all | solution.py:211
  108.5 31.7 %copy-start.12 = (bf16[10,128,640]{2,1,0:T(8,128)(2,1)S(1)}, bf16[10,128,640]{2,1,0:T(8,128)(2,1)}, u32[]{:S(2)}) copy-start(bf16[10,128,640]{2,1,0:T(8,128)(2,1)} %gather_fusion.1) | copy-start | bytes 4915204
  108.5 15.8 %all-to-all-start.1 = ((bf16[16,128,128]{2,1,0:T(8,128)(2,1)}), bf16[16,128,128]{2,1,0:T(8,128)(2,1)S(1)}, u32[]{:S(2)}, u32[]{:S(2)}) async-start(bf16[16,128,128]{2,1,0:T(8,128)(2,1)} %copy-done.6), calls=%async_computation.1 | async-start | bytes 1048576 | tf_op jit(solution)/shard_map/all_to_all | solution.py:211
  116.4 12.5 %collective-permute-start.13 = (bf16[128,1280]{1,0:T(8,128)(2,1)}, bf16[128,1280]{1,0:T(8,128)(2,1)S(1)}, u32[]{:S(2)}, u32[]{:S(2)}) collective-permute-start(bf16[128,1280]{1,0:T(8,128)(2,1)} %shard_map.77), channel_id=1, source_target_pairs={{0,4},{2,6},{4,0},{6,2},{1,5},{3,7},{5,1},{7,3},{8,12},{10,14},{12... | collective-permute-start | bytes 983048 | tf_op jit(solution)/shard_map/ppermute | solution.py:215
  119.7 15.8 %collective-permute-start.11 = (bf16[128,1280]{1,0:T(8,128)(2,1)}, bf16[128,1280]{1,0:T(8,128)(2,1)S(1)}, u32[]{:S(2)}, u32[]{:S(2)}) collective-permute-start(bf16[128,1280]{1,0:T(8,128)(2,1)} %shard_map.77), channel_id=1, source_target_pairs={{0,6},{2,0},{4,2},{6,4},{1,7},{3,1},{5,3},{7,5},{8,14},{10,8},{12,... | collective-permute-start | bytes 983048 | tf_op jit(solution)/shard_map/ppermute | solution.py:215
  120.1 19.2 %collective-permute-start.9 = (bf16[128,1280]{1,0:T(8,128)(2,1)}, bf16[128,1280]{1,0:T(8,128)(2,1)S(1)}, u32[]{:S(2)}, u32[]{:S(2)}) collective-permute-start(bf16[128,1280]{1,0:T(8,128)(2,1)} %shard_map.77), channel_id=1, source_target_pairs={{0,2},{2,4},{4,6},{6,0},{1,3},{3,5},{5,7},{7,1},{8,10},{10,12},{12... | collective-permute-start | bytes 983048 | tf_op jit(solution)/shard_map/ppermute | solution.py:215
  121.2 18.1 %collective-permute-start.8 = (bf16[128,1280]{1,0:T(8,128)(2,1)}, bf16[128,1280]{1,0:T(8,128)(2,1)S(1)}, u32[]{:S(2)}, u32[]{:S(2)}) collective-permute-start(bf16[128,1280]{1,0:T(8,128)(2,1)} %shard_map.77), channel_id=1, source_target_pairs={{0,1},{1,0},{2,3},{3,2},{4,5},{5,4},{6,7},{7,6},{8,9},{9,8},{10,11... | collective-permute-start | bytes 983048 | tf_op jit(solution)/shard_map/ppermute | solution.py:219
  127.0 15.0 %copy-start.14 = (bf16[128,1280]{1,0:T(8,128)(2,1)S(1)}, bf16[128,1280]{1,0:T(8,128)(2,1)}, u32[]{:S(2)}) copy-start(bf16[128,1280]{1,0:T(8,128)(2,1)} %shard_map.75) | copy-start | bytes 983044
  127.0 14.9 %collective-permute-start.1 = (bf16[128,1280]{1,0:T(8,128)(2,1)}, bf16[128,1280]{1,0:T(8,128)(2,1)}, u32[]{:S(2)}, u32[]{:S(2)}) collective-permute-start(bf16[128,1280]{1,0:T(8,128)(2,1)} %shard_map.75), channel_id=1, source_target_pairs={{0,1},{1,0},{2,3},{3,2},{4,5},{5,4},{6,7},{7,6},{8,9},{9,8},{10,11... | collective-permute-start | bytes 983048 | tf_op jit(solution)/shard_map/ppermute | solution.py:219
  128.9 14.9 %collective-permute-start.6 = (bf16[128,1280]{1,0:T(8,128)(2,1)}, bf16[128,1280]{1,0:T(8,128)(2,1)S(1)}, u32[]{:S(2)}, u32[]{:S(2)}) collective-permute-start(bf16[128,1280]{1,0:T(8,128)(2,1)} %shard_map.75), channel_id=1, source_target_pairs={{0,4},{2,6},{4,0},{6,2},{1,5},{3,7},{5,1},{7,3},{8,12},{10,14},{12... | collective-permute-start | bytes 983048 | tf_op jit(solution)/shard_map/ppermute | solution.py:215
  135.5 12.9 %collective-permute-start.4 = (bf16[128,1280]{1,0:T(8,128)(2,1)}, bf16[128,1280]{1,0:T(8,128)(2,1)S(1)}, u32[]{:S(2)}, u32[]{:S(2)}) collective-permute-start(bf16[128,1280]{1,0:T(8,128)(2,1)} %shard_map.75), channel_id=1, source_target_pairs={{0,6},{2,0},{4,2},{6,4},{1,7},{3,1},{5,3},{7,5},{8,14},{10,8},{12,... | collective-permute-start | bytes 983048 | tf_op jit(solution)/shard_map/ppermute | solution.py:215
  139.3 10.8 %collective-permute-start.2 = (bf16[128,1280]{1,0:T(8,128)(2,1)}, bf16[128,1280]{1,0:T(8,128)(2,1)S(1)}, u32[]{:S(2)}, u32[]{:S(2)}) collective-permute-start(bf16[128,1280]{1,0:T(8,128)(2,1)} %shard_map.75), channel_id=1, source_target_pairs={{0,2},{2,4},{4,6},{6,0},{1,3},{3,5},{5,7},{7,1},{8,10},{10,12},{12... | collective-permute-start | bytes 983048 | tf_op jit(solution)/shard_map/ppermute | solution.py:215
  139.3 11.5 %collective-permute-start.10 = (bf16[128,1280]{1,0:T(8,128)(2,1)S(1)}, bf16[128,1280]{1,0:T(8,128)(2,1)S(1)}, u32[]{:S(2)}, u32[]{:S(2)}) collective-permute-start(bf16[128,1280]{1,0:T(8,128)(2,1)S(1)} %collective-permute-done.9), channel_id=1, source_target_pairs={{0,1},{1,0},{2,3},{3,2},{4,5},{5,4},{6,7},{7,6},{8,9},{9,8},{10,11... | collective-permute-start | bytes 983048 | tf_op jit(solution)/shard_map/ppermute | solution.py:219
  141.9 8.9 %copy-start.8 = (bf16[10,128,640]{2,1,0:T(8,128)(2,1)S(1)}, bf16[10,128,640]{2,1,0:T(8,128)(2,1)}, u32[]{:S(2)}) copy-start(bf16[10,128,640]{2,1,0:T(8,128)(2,1)} %gather_fusion.2) | copy-start | bytes 4915204
  141.9 9.6 %collective-permute-start.14 = (bf16[128,1280]{1,0:T(8,128)(2,1)S(1)}, bf16[128,1280]{1,0:T(8,128)(2,1)S(1)}, u32[]{:S(2)}, u32[]{:S(2)}) collective-permute-start(bf16[128,1280]{1,0:T(8,128)(2,1)S(1)} %collective-permute-done.13), channel_id=1, source_target_pairs={{0,1},{1,0},{2,3},{3,2},{4,5},{5,4},{6,7},{7,6},{8,9},{9,8},{10,11... | collective-permute-start | bytes 983048 | tf_op jit(solution)/shard_map/ppermute | solution.py:219
  143.8 7.8 %copy-start.11 = (bf16[10,128,640]{2,1,0:T(8,128)(2,1)S(1)}, bf16[10,128,640]{2,1,0:T(8,128)(2,1)}, u32[]{:S(2)}) copy-start(bf16[10,128,640]{2,1,0:T(8,128)(2,1)} %gather_fusion.4) | copy-start | bytes 4915204
  143.8 8.4 %collective-permute-start.12 = (bf16[128,1280]{1,0:T(8,128)(2,1)S(1)}, bf16[128,1280]{1,0:T(8,128)(2,1)S(1)}, u32[]{:S(2)}, u32[]{:S(2)}) collective-permute-start(bf16[128,1280]{1,0:T(8,128)(2,1)S(1)} %collective-permute-done.11), channel_id=1, source_target_pairs={{0,1},{1,0},{2,3},{3,2},{4,5},{5,4},{6,7},{7,6},{8,9},{9,8},{10,11... | collective-permute-start | bytes 983048 | tf_op jit(solution)/shard_map/ppermute | solution.py:219
  148.3 5.3 %collective-permute-start.7 = (bf16[128,1280]{1,0:T(8,128)(2,1)S(1)}, bf16[128,1280]{1,0:T(8,128)(2,1)S(1)}, u32[]{:S(2)}, u32[]{:S(2)}) collective-permute-start(bf16[128,1280]{1,0:T(8,128)(2,1)S(1)} %collective-permute-done.6), channel_id=1, source_target_pairs={{0,1},{1,0},{2,3},{3,2},{4,5},{5,4},{6,7},{7,6},{8,9},{9,8},{10,11... | collective-permute-start | bytes 983048 | tf_op jit(solution)/shard_map/ppermute | solution.py:219
  150.1 5.0 %collective-permute-start.5 = (bf16[128,1280]{1,0:T(8,128)(2,1)S(1)}, bf16[128,1280]{1,0:T(8,128)(2,1)S(1)}, u32[]{:S(2)}, u32[]{:S(2)}) collective-permute-start(bf16[128,1280]{1,0:T(8,128)(2,1)S(1)} %collective-permute-done.4), channel_id=1, source_target_pairs={{0,1},{1,0},{2,3},{3,2},{4,5},{5,4},{6,7},{7,6},{8,9},{9,8},{10,11... | collective-permute-start | bytes 983048 | tf_op jit(solution)/shard_map/ppermute | solution.py:219
  150.8 3.6 %collective-permute-start.3 = (bf16[128,1280]{1,0:T(8,128)(2,1)S(1)}, bf16[128,1280]{1,0:T(8,128)(2,1)S(1)}, u32[]{:S(2)}, u32[]{:S(2)}) collective-permute-start(bf16[128,1280]{1,0:T(8,128)(2,1)S(1)} %collective-permute-done.2), channel_id=1, source_target_pairs={{0,1},{1,0},{2,3},{3,2},{4,5},{5,4},{6,7},{7,6},{8,9},{9,8},{10,11... | collective-permute-start | bytes 983048 | tf_op jit(solution)/shard_map/ppermute | solution.py:219
  (10 other events, 13.7 us)
where the time goes:
time: 161 us; the launch traced here: 158 us
  starting transfers between devices  45.3 us (28%)
  local copies, waits for them, and re-layouts  41.4 us (26%)
  Pallas kernels  29 us (18%)
  waiting for transfers between devices  17.9 us (11%)
  other arithmetic  9.82 us (6%)
  matrix products  7.9 us (5%)
  between operations  6.6 us (4%)
    all_to_all x3, starting transfers between devices, exchange(): lax.all_to_all(block, TOKENS_AXES, split_axis=0, concat_axis=0, tiled=True)  21.3 us
    gather x4, local copies, waits for them, and re-layouts, shards(): jnp.take(w_heads, w_order, axis=0, mode='clip')  19.6 us
    pallas_call x2, Pallas kernels, attend(): pl.pallas_call(functools.partial(attend_kernel, TILE ** (-0.5) * LOG2E),...  17.5 us
    unnamed x32, local copies, waits for them, and re-layouts  16.7 us
    ppermute x9, starting transfers between devices, swap(): return lax.ppermute(block, 'c', [(0, 1), (1, 0)])  12.1 us
    ppermute x6, starting transfers between devices, along_y(): lax.ppermute(block, 'y', [(i, (i + step) % PLANES) for i in range(PLANES)])  11.9 us
    pallas_call x1, Pallas kernels, pack(): pl.pallas_call(pack_kernel, in_specs=[pl.BlockSpec(memory_space=pltpu.SME...  7.6 us
    dot_general x8, matrix products, shards(): jnp.dot(both, weights[k], preferred_element_type=jnp.float32)  7.51 us
  transfers between devices with their start and end apart: 18, of which 4 were waited for; matrix products, arithmetic and copies ran while one was open for 23% of the time, Pallas kernels for 9%

commit v1 on v0

--- a/solution.py
+++ b/solution.py
@@ -15,7 +15,7 @@
 CHIPS = 16
 HALF = 256
 GROUP = 4
-UNROLL = 8
+UNROLL = 16
 ITEMS = 256
 LOG2E = 1.4426950408889634
 TOKENS_AXES = ("x", "z")
@@ -84,7 +84,7 @@
             pltpu.SemaphoreType.DMA((CHIPS, 3)),
             pltpu.SemaphoreType.DMA((CHIPS, 3)),
         ],
-        compiler_params=pltpu.CompilerParams(vmem_limit_bytes=16 * 2**20),
+        compiler_params=pltpu.CompilerParams(vmem_limit_bytes=60 * 2**20),
     )(scalars, queries, keys, values)
 
 
@@ -159,7 +159,7 @@
             pltpu.VMEM((CHIPS, 1, TILE), jnp.float32),
             pltpu.SemaphoreType.DMA((3,)),
         ],
-        compiler_params=pltpu.CompilerParams(vmem_limit_bytes=40 * 2**20),
+        compiler_params=pltpu.CompilerParams(vmem_limit_bytes=60 * 2**20),
     )(meta, q_of, k_of, valid_of, own, other)
 
 

time: 161 us -> 148 us (0.919); the launches traced: 158 us -> 147 us
  local copies, waits for them, and re-layouts: 41.4 us -> 28.4 us
  waiting for transfers between devices: 17.9 us -> 20.9 us
  other arithmetic: 9.82 us -> 12.1 us
  starting transfers between devices: 45.3 us -> 43.1 us
    unnamed x32 -> x24, local copies, waits for them, and re-layouts: 16.7 us -> 2.51 us
    ppermute x6, starting transfers between devices: 11.9 us -> 5.24 us  [along_y(): lax.ppermute(block, 'y', [(i, (i + step) % PLANES) for i in range(PLANES)])]
    all_to_all x3, starting transfers between devices: 21.3 us -> 26 us  [exchange(): lax.all_to_all(block, TOKENS_AXES, split_axis=0, concat_axis=0, tiled=True)]
    ppermute x6, waiting for transfers between devices: 7.32 us -> 10.9 us  [along_y(): lax.ppermute(block, 'y', [(i, (i + step) % PLANES) for i in range(PLANES)])]
    pallas_call x1, Pallas kernels: 7.6 us -> 4.77 us  [pack(): pl.pallas_call(pack_kernel, in_specs=[pl.BlockSpec(memory_space=pltpu.SME...]
    pallas_call x2, Pallas kernels: 17.5 us -> 19.4 us  [attend(): pl.pallas_call(functools.partial(attend_kernel, TILE ** (-0.5) * LOG2E),...]
  transfers between devices with their start and end apart: 18 -> 18, of which waited for: 4 -> 5; matrix products, arithmetic and copies ran while one was open for 23% -> 27% of each run, Pallas kernels for 9% -> 10%
where the time goes in v1:
time: 148 us; the launch traced here: 147 us
  starting transfers between devices  43.1 us (29%)
  local copies, waits for them, and re-layouts  28.4 us (19%)
  Pallas kernels  28 us (19%)
  waiting for transfers between devices  20.9 us (14%)
  other arithmetic  12.1 us (8%)
  matrix products  8 us (5%)
  between operations  6.74 us (5%)
    all_to_all x3, starting transfers between devices, exchange(): lax.all_to_all(block, TOKENS_AXES, split_axis=0, concat_axis=0, tiled=True)  26 us
    gather x4, local copies, waits for them, and re-layouts, shards(): jnp.take(w_heads, w_order, axis=0, mode='clip')  19.6 us
    pallas_call x2, Pallas kernels, attend(): pl.pallas_call(functools.partial(attend_kernel, TILE ** (-0.5) * LOG2E),...  19.4 us
    ppermute x9, starting transfers between devices, swap(): return lax.ppermute(block, 'c', [(0, 1), (1, 0)])  11.8 us
    ppermute x6, waiting for transfers between devices, along_y(): lax.ppermute(block, 'y', [(i, (i + step) % PLANES) for i in range(PLANES)])  10.9 us
    dot_general x8, matrix products, shards(): jnp.dot(both, weights[k], preferred_element_type=jnp.float32)  7.61 us
    ppermute x6, starting transfers between devices, along_y(): lax.ppermute(block, 'y', [(i, (i + step) % PLANES) for i in range(PLANES)])  5.24 us
    all_to_all x3, waiting for transfers between devices, exchange(): lax.all_to_all(block, TOKENS_AXES, split_axis=0, concat_axis=0, tiled=True)  5.22 us
  transfers between devices with their start and end apart: 18, of which 5 were waited for; matrix products, arithmetic and copies ran while one was open for 27% of the time, Pallas kernels for 10%

profile of v1, /device:TPU:1, one launch (start us, length us, event | category | flops | bytes accessed | tf_op | source)
XLA Modules:
  0.0 147.3 jit_solution(10746489448568680254)
XLA Ops:
  0.0 2.8 %fusion.72 = (s32[40,64]{1,0:T(8,128)S(1)}, s32[40]{0:T(128)S(1)}) fusion(s32[40,64,64]{2,1,0:T(8,128)} %param.13), kind=kLoop, calls=%fused_computation.196 | loop fusion | flops 325080 | bytes 665760 | tf_op jit(solution)/shard_map/reduce_sum | solution.py:226
  4.7 4.8 %shard_map.73 = bf16[16,3,256,128]{3,2,1,0:T(8,128)(2,1)} custom-call(s32[17]{0:T(128)} %pad_add_fusion.heads, bf16[512,5120]{1,0:T(8,128)(2,1)} %q_ref.1, bf16[512,5120]{1,0:T(8,128)(2,1)} %k_ref.1, bf16[512,5120]{1,0:T(8,128)(2,1)} %v_ref.1), custom_call_target="tpu_custom_call" | custom-call | tf_op jit(solution)/shard_map/pallas_call | solution.py:76
  9.5 8.4 %all-to-all-start = ((bf16[16,3,256,128]{3,2,1,0:T(8,128)(2,1)}), bf16[16,3,256,128]{3,2,1,0:T(8,128)(2,1)S(1)}, u32[]{:S(2)}, u32[]{:S(2)}) async-start(bf16[16,3,256,128]{3,2,1,0:T(8,128)(2,1)} %shard_map.73), calls=%async_computation | async-start | bytes 6291456 | tf_op jit(solution)/shard_map/all_to_all | solution.py:211
  31.2 1.9 %compare_select_fusion.4 = (s32[256]{0:T(256)}, s32[256]{0:T(256)S(1)}, s32[256]{0:T(256)S(1)}, s32[256]{0:T(256)}, s32[256]{0:T(256)S(1)}, /*index=5*/s32[256]{0:T(256)S(1)}) fusion(s32[]{:T(128)} %bitcast.10, s32[256]{0:T(256)S(1)} %get-tuple-element.42, s32[256]{0:T(256)S(1)} %get-tuple-element.41, s32[]{:T(128)S(6)} %sub.138, ...), kind=kLoop, calls=%fused_computation.132 | loop fusion | flops 4096 | bytes 10256 | tf_op jit(solution)/shard_map/mul | solution.py:191
  35.4 4.9 %gather_fusion.2 = bf16[10,128,640]{2,1,0:T(8,128)(2,1)} fusion(bf16[40,128,640]{2,1,0:T(8,128)(2,1)} %bitcast.45, s32[1024]{0:T(1024)S(1)} %get-tuple-element.83), kind=kCustom, calls=%fused_computation.2 | custom fusion | bytes 3276840 | tf_op jit(solution)/shard_map/jit(_take)/gather | solution.py:254
  40.3 4.9 %gather_fusion.4 = bf16[10,128,640]{2,1,0:T(8,128)(2,1)} fusion(bf16[40,128,640]{2,1,0:T(8,128)(2,1)} %bitcast.46, s32[1024]{0:T(1024)S(1)} %get-tuple-element.81), kind=kCustom, calls=%fused_computation.4 | custom fusion | bytes 3276840 | tf_op jit(solution)/shard_map/jit(_take)/gather | solution.py:254
  45.2 4.9 %gather_fusion.1 = bf16[10,128,640]{2,1,0:T(8,128)(2,1)} fusion(bf16[40,128,640]{2,1,0:T(8,128)(2,1)} %bitcast.47, s32[1024]{0:T(1024)S(1)} %get-tuple-element.84), kind=kCustom, calls=%fused_computation.1 | custom fusion | bytes 3276840 | tf_op jit(solution)/shard_map/jit(_take)/gather | solution.py:254
  50.1 4.9 %gather_fusion.3 = bf16[10,128,640]{2,1,0:T(8,128)(2,1)} fusion(bf16[40,128,640]{2,1,0:T(8,128)(2,1)} %bitcast.48, s32[1024]{0:T(1024)S(1)} %get-tuple-element.82), kind=kCustom, calls=%fused_computation.3 | custom fusion | bytes 3276840 | tf_op jit(solution)/shard_map/jit(_take)/gather | solution.py:254
  54.9 3.6 %all-to-all-done = bf16[16,3,256,128]{3,2,1,0:T(8,128)(2,1)S(1)} async-done(((bf16[16,3,256,128]{3,2,1,0:T(8,128)(2,1)}), bf16[16,3,256,128]{3,2,1,0:T(8,128)(2,1)S(1)}, u32[]{:S(2)}, u32[]{:S(2)}) %all-to-all-start) | async-done | bytes 3145760 | tf_op jit(solution)/shard_map/all_to_all | solution.py:211
  58.5 2.6 %collective-permute-start = (bf16[16,6,128,128]{3,2,1,0:T(8,128)(2,1)S(1)}, bf16[16,6,128,128]{3,2,1,0:T(8,128)(2,1)}, u32[]{:S(2)}, u32[]{:S(2)}) collective-permute-start(bf16[16,6,128,128]{3,2,1,0:T(8,128)(2,1)S(1)} %bitcast.38), channel_id=1, source_target_pairs={{0,1},{1,0},{2,3},{3,2},{4,5},{5,4},{6,7},{7,6},{8,9},{9,8},{10,11... | collective-permute-start | bytes 9437192 | tf_op jit(solution)/shard_map/ppermute | solution.py:219
  61.8 4.8 %collective-permute-done.other_ref = bf16[16,6,128,128]{3,2,1,0:T(8,128)(2,1)} collective-permute-done((bf16[16,6,128,128]{3,2,1,0:T(8,128)(2,1)S(1)}, bf16[16,6,128,128]{3,2,1,0:T(8,128)(2,1)}, u32[]{:S(2)}, u32[]{:S(2)}) %collective-permute-start) | collective-permute-done | bytes 3145760 | tf_op jit(solution)/shard_map/ppermute | solution.py:219
  66.6 7.8 %shard_map.76 = bf16[16,128,128]{2,1,0:T(8,128)(2,1)} custom-call(s32[3]{0:T(128)} %pad_add_fusion.2.meta, s32[256]{0:T(256)} %copy-done.10, s32[1024]{0:T(1024)} %convert_element_type.110.k_of, s32[256]{0:T(256)} %get-tuple-element.30.valid_of, bf16[16,6,128,128]{3,2,1,0:T(8,128)(2,1)} %bitcast.39, bf16[16,6,128,128]{3,2,1,0:T(8,128)(2,1)} %collective-permute-done.other_ref), custom_call_target="tpu_custom_call" | custom-call | tf_op jit(solution)/shard_map/pallas_call | solution.py:149
  74.4 10.8 %all-to-all-start.2 = ((bf16[16,128,128]{2,1,0:T(8,128)(2,1)}), bf16[16,128,128]{2,1,0:T(8,128)(2,1)S(1)}, u32[]{:S(2)}, u32[]{:S(2)}) async-start(bf16[16,128,128]{2,1,0:T(8,128)(2,1)} %shard_map.76), calls=%async_computation.2 | async-start | bytes 1048576 | tf_op jit(solution)/shard_map/all_to_all | solution.py:211
  85.8 11.6 %shard_map.74 = bf16[16,128,128]{2,1,0:T(8,128)(2,1)} custom-call(s32[3]{0:T(128)} %pad_add_fusion.1.meta, s32[256]{0:T(256)} %copy-done.9, s32[1024]{0:T(1024)} %convert_element_type.104.k_of, s32[256]{0:T(256)} %get-tuple-element.21.valid_of, bf16[16,6,128,128]{3,2,1,0:T(8,128)(2,1)} %bitcast.40, bf16[16,6,128,128]{3,2,1,0:T(8,128)(2,1)} %collective-permute-done.other_ref), custom_call_target="tpu_custom_call" | custom-call | tf_op jit(solution)/shard_map/pallas_call | solution.py:149
  97.4 6.8 %all-to-all-start.1 = ((bf16[16,128,128]{2,1,0:T(8,128)(2,1)}), bf16[16,128,128]{2,1,0:T(8,128)(2,1)S(1)}, u32[]{:S(2)}, u32[]{:S(2)}) async-start(bf16[16,128,128]{2,1,0:T(8,128)(2,1)} %shard_map.74), calls=%async_computation.1 | async-start | bytes 1048576 | tf_op jit(solution)/shard_map/all_to_all | solution.py:211
  105.0 1.9 %shard_map.77 = bf16[128,1280]{1,0:T(8,128)(2,1)} custom-call(s32[10]{0:T(128)} %get-tuple-element.38.source, bf16[16,128,128]{2,1,0:T(8,128)(2,1)} %copy-done.4), custom_call_target="tpu_custom_call" | custom-call | tf_op jit(solution)/shard_map/pallas_call | solution.py:202
  106.9 3.1 %collective-permute-start.11 = (bf16[128,1280]{1,0:T(8,128)(2,1)}, bf16[128,1280]{1,0:T(8,128)(2,1)S(1)}, u32[]{:S(2)}, u32[]{:S(2)}) collective-permute-start(bf16[128,1280]{1,0:T(8,128)(2,1)} %shard_map.77), channel_id=1, source_target_pairs={{0,6},{2,0},{4,2},{6,4},{1,7},{3,1},{5,3},{7,5},{8,14},{10,8},{12,... | collective-permute-start | bytes 983048 | tf_op jit(solution)/shard_map/ppermute | solution.py:215
  110.0 1.8 %collective-permute-start.8 = (bf16[128,1280]{1,0:T(8,128)(2,1)}, bf16[128,1280]{1,0:T(8,128)(2,1)}, u32[]{:S(2)}, u32[]{:S(2)}) collective-permute-start(bf16[128,1280]{1,0:T(8,128)(2,1)} %shard_map.77), channel_id=1, source_target_pairs={{0,1},{1,0},{2,3},{3,2},{4,5},{5,4},{6,7},{7,6},{8,9},{9,8},{10,11... | collective-permute-start | bytes 983048 | tf_op jit(solution)/shard_map/ppermute | solution.py:219
  114.3 1.9 %shard_map.75 = bf16[128,1280]{1,0:T(8,128)(2,1)} custom-call(s32[10]{0:T(128)} %get-tuple-element.37.source, bf16[16,128,128]{2,1,0:T(8,128)(2,1)} %copy-done.3), custom_call_target="tpu_custom_call" | custom-call | tf_op jit(solution)/shard_map/pallas_call | solution.py:202
  116.2 3.2 %collective-permute-start.1 = (bf16[128,1280]{1,0:T(8,128)(2,1)}, bf16[128,1280]{1,0:T(8,128)(2,1)}, u32[]{:S(2)}, u32[]{:S(2)}) collective-permute-start(bf16[128,1280]{1,0:T(8,128)(2,1)} %shard_map.75), channel_id=1, source_target_pairs={{0,1},{1,0},{2,3},{3,2},{4,5},{5,4},{6,7},{7,6},{8,9},{9,8},{10,11... | collective-permute-start | bytes 983048 | tf_op jit(solution)/shard_map/ppermute | solution.py:219
  119.4 5.9 %collective-permute-done.11 = bf16[128,1280]{1,0:T(8,128)(2,1)S(1)} collective-permute-done((bf16[128,1280]{1,0:T(8,128)(2,1)}, bf16[128,1280]{1,0:T(8,128)(2,1)S(1)}, u32[]{:S(2)}, u32[]{:S(2)}) %collective-permute-start.11) | collective-permute-done | bytes 327712 | tf_op jit(solution)/shard_map/ppermute | solution.py:215
  125.3 2.1 %collective-permute-start.4 = (bf16[128,1280]{1,0:T(8,128)(2,1)}, bf16[128,1280]{1,0:T(8,128)(2,1)S(1)}, u32[]{:S(2)}, u32[]{:S(2)}) collective-permute-start(bf16[128,1280]{1,0:T(8,128)(2,1)} %shard_map.75), channel_id=1, source_target_pairs={{0,6},{2,0},{4,2},{6,4},{1,7},{3,1},{5,3},{7,5},{8,14},{10,8},{12,... | collective-permute-start | bytes 983048 | tf_op jit(solution)/shard_map/ppermute | solution.py:215
  132.1 2.2 %collective-permute-start.12 = (bf16[128,1280]{1,0:T(8,128)(2,1)S(1)}, bf16[128,1280]{1,0:T(8,128)(2,1)S(1)}, u32[]{:S(2)}, u32[]{:S(2)}) collective-permute-start(bf16[128,1280]{1,0:T(8,128)(2,1)S(1)} %collective-permute-done.11), channel_id=1, source_target_pairs={{0,1},{1,0},{2,3},{3,2},{4,5},{5,4},{6,7},{7,6},{8,9},{9,8},{10,11... | collective-permute-start | bytes 983048 | tf_op jit(solution)/shard_map/ppermute | solution.py:219
  134.3 5.0 %collective-permute-done.4 = bf16[128,1280]{1,0:T(8,128)(2,1)S(1)} collective-permute-done((bf16[128,1280]{1,0:T(8,128)(2,1)}, bf16[128,1280]{1,0:T(8,128)(2,1)S(1)}, u32[]{:S(2)}, u32[]{:S(2)}) %collective-permute-start.4) | collective-permute-done | bytes 327712 | tf_op jit(solution)/shard_map/ppermute | solution.py:215
  (134 shorter events, 28.0 us)
Async XLA Ops:
  9.5 49.0 %all-to-all-start = ((bf16[16,3,256,128]{3,2,1,0:T(8,128)(2,1)}), bf16[16,3,256,128]{3,2,1,0:T(8,128)(2,1)S(1)}, u32[]{:S(2)}, u32[]{:S(2)}) async-start(bf16[16,3,256,128]{3,2,1,0:T(8,128)(2,1)} %shard_map.73), calls=%async_computation | async-start | bytes 6291456 | tf_op jit(solution)/shard_map/all_to_all | solution.py:211
  29.7 10.6 %copy-start.9 = (s32[256]{0:T(256)}, s32[256]{0:T(256)S(1)}, u32[]{:S(2)}) copy-start(s32[256]{0:T(256)S(1)} %broadcast_minimum_fusion.1.q_of) | copy-start | bytes 3076
  29.8 10.6 %copy-start.10 = (s32[256]{0:T(256)}, s32[256]{0:T(256)S(1)}, u32[]{:S(2)}) copy-start(s32[256]{0:T(256)S(1)} %broadcast_minimum_fusion.q_of) | copy-start | bytes 3076
  58.5 8.0 %collective-permute-start = (bf16[16,6,128,128]{3,2,1,0:T(8,128)(2,1)S(1)}, bf16[16,6,128,128]{3,2,1,0:T(8,128)(2,1)}, u32[]{:S(2)}, u32[]{:S(2)}) collective-permute-start(bf16[16,6,128,128]{3,2,1,0:T(8,128)(2,1)S(1)} %bitcast.38), channel_id=1, source_target_pairs={{0,1},{1,0},{2,3},{3,2},{4,5},{5,4},{6,7},{7,6},{8,9},{9,8},{10,11... | collective-permute-start | bytes 9437192 | tf_op jit(solution)/shard_map/ppermute | solution.py:219
  74.4 23.0 %all-to-all-start.2 = ((bf16[16,128,128]{2,1,0:T(8,128)(2,1)}), bf16[16,128,128]{2,1,0:T(8,128)(2,1)S(1)}, u32[]{:S(2)}, u32[]{:S(2)}) async-start(bf16[16,128,128]{2,1,0:T(8,128)(2,1)} %shard_map.76), calls=%async_computation.2 | async-start | bytes 1048576 | tf_op jit(solution)/shard_map/all_to_all | solution.py:211
  97.4 31.0 %copy-start.6 = (bf16[10,128,640]{2,1,0:T(8,128)(2,1)S(1)}, bf16[10,128,640]{2,1,0:T(8,128)(2,1)}, u32[]{:S(2)}) copy-start(bf16[10,128,640]{2,1,0:T(8,128)(2,1)} %gather_fusion.1) | copy-start | bytes 4915204
  97.4 16.0 %all-to-all-start.1 = ((bf16[16,128,128]{2,1,0:T(8,128)(2,1)}), bf16[16,128,128]{2,1,0:T(8,128)(2,1)S(1)}, u32[]{:S(2)}, u32[]{:S(2)}) async-start(bf16[16,128,128]{2,1,0:T(8,128)(2,1)} %shard_map.74), calls=%async_computation.1 | async-start | bytes 1048576 | tf_op jit(solution)/shard_map/all_to_all | solution.py:211
  106.9 12.5 %collective-permute-start.13 = (bf16[128,1280]{1,0:T(8,128)(2,1)}, bf16[128,1280]{1,0:T(8,128)(2,1)S(1)}, u32[]{:S(2)}, u32[]{:S(2)}) collective-permute-start(bf16[128,1280]{1,0:T(8,128)(2,1)} %shard_map.77), channel_id=1, source_target_pairs={{0,4},{2,6},{4,0},{6,2},{1,5},{3,7},{5,1},{7,3},{8,12},{10,14},{12... | collective-permute-start | bytes 983048 | tf_op jit(solution)/shard_map/ppermute | solution.py:215
  106.9 18.4 %collective-permute-start.11 = (bf16[128,1280]{1,0:T(8,128)(2,1)}, bf16[128,1280]{1,0:T(8,128)(2,1)S(1)}, u32[]{:S(2)}, u32[]{:S(2)}) collective-permute-start(bf16[128,1280]{1,0:T(8,128)(2,1)} %shard_map.77), channel_id=1, source_target_pairs={{0,6},{2,0},{4,2},{6,4},{1,7},{3,1},{5,3},{7,5},{8,14},{10,8},{12,... | collective-permute-start | bytes 983048 | tf_op jit(solution)/shard_map/ppermute | solution.py:215
  110.0 17.4 %collective-permute-start.9 = (bf16[128,1280]{1,0:T(8,128)(2,1)}, bf16[128,1280]{1,0:T(8,128)(2,1)S(1)}, u32[]{:S(2)}, u32[]{:S(2)}) collective-permute-start(bf16[128,1280]{1,0:T(8,128)(2,1)} %shard_map.77), channel_id=1, source_target_pairs={{0,2},{2,4},{4,6},{6,0},{1,3},{3,5},{5,7},{7,1},{8,10},{10,12},{12... | collective-permute-start | bytes 983048 | tf_op jit(solution)/shard_map/ppermute | solution.py:215
  110.0 17.4 %collective-permute-start.8 = (bf16[128,1280]{1,0:T(8,128)(2,1)}, bf16[128,1280]{1,0:T(8,128)(2,1)}, u32[]{:S(2)}, u32[]{:S(2)}) collective-permute-start(bf16[128,1280]{1,0:T(8,128)(2,1)} %shard_map.77), channel_id=1, source_target_pairs={{0,1},{1,0},{2,3},{3,2},{4,5},{5,4},{6,7},{7,6},{8,9},{9,8},{10,11... | collective-permute-start | bytes 983048 | tf_op jit(solution)/shard_map/ppermute | solution.py:219
  116.2 14.1 %copy-start.8 = (bf16[128,1280]{1,0:T(8,128)(2,1)S(1)}, bf16[128,1280]{1,0:T(8,128)(2,1)}, u32[]{:S(2)}) copy-start(bf16[128,1280]{1,0:T(8,128)(2,1)} %shard_map.75) | copy-start | bytes 983044
  116.2 14.0 %collective-permute-start.1 = (bf16[128,1280]{1,0:T(8,128)(2,1)}, bf16[128,1280]{1,0:T(8,128)(2,1)}, u32[]{:S(2)}, u32[]{:S(2)}) collective-permute-start(bf16[128,1280]{1,0:T(8,128)(2,1)} %shard_map.75), channel_id=1, source_target_pairs={{0,1},{1,0},{2,3},{3,2},{4,5},{5,4},{6,7},{7,6},{8,9},{9,8},{10,11... | collective-permute-start | bytes 983048 | tf_op jit(solution)/shard_map/ppermute | solution.py:219
  119.4 12.7 %collective-permute-start.6 = (bf16[128,1280]{1,0:T(8,128)(2,1)}, bf16[128,1280]{1,0:T(8,128)(2,1)S(1)}, u32[]{:S(2)}, u32[]{:S(2)}) collective-permute-start(bf16[128,1280]{1,0:T(8,128)(2,1)} %shard_map.75), channel_id=1, source_target_pairs={{0,4},{2,6},{4,0},{6,2},{1,5},{3,7},{5,1},{7,3},{8,12},{10,14},{12... | collective-permute-start | bytes 983048 | tf_op jit(solution)/shard_map/ppermute | solution.py:215
  125.3 13.9 %collective-permute-start.4 = (bf16[128,1280]{1,0:T(8,128)(2,1)}, bf16[128,1280]{1,0:T(8,128)(2,1)S(1)}, u32[]{:S(2)}, u32[]{:S(2)}) collective-permute-start(bf16[128,1280]{1,0:T(8,128)(2,1)} %shard_map.75), channel_id=1, source_target_pairs={{0,6},{2,0},{4,2},{6,4},{1,7},{3,1},{5,3},{7,5},{8,14},{10,8},{12,... | collective-permute-start | bytes 983048 | tf_op jit(solution)/shard_map/ppermute | solution.py:215
  127.5 12.1 %collective-permute-start.2 = (bf16[128,1280]{1,0:T(8,128)(2,1)}, bf16[128,1280]{1,0:T(8,128)(2,1)S(1)}, u32[]{:S(2)}, u32[]{:S(2)}) collective-permute-start(bf16[128,1280]{1,0:T(8,128)(2,1)} %shard_map.75), channel_id=1, source_target_pairs={{0,2},{2,4},{4,6},{6,0},{1,3},{3,5},{5,7},{7,1},{8,10},{10,12},{12... | collective-permute-start | bytes 983048 | tf_op jit(solution)/shard_map/ppermute | solution.py:215
  127.5 12.7 %collective-permute-start.10 = (bf16[128,1280]{1,0:T(8,128)(2,1)S(1)}, bf16[128,1280]{1,0:T(8,128)(2,1)S(1)}, u32[]{:S(2)}, u32[]{:S(2)}) collective-permute-start(bf16[128,1280]{1,0:T(8,128)(2,1)S(1)} %collective-permute-done.9), channel_id=1, source_target_pairs={{0,1},{1,0},{2,3},{3,2},{4,5},{5,4},{6,7},{7,6},{8,9},{9,8},{10,11... | collective-permute-start | bytes 983048 | tf_op jit(solution)/shard_map/ppermute | solution.py:219
  130.2 10.0 %copy-start.1 = (bf16[10,128,640]{2,1,0:T(8,128)(2,1)S(1)}, bf16[10,128,640]{2,1,0:T(8,128)(2,1)}, u32[]{:S(2)}) copy-start(bf16[10,128,640]{2,1,0:T(8,128)(2,1)} %gather_fusion.2) | copy-start | bytes 4915204
  130.2 10.7 %collective-permute-start.14 = (bf16[128,1280]{1,0:T(8,128)(2,1)S(1)}, bf16[128,1280]{1,0:T(8,128)(2,1)S(1)}, u32[]{:S(2)}, u32[]{:S(2)}) collective-permute-start(bf16[128,1280]{1,0:T(8,128)(2,1)S(1)} %collective-permute-done.13), channel_id=1, source_target_pairs={{0,1},{1,0},{2,3},{3,2},{4,5},{5,4},{6,7},{7,6},{8,9},{9,8},{10,11... | collective-permute-start | bytes 983048 | tf_op jit(solution)/shard_map/ppermute | solution.py:219
  132.1 8.8 %copy-start.5 = (bf16[10,128,640]{2,1,0:T(8,128)(2,1)S(1)}, bf16[10,128,640]{2,1,0:T(8,128)(2,1)}, u32[]{:S(2)}) copy-start(bf16[10,128,640]{2,1,0:T(8,128)(2,1)} %gather_fusion.4) | copy-start | bytes 4915204
  132.1 9.5 %collective-permute-start.12 = (bf16[128,1280]{1,0:T(8,128)(2,1)S(1)}, bf16[128,1280]{1,0:T(8,128)(2,1)S(1)}, u32[]{:S(2)}, u32[]{:S(2)}) collective-permute-start(bf16[128,1280]{1,0:T(8,128)(2,1)S(1)} %collective-permute-done.11), channel_id=1, source_target_pairs={{0,1},{1,0},{2,3},{3,2},{4,5},{5,4},{6,7},{7,6},{8,9},{9,8},{10,11... | collective-permute-start | bytes 983048 | tf_op jit(solution)/shard_map/ppermute | solution.py:219
  139.3 3.7 %collective-permute-start.7 = (bf16[128,1280]{1,0:T(8,128)(2,1)S(1)}, bf16[128,1280]{1,0:T(8,128)(2,1)S(1)}, u32[]{:S(2)}, u32[]{:S(2)}) collective-permute-start(bf16[128,1280]{1,0:T(8,128)(2,1)S(1)} %collective-permute-done.6), channel_id=1, source_target_pairs={{0,1},{1,0},{2,3},{3,2},{4,5},{5,4},{6,7},{7,6},{8,9},{9,8},{10,11... | collective-permute-start | bytes 983048 | tf_op jit(solution)/shard_map/ppermute | solution.py:219
  139.5 4.9 %collective-permute-start.5 = (bf16[128,1280]{1,0:T(8,128)(2,1)S(1)}, bf16[128,1280]{1,0:T(8,128)(2,1)S(1)}, u32[]{:S(2)}, u32[]{:S(2)}) collective-permute-start(bf16[128,1280]{1,0:T(8,128)(2,1)S(1)} %collective-permute-done.4), channel_id=1, source_target_pairs={{0,1},{1,0},{2,3},{3,2},{4,5},{5,4},{6,7},{7,6},{8,9},{9,8},{10,11... | collective-permute-start | bytes 983048 | tf_op jit(solution)/shard_map/ppermute | solution.py:219
  140.2 3.6 %collective-permute-start.3 = (bf16[128,1280]{1,0:T(8,128)(2,1)S(1)}, bf16[128,1280]{1,0:T(8,128)(2,1)S(1)}, u32[]{:S(2)}, u32[]{:S(2)}) collective-permute-start(bf16[128,1280]{1,0:T(8,128)(2,1)S(1)} %collective-permute-done.2), channel_id=1, source_target_pairs={{0,1},{1,0},{2,3},{3,2},{4,5},{5,4},{6,7},{7,6},{8,9},{9,8},{10,11... | collective-permute-start | bytes 983048 | tf_op jit(solution)/shard_map/ppermute | solution.py:219
  (6 other events, 20.0 us)

commit v2 on v1

--- a/solution.py
+++ b/solution.py
@@ -47,25 +47,37 @@
     return chips, first
 
 
-def pack_kernel(heads, q_ref, k_ref, v_ref, out_ref, held, turned, sem_in, sem_out):
-    rows = pl.ds(pl.multiple_of(heads[CHIPS] * HALF, HALF), HALF)
+def pack_kernel(heads, q_ref, k_ref, v_ref, first_ref, second_ref, held, turned, sem_in, sem_out):
+    start = pl.multiple_of(heads[CHIPS] * HALF, HALF)
+    rows = pl.ds(start, HALF)
     loads, stores = [], []
     for t in range(CHIPS):
         cols = pl.ds(pl.multiple_of(heads[t] * TILE, TILE), TILE)
-        for j, ref in enumerate((k_ref, v_ref, q_ref)):
-            loads.append(pltpu.make_async_copy(ref.at[rows, cols], held.at[t, j], sem_in.at[t, j]))
-            loads[-1].start()
+        loads.append(
+            [
+                pltpu.make_async_copy(k_ref.at[rows, cols], held.at[t, pl.ds(0, HALF)], sem_in.at[t, 0]),
+                pltpu.make_async_copy(v_ref.at[rows, cols], held.at[t, pl.ds(HALF, HALF)], sem_in.at[t, 1]),
+                pltpu.make_async_copy(q_ref.at[rows, cols], held.at[t, pl.ds(2 * HALF, HALF)], sem_in.at[t, 2]),
+            ]
+        )
+        for load in loads[-1]:
+            load.start()
     for t in range(CHIPS):
-        for j in range(3):
-            loads[3 * t + j].wait()
-            source = held.at[t, j]
-            if j == 1:
-                for sub in range(2):
-                    part = pl.ds(sub * TILE, TILE)
-                    turned[t, part, :] = held[t, 1, part, :].T
-                source = turned.at[t]
-            stores.append(pltpu.make_async_copy(source, out_ref.at[t, j], sem_out.at[t, j]))
-            stores[-1].start()
+        for load in loads[t]:
+            load.wait()
+        for sub in range(2):
+            part = pl.ds(sub * TILE, TILE)
+            turned[t, part, :] = held[t, pl.ds(HALF + sub * TILE, TILE), :].T
+        stores += [
+            pltpu.make_async_copy(held.at[t, pl.ds(0, HALF)], first_ref.at[t, pl.ds(0, HALF)], sem_out.at[t, 0]),
+            pltpu.make_async_copy(turned.at[t], first_ref.at[t, pl.ds(HALF, HALF)], sem_out.at[t, 1]),
+            pltpu.make_async_copy(
+                held.at[t, pl.ds(2 * HALF, TILE)], first_ref.at[t, pl.ds(2 * HALF, TILE)], sem_out.at[t, 2]
+            ),
+            pltpu.make_async_copy(held.at[t, pl.ds(2 * HALF + TILE, TILE)], second_ref.at[t], sem_out.at[t, 3]),
+        ]
+        for store in stores[-4:]:
+            store.start()
     for store in stores:
         store.wait()
 
@@ -76,24 +88,29 @@
     return pl.pallas_call(
         pack_kernel,
         in_specs=[pl.BlockSpec(memory_space=pltpu.SMEM)] + [hbm] * 3,
-        out_specs=hbm,
-        out_shape=jax.ShapeDtypeStruct((CHIPS, 3, HALF, TILE), jnp.bfloat16),
+        out_specs=[hbm, hbm],
+        out_shape=[
+            jax.ShapeDtypeStruct((CHIPS, 5 * TILE, TILE), jnp.bfloat16),
+            jax.ShapeDtypeStruct((CHIPS, TILE, TILE), jnp.bfloat16),
+        ],
         scratch_shapes=[
-            pltpu.VMEM((CHIPS, 3, HALF, TILE), jnp.bfloat16),
+            pltpu.VMEM((CHIPS, 3 * HALF, TILE), jnp.bfloat16),
             pltpu.VMEM((CHIPS, HALF, TILE), jnp.bfloat16),
             pltpu.SemaphoreType.DMA((CHIPS, 3)),
-            pltpu.SemaphoreType.DMA((CHIPS, 3)),
+            pltpu.SemaphoreType.DMA((CHIPS, 4)),
         ],
         compiler_params=pltpu.CompilerParams(vmem_limit_bytes=60 * 2**20),
     )(scalars, queries, keys, values)
 
 
-def attend_kernel(scale, meta, q_of, k_of, valid_of, own_ref, other_ref, out_ref, kv_s, q_s, acc_s, max_s, sum_s, sems):
-    core, sub = meta[0], meta[2]
+def attend_kernel(
+    scale, query_at, meta, q_of, k_of, valid_of, own_ref, other_ref, query_ref, out_ref, kv_s, q_s, acc_s, max_s, sum_s, sems
+):
+    core = meta[0]
     loads = [
         pltpu.make_async_copy(own_ref.at[:, pl.ds(0, 4)], kv_s.at[core], sems.at[0]),
         pltpu.make_async_copy(other_ref.at[:, pl.ds(0, 4)], kv_s.at[1 - core], sems.at[1]),
-        pltpu.make_async_copy(own_ref.at[:, pl.ds(4 + sub, 1)], q_s, sems.at[2]),
+        pltpu.make_async_copy(query_ref.at[:, pl.ds(query_at, 1)], q_s, sems.at[2]),
     ]
     for load in loads:
         load.start()
@@ -143,12 +160,12 @@
     lax.fori_loop(0, CHIPS, finish, 0)
 
 
-def attend(meta, q_of, k_of, valid_of, own, other):
+def attend(query_at, meta, q_of, k_of, valid_of, own, other, query):
     smem = pl.BlockSpec(memory_space=pltpu.SMEM)
     hbm = pl.BlockSpec(memory_space=pl.ANY)
     return pl.pallas_call(
-        functools.partial(attend_kernel, TILE**-0.5 * LOG2E),
-        in_specs=[smem] * 4 + [hbm] * 2,
+        functools.partial(attend_kernel, TILE**-0.5 * LOG2E, query_at),
+        in_specs=[smem] * 4 + [hbm] * 3,
         out_specs=pl.BlockSpec(memory_space=pltpu.VMEM),
         out_shape=jax.ShapeDtypeStruct((CHIPS, TILE, TILE), jnp.bfloat16),
         scratch_shapes=[
@@ -159,8 +176,8 @@
             pltpu.VMEM((CHIPS, 1, TILE), jnp.float32),
             pltpu.SemaphoreType.DMA((3,)),
         ],
-        compiler_params=pltpu.CompilerParams(vmem_limit_bytes=60 * 2**20),
-    )(meta, q_of, k_of, valid_of, own, other)
+        compiler_params=pltpu.CompilerParams(vmem_limit_bytes=24 * 2**20),
+    )(meta, q_of, k_of, valid_of, own, other, query)
 
 
 def item_lists(allowed, mine):
@@ -230,7 +247,8 @@
     chip_ids = jnp.arange(CHIPS)
     on_chip = (first[None, :] <= chip_ids[:, None]) & (chip_ids[:, None] < (first + chips)[None, :])
     chip_heads = jnp.sum(jnp.where(on_chip, plane_heads[None, :], 0), axis=1)
-    got = exchange(pack(queries, keys, values, chip_heads, core)).reshape(CHIPS, 6, TILE, TILE)
+    first_send, second_send = pack(queries, keys, values, chip_heads, core)
+    got = exchange(first_send).reshape(CHIPS, 5, TILE, TILE)
 
     half_work = lax.dynamic_index_in_dim(tile_work.reshape(HEADS, CHIPS, 2, 2), core, 2, keepdims=False)
     half_work = jnp.take(half_work.reshape(HEADS, 2 * CHIPS), plane_heads, axis=0, mode="clip")
@@ -253,14 +271,16 @@
         w_order = lax.dynamic_slice_in_dim(head_at, (plane + ahead) % PLANES * PLANE_HEADS, PLANE_HEADS)
         weights.append(jnp.take(w_heads, w_order, axis=0, mode="clip").reshape(PLANE_HEADS * TILE, -1))
     lists = [item_lists(allowed[:, sub], mine_tiles[:, sub]) for sub in range(2)]
-    got, lists, weights = lax.optimization_barrier((got, lists, weights))
+    got, lists, weights, second_send = lax.optimization_barrier((got, lists, weights, second_send))
     got_other = swap(got)
+    late = exchange(second_send).reshape(CHIPS, 1, TILE, TILE)
 
     halves = []
     for sub in range(2):
         steps, q_of, k_of, valid = lists[sub]
-        meta = jnp.stack([core, steps, jnp.int32(sub)]).astype(jnp.int32)
-        attended = attend(meta, q_of, k_of, valid, got, got_other)
+        meta = jnp.stack([core, steps]).astype(jnp.int32)
+        query_at, query = ((4, got), (0, late))[sub]
+        attended = attend(query_at, meta, q_of, k_of, valid, got, got_other, query)
         own = select(source[:, sub], exchange(attended))
         blocks = [own, along_y(own, 1), along_y(own, 3), along_y(own, 2)]
         total = jnp.zeros((2 * TILE, w_out.shape[1]), jnp.float32)

time: 148 us -> 145 us (0.980)
  starting transfers between devices: 43.1 us -> 49.6 us
  waiting for transfers between devices: 20.9 us -> 15.6 us
  other arithmetic: 12.1 us -> 10.5 us
    ppermute x6, starting transfers between devices: 5.24 us -> 11.1 us  [along_y(): lax.ppermute(block, 'y', [(i, (i + step) % PLANES) for i in range(PLANES)])]
    ppermute x6, waiting for transfers between devices: 10.9 us -> 5.56 us  [along_y(): lax.ppermute(block, 'y', [(i, (i + step) % PLANES) for i in range(PLANES)])]
    all_to_all x3 -> x4, waiting for transfers between devices: 5.22 us -> 10.1 us  [exchange(): lax.all_to_all(block, TOKENS_AXES, split_axis=0, concat_axis=0, tiled=True)]
    ppermute x9, waiting for transfers between devices: 4.77 us -> 0.02 us  [swap(): return lax.ppermute(block, 'c', [(0, 1), (1, 0)])]
    ppermute x9, starting transfers between devices: 11.8 us -> 13.5 us  [swap(): return lax.ppermute(block, 'c', [(0, 1), (1, 0)])]
    all_to_all x3 -> x4, starting transfers between devices: 26 us -> 25 us  [exchange(): lax.all_to_all(block, TOKENS_AXES, split_axis=0, concat_axis=0, tiled=True)]
  transfers between devices with their start and end apart: 18 -> 19, of which waited for: 5 -> 3; matrix products, arithmetic and copies ran while one was open for 27% -> 25% of each run, Pallas kernels for 10% -> 10%
where the time goes in v2:
time: 145 us
  starting transfers between devices  49.6 us (34%)
  local copies, waits for them, and re-layouts  27.4 us (19%)
  Pallas kernels  26.6 us (18%)
  waiting for transfers between devices  15.6 us (11%)
  other arithmetic  10.5 us (7%)
  matrix products  8 us (6%)
  between operations  6.91 us (5%)
    all_to_all x4, starting transfers between devices, exchange(): lax.all_to_all(block, TOKENS_AXES, split_axis=0, concat_axis=0, tiled=True)  25 us
    gather x4, local copies, waits for them, and re-layouts, shards(): jnp.take(w_heads, w_order, axis=0, mode='clip')  19.6 us
    pallas_call x2, Pallas kernels, attend(): pl.pallas_call(functools.partial(attend_kernel, TILE ** (-0.5) * LOG2E, q...  18 us
    ppermute x9, starting transfers between devices, swap(): return lax.ppermute(block, 'c', [(0, 1), (1, 0)])  13.5 us
    ppermute x6, starting transfers between devices, along_y(): lax.ppermute(block, 'y', [(i, (i + step) % PLANES) for i in range(PLANES)])  11.1 us
    all_to_all x4, waiting for transfers between devices, exchange(): lax.all_to_all(block, TOKENS_AXES, split_axis=0, concat_axis=0, tiled=True)  10.1 us
    dot_general x8, matrix products, shards(): jnp.dot(both, weights[k], preferred_element_type=jnp.float32)  7.6 us
    ppermute x6, waiting for transfers between devices, along_y(): lax.ppermute(block, 'y', [(i, (i + step) % PLANES) for i in range(PLANES)])  5.56 us
  transfers between devices with their start and end apart: 19, of which 3 were waited for; matrix products, arithmetic and copies ran while one was open for 25% of the time, Pallas kernels for 10%

profile of v2, /device:TPU:1, one launch (start us, length us, event | category | flops | bytes accessed | tf_op | source)
XLA Modules:
  0.0 144.6 jit_solution(8226283777177370369)
XLA Ops:
  0.0 2.8 %fusion.72 = (s32[40,64]{1,0:T(8,128)S(1)}, s32[40]{0:T(128)S(1)}) fusion(s32[40,64,64]{2,1,0:T(8,128)} %param.13), kind=kLoop, calls=%fused_computation.196 | loop fusion | flops 325080 | bytes 665760 | tf_op jit(solution)/shard_map/reduce_sum | solution.py:243
  4.7 4.8 %shard_map.73 = (bf16[16,640,128]{2,1,0:T(8,128)(2,1)}, bf16[16,128,128]{2,1,0:T(8,128)(2,1)}) custom-call(s32[17]{0:T(128)} %pad_add_fusion.heads, bf16[512,5120]{1,0:T(8,128)(2,1)} %q_ref.1, bf16[512,5120]{1,0:T(8,128)(2,1)} %k_ref.1, bf16[512,5120]{1,0:T(8,128)(2,1)} %v_ref.1), custom_call_target="tpu_custom_call" | custom-call | tf_op jit(solution)/shard_map/pallas_call | solution.py:88
  9.5 8.4 %all-to-all-start = ((bf16[16,640,128]{2,1,0:T(8,128)(2,1)}), bf16[16,640,128]{2,1,0:T(8,128)(2,1)S(1)}, u32[]{:S(2)}, u32[]{:S(2)}) async-start(bf16[16,640,128]{2,1,0:T(8,128)(2,1)} %get-tuple-element.21), calls=%async_computation | async-start | bytes 5242880 | tf_op jit(solution)/shard_map/all_to_all | solution.py:228
  33.9 4.9 %gather_fusion.2 = bf16[10,128,640]{2,1,0:T(8,128)(2,1)} fusion(bf16[40,128,640]{2,1,0:T(8,128)(2,1)} %bitcast.48, s32[1024]{0:T(1024)S(1)} %get-tuple-element.89), kind=kCustom, calls=%fused_computation.2 | custom fusion | bytes 3276840 | tf_op jit(solution)/shard_map/jit(_take)/gather | solution.py:272
  38.8 4.9 %gather_fusion.4 = bf16[10,128,640]{2,1,0:T(8,128)(2,1)} fusion(bf16[40,128,640]{2,1,0:T(8,128)(2,1)} %bitcast.49, s32[1024]{0:T(1024)S(1)} %get-tuple-element.87), kind=kCustom, calls=%fused_computation.4 | custom fusion | bytes 3276840 | tf_op jit(solution)/shard_map/jit(_take)/gather | solution.py:272
  43.6 5.0 %gather_fusion.1 = bf16[10,128,640]{2,1,0:T(8,128)(2,1)} fusion(bf16[40,128,640]{2,1,0:T(8,128)(2,1)} %bitcast.50, s32[1024]{0:T(1024)S(1)} %get-tuple-element.90), kind=kCustom, calls=%fused_computation.1 | custom fusion | bytes 3276840 | tf_op jit(solution)/shard_map/jit(_take)/gather | solution.py:272
  48.6 4.9 %gather_fusion.3 = bf16[10,128,640]{2,1,0:T(8,128)(2,1)} fusion(bf16[40,128,640]{2,1,0:T(8,128)(2,1)} %bitcast.51, s32[1024]{0:T(1024)S(1)} %get-tuple-element.88), kind=kCustom, calls=%fused_computation.3 | custom fusion | bytes 3276840 | tf_op jit(solution)/shard_map/jit(_take)/gather | solution.py:272
  53.5 2.5 %collective-permute-start = (bf16[16,5,128,128]{3,2,1,0:T(8,128)(2,1)S(1)}, bf16[16,5,128,128]{3,2,1,0:T(8,128)(2,1)}, u32[]{:S(2)}, u32[]{:S(2)}) collective-permute-start(bf16[16,5,128,128]{3,2,1,0:T(8,128)(2,1)S(1)} %bitcast.39), channel_id=1, source_target_pairs={{0,1},{1,0},{2,3},{3,2},{4,5},{5,4},{6,7},{7,6},{8,9},{9,8},{10,11... | collective-permute-start | bytes 7864328 | tf_op jit(solution)/shard_map/ppermute | solution.py:236
  56.0 5.4 %all-to-all-start.2 = ((bf16[16,128,128]{2,1,0:T(8,128)(2,1)}), bf16[16,128,128]{2,1,0:T(8,128)(2,1)S(1)}, u32[]{:S(2)}, u32[]{:S(2)}) async-start(bf16[16,128,128]{2,1,0:T(8,128)(2,1)} %get-tuple-element.36), calls=%async_computation.2 | async-start | bytes 1048576 | tf_op jit(solution)/shard_map/all_to_all | solution.py:228
  61.5 10.1 %all-to-all-done.2 = bf16[16,128,128]{2,1,0:T(8,128)(2,1)S(1)} async-done(((bf16[16,128,128]{2,1,0:T(8,128)(2,1)}), bf16[16,128,128]{2,1,0:T(8,128)(2,1)S(1)}, u32[]{:S(2)}, u32[]{:S(2)}) %all-to-all-start.2) | async-done | bytes 524320 | tf_op jit(solution)/shard_map/all_to_all | solution.py:228
  71.5 7.1 %shard_map.76 = bf16[16,128,128]{2,1,0:T(8,128)(2,1)} custom-call(s32[2]{0:T(128)S(1)} %pad_add_fusion.2.meta, s32[256]{0:T(256)S(1)} %broadcast_minimum_fusion.q_of, s32[1024]{0:T(1024)S(1)} %convert_element_type.110.k_of, s32[256]{0:T(256)S(1)} %get-tuple-element.35.valid_of, bf16[16,5,128,128]{3,2,1,0:T(8,128)(2,1)S(1)} %bitcast.40, ...), custom_call_target="tpu_custom_call" | custom-call | tf_op jit(solution)/shard_map/pallas_call | solution.py:166
  78.6 6.3 %all-to-all-start.3 = ((bf16[16,128,128]{2,1,0:T(8,128)(2,1)}), bf16[16,128,128]{2,1,0:T(8,128)(2,1)S(1)}, u32[]{:S(2)}, u32[]{:S(2)}) async-start(bf16[16,128,128]{2,1,0:T(8,128)(2,1)} %shard_map.76), calls=%async_computation.3 | async-start | bytes 1048576 | tf_op jit(solution)/shard_map/all_to_all | solution.py:228
  85.0 10.9 %shard_map.74 = bf16[16,128,128]{2,1,0:T(8,128)(2,1)} custom-call(s32[2]{0:T(128)S(1)} %pad_add_fusion.1.meta, s32[256]{0:T(256)S(1)} %broadcast_minimum_fusion.1.q_of, s32[1024]{0:T(1024)S(1)} %convert_element_type.104.k_of, s32[256]{0:T(256)S(1)} %get-tuple-element.26.valid_of, bf16[16,5,128,128]{3,2,1,0:T(8,128)(2,1)S(1)} %bitcast.41, ...), custom_call_target="tpu_custom_call" | custom-call | tf_op jit(solution)/shard_map/pallas_call | solution.py:166
  95.9 4.9 %all-to-all-start.1 = ((bf16[16,128,128]{2,1,0:T(8,128)(2,1)}), bf16[16,128,128]{2,1,0:T(8,128)(2,1)S(1)}, u32[]{:S(2)}, u32[]{:S(2)}) async-start(bf16[16,128,128]{2,1,0:T(8,128)(2,1)} %shard_map.74), calls=%async_computation.1 | async-start | bytes 1048576 | tf_op jit(solution)/shard_map/all_to_all | solution.py:228
  101.6 1.9 %shard_map.77 = bf16[128,1280]{1,0:T(8,128)(2,1)} custom-call(s32[10]{0:T(128)} %get-tuple-element.44.source, bf16[16,128,128]{2,1,0:T(8,128)(2,1)} %copy-done.3), custom_call_target="tpu_custom_call" | custom-call | tf_op jit(solution)/shard_map/pallas_call | solution.py:219
  103.5 2.9 %collective-permute-start.13 = (bf16[128,1280]{1,0:T(8,128)(2,1)}, bf16[128,1280]{1,0:T(8,128)(2,1)S(1)}, u32[]{:S(2)}, u32[]{:S(2)}) collective-permute-start(bf16[128,1280]{1,0:T(8,128)(2,1)} %shard_map.77), channel_id=1, source_target_pairs={{0,4},{2,6},{4,0},{6,2},{1,5},{3,7},{5,1},{7,3},{8,12},{10,14},{12... | collective-permute-start | bytes 983048 | tf_op jit(solution)/shard_map/ppermute | solution.py:232
  107.9 4.7 %collective-permute-start.8 = (bf16[128,1280]{1,0:T(8,128)(2,1)}, bf16[128,1280]{1,0:T(8,128)(2,1)}, u32[]{:S(2)}, u32[]{:S(2)}) collective-permute-start(bf16[128,1280]{1,0:T(8,128)(2,1)} %shard_map.77), channel_id=1, source_target_pairs={{0,1},{1,0},{2,3},{3,2},{4,5},{5,4},{6,7},{7,6},{8,9},{9,8},{10,11... | collective-permute-start | bytes 983048 | tf_op jit(solution)/shard_map/ppermute | solution.py:236
  113.4 1.9 %shard_map.75 = bf16[128,1280]{1,0:T(8,128)(2,1)} custom-call(s32[10]{0:T(128)} %get-tuple-element.43.source, bf16[16,128,128]{2,1,0:T(8,128)(2,1)} %copy-done.2), custom_call_target="tpu_custom_call" | custom-call | tf_op jit(solution)/shard_map/pallas_call | solution.py:219
  115.3 2.2 %collective-permute-start.1 = (bf16[128,1280]{1,0:T(8,128)(2,1)}, bf16[128,1280]{1,0:T(8,128)(2,1)}, u32[]{:S(2)}, u32[]{:S(2)}) collective-permute-start(bf16[128,1280]{1,0:T(8,128)(2,1)} %shard_map.75), channel_id=1, source_target_pairs={{0,1},{1,0},{2,3},{3,2},{4,5},{5,4},{6,7},{7,6},{8,9},{9,8},{10,11... | collective-permute-start | bytes 983048 | tf_op jit(solution)/shard_map/ppermute | solution.py:236
  117.5 2.9 %collective-permute-start.6 = (bf16[128,1280]{1,0:T(8,128)(2,1)}, bf16[128,1280]{1,0:T(8,128)(2,1)S(1)}, u32[]{:S(2)}, u32[]{:S(2)}) collective-permute-start(bf16[128,1280]{1,0:T(8,128)(2,1)} %shard_map.75), channel_id=1, source_target_pairs={{0,4},{2,6},{4,0},{6,2},{1,5},{3,7},{5,1},{7,3},{8,12},{10,14},{12... | collective-permute-start | bytes 983048 | tf_op jit(solution)/shard_map/ppermute | solution.py:232
  122.1 3.8 %collective-permute-start.4 = (bf16[128,1280]{1,0:T(8,128)(2,1)}, bf16[128,1280]{1,0:T(8,128)(2,1)S(1)}, u32[]{:S(2)}, u32[]{:S(2)}) collective-permute-start(bf16[128,1280]{1,0:T(8,128)(2,1)} %shard_map.75), channel_id=1, source_target_pairs={{0,6},{2,0},{4,2},{6,4},{1,7},{3,1},{5,3},{7,5},{8,14},{10,8},{12,... | collective-permute-start | bytes 983048 | tf_op jit(solution)/shard_map/ppermute | solution.py:232
  126.8 1.8 %fusion.18 = f32[256,640]{1,0:T(8,128)S(1)} fusion(bf16[1280,640]{1,0:T(8,128)(2,1)S(1)} %bitcast.54, bf16[128,1280]{1,0:T(8,128)(2,1)} %collective-permute-done.8, bf16[128,1280]{1,0:T(8,128)(2,1)} %shard_map.77), kind=kOutput, calls=%fused_computation.28 | convolution fusion | flops 420741120 | bytes 2949120 | tf_op jit(solution)/shard_map/dot_general | solution.py:289
  131.0 3.9 %collective-permute-done.4 = bf16[128,1280]{1,0:T(8,128)(2,1)S(1)} collective-permute-done((bf16[128,1280]{1,0:T(8,128)(2,1)}, bf16[128,1280]{1,0:T(8,128)(2,1)S(1)}, u32[]{:S(2)}, u32[]{:S(2)}) %collective-permute-start.4) | collective-permute-done | bytes 327712 | tf_op jit(solution)/shard_map/ppermute | solution.py:232
  134.9 1.8 %collective-permute-start.7 = (bf16[128,1280]{1,0:T(8,128)(2,1)S(1)}, bf16[128,1280]{1,0:T(8,128)(2,1)S(1)}, u32[]{:S(2)}, u32[]{:S(2)}) collective-permute-start(bf16[128,1280]{1,0:T(8,128)(2,1)S(1)} %collective-permute-done.6), channel_id=1, source_target_pairs={{0,1},{1,0},{2,3},{3,2},{4,5},{5,4},{6,7},{7,6},{8,9},{9,8},{10,11... | collective-permute-start | bytes 983048 | tf_op jit(solution)/shard_map/ppermute | solution.py:236
  (130 shorter events, 27.2 us)
Async XLA Ops:
  9.5 44.0 %all-to-all-start = ((bf16[16,640,128]{2,1,0:T(8,128)(2,1)}), bf16[16,640,128]{2,1,0:T(8,128)(2,1)S(1)}, u32[]{:S(2)}, u32[]{:S(2)}) async-start(bf16[16,640,128]{2,1,0:T(8,128)(2,1)} %get-tuple-element.21), calls=%async_computation | async-start | bytes 5242880 | tf_op jit(solution)/shard_map/all_to_all | solution.py:228
  53.5 18.0 %collective-permute-start = (bf16[16,5,128,128]{3,2,1,0:T(8,128)(2,1)S(1)}, bf16[16,5,128,128]{3,2,1,0:T(8,128)(2,1)}, u32[]{:S(2)}, u32[]{:S(2)}) collective-permute-start(bf16[16,5,128,128]{3,2,1,0:T(8,128)(2,1)S(1)} %bitcast.39), channel_id=1, source_target_pairs={{0,1},{1,0},{2,3},{3,2},{4,5},{5,4},{6,7},{7,6},{8,9},{9,8},{10,11... | collective-permute-start | bytes 7864328 | tf_op jit(solution)/shard_map/ppermute | solution.py:236
  56.0 15.5 %all-to-all-start.2 = ((bf16[16,128,128]{2,1,0:T(8,128)(2,1)}), bf16[16,128,128]{2,1,0:T(8,128)(2,1)S(1)}, u32[]{:S(2)}, u32[]{:S(2)}) async-start(bf16[16,128,128]{2,1,0:T(8,128)(2,1)} %get-tuple-element.36), calls=%async_computation.2 | async-start | bytes 1048576 | tf_op jit(solution)/shard_map/all_to_all | solution.py:228
  78.6 17.2 %all-to-all-start.3 = ((bf16[16,128,128]{2,1,0:T(8,128)(2,1)}), bf16[16,128,128]{2,1,0:T(8,128)(2,1)S(1)}, u32[]{:S(2)}, u32[]{:S(2)}) async-start(bf16[16,128,128]{2,1,0:T(8,128)(2,1)} %shard_map.76), calls=%async_computation.3 | async-start | bytes 1048576 | tf_op jit(solution)/shard_map/all_to_all | solution.py:228
  95.8 31.0 %copy-start.5 = (bf16[10,128,640]{2,1,0:T(8,128)(2,1)S(1)}, bf16[10,128,640]{2,1,0:T(8,128)(2,1)}, u32[]{:S(2)}) copy-start(bf16[10,128,640]{2,1,0:T(8,128)(2,1)} %gather_fusion.1) | copy-start | bytes 4915204
  95.9 5.7 %copy-start.3 = (bf16[16,128,128]{2,1,0:T(8,128)(2,1)}, bf16[16,128,128]{2,1,0:T(8,128)(2,1)S(1)}, u32[]{:S(2)}) copy-start(bf16[16,128,128]{2,1,0:T(8,128)(2,1)S(1)} %all-to-all-done.3.got_ref) | copy-start | bytes 1572868
  95.9 16.7 %all-to-all-start.1 = ((bf16[16,128,128]{2,1,0:T(8,128)(2,1)}), bf16[16,128,128]{2,1,0:T(8,128)(2,1)S(1)}, u32[]{:S(2)}, u32[]{:S(2)}) async-start(bf16[16,128,128]{2,1,0:T(8,128)(2,1)} %shard_map.74), calls=%async_computation.1 | async-start | bytes 1048576 | tf_op jit(solution)/shard_map/all_to_all | solution.py:228
  103.5 14.0 %collective-permute-start.13 = (bf16[128,1280]{1,0:T(8,128)(2,1)}, bf16[128,1280]{1,0:T(8,128)(2,1)S(1)}, u32[]{:S(2)}, u32[]{:S(2)}) collective-permute-start(bf16[128,1280]{1,0:T(8,128)(2,1)} %shard_map.77), channel_id=1, source_target_pairs={{0,4},{2,6},{4,0},{6,2},{1,5},{3,7},{5,1},{7,3},{8,12},{10,14},{12... | collective-permute-start | bytes 983048 | tf_op jit(solution)/shard_map/ppermute | solution.py:232
  106.4 15.6 %collective-permute-start.11 = (bf16[128,1280]{1,0:T(8,128)(2,1)}, bf16[128,1280]{1,0:T(8,128)(2,1)S(1)}, u32[]{:S(2)}, u32[]{:S(2)}) collective-permute-start(bf16[128,1280]{1,0:T(8,128)(2,1)} %shard_map.77), channel_id=1, source_target_pairs={{0,6},{2,0},{4,2},{6,4},{1,7},{3,1},{5,3},{7,5},{8,14},{10,8},{12,... | collective-permute-start | bytes 983048 | tf_op jit(solution)/shard_map/ppermute | solution.py:232
  107.2 18.7 %collective-permute-start.9 = (bf16[128,1280]{1,0:T(8,128)(2,1)}, bf16[128,1280]{1,0:T(8,128)(2,1)S(1)}, u32[]{:S(2)}, u32[]{:S(2)}) collective-permute-start(bf16[128,1280]{1,0:T(8,128)(2,1)} %shard_map.77), channel_id=1, source_target_pairs={{0,2},{2,4},{4,6},{6,0},{1,3},{3,5},{5,7},{7,1},{8,10},{10,12},{12... | collective-permute-start | bytes 983048 | tf_op jit(solution)/shard_map/ppermute | solution.py:232
  107.9 18.0 %collective-permute-start.8 = (bf16[128,1280]{1,0:T(8,128)(2,1)}, bf16[128,1280]{1,0:T(8,128)(2,1)}, u32[]{:S(2)}, u32[]{:S(2)}) collective-permute-start(bf16[128,1280]{1,0:T(8,128)(2,1)} %shard_map.77), channel_id=1, source_target_pairs={{0,1},{1,0},{2,3},{3,2},{4,5},{5,4},{6,7},{7,6},{8,9},{9,8},{10,11... | collective-permute-start | bytes 983048 | tf_op jit(solution)/shard_map/ppermute | solution.py:236
  115.3 13.4 %copy-start.7 = (bf16[128,1280]{1,0:T(8,128)(2,1)S(1)}, bf16[128,1280]{1,0:T(8,128)(2,1)}, u32[]{:S(2)}) copy-start(bf16[128,1280]{1,0:T(8,128)(2,1)} %shard_map.75) | copy-start | bytes 983044
  115.3 13.3 %collective-permute-start.1 = (bf16[128,1280]{1,0:T(8,128)(2,1)}, bf16[128,1280]{1,0:T(8,128)(2,1)}, u32[]{:S(2)}, u32[]{:S(2)}) collective-permute-start(bf16[128,1280]{1,0:T(8,128)(2,1)} %shard_map.75), channel_id=1, source_target_pairs={{0,1},{1,0},{2,3},{3,2},{4,5},{5,4},{6,7},{7,6},{8,9},{9,8},{10,11... | collective-permute-start | bytes 983048 | tf_op jit(solution)/shard_map/ppermute | solution.py:236
  117.5 13.0 %collective-permute-start.6 = (bf16[128,1280]{1,0:T(8,128)(2,1)}, bf16[128,1280]{1,0:T(8,128)(2,1)S(1)}, u32[]{:S(2)}, u32[]{:S(2)}) collective-permute-start(bf16[128,1280]{1,0:T(8,128)(2,1)} %shard_map.75), channel_id=1, source_target_pairs={{0,4},{2,6},{4,0},{6,2},{1,5},{3,7},{5,1},{7,3},{8,12},{10,14},{12... | collective-permute-start | bytes 983048 | tf_op jit(solution)/shard_map/ppermute | solution.py:232
  122.1 12.8 %collective-permute-start.4 = (bf16[128,1280]{1,0:T(8,128)(2,1)}, bf16[128,1280]{1,0:T(8,128)(2,1)S(1)}, u32[]{:S(2)}, u32[]{:S(2)}) collective-permute-start(bf16[128,1280]{1,0:T(8,128)(2,1)} %shard_map.75), channel_id=1, source_target_pairs={{0,6},{2,0},{4,2},{6,4},{1,7},{3,1},{5,3},{7,5},{8,14},{10,8},{12,... | collective-permute-start | bytes 983048 | tf_op jit(solution)/shard_map/ppermute | solution.py:232
  125.9 10.8 %collective-permute-start.2 = (bf16[128,1280]{1,0:T(8,128)(2,1)}, bf16[128,1280]{1,0:T(8,128)(2,1)S(1)}, u32[]{:S(2)}, u32[]{:S(2)}) collective-permute-start(bf16[128,1280]{1,0:T(8,128)(2,1)} %shard_map.75), channel_id=1, source_target_pairs={{0,2},{2,4},{4,6},{6,0},{1,3},{3,5},{5,7},{7,1},{8,10},{10,12},{12... | collective-permute-start | bytes 983048 | tf_op jit(solution)/shard_map/ppermute | solution.py:232
  125.9 11.5 %collective-permute-start.10 = (bf16[128,1280]{1,0:T(8,128)(2,1)S(1)}, bf16[128,1280]{1,0:T(8,128)(2,1)S(1)}, u32[]{:S(2)}, u32[]{:S(2)}) collective-permute-start(bf16[128,1280]{1,0:T(8,128)(2,1)S(1)} %collective-permute-done.9), channel_id=1, source_target_pairs={{0,1},{1,0},{2,3},{3,2},{4,5},{5,4},{6,7},{7,6},{8,9},{9,8},{10,11... | collective-permute-start | bytes 983048 | tf_op jit(solution)/shard_map/ppermute | solution.py:236
  128.6 8.8 %copy-start = (bf16[10,128,640]{2,1,0:T(8,128)(2,1)S(1)}, bf16[10,128,640]{2,1,0:T(8,128)(2,1)}, u32[]{:S(2)}) copy-start(bf16[10,128,640]{2,1,0:T(8,128)(2,1)} %gather_fusion.2) | copy-start | bytes 4915204
  128.6 9.5 %collective-permute-start.14 = (bf16[128,1280]{1,0:T(8,128)(2,1)S(1)}, bf16[128,1280]{1,0:T(8,128)(2,1)S(1)}, u32[]{:S(2)}, u32[]{:S(2)}) collective-permute-start(bf16[128,1280]{1,0:T(8,128)(2,1)S(1)} %collective-permute-done.13), channel_id=1, source_target_pairs={{0,1},{1,0},{2,3},{3,2},{4,5},{5,4},{6,7},{7,6},{8,9},{9,8},{10,11... | collective-permute-start | bytes 983048 | tf_op jit(solution)/shard_map/ppermute | solution.py:236
  130.5 7.7 %copy-start.4 = (bf16[10,128,640]{2,1,0:T(8,128)(2,1)S(1)}, bf16[10,128,640]{2,1,0:T(8,128)(2,1)}, u32[]{:S(2)}) copy-start(bf16[10,128,640]{2,1,0:T(8,128)(2,1)} %gather_fusion.4) | copy-start | bytes 4915204
  130.5 8.3 %collective-permute-start.12 = (bf16[128,1280]{1,0:T(8,128)(2,1)S(1)}, bf16[128,1280]{1,0:T(8,128)(2,1)S(1)}, u32[]{:S(2)}, u32[]{:S(2)}) collective-permute-start(bf16[128,1280]{1,0:T(8,128)(2,1)S(1)} %collective-permute-done.11), channel_id=1, source_target_pairs={{0,1},{1,0},{2,3},{3,2},{4,5},{5,4},{6,7},{7,6},{8,9},{9,8},{10,11... | collective-permute-start | bytes 983048 | tf_op jit(solution)/shard_map/ppermute | solution.py:236
  134.9 5.4 %collective-permute-start.7 = (bf16[128,1280]{1,0:T(8,128)(2,1)S(1)}, bf16[128,1280]{1,0:T(8,128)(2,1)S(1)}, u32[]{:S(2)}, u32[]{:S(2)}) collective-permute-start(bf16[128,1280]{1,0:T(8,128)(2,1)S(1)} %collective-permute-done.6), channel_id=1, source_target_pairs={{0,1},{1,0},{2,3},{3,2},{4,5},{5,4},{6,7},{7,6},{8,9},{9,8},{10,11... | collective-permute-start | bytes 983048 | tf_op jit(solution)/shard_map/ppermute | solution.py:236
  136.7 5.0 %collective-permute-start.5 = (bf16[128,1280]{1,0:T(8,128)(2,1)S(1)}, bf16[128,1280]{1,0:T(8,128)(2,1)S(1)}, u32[]{:S(2)}, u32[]{:S(2)}) collective-permute-start(bf16[128,1280]{1,0:T(8,128)(2,1)S(1)} %collective-permute-done.4), channel_id=1, source_target_pairs={{0,1},{1,0},{2,3},{3,2},{4,5},{5,4},{6,7},{7,6},{8,9},{9,8},{10,11... | collective-permute-start | bytes 983048 | tf_op jit(solution)/shard_map/ppermute | solution.py:236
  137.4 3.6 %collective-permute-start.3 = (bf16[128,1280]{1,0:T(8,128)(2,1)S(1)}, bf16[128,1280]{1,0:T(8,128)(2,1)S(1)}, u32[]{:S(2)}, u32[]{:S(2)}) collective-permute-start(bf16[128,1280]{1,0:T(8,128)(2,1)S(1)} %collective-permute-done.2), channel_id=1, source_target_pairs={{0,1},{1,0},{2,3},{3,2},{4,5},{5,4},{6,7},{7,6},{8,9},{9,8},{10,11... | collective-permute-start | bytes 983048 | tf_op jit(solution)/shard_map/ppermute | solution.py:236
  (4 other events, 4.4 us)

commit v3 on v2

--- a/solution.py
+++ b/solution.py
@@ -177,7 +177,33 @@
             pltpu.SemaphoreType.DMA((3,)),
         ],
         compiler_params=pltpu.CompilerParams(vmem_limit_bytes=24 * 2**20),
+        cost_estimate=pl.CostEstimate(flops=8 * 10**9, bytes_accessed=8 * 2**20, transcendentals=4 * 10**6),
     )(meta, q_of, k_of, valid_of, own, other, query)
+
+
+def gather_kernel(heads, w_ref, *rest):
+    out_refs, sems = rest[:PLANES], rest[PLANES]
+    copies = []
+    for n in range(HEADS):
+        rows = pl.ds(pl.multiple_of(heads[n] * TILE, TILE), TILE)
+        part = out_refs[n // PLANE_HEADS].at[pl.ds(n % PLANE_HEADS * TILE, TILE)]
+        copies.append(pltpu.make_async_copy(w_ref.at[rows], part, sems.at[n]))
+        copies[-1].start()
+    for copy in copies:
+        copy.wait()
+
+
+def gather(w_out, heads):
+    rows = PLANE_HEADS * TILE
+    return pl.pallas_call(
+        gather_kernel,
+        in_specs=[pl.BlockSpec(memory_space=pltpu.SMEM), pl.BlockSpec(memory_space=pl.ANY)],
+        out_specs=[pl.BlockSpec(memory_space=pltpu.VMEM)] * PLANES,
+        out_shape=[jax.ShapeDtypeStruct((rows, w_out.shape[1]), w_out.dtype)] * PLANES,
+        scratch_shapes=[pltpu.SemaphoreType.DMA((HEADS,))],
+        compiler_params=pltpu.CompilerParams(vmem_limit_bytes=20 * 2**20),
+        cost_estimate=pl.CostEstimate(flops=0, bytes_accessed=13 * 2**20, transcendentals=0),
+    )(heads, w_out)
 
 
 def item_lists(allowed, mine):
@@ -240,7 +266,7 @@
     chip = lax.axis_index("x") * 4 + lax.axis_index("z")
     plane = lax.axis_index("y")
     core = lax.axis_index("c")
-    tile_work = jnp.sum(tile_mask, axis=2)
+    tile_work = jnp.sum(tile_mask, axis=1)
     head_at, work_at = head_plan(jnp.sum(tile_work, axis=1))
     plane_heads = lax.dynamic_slice_in_dim(head_at, plane * PLANE_HEADS, PLANE_HEADS)
     chips, first = chip_plan(lax.dynamic_slice_in_dim(work_at, plane * PLANE_HEADS, PLANE_HEADS))
@@ -265,11 +291,10 @@
     allowed = lax.dynamic_index_in_dim(allowed.reshape(CHIPS, 2, 2, 4 * CHIPS), core, 1, keepdims=False)
     source = lax.dynamic_slice_in_dim(owner, 2 * chip, 2, 1)
 
-    w_heads = w_out.reshape(HEADS, TILE, w_out.shape[1])
-    weights = []
-    for ahead in (0, 3, 1, 2):
-        w_order = lax.dynamic_slice_in_dim(head_at, (plane + ahead) % PLANES * PLANE_HEADS, PLANE_HEADS)
-        weights.append(jnp.take(w_heads, w_order, axis=0, mode="clip").reshape(PLANE_HEADS * TILE, -1))
+    w_order = jnp.concatenate(
+        [lax.dynamic_slice_in_dim(head_at, (plane + k) % PLANES * PLANE_HEADS, PLANE_HEADS) for k in (0, 3, 1, 2)]
+    )
+    weights = gather(w_out, w_order)
     lists = [item_lists(allowed[:, sub], mine_tiles[:, sub]) for sub in range(2)]
     got, lists, weights, second_send = lax.optimization_barrier((got, lists, weights, second_send))
     got_other = swap(got)

time: 145 us -> 148 us (1.021)
  local copies, waits for them, and re-layouts: 27.4 us -> 13.1 us
  Pallas kernels: 26.6 us -> 35.8 us
  starting transfers between devices: 49.6 us -> 54 us
  matrix products: 8 us -> 11.5 us
    gather x4 -> x0, local copies, waits for them, and re-layouts: 19.6 us -> none  [shards(): jnp.take(w_heads, w_order, axis=0, mode='clip')]
    pallas_call x0 -> x1, Pallas kernels: none -> 9.59 us  [gather(): pl.pallas_call(gather_kernel, in_specs=[pl.BlockSpec(memory_space=pltpu.S...]
    unnamed x18 -> x20, local copies, waits for them, and re-layouts: 2.5 us -> 7.85 us
    ppermute x6, starting transfers between devices: 11.1 us -> 16.4 us  [along_y(): lax.ppermute(block, 'y', [(i, (i + step) % PLANES) for i in range(PLANES)])]
    all_to_all x4, waiting for transfers between devices: 10.1 us -> 13.8 us  [exchange(): lax.all_to_all(block, TOKENS_AXES, split_axis=0, concat_axis=0, tiled=True)]
    ppermute x6, waiting for transfers between devices: 5.56 us -> 2.05 us  [along_y(): lax.ppermute(block, 'y', [(i, (i + step) % PLANES) for i in range(PLANES)])]
    dot_general x8, matrix products: 7.6 us -> 11.1 us  [shards(): jnp.dot(both, weights[k], preferred_element_type=jnp.float32)]
  transfers between devices with their start and end apart: 19 -> 19, of which waited for: 3 -> 4; matrix products, arithmetic and copies ran while one was open for 25% -> 14% of each run, Pallas kernels for 10% -> 16%
where the time goes in v3:
time: 148 us; the launch traced here: 147 us
  starting transfers between devices  54 us (36%)
  Pallas kernels  35.8 us (24%)
  waiting for transfers between devices  15.9 us (11%)
  local copies, waits for them, and re-layouts  13.1 us (9%)
  matrix products  11.5 us (8%)
  other arithmetic  10 us (7%)
  between operations  7.02 us (5%)
    all_to_all x4, starting transfers between devices, exchange(): lax.all_to_all(block, TOKENS_AXES, split_axis=0, concat_axis=0, tiled=True)  24.6 us
    pallas_call x2, Pallas kernels, attend(): pl.pallas_call(functools.partial(attend_kernel, TILE ** (-0.5) * LOG2E, q...  17.5 us
    ppermute x6, starting transfers between devices, along_y(): lax.ppermute(block, 'y', [(i, (i + step) % PLANES) for i in range(PLANES)])  16.4 us
    all_to_all x4, waiting for transfers between devices, exchange(): lax.all_to_all(block, TOKENS_AXES, split_axis=0, concat_axis=0, tiled=True)  13.8 us
    ppermute x9, starting transfers between devices, swap(): return lax.ppermute(block, 'c', [(0, 1), (1, 0)])  13 us
    dot_general x8, matrix products, shards(): jnp.dot(both, weights[k], preferred_element_type=jnp.float32)  11.1 us
    pallas_call x1, Pallas kernels, gather(): pl.pallas_call(gather_kernel, in_specs=[pl.BlockSpec(memory_space=pltpu.S...  9.59 us
    unnamed x20, local copies, waits for them, and re-layouts  7.85 us
  transfers between devices with their start and end apart: 19, of which 4 were waited for; matrix products, arithmetic and copies ran while one was open for 14% of the time, Pallas kernels for 16%

profile of v3, /device:TPU:1, one launch (start us, length us, event | category | flops | bytes accessed | tf_op | source)
XLA Modules:
  0.0 147.3 jit_solution(5210551101634942859)
XLA Ops:
  0.0 2.1 %fusion.72 = (s32[40,64]{1,0:T(8,128)S(1)}, s32[40]{0:T(128)S(1)}) fusion(s32[40,64,64]{2,1,0:T(8,128)} %param.13), kind=kLoop, calls=%fused_computation.189 | loop fusion | flops 325080 | bytes 665760 | tf_op jit(solution)/shard_map/reduce_sum | solution.py:269
  4.1 4.8 %shard_map.73 = (bf16[16,640,128]{2,1,0:T(8,128)(2,1)}, bf16[16,128,128]{2,1,0:T(8,128)(2,1)}) custom-call(s32[17]{0:T(128)} %pad_add_fusion.heads, bf16[512,5120]{1,0:T(8,128)(2,1)} %q_ref.1, bf16[512,5120]{1,0:T(8,128)(2,1)} %k_ref.1, bf16[512,5120]{1,0:T(8,128)(2,1)} %v_ref.1), custom_call_target="tpu_custom_call" | custom-call | tf_op jit(solution)/shard_map/pallas_call | solution.py:88
  9.0 8.5 %all-to-all-start = ((bf16[16,640,128]{2,1,0:T(8,128)(2,1)}), bf16[16,640,128]{2,1,0:T(8,128)(2,1)}, u32[]{:S(2)}, u32[]{:S(2)}) async-start(bf16[16,640,128]{2,1,0:T(8,128)(2,1)} %get-tuple-element.25), calls=%async_computation | async-start | bytes 5242880 | tf_op jit(solution)/shard_map/all_to_all | solution.py:254
  33.6 2.9 %copy-done = bf16[5120,640]{1,0:T(8,128)(2,1)S(1)} copy-done((bf16[5120,640]{1,0:T(8,128)(2,1)S(1)}, bf16[5120,640]{1,0:T(8,128)(2,1)}, u32[]{:S(2)}) %copy-start) | copy-done | bytes 6553624
  36.5 9.6 %shard_map.74 = (bf16[1280,640]{1,0:T(8,128)(2,1)S(1)}, bf16[1280,640]{1,0:T(8,128)(2,1)S(1)}, bf16[1280,640]{1,0:T(8,128)(2,1)S(1)}, bf16[1280,640]{1,0:T(8,128)(2,1)S(1)}) custom-call(s32[40]{0:T(128)S(1)} %pad_add_fusion.1.heads, bf16[5120,640]{1,0:T(8,128)(2,1)S(1)} %copy-done), custom_call_target="tpu_custom_call" | custom-call | bytes 13631488 | tf_op jit(solution)/shard_map/pallas_call | solution.py:198
  48.5 3.7 %all-to-all-done = bf16[16,640,128]{2,1,0:T(8,128)(2,1)} async-done(((bf16[16,640,128]{2,1,0:T(8,128)(2,1)}), bf16[16,640,128]{2,1,0:T(8,128)(2,1)}, u32[]{:S(2)}, u32[]{:S(2)}) %all-to-all-start) | async-done | bytes 2621472 | tf_op jit(solution)/shard_map/all_to_all | solution.py:254
  52.2 2.7 %collective-permute-start = (bf16[16,5,128,128]{3,2,1,0:T(8,128)(2,1)}, bf16[16,5,128,128]{3,2,1,0:T(8,128)(2,1)}, u32[]{:S(2)}, u32[]{:S(2)}) collective-permute-start(bf16[16,5,128,128]{3,2,1,0:T(8,128)(2,1)} %bitcast.3.own_ref.query_ref), channel_id=1, source_target_pairs={{0,1},{1,0},{2,3},{3,2},{4,5},{5,4},{6,7},{7,6},{8,9},{9,8},{10,11... | collective-permute-start | bytes 7864328 | tf_op jit(solution)/shard_map/ppermute | solution.py:262
  54.9 5.9 %all-to-all-start.2 = ((bf16[16,128,128]{2,1,0:T(8,128)(2,1)}), bf16[16,128,128]{2,1,0:T(8,128)(2,1)}, u32[]{:S(2)}, u32[]{:S(2)}) async-start(bf16[16,128,128]{2,1,0:T(8,128)(2,1)} %get-tuple-element.44), calls=%async_computation.2 | async-start | bytes 1048576 | tf_op jit(solution)/shard_map/all_to_all | solution.py:254
  61.0 10.0 %all-to-all-done.2 = bf16[16,128,128]{2,1,0:T(8,128)(2,1)} async-done(((bf16[16,128,128]{2,1,0:T(8,128)(2,1)}), bf16[16,128,128]{2,1,0:T(8,128)(2,1)}, u32[]{:S(2)}, u32[]{:S(2)}) %all-to-all-start.2) | async-done | bytes 524320 | tf_op jit(solution)/shard_map/all_to_all | solution.py:254
  71.1 6.9 %shard_map.77 = bf16[16,128,128]{2,1,0:T(8,128)(2,1)S(1)} custom-call(s32[2]{0:T(128)S(1)} %pad_add_fusion.3.meta, s32[256]{0:T(256)S(1)} %broadcast_minimum_fusion.q_of, s32[1024]{0:T(1024)S(1)} %convert_element_type.110.k_of, s32[256]{0:T(256)S(1)} %get-tuple-element.43.valid_of, bf16[16,5,128,128]{3,2,1,0:T(8,128)(2,1)} %bitcast.3.own_ref.query_ref, ...), custom_call_target="tpu_custom_call" | custom-call | flops 8000000000 | bytes 8388608 | tf_op jit(solution)/shard_map/pallas_call | solution.py:166
  78.8 5.0 %all-to-all-start.3 = ((bf16[16,128,128]{2,1,0:T(8,128)(2,1)}), bf16[16,128,128]{2,1,0:T(8,128)(2,1)}, u32[]{:S(2)}, u32[]{:S(2)}) async-start(bf16[16,128,128]{2,1,0:T(8,128)(2,1)} %copy-done.2), calls=%async_computation.3 | async-start | bytes 1048576 | tf_op jit(solution)/shard_map/all_to_all | solution.py:254
  83.8 10.6 %shard_map.75 = bf16[16,128,128]{2,1,0:T(8,128)(2,1)S(1)} custom-call(s32[2]{0:T(128)S(1)} %pad_add_fusion.2.meta, s32[256]{0:T(256)S(1)} %broadcast_minimum_fusion.1.q_of, s32[1024]{0:T(1024)S(1)} %convert_element_type.104.k_of, s32[256]{0:T(256)S(1)} %get-tuple-element.34.valid_of, bf16[16,5,128,128]{3,2,1,0:T(8,128)(2,1)} %bitcast.3.own_ref.query_ref, ...), custom_call_target="tpu_custom_call" | custom-call | flops 8000000000 | bytes 8388608 | tf_op jit(solution)/shard_map/pallas_call | solution.py:166
  95.2 5.2 %all-to-all-start.1 = ((bf16[16,128,128]{2,1,0:T(8,128)(2,1)}), bf16[16,128,128]{2,1,0:T(8,128)(2,1)}, u32[]{:S(2)}, u32[]{:S(2)}) async-start(bf16[16,128,128]{2,1,0:T(8,128)(2,1)} %copy-done.1), calls=%async_computation.1 | async-start | bytes 1048576 | tf_op jit(solution)/shard_map/all_to_all | solution.py:254
  101.2 1.9 %shard_map.78 = bf16[128,1280]{1,0:T(8,128)(2,1)} custom-call(s32[10]{0:T(128)} %get-tuple-element.52.source, bf16[16,128,128]{2,1,0:T(8,128)(2,1)} %all-to-all-done.3.got_ref), custom_call_target="tpu_custom_call" | custom-call | tf_op jit(solution)/shard_map/pallas_call | solution.py:245
  103.1 4.8 %collective-permute-start.13 = (bf16[128,1280]{1,0:T(8,128)(2,1)}, bf16[128,1280]{1,0:T(8,128)(2,1)}, u32[]{:S(2)}, u32[]{:S(2)}) collective-permute-start(bf16[128,1280]{1,0:T(8,128)(2,1)} %shard_map.78), channel_id=1, source_target_pairs={{0,4},{2,6},{4,0},{6,2},{1,5},{3,7},{5,1},{7,3},{8,12},{10,14},{12... | collective-permute-start | bytes 983048 | tf_op jit(solution)/shard_map/ppermute | solution.py:258
  109.4 3.6 %collective-permute-start.8 = (bf16[128,1280]{1,0:T(8,128)(2,1)}, bf16[128,1280]{1,0:T(8,128)(2,1)}, u32[]{:S(2)}, u32[]{:S(2)}) collective-permute-start(bf16[128,1280]{1,0:T(8,128)(2,1)} %shard_map.78), channel_id=1, source_target_pairs={{0,1},{1,0},{2,3},{3,2},{4,5},{5,4},{6,7},{7,6},{8,9},{9,8},{10,11... | collective-permute-start | bytes 983048 | tf_op jit(solution)/shard_map/ppermute | solution.py:262
  113.0 1.9 %shard_map.76 = bf16[128,1280]{1,0:T(8,128)(2,1)} custom-call(s32[10]{0:T(128)} %get-tuple-element.51.source, bf16[16,128,128]{2,1,0:T(8,128)(2,1)} %all-to-all-done.1.got_ref), custom_call_target="tpu_custom_call" | custom-call | tf_op jit(solution)/shard_map/pallas_call | solution.py:245
  115.0 5.1 %collective-permute-start.6 = (bf16[128,1280]{1,0:T(8,128)(2,1)}, bf16[128,1280]{1,0:T(8,128)(2,1)S(1)}, u32[]{:S(2)}, u32[]{:S(2)}) collective-permute-start(bf16[128,1280]{1,0:T(8,128)(2,1)} %shard_map.76), channel_id=1, source_target_pairs={{0,4},{2,6},{4,0},{6,2},{1,5},{3,7},{5,1},{7,3},{8,12},{10,14},{12... | collective-permute-start | bytes 983048 | tf_op jit(solution)/shard_map/ppermute | solution.py:258
  120.1 2.6 %collective-permute-start.4 = (bf16[128,1280]{1,0:T(8,128)(2,1)}, bf16[128,1280]{1,0:T(8,128)(2,1)S(1)}, u32[]{:S(2)}, u32[]{:S(2)}) collective-permute-start(bf16[128,1280]{1,0:T(8,128)(2,1)} %shard_map.76), channel_id=1, source_target_pairs={{0,6},{2,0},{4,2},{6,4},{1,7},{3,1},{5,3},{7,5},{8,14},{10,8},{12,... | collective-permute-start | bytes 983048 | tf_op jit(solution)/shard_map/ppermute | solution.py:258
  122.7 2.4 %collective-permute-start.2 = (bf16[128,1280]{1,0:T(8,128)(2,1)}, bf16[128,1280]{1,0:T(8,128)(2,1)S(1)}, u32[]{:S(2)}, u32[]{:S(2)}) collective-permute-start(bf16[128,1280]{1,0:T(8,128)(2,1)} %shard_map.76), channel_id=1, source_target_pairs={{0,2},{2,4},{4,6},{6,0},{1,3},{3,5},{5,7},{7,1},{8,10},{10,12},{12... | collective-permute-start | bytes 983048 | tf_op jit(solution)/shard_map/ppermute | solution.py:258
  125.1 2.5 %collective-permute-start.10 = (bf16[128,1280]{1,0:T(8,128)(2,1)}, bf16[128,1280]{1,0:T(8,128)(2,1)S(1)}, u32[]{:S(2)}, u32[]{:S(2)}) collective-permute-start(bf16[128,1280]{1,0:T(8,128)(2,1)} %collective-permute-done.9), channel_id=1, source_target_pairs={{0,1},{1,0},{2,3},{3,2},{4,5},{5,4},{6,7},{7,6},{8,9},{9,8},{10,11... | collective-permute-start | bytes 983048 | tf_op jit(solution)/shard_map/ppermute | solution.py:262
  127.6 2.3 %fusion.18 = f32[256,640]{1,0:T(8,128)S(1)} fusion(bf16[1280,640]{1,0:T(8,128)(2,1)} %copy-done.5, bf16[128,1280]{1,0:T(8,128)(2,1)} %collective-permute-done.8, bf16[128,1280]{1,0:T(8,128)(2,1)} %shard_map.78), kind=kOutput, calls=%fused_computation.24 | convolution fusion | flops 420741120 | bytes 2949120 | tf_op jit(solution)/shard_map/dot_general | solution.py:314
  133.9 2.3 %collective-permute-start.7 = (bf16[128,1280]{1,0:T(8,128)(2,1)S(1)}, bf16[128,1280]{1,0:T(8,128)(2,1)S(1)}, u32[]{:S(2)}, u32[]{:S(2)}) collective-permute-start(bf16[128,1280]{1,0:T(8,128)(2,1)S(1)} %collective-permute-done.6), channel_id=1, source_target_pairs={{0,1},{1,0},{2,3},{3,2},{4,5},{5,4},{6,7},{7,6},{8,9},{9,8},{10,11... | collective-permute-start | bytes 983048 | tf_op jit(solution)/shard_map/ppermute | solution.py:262
  141.3 1.7 %fusion.2 = f32[256,640]{1,0:T(8,128)S(1)} fusion(f32[256,640]{1,0:T(8,128)S(1)} %fusion.28, f32[256,640]{1,0:T(8,128)S(1)} %convolution_add_fusion.1, bf16[1280,640]{1,0:T(8,128)(2,1)S(1)} %get-tuple-element.38, bf16[128,1280]{1,0:T(8,128)(2,1)S(1)} %collective-permute-done.12, bf16[128,1280]{1,0:T(8,128)(2,1)} %collective-permute-done.11), kind=kOutput, calls=%fused_computation.5 | convolution fusion | flops 421068800 | bytes 4259840 | tf_op jit(solution)/shard_map/dot_general | solution.py:314
  (128 shorter events, 31.1 us)
Async XLA Ops:
  9.0 43.2 %all-to-all-start = ((bf16[16,640,128]{2,1,0:T(8,128)(2,1)}), bf16[16,640,128]{2,1,0:T(8,128)(2,1)}, u32[]{:S(2)}, u32[]{:S(2)}) async-start(bf16[16,640,128]{2,1,0:T(8,128)(2,1)} %get-tuple-element.25), calls=%async_computation | async-start | bytes 5242880 | tf_op jit(solution)/shard_map/all_to_all | solution.py:254
  33.6 2.9 %copy-start = (bf16[5120,640]{1,0:T(8,128)(2,1)S(1)}, bf16[5120,640]{1,0:T(8,128)(2,1)}, u32[]{:S(2)}) copy-start(bf16[5120,640]{1,0:T(8,128)(2,1)} %w_ref.1) | copy-start | bytes 19660804
  46.1 1.2 copy-start.3
  52.2 18.8 %collective-permute-start = (bf16[16,5,128,128]{3,2,1,0:T(8,128)(2,1)}, bf16[16,5,128,128]{3,2,1,0:T(8,128)(2,1)}, u32[]{:S(2)}, u32[]{:S(2)}) collective-permute-start(bf16[16,5,128,128]{3,2,1,0:T(8,128)(2,1)} %bitcast.3.own_ref.query_ref), channel_id=1, source_target_pairs={{0,1},{1,0},{2,3},{3,2},{4,5},{5,4},{6,7},{7,6},{8,9},{9,8},{10,11... | collective-permute-start | bytes 7864328 | tf_op jit(solution)/shard_map/ppermute | solution.py:262
  54.9 16.1 %all-to-all-start.2 = ((bf16[16,128,128]{2,1,0:T(8,128)(2,1)}), bf16[16,128,128]{2,1,0:T(8,128)(2,1)}, u32[]{:S(2)}, u32[]{:S(2)}) async-start(bf16[16,128,128]{2,1,0:T(8,128)(2,1)} %get-tuple-element.44), calls=%async_computation.2 | async-start | bytes 1048576 | tf_op jit(solution)/shard_map/all_to_all | solution.py:254
  78.8 16.5 %all-to-all-start.3 = ((bf16[16,128,128]{2,1,0:T(8,128)(2,1)}), bf16[16,128,128]{2,1,0:T(8,128)(2,1)}, u32[]{:S(2)}, u32[]{:S(2)}) async-start(bf16[16,128,128]{2,1,0:T(8,128)(2,1)} %copy-done.2), calls=%async_computation.3 | async-start | bytes 1048576 | tf_op jit(solution)/shard_map/all_to_all | solution.py:254
  95.2 17.8 %all-to-all-start.1 = ((bf16[16,128,128]{2,1,0:T(8,128)(2,1)}), bf16[16,128,128]{2,1,0:T(8,128)(2,1)}, u32[]{:S(2)}, u32[]{:S(2)}) async-start(bf16[16,128,128]{2,1,0:T(8,128)(2,1)} %copy-done.1), calls=%async_computation.1 | async-start | bytes 1048576 | tf_op jit(solution)/shard_map/all_to_all | solution.py:254
  103.1 11.9 %collective-permute-start.13 = (bf16[128,1280]{1,0:T(8,128)(2,1)}, bf16[128,1280]{1,0:T(8,128)(2,1)}, u32[]{:S(2)}, u32[]{:S(2)}) collective-permute-start(bf16[128,1280]{1,0:T(8,128)(2,1)} %shard_map.78), channel_id=1, source_target_pairs={{0,4},{2,6},{4,0},{6,2},{1,5},{3,7},{5,1},{7,3},{8,12},{10,14},{12... | collective-permute-start | bytes 983048 | tf_op jit(solution)/shard_map/ppermute | solution.py:258
  107.9 12.2 %collective-permute-start.11 = (bf16[128,1280]{1,0:T(8,128)(2,1)}, bf16[128,1280]{1,0:T(8,128)(2,1)}, u32[]{:S(2)}, u32[]{:S(2)}) collective-permute-start(bf16[128,1280]{1,0:T(8,128)(2,1)} %shard_map.78), channel_id=1, source_target_pairs={{0,6},{2,0},{4,2},{6,4},{1,7},{3,1},{5,3},{7,5},{8,14},{10,8},{12,... | collective-permute-start | bytes 983048 | tf_op jit(solution)/shard_map/ppermute | solution.py:258
  108.6 14.1 %collective-permute-start.9 = (bf16[128,1280]{1,0:T(8,128)(2,1)}, bf16[128,1280]{1,0:T(8,128)(2,1)}, u32[]{:S(2)}, u32[]{:S(2)}) collective-permute-start(bf16[128,1280]{1,0:T(8,128)(2,1)} %shard_map.78), channel_id=1, source_target_pairs={{0,2},{2,4},{4,6},{6,0},{1,3},{3,5},{5,7},{7,1},{8,10},{10,12},{12... | collective-permute-start | bytes 983048 | tf_op jit(solution)/shard_map/ppermute | solution.py:258
  109.4 15.7 %collective-permute-start.8 = (bf16[128,1280]{1,0:T(8,128)(2,1)}, bf16[128,1280]{1,0:T(8,128)(2,1)}, u32[]{:S(2)}, u32[]{:S(2)}) collective-permute-start(bf16[128,1280]{1,0:T(8,128)(2,1)} %shard_map.78), channel_id=1, source_target_pairs={{0,1},{1,0},{2,3},{3,2},{4,5},{5,4},{6,7},{7,6},{8,9},{9,8},{10,11... | collective-permute-start | bytes 983048 | tf_op jit(solution)/shard_map/ppermute | solution.py:262
  115.0 15.0 %collective-permute-start.1 = (bf16[128,1280]{1,0:T(8,128)(2,1)}, bf16[128,1280]{1,0:T(8,128)(2,1)}, u32[]{:S(2)}, u32[]{:S(2)}) collective-permute-start(bf16[128,1280]{1,0:T(8,128)(2,1)} %shard_map.76), channel_id=1, source_target_pairs={{0,1},{1,0},{2,3},{3,2},{4,5},{5,4},{6,7},{7,6},{8,9},{9,8},{10,11... | collective-permute-start | bytes 983048 | tf_op jit(solution)/shard_map/ppermute | solution.py:262
  115.0 15.1 %copy-start.6 = (bf16[1280,640]{1,0:T(8,128)(2,1)S(1)}, bf16[1280,640]{1,0:T(8,128)(2,1)}, u32[]{:S(2)}) copy-start(bf16[1280,640]{1,0:T(8,128)(2,1)} %copy-done.5) | copy-start | bytes 4915204
  115.0 15.1 %copy-start.8 = (bf16[128,1280]{1,0:T(8,128)(2,1)S(1)}, bf16[128,1280]{1,0:T(8,128)(2,1)}, u32[]{:S(2)}) copy-start(bf16[128,1280]{1,0:T(8,128)(2,1)} %shard_map.76) | copy-start | bytes 983044
  115.0 16.7 %collective-permute-start.6 = (bf16[128,1280]{1,0:T(8,128)(2,1)}, bf16[128,1280]{1,0:T(8,128)(2,1)S(1)}, u32[]{:S(2)}, u32[]{:S(2)}) collective-permute-start(bf16[128,1280]{1,0:T(8,128)(2,1)} %shard_map.76), channel_id=1, source_target_pairs={{0,4},{2,6},{4,0},{6,2},{1,5},{3,7},{5,1},{7,3},{8,12},{10,14},{12... | collective-permute-start | bytes 983048 | tf_op jit(solution)/shard_map/ppermute | solution.py:258
  120.1 13.8 %collective-permute-start.4 = (bf16[128,1280]{1,0:T(8,128)(2,1)}, bf16[128,1280]{1,0:T(8,128)(2,1)S(1)}, u32[]{:S(2)}, u32[]{:S(2)}) collective-permute-start(bf16[128,1280]{1,0:T(8,128)(2,1)} %shard_map.76), channel_id=1, source_target_pairs={{0,6},{2,0},{4,2},{6,4},{1,7},{3,1},{5,3},{7,5},{8,14},{10,8},{12,... | collective-permute-start | bytes 983048 | tf_op jit(solution)/shard_map/ppermute | solution.py:258
  122.7 13.9 %collective-permute-start.2 = (bf16[128,1280]{1,0:T(8,128)(2,1)}, bf16[128,1280]{1,0:T(8,128)(2,1)S(1)}, u32[]{:S(2)}, u32[]{:S(2)}) collective-permute-start(bf16[128,1280]{1,0:T(8,128)(2,1)} %shard_map.76), channel_id=1, source_target_pairs={{0,2},{2,4},{4,6},{6,0},{1,3},{3,5},{5,7},{7,1},{8,10},{10,12},{12... | collective-permute-start | bytes 983048 | tf_op jit(solution)/shard_map/ppermute | solution.py:258
  125.1 12.8 %collective-permute-start.10 = (bf16[128,1280]{1,0:T(8,128)(2,1)}, bf16[128,1280]{1,0:T(8,128)(2,1)S(1)}, u32[]{:S(2)}, u32[]{:S(2)}) collective-permute-start(bf16[128,1280]{1,0:T(8,128)(2,1)} %collective-permute-done.9), channel_id=1, source_target_pairs={{0,1},{1,0},{2,3},{3,2},{4,5},{5,4},{6,7},{7,6},{8,9},{9,8},{10,11... | collective-permute-start | bytes 983048 | tf_op jit(solution)/shard_map/ppermute | solution.py:262
  129.9 9.6 %collective-permute-start.14 = (bf16[128,1280]{1,0:T(8,128)(2,1)}, bf16[128,1280]{1,0:T(8,128)(2,1)S(1)}, u32[]{:S(2)}, u32[]{:S(2)}) collective-permute-start(bf16[128,1280]{1,0:T(8,128)(2,1)} %collective-permute-done.13), channel_id=1, source_target_pairs={{0,1},{1,0},{2,3},{3,2},{4,5},{5,4},{6,7},{7,6},{8,9},{9,8},{10,11... | collective-permute-start | bytes 983048 | tf_op jit(solution)/shard_map/ppermute | solution.py:262
  131.7 7.9 %copy-start.4 = (bf16[1280,640]{1,0:T(8,128)(2,1)S(1)}, bf16[1280,640]{1,0:T(8,128)(2,1)}, u32[]{:S(2)}) copy-start(bf16[1280,640]{1,0:T(8,128)(2,1)} %copy-done.3) | copy-start | bytes 4915204
  131.7 9.5 %collective-permute-start.12 = (bf16[128,1280]{1,0:T(8,128)(2,1)}, bf16[128,1280]{1,0:T(8,128)(2,1)S(1)}, u32[]{:S(2)}, u32[]{:S(2)}) collective-permute-start(bf16[128,1280]{1,0:T(8,128)(2,1)} %collective-permute-done.11), channel_id=1, source_target_pairs={{0,1},{1,0},{2,3},{3,2},{4,5},{5,4},{6,7},{7,6},{8,9},{9,8},{10,11... | collective-permute-start | bytes 983048 | tf_op jit(solution)/shard_map/ppermute | solution.py:262
  133.9 9.0 %collective-permute-start.7 = (bf16[128,1280]{1,0:T(8,128)(2,1)S(1)}, bf16[128,1280]{1,0:T(8,128)(2,1)S(1)}, u32[]{:S(2)}, u32[]{:S(2)}) collective-permute-start(bf16[128,1280]{1,0:T(8,128)(2,1)S(1)} %collective-permute-done.6), channel_id=1, source_target_pairs={{0,1},{1,0},{2,3},{3,2},{4,5},{5,4},{6,7},{7,6},{8,9},{9,8},{10,11... | collective-permute-start | bytes 983048 | tf_op jit(solution)/shard_map/ppermute | solution.py:262
  136.6 7.8 %collective-permute-start.5 = (bf16[128,1280]{1,0:T(8,128)(2,1)S(1)}, bf16[128,1280]{1,0:T(8,128)(2,1)S(1)}, u32[]{:S(2)}, u32[]{:S(2)}) collective-permute-start(bf16[128,1280]{1,0:T(8,128)(2,1)S(1)} %collective-permute-done.4), channel_id=1, source_target_pairs={{0,1},{1,0},{2,3},{3,2},{4,5},{5,4},{6,7},{7,6},{8,9},{9,8},{10,11... | collective-permute-start | bytes 983048 | tf_op jit(solution)/shard_map/ppermute | solution.py:262
  137.9 5.8 %collective-permute-start.3 = (bf16[128,1280]{1,0:T(8,128)(2,1)S(1)}, bf16[128,1280]{1,0:T(8,128)(2,1)S(1)}, u32[]{:S(2)}, u32[]{:S(2)}) collective-permute-start(bf16[128,1280]{1,0:T(8,128)(2,1)S(1)} %collective-permute-done.2), channel_id=1, source_target_pairs={{0,1},{1,0},{2,3},{3,2},{4,5},{5,4},{6,7},{7,6},{8,9},{9,8},{10,11... | collective-permute-start | bytes 983048 | tf_op jit(solution)/shard_map/ppermute | solution.py:262
  (5 other events, 5.0 us)

commit v4 on v2

--- a/solution.py
+++ b/solution.py
@@ -47,7 +47,7 @@
     return chips, first
 
 
-def pack_kernel(heads, q_ref, k_ref, v_ref, first_ref, second_ref, held, turned, sem_in, sem_out):
+def pack_kernel(heads, q_ref, k_ref, v_ref, out_ref, held, turned, sem_in, sem_out):
     start = pl.multiple_of(heads[CHIPS] * HALF, HALF)
     rows = pl.ds(start, HALF)
     loads, stores = [], []
@@ -69,14 +69,13 @@
             part = pl.ds(sub * TILE, TILE)
             turned[t, part, :] = held[t, pl.ds(HALF + sub * TILE, TILE), :].T
         stores += [
-            pltpu.make_async_copy(held.at[t, pl.ds(0, HALF)], first_ref.at[t, pl.ds(0, HALF)], sem_out.at[t, 0]),
-            pltpu.make_async_copy(turned.at[t], first_ref.at[t, pl.ds(HALF, HALF)], sem_out.at[t, 1]),
+            pltpu.make_async_copy(held.at[t, pl.ds(0, HALF)], out_ref.at[t, pl.ds(0, HALF)], sem_out.at[t, 0]),
+            pltpu.make_async_copy(turned.at[t], out_ref.at[t, pl.ds(HALF, HALF)], sem_out.at[t, 1]),
             pltpu.make_async_copy(
-                held.at[t, pl.ds(2 * HALF, TILE)], first_ref.at[t, pl.ds(2 * HALF, TILE)], sem_out.at[t, 2]
+                held.at[t, pl.ds(2 * HALF, HALF)], out_ref.at[t, pl.ds(2 * HALF, HALF)], sem_out.at[t, 2]
             ),
-            pltpu.make_async_copy(held.at[t, pl.ds(2 * HALF + TILE, TILE)], second_ref.at[t], sem_out.at[t, 3]),
         ]
-        for store in stores[-4:]:
+        for store in stores[-3:]:
             store.start()
     for store in stores:
         store.wait()
@@ -88,29 +87,26 @@
     return pl.pallas_call(
         pack_kernel,
         in_specs=[pl.BlockSpec(memory_space=pltpu.SMEM)] + [hbm] * 3,
-        out_specs=[hbm, hbm],
-        out_shape=[
-            jax.ShapeDtypeStruct((CHIPS, 5 * TILE, TILE), jnp.bfloat16),
-            jax.ShapeDtypeStruct((CHIPS, TILE, TILE), jnp.bfloat16),
-        ],
+        out_specs=hbm,
+        out_shape=jax.ShapeDtypeStruct((CHIPS, 6 * TILE, TILE), jnp.bfloat16),
         scratch_shapes=[
             pltpu.VMEM((CHIPS, 3 * HALF, TILE), jnp.bfloat16),
             pltpu.VMEM((CHIPS, HALF, TILE), jnp.bfloat16),
             pltpu.SemaphoreType.DMA((CHIPS, 3)),
-            pltpu.SemaphoreType.DMA((CHIPS, 4)),
+            pltpu.SemaphoreType.DMA((CHIPS, 3)),
         ],
         compiler_params=pltpu.CompilerParams(vmem_limit_bytes=60 * 2**20),
     )(scalars, queries, keys, values)
 
 
 def attend_kernel(
-    scale, query_at, meta, q_of, k_of, valid_of, own_ref, other_ref, query_ref, out_ref, kv_s, q_s, acc_s, max_s, sum_s, sems
+    scale, query_at, meta, q_of, k_of, valid_of, own_ref, other_ref, out_ref, kv_s, q_s, acc_s, max_s, sum_s, sems
 ):
     core = meta[0]
     loads = [
         pltpu.make_async_copy(own_ref.at[:, pl.ds(0, 4)], kv_s.at[core], sems.at[0]),
         pltpu.make_async_copy(other_ref.at[:, pl.ds(0, 4)], kv_s.at[1 - core], sems.at[1]),
-        pltpu.make_async_copy(query_ref.at[:, pl.ds(query_at, 1)], q_s, sems.at[2]),
+        pltpu.make_async_copy(own_ref.at[:, pl.ds(query_at, 1)], q_s, sems.at[2]),
     ]
     for load in loads:
         load.start()
@@ -160,12 +156,12 @@
     lax.fori_loop(0, CHIPS, finish, 0)
 
 
-def attend(query_at, meta, q_of, k_of, valid_of, own, other, query):
+def attend(query_at, meta, q_of, k_of, valid_of, own, other):
     smem = pl.BlockSpec(memory_space=pltpu.SMEM)
     hbm = pl.BlockSpec(memory_space=pl.ANY)
     return pl.pallas_call(
         functools.partial(attend_kernel, TILE**-0.5 * LOG2E, query_at),
-        in_specs=[smem] * 4 + [hbm] * 3,
+        in_specs=[smem] * 4 + [hbm] * 2,
         out_specs=pl.BlockSpec(memory_space=pltpu.VMEM),
         out_shape=jax.ShapeDtypeStruct((CHIPS, TILE, TILE), jnp.bfloat16),
         scratch_shapes=[
@@ -177,7 +173,7 @@
             pltpu.SemaphoreType.DMA((3,)),
         ],
         compiler_params=pltpu.CompilerParams(vmem_limit_bytes=24 * 2**20),
-    )(meta, q_of, k_of, valid_of, own, other, query)
+    )(meta, q_of, k_of, valid_of, own, other)
 
 
 def item_lists(allowed, mine):
@@ -240,15 +236,14 @@
     chip = lax.axis_index("x") * 4 + lax.axis_index("z")
     plane = lax.axis_index("y")
     core = lax.axis_index("c")
-    tile_work = jnp.sum(tile_mask, axis=2)
+    tile_work = jnp.sum(tile_mask, axis=1)
     head_at, work_at = head_plan(jnp.sum(tile_work, axis=1))
     plane_heads = lax.dynamic_slice_in_dim(head_at, plane * PLANE_HEADS, PLANE_HEADS)
     chips, first = chip_plan(lax.dynamic_slice_in_dim(work_at, plane * PLANE_HEADS, PLANE_HEADS))
     chip_ids = jnp.arange(CHIPS)
     on_chip = (first[None, :] <= chip_ids[:, None]) & (chip_ids[:, None] < (first + chips)[None, :])
     chip_heads = jnp.sum(jnp.where(on_chip, plane_heads[None, :], 0), axis=1)
-    first_send, second_send = pack(queries, keys, values, chip_heads, core)
-    got = exchange(first_send).reshape(CHIPS, 5, TILE, TILE)
+    got = exchange(pack(queries, keys, values, chip_heads, core)).reshape(CHIPS, 6, TILE, TILE)
 
     half_work = lax.dynamic_index_in_dim(tile_work.reshape(HEADS, CHIPS, 2, 2), core, 2, keepdims=False)
     half_work = jnp.take(half_work.reshape(HEADS, 2 * CHIPS), plane_heads, axis=0, mode="clip")
@@ -271,16 +266,14 @@
         w_order = lax.dynamic_slice_in_dim(head_at, (plane + ahead) % PLANES * PLANE_HEADS, PLANE_HEADS)
         weights.append(jnp.take(w_heads, w_order, axis=0, mode="clip").reshape(PLANE_HEADS * TILE, -1))
     lists = [item_lists(allowed[:, sub], mine_tiles[:, sub]) for sub in range(2)]
-    got, lists, weights, second_send = lax.optimization_barrier((got, lists, weights, second_send))
+    got, lists, weights = lax.optimization_barrier((got, lists, weights))
     got_other = swap(got)
-    late = exchange(second_send).reshape(CHIPS, 1, TILE, TILE)
 
     halves = []
     for sub in range(2):
         steps, q_of, k_of, valid = lists[sub]
         meta = jnp.stack([core, steps]).astype(jnp.int32)
-        query_at, query = ((4, got), (0, late))[sub]
-        attended = attend(query_at, meta, q_of, k_of, valid, got, got_other, query)
+        attended = attend(4 + sub, meta, q_of, k_of, valid, got, got_other)
         own = select(source[:, sub], exchange(attended))
         blocks = [own, along_y(own, 1), along_y(own, 3), along_y(own, 2)]
         total = jnp.zeros((2 * TILE, w_out.shape[1]), jnp.float32)

time: 145 us -> 146 us (level)
  waiting for transfers between devices: 15.6 us -> 21.9 us
  starting transfers between devices: 49.6 us -> 44.4 us
  local copies, waits for them, and re-layouts: 27.4 us -> 32.3 us
  Pallas kernels: 26.6 us -> 22.1 us
    ppermute x6, starting transfers between devices: 11.1 us -> 5.27 us  [along_y(): lax.ppermute(block, 'y', [(i, (i + step) % PLANES) for i in range(PLANES)])]
    ppermute x9, waiting for transfers between devices: 0.02 us -> 5.23 us  [swap(): return lax.ppermute(block, 'c', [(0, 1), (1, 0)])]
    unnamed x18 -> x24, local copies, waits for them, and re-layouts: 2.5 us -> 7.62 us
    pallas_call x2, Pallas kernels: 18 us -> 13.7 us  [attend(): pl.pallas_call(functools.partial(attend_kernel, TILE ** (-0.5) * LOG2E, q...]
    ppermute x6, waiting for transfers between devices: 5.56 us -> 7.15 us  [along_y(): lax.ppermute(block, 'y', [(i, (i + step) % PLANES) for i in range(PLANES)])]
    all_to_all x4 -> x3, starting transfers between devices: 25 us -> 25.9 us  [exchange(): lax.all_to_all(block, TOKENS_AXES, split_axis=0, concat_axis=0, tiled=True)]
    all_to_all x4 -> x3, waiting for transfers between devices: 10.1 us -> 9.48 us  [exchange(): lax.all_to_all(block, TOKENS_AXES, split_axis=0, concat_axis=0, tiled=True)]
  transfers between devices with their start and end apart: 19 -> 18, of which waited for: 3 -> 7; matrix products, arithmetic and copies ran while one was open for 25% -> 25% of each run, Pallas kernels for 10% -> 9%
where the time goes in v4:
time: 146 us; the launch traced here: 145 us
  starting transfers between devices  44.4 us (30%)
  local copies, waits for them, and re-layouts  32.3 us (22%)
  Pallas kernels  22.1 us (15%)
  waiting for transfers between devices  21.9 us (15%)
  other arithmetic  9.67 us (7%)
  matrix products  7.9 us (5%)
  between operations  6.58 us (5%)
    all_to_all x3, starting transfers between devices, exchange(): lax.all_to_all(block, TOKENS_AXES, split_axis=0, concat_axis=0, tiled=True)  25.9 us
    gather x4, local copies, waits for them, and re-layouts, shards(): jnp.take(w_heads, w_order, axis=0, mode='clip')  19.6 us
    pallas_call x2, Pallas kernels, attend(): pl.pallas_call(functools.partial(attend_kernel, TILE ** (-0.5) * LOG2E, q...  13.7 us
    ppermute x9, starting transfers between devices, swap(): return lax.ppermute(block, 'c', [(0, 1), (1, 0)])  13.3 us
    all_to_all x3, waiting for transfers between devices, exchange(): lax.all_to_all(block, TOKENS_AXES, split_axis=0, concat_axis=0, tiled=True)  9.48 us
    unnamed x24, local copies, waits for them, and re-layouts  7.62 us
    dot_general x8, matrix products, shards(): jnp.dot(both, weights[k], preferred_element_type=jnp.float32)  7.5 us
    ppermute x6, waiting for transfers between devices, along_y(): lax.ppermute(block, 'y', [(i, (i + step) % PLANES) for i in range(PLANES)])  7.15 us
  transfers between devices with their start and end apart: 18, of which 7 were waited for; matrix products, arithmetic and copies ran while one was open for 25% of the time, Pallas kernels for 9%

profile of v4, /device:TPU:1, one launch (start us, length us, event | category | flops | bytes accessed | tf_op | source)
XLA Modules:
  0.0 144.8 jit_solution(8910509165552515834)
XLA Ops:
  0.0 2.1 %fusion.72 = (s32[40,64]{1,0:T(8,128)S(1)}, s32[40]{0:T(128)S(1)}) fusion(s32[40,64,64]{2,1,0:T(8,128)} %param.13), kind=kLoop, calls=%fused_computation.196 | loop fusion | flops 325080 | bytes 665760 | tf_op jit(solution)/shard_map/reduce_sum | solution.py:239
  4.1 4.6 %shard_map.73 = bf16[16,768,128]{2,1,0:T(8,128)(2,1)} custom-call(s32[17]{0:T(128)} %pad_add_fusion.heads, bf16[512,5120]{1,0:T(8,128)(2,1)} %q_ref.1, bf16[512,5120]{1,0:T(8,128)(2,1)} %k_ref.1, bf16[512,5120]{1,0:T(8,128)(2,1)} %v_ref.1), custom_call_target="tpu_custom_call" | custom-call | tf_op jit(solution)/shard_map/pallas_call | solution.py:87
  8.6 8.4 %all-to-all-start = ((bf16[16,768,128]{2,1,0:T(8,128)(2,1)}), bf16[16,768,128]{2,1,0:T(8,128)(2,1)S(1)}, u32[]{:S(2)}, u32[]{:S(2)}) async-start(bf16[16,768,128]{2,1,0:T(8,128)(2,1)} %shard_map.73), calls=%async_computation | async-start | bytes 6291456 | tf_op jit(solution)/shard_map/all_to_all | solution.py:224
  32.4 4.9 %gather_fusion.2 = bf16[10,128,640]{2,1,0:T(8,128)(2,1)} fusion(bf16[40,128,640]{2,1,0:T(8,128)(2,1)} %bitcast.45, s32[1024]{0:T(1024)S(1)} %get-tuple-element.83), kind=kCustom, calls=%fused_computation.2 | custom fusion | bytes 3276840 | tf_op jit(solution)/shard_map/jit(_take)/gather | solution.py:267
  37.3 4.9 %gather_fusion.4 = bf16[10,128,640]{2,1,0:T(8,128)(2,1)} fusion(bf16[40,128,640]{2,1,0:T(8,128)(2,1)} %bitcast.46, s32[1024]{0:T(1024)S(1)} %get-tuple-element.81), kind=kCustom, calls=%fused_computation.4 | custom fusion | bytes 3276840 | tf_op jit(solution)/shard_map/jit(_take)/gather | solution.py:267
  42.2 5.0 %gather_fusion.1 = bf16[10,128,640]{2,1,0:T(8,128)(2,1)} fusion(bf16[40,128,640]{2,1,0:T(8,128)(2,1)} %bitcast.47, s32[1024]{0:T(1024)S(1)} %get-tuple-element.84), kind=kCustom, calls=%fused_computation.1 | custom fusion | bytes 3276840 | tf_op jit(solution)/shard_map/jit(_take)/gather | solution.py:267
  47.2 4.9 %gather_fusion.3 = bf16[10,128,640]{2,1,0:T(8,128)(2,1)} fusion(bf16[40,128,640]{2,1,0:T(8,128)(2,1)} %bitcast.48, s32[1024]{0:T(1024)S(1)} %get-tuple-element.82), kind=kCustom, calls=%fused_computation.3 | custom fusion | bytes 3276840 | tf_op jit(solution)/shard_map/jit(_take)/gather | solution.py:267
  52.0 5.4 %all-to-all-done = bf16[16,768,128]{2,1,0:T(8,128)(2,1)S(1)} async-done(((bf16[16,768,128]{2,1,0:T(8,128)(2,1)}), bf16[16,768,128]{2,1,0:T(8,128)(2,1)S(1)}, u32[]{:S(2)}, u32[]{:S(2)}) %all-to-all-start) | async-done | bytes 3145760 | tf_op jit(solution)/shard_map/all_to_all | solution.py:224
  57.4 3.0 %collective-permute-start = (bf16[16,6,128,128]{3,2,1,0:T(8,128)(2,1)S(1)}, bf16[16,6,128,128]{3,2,1,0:T(8,128)(2,1)S(1)}, u32[]{:S(2)}, u32[]{:S(2)}) collective-permute-start(bf16[16,6,128,128]{3,2,1,0:T(8,128)(2,1)S(1)} %bitcast.38), channel_id=1, source_target_pairs={{0,1},{1,0},{2,3},{3,2},{4,5},{5,4},{6,7},{7,6},{8,9},{9,8},{10,11... | collective-permute-start | bytes 9437192 | tf_op jit(solution)/shard_map/ppermute | solution.py:232
  60.5 5.2 %collective-permute-done.other_ref = bf16[16,6,128,128]{3,2,1,0:T(8,128)(2,1)S(1)} collective-permute-done((bf16[16,6,128,128]{3,2,1,0:T(8,128)(2,1)S(1)}, bf16[16,6,128,128]{3,2,1,0:T(8,128)(2,1)S(1)}, u32[]{:S(2)}, u32[]{:S(2)}) %collective-permute-start) | collective-permute-done | bytes 3145760 | tf_op jit(solution)/shard_map/ppermute | solution.py:232
  65.7 5.0 %shard_map.76 = bf16[16,128,128]{2,1,0:T(8,128)(2,1)S(1)} custom-call(s32[2]{0:T(128)S(1)} %pad_add_fusion.2.meta, s32[256]{0:T(256)S(1)} %broadcast_minimum_fusion.q_of, s32[1024]{0:T(1024)S(1)} %convert_element_type.110.k_of, s32[256]{0:T(256)S(1)} %get-tuple-element.30.valid_of, bf16[16,6,128,128]{3,2,1,0:T(8,128)(2,1)S(1)} %bitcast.39, ...), custom_call_target="tpu_custom_call" | custom-call | tf_op jit(solution)/shard_map/pallas_call | solution.py:162
  73.2 10.7 %all-to-all-start.2 = ((bf16[16,128,128]{2,1,0:T(8,128)(2,1)}), bf16[16,128,128]{2,1,0:T(8,128)(2,1)}, u32[]{:S(2)}, u32[]{:S(2)}) async-start(bf16[16,128,128]{2,1,0:T(8,128)(2,1)} %copy-done.3), calls=%async_computation.2 | async-start | bytes 1048576 | tf_op jit(solution)/shard_map/all_to_all | solution.py:224
  83.9 1.9 %copy-done.1 = bf16[16,6,128,128]{3,2,1,0:T(8,128)(2,1)S(1)} copy-done((bf16[16,6,128,128]{3,2,1,0:T(8,128)(2,1)S(1)}, bf16[16,6,128,128]{3,2,1,0:T(8,128)(2,1)}, u32[]{:S(2)}) %copy-start.1) | copy-done | bytes 3145752
  85.8 8.7 %shard_map.74 = bf16[16,128,128]{2,1,0:T(8,128)(2,1)S(1)} custom-call(s32[2]{0:T(128)S(1)} %pad_add_fusion.1.meta, s32[256]{0:T(256)S(1)} %broadcast_minimum_fusion.1.q_of, s32[1024]{0:T(1024)S(1)} %convert_element_type.104.k_of, s32[256]{0:T(256)S(1)} %get-tuple-element.21.valid_of, bf16[16,6,128,128]{3,2,1,0:T(8,128)(2,1)S(1)} %bitcast.40, ...), custom_call_target="tpu_custom_call" | custom-call | tf_op jit(solution)/shard_map/pallas_call | solution.py:162
  95.4 6.7 %all-to-all-start.1 = ((bf16[16,128,128]{2,1,0:T(8,128)(2,1)}), bf16[16,128,128]{2,1,0:T(8,128)(2,1)S(1)}, u32[]{:S(2)}, u32[]{:S(2)}) async-start(bf16[16,128,128]{2,1,0:T(8,128)(2,1)} %copy-done.2), calls=%async_computation.1 | async-start | bytes 1048576 | tf_op jit(solution)/shard_map/all_to_all | solution.py:224
  102.8 1.9 %shard_map.77 = bf16[128,1280]{1,0:T(8,128)(2,1)} custom-call(s32[10]{0:T(128)} %get-tuple-element.38.source, bf16[16,128,128]{2,1,0:T(8,128)(2,1)} %all-to-all-done.2.got_ref), custom_call_target="tpu_custom_call" | custom-call | tf_op jit(solution)/shard_map/pallas_call | solution.py:215
  106.2 1.8 %collective-permute-start.8 = (bf16[128,1280]{1,0:T(8,128)(2,1)}, bf16[128,1280]{1,0:T(8,128)(2,1)S(1)}, u32[]{:S(2)}, u32[]{:S(2)}) collective-permute-start(bf16[128,1280]{1,0:T(8,128)(2,1)} %shard_map.77), channel_id=1, source_target_pairs={{0,1},{1,0},{2,3},{3,2},{4,5},{5,4},{6,7},{7,6},{8,9},{9,8},{10,11... | collective-permute-start | bytes 983048 | tf_op jit(solution)/shard_map/ppermute | solution.py:232
  108.0 4.1 %all-to-all-done.1.got_ref = bf16[16,128,128]{2,1,0:T(8,128)(2,1)S(1)} async-done(((bf16[16,128,128]{2,1,0:T(8,128)(2,1)}), bf16[16,128,128]{2,1,0:T(8,128)(2,1)S(1)}, u32[]{:S(2)}, u32[]{:S(2)}) %all-to-all-start.1) | async-done | bytes 524320 | tf_op jit(solution)/shard_map/all_to_all | solution.py:224
  112.8 1.9 %shard_map.75 = bf16[128,1280]{1,0:T(8,128)(2,1)} custom-call(s32[10]{0:T(128)} %get-tuple-element.37.source, bf16[16,128,128]{2,1,0:T(8,128)(2,1)} %copy-done.6), custom_call_target="tpu_custom_call" | custom-call | tf_op jit(solution)/shard_map/pallas_call | solution.py:215
  114.8 2.5 %collective-permute-start.1 = (bf16[128,1280]{1,0:T(8,128)(2,1)}, bf16[128,1280]{1,0:T(8,128)(2,1)}, u32[]{:S(2)}, u32[]{:S(2)}) collective-permute-start(bf16[128,1280]{1,0:T(8,128)(2,1)} %shard_map.75), channel_id=1, source_target_pairs={{0,1},{1,0},{2,3},{3,2},{4,5},{5,4},{6,7},{7,6},{8,9},{9,8},{10,11... | collective-permute-start | bytes 983048 | tf_op jit(solution)/shard_map/ppermute | solution.py:232
  118.6 3.8 %collective-permute-start.4 = (bf16[128,1280]{1,0:T(8,128)(2,1)}, bf16[128,1280]{1,0:T(8,128)(2,1)S(1)}, u32[]{:S(2)}, u32[]{:S(2)}) collective-permute-start(bf16[128,1280]{1,0:T(8,128)(2,1)} %shard_map.75), channel_id=1, source_target_pairs={{0,6},{2,0},{4,2},{6,4},{1,7},{3,1},{5,3},{7,5},{8,14},{10,8},{12,... | collective-permute-start | bytes 983048 | tf_op jit(solution)/shard_map/ppermute | solution.py:228
  122.4 2.1 %collective-permute-done.9 = bf16[128,1280]{1,0:T(8,128)(2,1)S(1)} collective-permute-done((bf16[128,1280]{1,0:T(8,128)(2,1)}, bf16[128,1280]{1,0:T(8,128)(2,1)S(1)}, u32[]{:S(2)}, u32[]{:S(2)}) %collective-permute-start.9) | collective-permute-done | bytes 327712 | tf_op jit(solution)/shard_map/ppermute | solution.py:228
  128.8 3.4 %collective-permute-start.12 = (bf16[128,1280]{1,0:T(8,128)(2,1)S(1)}, bf16[128,1280]{1,0:T(8,128)(2,1)S(1)}, u32[]{:S(2)}, u32[]{:S(2)}) collective-permute-start(bf16[128,1280]{1,0:T(8,128)(2,1)S(1)} %collective-permute-done.11), channel_id=1, source_target_pairs={{0,1},{1,0},{2,3},{3,2},{4,5},{5,4},{6,7},{7,6},{8,9},{9,8},{10,11... | collective-permute-start | bytes 983048 | tf_op jit(solution)/shard_map/ppermute | solution.py:232
  133.2 3.6 %collective-permute-done.2 = bf16[128,1280]{1,0:T(8,128)(2,1)S(1)} collective-permute-done((bf16[128,1280]{1,0:T(8,128)(2,1)}, bf16[128,1280]{1,0:T(8,128)(2,1)S(1)}, u32[]{:S(2)}, u32[]{:S(2)}) %collective-permute-start.2) | collective-permute-done | bytes 327712 | tf_op jit(solution)/shard_map/ppermute | solution.py:228
  (134 shorter events, 31.8 us)
Async XLA Ops:
  8.6 48.8 %all-to-all-start = ((bf16[16,768,128]{2,1,0:T(8,128)(2,1)}), bf16[16,768,128]{2,1,0:T(8,128)(2,1)S(1)}, u32[]{:S(2)}, u32[]{:S(2)}) async-start(bf16[16,768,128]{2,1,0:T(8,128)(2,1)} %shard_map.73), calls=%async_computation | async-start | bytes 6291456 | tf_op jit(solution)/shard_map/all_to_all | solution.py:224
  57.4 8.3 %collective-permute-start = (bf16[16,6,128,128]{3,2,1,0:T(8,128)(2,1)S(1)}, bf16[16,6,128,128]{3,2,1,0:T(8,128)(2,1)S(1)}, u32[]{:S(2)}, u32[]{:S(2)}) collective-permute-start(bf16[16,6,128,128]{3,2,1,0:T(8,128)(2,1)S(1)} %bitcast.38), channel_id=1, source_target_pairs={{0,1},{1,0},{2,3},{3,2},{4,5},{5,4},{6,7},{7,6},{8,9},{9,8},{10,11... | collective-permute-start | bytes 9437192 | tf_op jit(solution)/shard_map/ppermute | solution.py:232
  70.7 1.7 %copy-start = (bf16[16,6,128,128]{3,2,1,0:T(8,128)(2,1)}, bf16[16,6,128,128]{3,2,1,0:T(8,128)(2,1)S(1)}, u32[]{:S(2)}) copy-start(bf16[16,6,128,128]{3,2,1,0:T(8,128)(2,1)S(1)} %collective-permute-done.other_ref) | copy-start | bytes 9437188
  73.2 22.2 %all-to-all-start.2 = ((bf16[16,128,128]{2,1,0:T(8,128)(2,1)}), bf16[16,128,128]{2,1,0:T(8,128)(2,1)}, u32[]{:S(2)}, u32[]{:S(2)}) async-start(bf16[16,128,128]{2,1,0:T(8,128)(2,1)} %copy-done.3), calls=%async_computation.2 | async-start | bytes 1048576 | tf_op jit(solution)/shard_map/all_to_all | solution.py:224
  83.9 1.9 %copy-start.1 = (bf16[16,6,128,128]{3,2,1,0:T(8,128)(2,1)S(1)}, bf16[16,6,128,128]{3,2,1,0:T(8,128)(2,1)}, u32[]{:S(2)}) copy-start(bf16[16,6,128,128]{3,2,1,0:T(8,128)(2,1)} %copy-done) | copy-start | bytes 9437188
  95.3 29.7 %copy-start.8 = (bf16[10,128,640]{2,1,0:T(8,128)(2,1)S(1)}, bf16[10,128,640]{2,1,0:T(8,128)(2,1)}, u32[]{:S(2)}) copy-start(bf16[10,128,640]{2,1,0:T(8,128)(2,1)} %gather_fusion.1) | copy-start | bytes 4915204
  95.4 16.7 %all-to-all-start.1 = ((bf16[16,128,128]{2,1,0:T(8,128)(2,1)}), bf16[16,128,128]{2,1,0:T(8,128)(2,1)S(1)}, u32[]{:S(2)}, u32[]{:S(2)}) async-start(bf16[16,128,128]{2,1,0:T(8,128)(2,1)} %copy-done.2), calls=%async_computation.1 | async-start | bytes 1048576 | tf_op jit(solution)/shard_map/all_to_all | solution.py:224
  104.7 12.5 %collective-permute-start.13 = (bf16[128,1280]{1,0:T(8,128)(2,1)}, bf16[128,1280]{1,0:T(8,128)(2,1)S(1)}, u32[]{:S(2)}, u32[]{:S(2)}) collective-permute-start(bf16[128,1280]{1,0:T(8,128)(2,1)} %shard_map.77), channel_id=1, source_target_pairs={{0,4},{2,6},{4,0},{6,2},{1,5},{3,7},{5,1},{7,3},{8,12},{10,14},{12... | collective-permute-start | bytes 983048 | tf_op jit(solution)/shard_map/ppermute | solution.py:228
  104.7 13.9 %collective-permute-start.11 = (bf16[128,1280]{1,0:T(8,128)(2,1)}, bf16[128,1280]{1,0:T(8,128)(2,1)S(1)}, u32[]{:S(2)}, u32[]{:S(2)}) collective-permute-start(bf16[128,1280]{1,0:T(8,128)(2,1)} %shard_map.77), channel_id=1, source_target_pairs={{0,6},{2,0},{4,2},{6,4},{1,7},{3,1},{5,3},{7,5},{8,14},{10,8},{12,... | collective-permute-start | bytes 983048 | tf_op jit(solution)/shard_map/ppermute | solution.py:228
  104.7 19.7 %collective-permute-start.9 = (bf16[128,1280]{1,0:T(8,128)(2,1)}, bf16[128,1280]{1,0:T(8,128)(2,1)S(1)}, u32[]{:S(2)}, u32[]{:S(2)}) collective-permute-start(bf16[128,1280]{1,0:T(8,128)(2,1)} %shard_map.77), channel_id=1, source_target_pairs={{0,2},{2,4},{4,6},{6,0},{1,3},{3,5},{5,7},{7,1},{8,10},{10,12},{12... | collective-permute-start | bytes 983048 | tf_op jit(solution)/shard_map/ppermute | solution.py:228
  106.2 18.3 %collective-permute-start.8 = (bf16[128,1280]{1,0:T(8,128)(2,1)}, bf16[128,1280]{1,0:T(8,128)(2,1)S(1)}, u32[]{:S(2)}, u32[]{:S(2)}) collective-permute-start(bf16[128,1280]{1,0:T(8,128)(2,1)} %shard_map.77), channel_id=1, source_target_pairs={{0,1},{1,0},{2,3},{3,2},{4,5},{5,4},{6,7},{7,6},{8,9},{9,8},{10,11... | collective-permute-start | bytes 983048 | tf_op jit(solution)/shard_map/ppermute | solution.py:232
  114.8 12.1 %copy-start.10 = (bf16[128,1280]{1,0:T(8,128)(2,1)S(1)}, bf16[128,1280]{1,0:T(8,128)(2,1)}, u32[]{:S(2)}) copy-start(bf16[128,1280]{1,0:T(8,128)(2,1)} %shard_map.75) | copy-start | bytes 983044
  114.8 12.0 %collective-permute-start.1 = (bf16[128,1280]{1,0:T(8,128)(2,1)}, bf16[128,1280]{1,0:T(8,128)(2,1)}, u32[]{:S(2)}, u32[]{:S(2)}) collective-permute-start(bf16[128,1280]{1,0:T(8,128)(2,1)} %shard_map.75), channel_id=1, source_target_pairs={{0,1},{1,0},{2,3},{3,2},{4,5},{5,4},{6,7},{7,6},{8,9},{9,8},{10,11... | collective-permute-start | bytes 983048 | tf_op jit(solution)/shard_map/ppermute | solution.py:232
  117.2 11.5 %collective-permute-start.6 = (bf16[128,1280]{1,0:T(8,128)(2,1)}, bf16[128,1280]{1,0:T(8,128)(2,1)S(1)}, u32[]{:S(2)}, u32[]{:S(2)}) collective-permute-start(bf16[128,1280]{1,0:T(8,128)(2,1)} %shard_map.75), channel_id=1, source_target_pairs={{0,4},{2,6},{4,0},{6,2},{1,5},{3,7},{5,1},{7,3},{8,12},{10,14},{12... | collective-permute-start | bytes 983048 | tf_op jit(solution)/shard_map/ppermute | solution.py:228
  118.6 13.6 %collective-permute-start.4 = (bf16[128,1280]{1,0:T(8,128)(2,1)}, bf16[128,1280]{1,0:T(8,128)(2,1)S(1)}, u32[]{:S(2)}, u32[]{:S(2)}) collective-permute-start(bf16[128,1280]{1,0:T(8,128)(2,1)} %shard_map.75), channel_id=1, source_target_pairs={{0,6},{2,0},{4,2},{6,4},{1,7},{3,1},{5,3},{7,5},{8,14},{10,8},{12,... | collective-permute-start | bytes 983048 | tf_op jit(solution)/shard_map/ppermute | solution.py:228
  124.5 12.4 %collective-permute-start.2 = (bf16[128,1280]{1,0:T(8,128)(2,1)}, bf16[128,1280]{1,0:T(8,128)(2,1)S(1)}, u32[]{:S(2)}, u32[]{:S(2)}) collective-permute-start(bf16[128,1280]{1,0:T(8,128)(2,1)} %shard_map.75), channel_id=1, source_target_pairs={{0,2},{2,4},{4,6},{6,0},{1,3},{3,5},{5,7},{7,1},{8,10},{10,12},{12... | collective-permute-start | bytes 983048 | tf_op jit(solution)/shard_map/ppermute | solution.py:228
  124.5 13.2 %collective-permute-start.10 = (bf16[128,1280]{1,0:T(8,128)(2,1)S(1)}, bf16[128,1280]{1,0:T(8,128)(2,1)S(1)}, u32[]{:S(2)}, u32[]{:S(2)}) collective-permute-start(bf16[128,1280]{1,0:T(8,128)(2,1)S(1)} %collective-permute-done.9), channel_id=1, source_target_pairs={{0,1},{1,0},{2,3},{3,2},{4,5},{5,4},{6,7},{7,6},{8,9},{9,8},{10,11... | collective-permute-start | bytes 983048 | tf_op jit(solution)/shard_map/ppermute | solution.py:232
  126.7 11.0 %copy-start.4 = (bf16[10,128,640]{2,1,0:T(8,128)(2,1)S(1)}, bf16[10,128,640]{2,1,0:T(8,128)(2,1)}, u32[]{:S(2)}) copy-start(bf16[10,128,640]{2,1,0:T(8,128)(2,1)} %gather_fusion.2) | copy-start | bytes 4915204
  126.8 11.6 %collective-permute-start.14 = (bf16[128,1280]{1,0:T(8,128)(2,1)S(1)}, bf16[128,1280]{1,0:T(8,128)(2,1)S(1)}, u32[]{:S(2)}, u32[]{:S(2)}) collective-permute-start(bf16[128,1280]{1,0:T(8,128)(2,1)S(1)} %collective-permute-done.13), channel_id=1, source_target_pairs={{0,1},{1,0},{2,3},{3,2},{4,5},{5,4},{6,7},{7,6},{8,9},{9,8},{10,11... | collective-permute-start | bytes 983048 | tf_op jit(solution)/shard_map/ppermute | solution.py:232
  128.6 9.8 %copy-start.7 = (bf16[10,128,640]{2,1,0:T(8,128)(2,1)S(1)}, bf16[10,128,640]{2,1,0:T(8,128)(2,1)}, u32[]{:S(2)}) copy-start(bf16[10,128,640]{2,1,0:T(8,128)(2,1)} %gather_fusion.4) | copy-start | bytes 4915204
  128.8 10.4 %collective-permute-start.12 = (bf16[128,1280]{1,0:T(8,128)(2,1)S(1)}, bf16[128,1280]{1,0:T(8,128)(2,1)S(1)}, u32[]{:S(2)}, u32[]{:S(2)}) collective-permute-start(bf16[128,1280]{1,0:T(8,128)(2,1)S(1)} %collective-permute-done.11), channel_id=1, source_target_pairs={{0,1},{1,0},{2,3},{3,2},{4,5},{5,4},{6,7},{7,6},{8,9},{9,8},{10,11... | collective-permute-start | bytes 983048 | tf_op jit(solution)/shard_map/ppermute | solution.py:232
  132.2 8.3 %collective-permute-start.7 = (bf16[128,1280]{1,0:T(8,128)(2,1)S(1)}, bf16[128,1280]{1,0:T(8,128)(2,1)S(1)}, u32[]{:S(2)}, u32[]{:S(2)}) collective-permute-start(bf16[128,1280]{1,0:T(8,128)(2,1)S(1)} %collective-permute-done.6), channel_id=1, source_target_pairs={{0,1},{1,0},{2,3},{3,2},{4,5},{5,4},{6,7},{7,6},{8,9},{9,8},{10,11... | collective-permute-start | bytes 983048 | tf_op jit(solution)/shard_map/ppermute | solution.py:232
  136.8 5.1 %collective-permute-start.5 = (bf16[128,1280]{1,0:T(8,128)(2,1)S(1)}, bf16[128,1280]{1,0:T(8,128)(2,1)S(1)}, u32[]{:S(2)}, u32[]{:S(2)}) collective-permute-start(bf16[128,1280]{1,0:T(8,128)(2,1)S(1)} %collective-permute-done.4), channel_id=1, source_target_pairs={{0,1},{1,0},{2,3},{3,2},{4,5},{5,4},{6,7},{7,6},{8,9},{9,8},{10,11... | collective-permute-start | bytes 983048 | tf_op jit(solution)/shard_map/ppermute | solution.py:232
  137.7 3.6 %collective-permute-start.3 = (bf16[128,1280]{1,0:T(8,128)(2,1)S(1)}, bf16[128,1280]{1,0:T(8,128)(2,1)S(1)}, u32[]{:S(2)}, u32[]{:S(2)}) collective-permute-start(bf16[128,1280]{1,0:T(8,128)(2,1)S(1)} %collective-permute-done.2), channel_id=1, source_target_pairs={{0,1},{1,0},{2,3},{3,2},{4,5},{5,4},{6,7},{7,6},{8,9},{9,8},{10,11... | collective-permute-start | bytes 983048 | tf_op jit(solution)/shard_map/ppermute | solution.py:232
  (6 other events, 6.0 us)

commit v5 on v4

--- a/solution.py
+++ b/solution.py
@@ -16,7 +16,7 @@
 HALF = 256
 GROUP = 4
 UNROLL = 16
-ITEMS = 256
+ITEMS = 512
 LOG2E = 1.4426950408889634
 TOKENS_AXES = ("x", "z")
 LOW = -1e30
@@ -100,13 +100,13 @@
 
 
 def attend_kernel(
-    scale, query_at, meta, q_of, k_of, valid_of, own_ref, other_ref, out_ref, kv_s, q_s, acc_s, max_s, sum_s, sems
+    scale, meta, q_of, k_of, valid_of, own_ref, other_ref, out_ref, kv_s, q_s, acc_s, max_s, sum_s, sems
 ):
     core = meta[0]
     loads = [
         pltpu.make_async_copy(own_ref.at[:, pl.ds(0, 4)], kv_s.at[core], sems.at[0]),
         pltpu.make_async_copy(other_ref.at[:, pl.ds(0, 4)], kv_s.at[1 - core], sems.at[1]),
-        pltpu.make_async_copy(own_ref.at[:, pl.ds(query_at, 1)], q_s, sems.at[2]),
+        pltpu.make_async_copy(own_ref.at[:, pl.ds(4, 2)], q_s, sems.at[2]),
     ]
     for load in loads:
         load.start()
@@ -124,7 +124,7 @@
             kid = [k_of[e * GROUP + g] for g in range(GROUP)]
             valid = valid_of[e]
             keys = jnp.concatenate([kv_s[i // 64, i % 64 // 4, i % 4] for i in kid], axis=0)
-            scores = lax.dot_general(keys, q_s[t, 0], (((1,), (1,)), ((), ())), preferred_element_type=jnp.float32)
+            scores = lax.dot_general(keys, q_s[t // 2, t % 2], (((1,), (1,)), ((), ())), preferred_element_type=jnp.float32)
             top = jnp.max(scores, axis=0, keepdims=True) * scale
             weights = []
             total = jnp.zeros((1, TILE), jnp.float32)
@@ -153,26 +153,26 @@
         out_ref[t] = (acc_s[t] * inverse).astype(jnp.bfloat16)
         return 0
 
-    lax.fori_loop(0, CHIPS, finish, 0)
-
-
-def attend(query_at, meta, q_of, k_of, valid_of, own, other):
+    lax.fori_loop(0, 2 * CHIPS, finish, 0)
+
+
+def attend(meta, q_of, k_of, valid_of, own, other):
     smem = pl.BlockSpec(memory_space=pltpu.SMEM)
     hbm = pl.BlockSpec(memory_space=pl.ANY)
     return pl.pallas_call(
-        functools.partial(attend_kernel, TILE**-0.5 * LOG2E, query_at),
+        functools.partial(attend_kernel, TILE**-0.5 * LOG2E),
         in_specs=[smem] * 4 + [hbm] * 2,
         out_specs=pl.BlockSpec(memory_space=pltpu.VMEM),
-        out_shape=jax.ShapeDtypeStruct((CHIPS, TILE, TILE), jnp.bfloat16),
+        out_shape=jax.ShapeDtypeStruct((2 * CHIPS, TILE, TILE), jnp.bfloat16),
         scratch_shapes=[
             pltpu.VMEM((2, CHIPS, 4, TILE, TILE), jnp.bfloat16),
-            pltpu.VMEM((CHIPS, 1, TILE, TILE), jnp.bfloat16),
-            pltpu.VMEM((CHIPS, TILE, TILE), jnp.float32),
-            pltpu.VMEM((CHIPS, 1, TILE), jnp.float32),
-            pltpu.VMEM((CHIPS, 1, TILE), jnp.float32),
+            pltpu.VMEM((CHIPS, 2, TILE, TILE), jnp.bfloat16),
+            pltpu.VMEM((2 * CHIPS, TILE, TILE), jnp.float32),
+            pltpu.VMEM((2 * CHIPS, 1, TILE), jnp.float32),
+            pltpu.VMEM((2 * CHIPS, 1, TILE), jnp.float32),
             pltpu.SemaphoreType.DMA((3,)),
         ],
-        compiler_params=pltpu.CompilerParams(vmem_limit_bytes=24 * 2**20),
+        compiler_params=pltpu.CompilerParams(vmem_limit_bytes=20 * 2**20),
     )(meta, q_of, k_of, valid_of, own, other)
 
 
@@ -193,7 +193,7 @@
     item = jnp.arange(ITEMS)
     real = (item < end[-1]).astype(jnp.int32)
     held = jnp.maximum(jnp.minimum(item, end[-1] - 1), 0)
-    q_of = jnp.minimum(jnp.sum((end[None, :] <= held[:, None]).astype(jnp.int32), axis=1), CHIPS - 1)
+    q_of = jnp.minimum(jnp.sum((end[None, :] <= held[:, None]).astype(jnp.int32), axis=1), 2 * CHIPS - 1)
     pick = (q_of[:, None] == slots[None, :]).astype(jnp.int32)
     start = GROUP * (held - jnp.sum(pick * (end - groups)[None, :], axis=1))
     left = jnp.sum(pick * count[None, :], axis=1) - start
@@ -205,9 +205,10 @@
     return steps, q_of, k_of.astype(jnp.int32).reshape(-1), valid
 
 
-def select_kernel(source, got_ref, out_ref):
-    for i in range(PLANE_HEADS):
-        out_ref[:, pl.ds(i * TILE, TILE)] = got_ref[source[i]].T
+def select_kernel(source, got_ref, *out_refs):
+    for sub, out_ref in enumerate(out_refs):
+        for i in range(PLANE_HEADS):
+            out_ref[:, pl.ds(i * TILE, TILE)] = got_ref[source[2 * i + sub], sub].T
 
 
 def select(source, got):
@@ -215,8 +216,8 @@
     return pl.pallas_call(
         select_kernel,
         in_specs=[pl.BlockSpec(memory_space=pltpu.SMEM), vmem],
-        out_specs=vmem,
-        out_shape=jax.ShapeDtypeStruct((TILE, PLANE_HEADS * TILE), jnp.bfloat16),
+        out_specs=[vmem] * 2,
+        out_shape=[jax.ShapeDtypeStruct((TILE, PLANE_HEADS * TILE), jnp.bfloat16)] * 2,
     )(source, got)
 
 
@@ -255,37 +256,44 @@
     owner = first[:, None] + ((2 * done + half_work) * chips[:, None]) // (2 * total)
     my_slot = jnp.sum(jnp.where(on_chip[chip], jnp.arange(PLANE_HEADS), 0))
     my_head = chip_heads[chip]
-    mine_tiles = (owner[my_slot] == chip).astype(jnp.int32).reshape(CHIPS, 2)
+    mine_tiles = (owner[my_slot] == chip).astype(jnp.int32)
     allowed = lax.dynamic_index_in_dim(tile_mask, my_head, 0, keepdims=False)
     allowed = lax.dynamic_index_in_dim(allowed.reshape(CHIPS, 2, 2, 4 * CHIPS), core, 1, keepdims=False)
-    source = lax.dynamic_slice_in_dim(owner, 2 * chip, 2, 1)
+    source = lax.dynamic_slice_in_dim(owner, 2 * chip, 2, 1).reshape(-1)
 
     w_heads = w_out.reshape(HEADS, TILE, w_out.shape[1])
     weights = []
     for ahead in (0, 3, 1, 2):
         w_order = lax.dynamic_slice_in_dim(head_at, (plane + ahead) % PLANES * PLANE_HEADS, PLANE_HEADS)
         weights.append(jnp.take(w_heads, w_order, axis=0, mode="clip").reshape(PLANE_HEADS * TILE, -1))
-    lists = [item_lists(allowed[:, sub], mine_tiles[:, sub]) for sub in range(2)]
-    got, lists, weights = lax.optimization_barrier((got, lists, weights))
+    lists = item_lists(allowed.reshape(2 * CHIPS, 4 * CHIPS), mine_tiles)
+    got, lists, source, weights = lax.optimization_barrier((got, lists, source, weights))
     got_other = swap(got)
 
+    def project(block, weight):
+        both = jnp.concatenate([block, swap(block)], axis=0)
+        return jnp.dot(both, weight, preferred_element_type=jnp.float32)
+
+    def by_rows(total):
+        mine, theirs = total[:TILE], total[TILE:]
+        return jnp.where(core == 0, mine, theirs), jnp.where(core == 0, theirs, mine)
+
+    steps, q_of, k_of, valid = lists
+    meta = jnp.stack([core, steps]).astype(jnp.int32)
+    attended = attend(meta, q_of, k_of, valid, got, got_other)
+    own_rows = select(source, exchange(attended.reshape(CHIPS, 2, TILE, TILE)))
+
+    residual = residual_in.astype(jnp.float32).reshape(2, 2, TILE, -1)
+    width = PLANE_HEADS * TILE // 2
     halves = []
-    for sub in range(2):
-        steps, q_of, k_of, valid = lists[sub]
-        meta = jnp.stack([core, steps]).astype(jnp.int32)
-        attended = attend(4 + sub, meta, q_of, k_of, valid, got, got_other)
-        own = select(source[:, sub], exchange(attended))
-        blocks = [own, along_y(own, 1), along_y(own, 3), along_y(own, 2)]
-        total = jnp.zeros((2 * TILE, w_out.shape[1]), jnp.float32)
-        for k, block in enumerate(blocks):
-            both = jnp.concatenate([block, swap(block)], axis=0)
-            total = total + jnp.dot(both, weights[k], preferred_element_type=jnp.float32)
-        halves.append(total.reshape(2, TILE, -1))
-    mine, theirs = (jnp.concatenate([halves[0][i], halves[1][i]], axis=0) for i in range(2))
-    low = jnp.where(core == 0, mine, theirs)
-    high = jnp.where(core == 0, theirs, mine)
-    projected = jnp.concatenate([low, high], axis=0)
-    return (residual_in.astype(jnp.float32) + gate_scale * projected).astype(jnp.bfloat16)
+    for sub, own in enumerate(own_rows):
+        below, above = along_y(own, 1), along_y(own, 3)
+        far_low, far_high = along_y(below[:, :width], 1), along_y(above[:, width:], 3)
+        total = project(own, weights[0]) + project(below, weights[1]) + project(above, weights[2])
+        near = lax.optimization_barrier([residual[c, sub] + gate_scale * rows for c, rows in enumerate(by_rows(total))])
+        far = project(jnp.concatenate([far_low, far_high], axis=1), weights[3])
+        halves.append([(near[c] + gate_scale * rows).astype(jnp.bfloat16) for c, rows in enumerate(by_rows(far))])
+    return jnp.concatenate([halves[0][0], halves[1][0], halves[0][1], halves[1][1]], axis=0)
 
 
 def solution(mesh):

time: 146 us -> 141 us (0.966)
  blocking collectives: 0 us -> 25 us
  starting transfers between devices: 44.4 us -> 35.1 us
  waiting for transfers between devices: 21.9 us -> 14 us
  local copies, waits for them, and re-layouts: 32.3 us -> 25.7 us
  matrix products: 7.9 us -> 5.77 us
  Pallas kernels: 22.1 us -> 20.4 us
    all_to_all x0 -> x1, blocking collectives: none -> 25 us  [exchange(): lax.all_to_all(block, TOKENS_AXES, split_axis=0, concat_axis=0, tiled=True)]
    all_to_all x3 -> x1, starting transfers between devices: 25.9 us -> 8.44 us  [exchange(): lax.all_to_all(block, TOKENS_AXES, split_axis=0, concat_axis=0, tiled=True)]
    ppermute x6 -> x8, waiting for transfers between devices: 7.15 us -> 1.17 us  [along_y(): lax.ppermute(block, 'y', [(i, (i + step) % PLANES) for i in range(PLANES)])]
    unnamed x24 -> x18, local copies, waits for them, and re-layouts: 7.62 us -> 2 us
    ppermute x6 -> x8, starting transfers between devices: 5.27 us -> 9.99 us  [along_y(): lax.ppermute(block, 'y', [(i, (i + step) % PLANES) for i in range(PLANES)])]
    ppermute x9, starting transfers between devices: 13.3 us -> 16.6 us  [swap(): return lax.ppermute(block, 'c', [(0, 1), (1, 0)])]
    dot_general x8, matrix products: 7.5 us -> 5.57 us  [project(): return jnp.dot(both, weight, preferred_element_type=jnp.float32)]
    all_to_all x3 -> x1, waiting for transfers between devices: 9.48 us -> 7.63 us  [exchange(): lax.all_to_all(block, TOKENS_AXES, split_axis=0, concat_axis=0, tiled=True)]
  transfers between devices with their start and end apart: 18 -> 18, of which waited for: 7 -> 3; matrix products, arithmetic and copies ran while one was open for 25% -> 23% of each run, Pallas kernels for 9% -> 0%
where the time goes in v5:
time: 141 us
  starting transfers between devices  35.1 us (25%)
  local copies, waits for them, and re-layouts  25.7 us (18%)
  blocking collectives  25 us (18%)
  Pallas kernels  20.4 us (14%)
  waiting for transfers between devices  14 us (10%)
  other arithmetic  9.17 us (7%)
  matrix products  5.77 us (4%)
  between operations  5.46 us (4%)
    all_to_all x1, blocking collectives, exchange(): lax.all_to_all(block, TOKENS_AXES, split_axis=0, concat_axis=0, tiled=True)  25 us
    gather x4, local copies, waits for them, and re-layouts, shards(): jnp.take(w_heads, w_order, axis=0, mode='clip')  19.6 us
    ppermute x9, starting transfers between devices, swap(): return lax.ppermute(block, 'c', [(0, 1), (1, 0)])  16.6 us
    pallas_call x1, Pallas kernels, attend(): pl.pallas_call(functools.partial(attend_kernel, TILE ** (-0.5) * LOG2E),...  13.6 us
    ppermute x8, starting transfers between devices, along_y(): lax.ppermute(block, 'y', [(i, (i + step) % PLANES) for i in range(PLANES)])  9.99 us
    all_to_all x1, starting transfers between devices, exchange(): lax.all_to_all(block, TOKENS_AXES, split_axis=0, concat_axis=0, tiled=True)  8.44 us
    all_to_all x1, waiting for transfers between devices, exchange(): lax.all_to_all(block, TOKENS_AXES, split_axis=0, concat_axis=0, tiled=True)  7.63 us
    dot_general x8, matrix products, project(): return jnp.dot(both, weight, preferred_element_type=jnp.float32)  5.57 us
  transfers between devices with their start and end apart: 18, of which 3 were waited for; matrix products, arithmetic and copies ran while one was open for 23% of the time, Pallas kernels for 0%

profile of v5, /device:TPU:1, one launch (start us, length us, event | category | flops | bytes accessed | tf_op | source)
XLA Modules:
  0.0 140.6 jit_solution(5162649722294828922)
XLA Ops:
  0.0 2.1 %fusion.64 = (s32[40,64]{1,0:T(8,128)S(1)}, s32[40]{0:T(128)S(1)}) fusion(s32[40,64,64]{2,1,0:T(8,128)} %param.13), kind=kLoop, calls=%fused_computation.170 | loop fusion | flops 325080 | bytes 665760 | tf_op jit(solution)/shard_map/reduce_sum | solution.py:240
  4.0 4.6 %shard_map.73 = bf16[16,768,128]{2,1,0:T(8,128)(2,1)} custom-call(s32[17]{0:T(128)} %pad_add_fusion.heads, bf16[512,5120]{1,0:T(8,128)(2,1)} %q_ref.1, bf16[512,5120]{1,0:T(8,128)(2,1)} %k_ref.1, bf16[512,5120]{1,0:T(8,128)(2,1)} %v_ref.1), custom_call_target="tpu_custom_call" | custom-call | tf_op jit(solution)/shard_map/pallas_call | solution.py:87
  8.5 8.4 %all-to-all-start = ((bf16[16,768,128]{2,1,0:T(8,128)(2,1)}), bf16[16,768,128]{2,1,0:T(8,128)(2,1)S(1)}, u32[]{:S(2)}, u32[]{:S(2)}) async-start(bf16[16,768,128]{2,1,0:T(8,128)(2,1)} %shard_map.73), calls=%async_computation | async-start | bytes 6291456 | tf_op jit(solution)/shard_map/all_to_all | solution.py:225
  30.1 5.0 %gather_fusion.1 = bf16[10,128,640]{2,1,0:T(8,128)(2,1)} fusion(bf16[40,128,640]{2,1,0:T(8,128)(2,1)} %bitcast.60, s32[1024]{0:T(1024)S(1)} %pad_clamp_fusion.3), kind=kCustom, calls=%fused_computation.1 | custom fusion | bytes 3276840 | tf_op jit(solution)/shard_map/jit(_take)/gather | solution.py:268
  35.0 4.9 %gather_fusion.2 = bf16[10,128,640]{2,1,0:T(8,128)(2,1)} fusion(bf16[40,128,640]{2,1,0:T(8,128)(2,1)} %bitcast.61, s32[1024]{0:T(1024)S(1)} %pad_clamp_fusion.2), kind=kCustom, calls=%fused_computation.2 | custom fusion | bytes 3276840 | tf_op jit(solution)/shard_map/jit(_take)/gather | solution.py:268
  39.9 4.9 %gather_fusion.3 = bf16[10,128,640]{2,1,0:T(8,128)(2,1)} fusion(bf16[40,128,640]{2,1,0:T(8,128)(2,1)} %bitcast.62, s32[1024]{0:T(1024)S(1)} %pad_clamp_fusion.1), kind=kCustom, calls=%fused_computation.3 | custom fusion | bytes 3276840 | tf_op jit(solution)/shard_map/jit(_take)/gather | solution.py:268
  44.8 4.9 %gather_fusion.4 = bf16[10,128,640]{2,1,0:T(8,128)(2,1)} fusion(bf16[40,128,640]{2,1,0:T(8,128)(2,1)} %bitcast.63, s32[1024]{0:T(1024)S(1)} %pad_clamp_fusion), kind=kCustom, calls=%fused_computation.4 | custom fusion | bytes 3276840 | tf_op jit(solution)/shard_map/jit(_take)/gather | solution.py:268
  49.7 7.6 %all-to-all-done = bf16[16,768,128]{2,1,0:T(8,128)(2,1)S(1)} async-done(((bf16[16,768,128]{2,1,0:T(8,128)(2,1)}), bf16[16,768,128]{2,1,0:T(8,128)(2,1)S(1)}, u32[]{:S(2)}, u32[]{:S(2)}) %all-to-all-start) | async-done | bytes 3145760 | tf_op jit(solution)/shard_map/all_to_all | solution.py:225
  57.3 3.0 %collective-permute-start = (bf16[16,6,128,128]{3,2,1,0:T(8,128)(2,1)S(1)}, bf16[16,6,128,128]{3,2,1,0:T(8,128)(2,1)S(1)}, u32[]{:S(2)}, u32[]{:S(2)}) collective-permute-start(bf16[16,6,128,128]{3,2,1,0:T(8,128)(2,1)S(1)} %bitcast.53), channel_id=1, source_target_pairs={{0,1},{1,0},{2,3},{3,2},{4,5},{5,4},{6,7},{7,6},{8,9},{9,8},{10,11... | collective-permute-start | bytes 9437192 | tf_op jit(solution)/shard_map/ppermute | solution.py:233
  60.4 5.2 %collective-permute-done.other_ref = bf16[16,6,128,128]{3,2,1,0:T(8,128)(2,1)S(1)} collective-permute-done((bf16[16,6,128,128]{3,2,1,0:T(8,128)(2,1)S(1)}, bf16[16,6,128,128]{3,2,1,0:T(8,128)(2,1)S(1)}, u32[]{:S(2)}, u32[]{:S(2)}) %collective-permute-start) | collective-permute-done | bytes 3145760 | tf_op jit(solution)/shard_map/ppermute | solution.py:233
  65.6 13.6 %shard_map.74 = bf16[32,128,128]{2,1,0:T(8,128)(2,1)S(1)} custom-call(s32[2]{0:T(128)S(1)} %pad_add_fusion.1.meta, s32[512]{0:T(512)S(1)} %broadcast_minimum_fusion.q_of, s32[2048]{0:T(1024)S(1)} %convert_element_type.79.k_of, s32[512]{0:T(512)S(1)} %get-tuple-element.25.valid_of, bf16[16,6,128,128]{3,2,1,0:T(8,128)(2,1)S(1)} %bitcast.54, ...), custom_call_target="tpu_custom_call" | custom-call | tf_op jit(solution)/shard_map/pallas_call | solution.py:162
  79.3 25.0 %all_to_all.10.got_ref = bf16[16,2,128,128]{3,2,1,0:T(8,128)(2,1)} all-to-all(bf16[16,2,128,128]{3,2,1,0:T(8,128)(2,1)S(1)} %bitcast.55), channel_id=1, replica_groups=mesh['x'=4,'z'=4,'y'=4,'c'=2] {'x','z'}, dimensions={0} | all-to-all | bytes 2097152 | tf_op jit(solution)/shard_map/all_to_all | solution.py:225
  104.3 2.2 %shard_map.75 = (bf16[128,1280]{1,0:T(8,128)(2,1)}, bf16[128,1280]{1,0:T(8,128)(2,1)}) custom-call(s32[20]{0:T(128)} %reshape.316.source, bf16[16,2,128,128]{3,2,1,0:T(8,128)(2,1)} %all_to_all.10.got_ref), custom_call_target="tpu_custom_call" | custom-call | tf_op jit(solution)/shard_map/pallas_call | solution.py:216
  106.5 2.7 %collective-permute-start.12 = (bf16[128,1280]{1,0:T(8,128)(2,1)}, bf16[128,1280]{1,0:T(8,128)(2,1)S(1)}, u32[]{:S(2)}, u32[]{:S(2)}) collective-permute-start(bf16[128,1280]{1,0:T(8,128)(2,1)} %get-tuple-element.33), channel_id=1, source_target_pairs={{0,6},{2,0},{4,2},{6,4},{1,7},{3,1},{5,3},{7,5},{8,14},{10,8},{12,... | collective-permute-start | bytes 983048 | tf_op jit(solution)/shard_map/ppermute | solution.py:229
  109.2 2.7 %collective-permute-start.4 = (bf16[128,1280]{1,0:T(8,128)(2,1)}, bf16[128,1280]{1,0:T(8,128)(2,1)S(1)}, u32[]{:S(2)}, u32[]{:S(2)}) collective-permute-start(bf16[128,1280]{1,0:T(8,128)(2,1)} %get-tuple-element.27), channel_id=1, source_target_pairs={{0,6},{2,0},{4,2},{6,4},{1,7},{3,1},{5,3},{7,5},{8,14},{10,8},{12,... | collective-permute-start | bytes 983048 | tf_op jit(solution)/shard_map/ppermute | solution.py:229
  111.9 3.2 %collective-permute-start.9 = (bf16[128,1280]{1,0:T(8,128)(2,1)}, bf16[128,1280]{1,0:T(8,128)(2,1)S(1)}, u32[]{:S(2)}, u32[]{:S(2)}) collective-permute-start(bf16[128,1280]{1,0:T(8,128)(2,1)} %get-tuple-element.33), channel_id=1, source_target_pairs={{0,1},{1,0},{2,3},{3,2},{4,5},{5,4},{6,7},{7,6},{8,9},{9,8},{10,11... | collective-permute-start | bytes 983048 | tf_op jit(solution)/shard_map/ppermute | solution.py:233
  115.1 5.6 %collective-permute-start.1 = (bf16[128,1280]{1,0:T(8,128)(2,1)}, bf16[128,1280]{1,0:T(8,128)(2,1)S(1)}, u32[]{:S(2)}, u32[]{:S(2)}) collective-permute-start(bf16[128,1280]{1,0:T(8,128)(2,1)} %get-tuple-element.27), channel_id=1, source_target_pairs={{0,1},{1,0},{2,3},{3,2},{4,5},{5,4},{6,7},{7,6},{8,9},{9,8},{10,11... | collective-permute-start | bytes 983048 | tf_op jit(solution)/shard_map/ppermute | solution.py:233
  120.9 1.2 collective-permute-done.2
  122.1 1.6 %collective-permute-start.15 = (bf16[128,640]{1,0:T(8,128)(2,1)S(1)}, bf16[128,640]{1,0:T(8,128)(2,1)S(1)}, u32[]{:S(2)}, u32[]{:S(2)}) collective-permute-start(bf16[128,640]{1,0:T(8,128)(2,1)S(1)} %slice.93), channel_id=1, source_target_pairs={{0,6},{2,0},{4,2},{6,4},{1,7},{3,1},{5,3},{7,5},{8,14},{10,8},{12,... | collective-permute-start | bytes 491528 | tf_op jit(solution)/shard_map/ppermute | solution.py:229
  124.0 2.7 %collective-permute-start.7 = (bf16[128,640]{1,0:T(8,128)(2,1)S(1)}, bf16[128,640]{1,0:T(8,128)(2,1)S(1)}, u32[]{:S(2)}, u32[]{:S(2)}) collective-permute-start(bf16[128,640]{1,0:T(8,128)(2,1)S(1)} %slice.85), channel_id=1, source_target_pairs={{0,6},{2,0},{4,2},{6,4},{1,7},{3,1},{5,3},{7,5},{8,14},{10,8},{12,... | collective-permute-start | bytes 491528 | tf_op jit(solution)/shard_map/ppermute | solution.py:229
  127.4 2.1 %collective-permute-start.11 = (bf16[128,1280]{1,0:T(8,128)(2,1)S(1)}, bf16[128,1280]{1,0:T(8,128)(2,1)S(1)}, u32[]{:S(2)}, u32[]{:S(2)}) collective-permute-start(bf16[128,1280]{1,0:T(8,128)(2,1)S(1)} %collective-permute-done.10), channel_id=1, source_target_pairs={{0,1},{1,0},{2,3},{3,2},{4,5},{5,4},{6,7},{7,6},{8,9},{9,8},{10,11... | collective-permute-start | bytes 983048 | tf_op jit(solution)/shard_map/ppermute | solution.py:233
  130.3 1.9 %collective-permute-start.3 = (bf16[128,1280]{1,0:T(8,128)(2,1)S(1)}, bf16[128,1280]{1,0:T(8,128)(2,1)S(1)}, u32[]{:S(2)}, u32[]{:S(2)}) collective-permute-start(bf16[128,1280]{1,0:T(8,128)(2,1)S(1)} %collective-permute-done.2), channel_id=1, source_target_pairs={{0,1},{1,0},{2,3},{3,2},{4,5},{5,4},{6,7},{7,6},{8,9},{9,8},{10,11... | collective-permute-start | bytes 983048 | tf_op jit(solution)/shard_map/ppermute | solution.py:233
  136.9 1.2 copy-done.2
  139.7 0.9 pad_maximum_fusion
  (116 shorter events, 18.0 us)
Async XLA Ops:
  8.5 48.8 %all-to-all-start = ((bf16[16,768,128]{2,1,0:T(8,128)(2,1)}), bf16[16,768,128]{2,1,0:T(8,128)(2,1)S(1)}, u32[]{:S(2)}, u32[]{:S(2)}) async-start(bf16[16,768,128]{2,1,0:T(8,128)(2,1)} %shard_map.73), calls=%async_computation | async-start | bytes 6291456 | tf_op jit(solution)/shard_map/all_to_all | solution.py:225
  57.3 8.3 %collective-permute-start = (bf16[16,6,128,128]{3,2,1,0:T(8,128)(2,1)S(1)}, bf16[16,6,128,128]{3,2,1,0:T(8,128)(2,1)S(1)}, u32[]{:S(2)}, u32[]{:S(2)}) collective-permute-start(bf16[16,6,128,128]{3,2,1,0:T(8,128)(2,1)S(1)} %bitcast.53), channel_id=1, source_target_pairs={{0,1},{1,0},{2,3},{3,2},{4,5},{5,4},{6,7},{7,6},{8,9},{9,8},{10,11... | collective-permute-start | bytes 9437192 | tf_op jit(solution)/shard_map/ppermute | solution.py:233
  79.3 41.4 %copy-start.4 = (bf16[512,640]{1,0:T(8,128)(2,1)S(1)}, bf16[512,640]{1,0:T(8,128)(2,1)}, u32[]{:S(2)}) copy-start(bf16[512,640]{1,0:T(8,128)(2,1)} %param.7) | copy-start | bytes 1966084
  106.5 8.6 %collective-permute-start.10 = (bf16[128,1280]{1,0:T(8,128)(2,1)}, bf16[128,1280]{1,0:T(8,128)(2,1)S(1)}, u32[]{:S(2)}, u32[]{:S(2)}) collective-permute-start(bf16[128,1280]{1,0:T(8,128)(2,1)} %get-tuple-element.33), channel_id=1, source_target_pairs={{0,2},{2,4},{4,6},{6,0},{1,3},{3,5},{5,7},{7,1},{8,10},{10,12},{12... | collective-permute-start | bytes 983048 | tf_op jit(solution)/shard_map/ppermute | solution.py:229
  106.5 14.3 %collective-permute-start.12 = (bf16[128,1280]{1,0:T(8,128)(2,1)}, bf16[128,1280]{1,0:T(8,128)(2,1)S(1)}, u32[]{:S(2)}, u32[]{:S(2)}) collective-permute-start(bf16[128,1280]{1,0:T(8,128)(2,1)} %get-tuple-element.33), channel_id=1, source_target_pairs={{0,6},{2,0},{4,2},{6,4},{1,7},{3,1},{5,3},{7,5},{8,14},{10,8},{12,... | collective-permute-start | bytes 983048 | tf_op jit(solution)/shard_map/ppermute | solution.py:229
  109.2 12.9 %collective-permute-start.2 = (bf16[128,1280]{1,0:T(8,128)(2,1)}, bf16[128,1280]{1,0:T(8,128)(2,1)S(1)}, u32[]{:S(2)}, u32[]{:S(2)}) collective-permute-start(bf16[128,1280]{1,0:T(8,128)(2,1)} %get-tuple-element.27), channel_id=1, source_target_pairs={{0,2},{2,4},{4,6},{6,0},{1,3},{3,5},{5,7},{7,1},{8,10},{10,12},{12... | collective-permute-start | bytes 983048 | tf_op jit(solution)/shard_map/ppermute | solution.py:229
  109.2 14.5 %collective-permute-start.4 = (bf16[128,1280]{1,0:T(8,128)(2,1)}, bf16[128,1280]{1,0:T(8,128)(2,1)S(1)}, u32[]{:S(2)}, u32[]{:S(2)}) collective-permute-start(bf16[128,1280]{1,0:T(8,128)(2,1)} %get-tuple-element.27), channel_id=1, source_target_pairs={{0,6},{2,0},{4,2},{6,4},{1,7},{3,1},{5,3},{7,5},{8,14},{10,8},{12,... | collective-permute-start | bytes 983048 | tf_op jit(solution)/shard_map/ppermute | solution.py:229
  111.9 12.1 %collective-permute-start.9 = (bf16[128,1280]{1,0:T(8,128)(2,1)}, bf16[128,1280]{1,0:T(8,128)(2,1)S(1)}, u32[]{:S(2)}, u32[]{:S(2)}) collective-permute-start(bf16[128,1280]{1,0:T(8,128)(2,1)} %get-tuple-element.33), channel_id=1, source_target_pairs={{0,1},{1,0},{2,3},{3,2},{4,5},{5,4},{6,7},{7,6},{8,9},{9,8},{10,11... | collective-permute-start | bytes 983048 | tf_op jit(solution)/shard_map/ppermute | solution.py:233
  115.1 12.3 %collective-permute-start.1 = (bf16[128,1280]{1,0:T(8,128)(2,1)}, bf16[128,1280]{1,0:T(8,128)(2,1)S(1)}, u32[]{:S(2)}, u32[]{:S(2)}) collective-permute-start(bf16[128,1280]{1,0:T(8,128)(2,1)} %get-tuple-element.27), channel_id=1, source_target_pairs={{0,1},{1,0},{2,3},{3,2},{4,5},{5,4},{6,7},{7,6},{8,9},{9,8},{10,11... | collective-permute-start | bytes 983048 | tf_op jit(solution)/shard_map/ppermute | solution.py:233
  120.7 6.0 %copy-start.3 = (bf16[10,128,640]{2,1,0:T(8,128)(2,1)S(1)}, bf16[10,128,640]{2,1,0:T(8,128)(2,1)}, u32[]{:S(2)}) copy-start(bf16[10,128,640]{2,1,0:T(8,128)(2,1)} %gather_fusion.1) | copy-start | bytes 4915204
  120.7 6.0 %copy-start.7 = (bf16[128,1280]{1,0:T(8,128)(2,1)S(1)}, bf16[128,1280]{1,0:T(8,128)(2,1)}, u32[]{:S(2)}) copy-start(bf16[128,1280]{1,0:T(8,128)(2,1)} %get-tuple-element.33) | copy-start | bytes 983044
  120.8 9.4 %collective-permute-start.14 = (bf16[128,640]{1,0:T(8,128)(2,1)S(1)}, bf16[128,640]{1,0:T(8,128)(2,1)S(1)}, u32[]{:S(2)}, u32[]{:S(2)}) collective-permute-start(bf16[128,640]{1,0:T(8,128)(2,1)S(1)} %slice.92), channel_id=1, source_target_pairs={{0,2},{2,4},{4,6},{6,0},{1,3},{3,5},{5,7},{7,1},{8,10},{10,12},{12... | collective-permute-start | bytes 491528 | tf_op jit(solution)/shard_map/ppermute | solution.py:229
  122.1 10.2 %collective-permute-start.15 = (bf16[128,640]{1,0:T(8,128)(2,1)S(1)}, bf16[128,640]{1,0:T(8,128)(2,1)S(1)}, u32[]{:S(2)}, u32[]{:S(2)}) collective-permute-start(bf16[128,640]{1,0:T(8,128)(2,1)S(1)} %slice.93), channel_id=1, source_target_pairs={{0,6},{2,0},{4,2},{6,4},{1,7},{3,1},{5,3},{7,5},{8,14},{10,8},{12,... | collective-permute-start | bytes 491528 | tf_op jit(solution)/shard_map/ppermute | solution.py:229
  123.7 6.6 %collective-permute-start.6 = (bf16[128,640]{1,0:T(8,128)(2,1)S(1)}, bf16[128,640]{1,0:T(8,128)(2,1)S(1)}, u32[]{:S(2)}, u32[]{:S(2)}) collective-permute-start(bf16[128,640]{1,0:T(8,128)(2,1)S(1)} %slice.84), channel_id=1, source_target_pairs={{0,2},{2,4},{4,6},{6,0},{1,3},{3,5},{5,7},{7,1},{8,10},{10,12},{12... | collective-permute-start | bytes 491528 | tf_op jit(solution)/shard_map/ppermute | solution.py:229
  124.0 5.5 %copy-start.6 = (bf16[128,1280]{1,0:T(8,128)(2,1)S(1)}, bf16[128,1280]{1,0:T(8,128)(2,1)}, u32[]{:S(2)}) copy-start(bf16[128,1280]{1,0:T(8,128)(2,1)} %get-tuple-element.27) | copy-start | bytes 983044
  124.0 8.4 %collective-permute-start.7 = (bf16[128,640]{1,0:T(8,128)(2,1)S(1)}, bf16[128,640]{1,0:T(8,128)(2,1)S(1)}, u32[]{:S(2)}, u32[]{:S(2)}) collective-permute-start(bf16[128,640]{1,0:T(8,128)(2,1)S(1)} %slice.85), channel_id=1, source_target_pairs={{0,6},{2,0},{4,2},{6,4},{1,7},{3,1},{5,3},{7,5},{8,14},{10,8},{12,... | collective-permute-start | bytes 491528 | tf_op jit(solution)/shard_map/ppermute | solution.py:229
  127.4 5.7 %copy-start.1 = (bf16[10,128,640]{2,1,0:T(8,128)(2,1)S(1)}, bf16[10,128,640]{2,1,0:T(8,128)(2,1)}, u32[]{:S(2)}) copy-start(bf16[10,128,640]{2,1,0:T(8,128)(2,1)} %gather_fusion.2) | copy-start | bytes 4915204
  127.4 5.5 %collective-permute-start.11 = (bf16[128,1280]{1,0:T(8,128)(2,1)S(1)}, bf16[128,1280]{1,0:T(8,128)(2,1)S(1)}, u32[]{:S(2)}, u32[]{:S(2)}) collective-permute-start(bf16[128,1280]{1,0:T(8,128)(2,1)S(1)} %collective-permute-done.10), channel_id=1, source_target_pairs={{0,1},{1,0},{2,3},{3,2},{4,5},{5,4},{6,7},{7,6},{8,9},{9,8},{10,11... | collective-permute-start | bytes 983048 | tf_op jit(solution)/shard_map/ppermute | solution.py:233
  130.2 4.3 %collective-permute-start.13 = (bf16[128,1280]{1,0:T(8,128)(2,1)S(1)}, bf16[128,1280]{1,0:T(8,128)(2,1)S(1)}, u32[]{:S(2)}, u32[]{:S(2)}) collective-permute-start(bf16[128,1280]{1,0:T(8,128)(2,1)S(1)} %collective-permute-done.12), channel_id=1, source_target_pairs={{0,1},{1,0},{2,3},{3,2},{4,5},{5,4},{6,7},{7,6},{8,9},{9,8},{10,11... | collective-permute-start | bytes 983048 | tf_op jit(solution)/shard_map/ppermute | solution.py:233
  130.3 3.5 %collective-permute-start.3 = (bf16[128,1280]{1,0:T(8,128)(2,1)S(1)}, bf16[128,1280]{1,0:T(8,128)(2,1)S(1)}, u32[]{:S(2)}, u32[]{:S(2)}) collective-permute-start(bf16[128,1280]{1,0:T(8,128)(2,1)S(1)} %collective-permute-done.2), channel_id=1, source_target_pairs={{0,1},{1,0},{2,3},{3,2},{4,5},{5,4},{6,7},{7,6},{8,9},{9,8},{10,11... | collective-permute-start | bytes 983048 | tf_op jit(solution)/shard_map/ppermute | solution.py:233
  132.3 3.7 %collective-permute-start.5 = (bf16[128,1280]{1,0:T(8,128)(2,1)S(1)}, bf16[128,1280]{1,0:T(8,128)(2,1)S(1)}, u32[]{:S(2)}, u32[]{:S(2)}) collective-permute-start(bf16[128,1280]{1,0:T(8,128)(2,1)S(1)} %collective-permute-done.4), channel_id=1, source_target_pairs={{0,1},{1,0},{2,3},{3,2},{4,5},{5,4},{6,7},{7,6},{8,9},{9,8},{10,11... | collective-permute-start | bytes 983048 | tf_op jit(solution)/shard_map/ppermute | solution.py:233
  132.4 4.5 %collective-permute-start.16 = (bf16[128,1280]{1,0:T(8,128)(2,1)S(1)}, bf16[128,1280]{1,0:T(8,128)(2,1)S(1)}, u32[]{:S(2)}, u32[]{:S(2)}) collective-permute-start(bf16[128,1280]{1,0:T(8,128)(2,1)S(1)} %constant_dynamic-update-slice_fusion.2), channel_id=1, source_target_pairs={{0,1},{1,0},{2,3},{3,2},{4,5},{5,4},{6,7},{7,6},{8,9},{9,8},{10,11... | collective-permute-start | bytes 983048 | tf_op jit(solution)/shard_map/ppermute | solution.py:233
  133.0 5.8 %collective-permute-start.8 = (bf16[128,1280]{1,0:T(8,128)(2,1)S(1)}, bf16[128,1280]{1,0:T(8,128)(2,1)S(1)}, u32[]{:S(2)}, u32[]{:S(2)}) collective-permute-start(bf16[128,1280]{1,0:T(8,128)(2,1)S(1)} %constant_dynamic-update-slice_fusion), channel_id=1, source_target_pairs={{0,1},{1,0},{2,3},{3,2},{4,5},{5,4},{6,7},{7,6},{8,9},{9,8},{10,11... | collective-permute-start | bytes 983048 | tf_op jit(solution)/shard_map/ppermute | solution.py:233
  133.8 1.4 %copy-start = (bf16[10,128,640]{2,1,0:T(8,128)(2,1)S(1)}, bf16[10,128,640]{2,1,0:T(8,128)(2,1)}, u32[]{:S(2)}) copy-start(bf16[10,128,640]{2,1,0:T(8,128)(2,1)} %gather_fusion.3) | copy-start | bytes 4915204
  (2 other events, 2.2 us)

commit v6 on v5

--- a/solution.py
+++ b/solution.py
@@ -16,7 +16,7 @@
 HALF = 256
 GROUP = 4
 UNROLL = 16
-ITEMS = 512
+ITEMS = 256
 LOG2E = 1.4426950408889634
 TOKENS_AXES = ("x", "z")
 LOW = -1e30
@@ -99,23 +99,7 @@
     )(scalars, queries, keys, values)
 
 
-def attend_kernel(
-    scale, meta, q_of, k_of, valid_of, own_ref, other_ref, out_ref, kv_s, q_s, acc_s, max_s, sum_s, sems
-):
-    core = meta[0]
-    loads = [
-        pltpu.make_async_copy(own_ref.at[:, pl.ds(0, 4)], kv_s.at[core], sems.at[0]),
-        pltpu.make_async_copy(other_ref.at[:, pl.ds(0, 4)], kv_s.at[1 - core], sems.at[1]),
-        pltpu.make_async_copy(own_ref.at[:, pl.ds(4, 2)], q_s, sems.at[2]),
-    ]
-    for load in loads:
-        load.start()
-    acc_s[...] = jnp.zeros_like(acc_s)
-    sum_s[...] = jnp.zeros_like(sum_s)
-    max_s[...] = jnp.full_like(max_s, LOW)
-    for load in loads:
-        load.wait()
-
+def attend_items(scale, meta, q_of, k_of, valid_of, query_ref, key_ref, acc_ref, max_ref, sum_ref):
     def body(step, _):
         parts = []
         for u in range(UNROLL):
@@ -123,8 +107,10 @@
             t = q_of[e]
             kid = [k_of[e * GROUP + g] for g in range(GROUP)]
             valid = valid_of[e]
-            keys = jnp.concatenate([kv_s[i // 64, i % 64 // 4, i % 4] for i in kid], axis=0)
-            scores = lax.dot_general(keys, q_s[t // 2, t % 2], (((1,), (1,)), ((), ())), preferred_element_type=jnp.float32)
+            keys = jnp.concatenate([key_ref[i // 2, i % 2] for i in kid], axis=0)
+            scores = lax.dot_general(
+                keys, query_ref[t // 2, 4 + t % 2], (((1,), (1,)), ((), ())), preferred_element_type=jnp.float32
+            )
             top = jnp.max(scores, axis=0, keepdims=True) * scale
             weights = []
             total = jnp.zeros((1, TILE), jnp.float32)
@@ -133,20 +119,34 @@
                 w = jnp.exp2(scores[g * TILE : (g + 1) * TILE] * scale - shift)
                 total = total + jnp.sum(w, axis=0, keepdims=True)
                 weights.append(w.astype(jnp.bfloat16))
-            vals = jnp.concatenate([kv_s[i // 64, i % 64 // 4, i % 4 + 2] for i in kid], axis=1)
+            vals = jnp.concatenate([key_ref[i // 2, 2 + i % 2] for i in kid], axis=1)
             part = jnp.dot(vals, jnp.concatenate(weights, axis=0), preferred_element_type=jnp.float32)
             parts.append((t, top, total, part))
         for t, top, total, part in parts:
-            old = max_s[t]
+            old = max_ref[t]
             new = jnp.maximum(old, top)
             a = jnp.exp2(old - new)
             b = jnp.exp2(top - new)
-            max_s[t] = new
-            sum_s[t] = sum_s[t] * a + total * b
-            acc_s[t] = acc_s[t] * a + part * b
+            max_ref[t] = new
+            sum_ref[t] = sum_ref[t] * a + total * b
+            acc_ref[t] = acc_ref[t] * a + part * b
         return 0
 
-    lax.fori_loop(0, meta[1], body, 0)
+    lax.fori_loop(0, meta[0], body, 0)
+
+
+def first_kernel(scale, meta, q_of, k_of, valid_of, own_ref, acc_ref, max_ref, sum_ref):
+    acc_ref[...] = jnp.zeros_like(acc_ref)
+    sum_ref[...] = jnp.zeros_like(sum_ref)
+    max_ref[...] = jnp.full_like(max_ref, LOW)
+    attend_items(scale, meta, q_of, k_of, valid_of, own_ref, own_ref, acc_ref, max_ref, sum_ref)
+
+
+def second_kernel(scale, meta, q_of, k_of, valid_of, own_ref, other_ref, acc_in, max_in, sum_in, out_ref, acc_s, max_s, sum_s):
+    acc_s[...] = acc_in[...]
+    max_s[...] = max_in[...]
+    sum_s[...] = sum_in[...]
+    attend_items(scale, meta, q_of, k_of, valid_of, own_ref, other_ref, acc_s, max_s, sum_s)
 
     def finish(t, _):
         inverse = 1.0 / jnp.maximum(sum_s[t], 1e-30)
@@ -156,24 +156,32 @@
     lax.fori_loop(0, 2 * CHIPS, finish, 0)
 
 
-def attend(meta, q_of, k_of, valid_of, own, other):
+def attend(lists, own, other=None, state=None):
+    tiles = 2 * CHIPS
     smem = pl.BlockSpec(memory_space=pltpu.SMEM)
-    hbm = pl.BlockSpec(memory_space=pl.ANY)
+    vmem = pl.BlockSpec(memory_space=pltpu.VMEM)
+    shapes = [((tiles, TILE, TILE), jnp.float32), ((tiles, 1, TILE), jnp.float32), ((tiles, 1, TILE), jnp.float32)]
+    options = dict(
+        compiler_params=pltpu.CompilerParams(vmem_limit_bytes=24 * 2**20),
+        cost_estimate=pl.CostEstimate(flops=4 * 10**9, bytes_accessed=8 * 2**20, transcendentals=4 * 10**6),
+    )
+    scale = TILE**-0.5 * LOG2E
+    if other is None:
+        return pl.pallas_call(
+            functools.partial(first_kernel, scale),
+            in_specs=[smem] * 4 + [vmem],
+            out_specs=[vmem] * 3,
+            out_shape=[jax.ShapeDtypeStruct(*shape) for shape in shapes],
+            **options,
+        )(*lists, own)
     return pl.pallas_call(
-        functools.partial(attend_kernel, TILE**-0.5 * LOG2E),
-        in_specs=[smem] * 4 + [hbm] * 2,
-        out_specs=pl.BlockSpec(memory_space=pltpu.VMEM),
-        out_shape=jax.ShapeDtypeStruct((2 * CHIPS, TILE, TILE), jnp.bfloat16),
-        scratch_shapes=[
-            pltpu.VMEM((2, CHIPS, 4, TILE, TILE), jnp.bfloat16),
-            pltpu.VMEM((CHIPS, 2, TILE, TILE), jnp.bfloat16),
-            pltpu.VMEM((2 * CHIPS, TILE, TILE), jnp.float32),
-            pltpu.VMEM((2 * CHIPS, 1, TILE), jnp.float32),
-            pltpu.VMEM((2 * CHIPS, 1, TILE), jnp.float32),
-            pltpu.SemaphoreType.DMA((3,)),
-        ],
-        compiler_params=pltpu.CompilerParams(vmem_limit_bytes=20 * 2**20),
-    )(meta, q_of, k_of, valid_of, own, other)
+        functools.partial(second_kernel, scale),
+        in_specs=[smem] * 4 + [vmem] * 5,
+        out_specs=vmem,
+        out_shape=jax.ShapeDtypeStruct((tiles, TILE, TILE), jnp.bfloat16),
+        scratch_shapes=[pltpu.VMEM(*shape) for shape in shapes],
+        **options,
+    )(*lists, own, other, *state)
 
 
 def item_lists(allowed, mine):
@@ -185,9 +193,8 @@
     steps = (end[-1] + UNROLL - 1) // UNROLL
     key_ids = jnp.arange(tiles)
     before = jnp.sum(allowed[:, None, :] * (key_ids[None, :] < key_ids[:, None])[None].astype(jnp.int32), axis=2)
-    held_at = (key_ids // 2 % 2) * 64 + key_ids // 4 * 4 + key_ids % 2
     listed = jnp.sum(
-        jnp.where((before[:, :, None] == key_ids[None, None, :]) & (allowed[:, :, None] > 0), held_at[None, :, None], 0),
+        jnp.where((before[:, :, None] == key_ids[None, None, :]) & (allowed[:, :, None] > 0), key_ids[None, :, None], 0),
         axis=1,
     )
     item = jnp.arange(ITEMS)
@@ -202,7 +209,7 @@
     where = start[:, None] + jnp.where(offset[None, :] < left[:, None], offset[None, :], 0)
     k_of = jnp.sum(jnp.where(where[:, :, None] == key_ids[None, None, :], rows[:, None, :], 0.0), axis=2)
     valid = jnp.minimum(left, GROUP) * real
-    return steps, q_of, k_of.astype(jnp.int32).reshape(-1), valid
+    return steps[None], q_of, k_of.astype(jnp.int32).reshape(-1), valid
 
 
 def select_kernel(source, got_ref, *out_refs):
@@ -266,7 +273,11 @@
     for ahead in (0, 3, 1, 2):
         w_order = lax.dynamic_slice_in_dim(head_at, (plane + ahead) % PLANES * PLANE_HEADS, PLANE_HEADS)
         weights.append(jnp.take(w_heads, w_order, axis=0, mode="clip").reshape(PLANE_HEADS * TILE, -1))
-    lists = item_lists(allowed.reshape(2 * CHIPS, 4 * CHIPS), mine_tiles)
+    allowed = allowed.reshape(2 * CHIPS, CHIPS, 2, 2)
+    lists = [
+        item_lists(lax.dynamic_index_in_dim(allowed, c, 2, keepdims=False).reshape(2 * CHIPS, 2 * CHIPS), mine_tiles)
+        for c in (core, 1 - core)
+    ]
     got, lists, source, weights = lax.optimization_barrier((got, lists, source, weights))
     got_other = swap(got)
 
@@ -278,9 +289,7 @@
         mine, theirs = total[:TILE], total[TILE:]
         return jnp.where(core == 0, mine, theirs), jnp.where(core == 0, theirs, mine)
 
-    steps, q_of, k_of, valid = lists
-    meta = jnp.stack([core, steps]).astype(jnp.int32)
-    attended = attend(meta, q_of, k_of, valid, got, got_other)
+    attended = attend(lists[1], got, got_other, attend(lists[0], got))
     own_rows = select(source, exchange(attended.reshape(CHIPS, 2, TILE, TILE)))
 
     residual = residual_in.astype(jnp.float32).reshape(2, 2, TILE, -1)

time: 141 us -> 135 us (0.957); the launches traced: 141 us -> 136 us
  waiting for transfers between devices: 14 us -> 0.05 us
  other arithmetic: 9.17 us -> 13.2 us
  local copies, waits for them, and re-layouts: 25.7 us -> 29.7 us
  starting transfers between devices: 35.1 us -> 38.5 us
  Pallas kernels: 20.4 us -> 17.8 us
    all_to_all x1, waiting for transfers between devices: 7.63 us -> 0.01 us  [exchange(): lax.all_to_all(block, TOKENS_AXES, split_axis=0, concat_axis=0, tiled=True)]
    ppermute x9, waiting for transfers between devices: 5.23 us -> 0.02 us  [swap(): return lax.ppermute(block, 'c', [(0, 1), (1, 0)])]
    ppermute x8, starting transfers between devices: 9.99 us -> 12.7 us  [along_y(): lax.ppermute(block, 'y', [(i, (i + step) % PLANES) for i in range(PLANES)])]
    reduce_sum x1, other arithmetic: 0.34 us -> 3.07 us  [item_lists(): count = jnp.sum(allowed, axis=1) * mine]
    pallas_call x1 -> x2, Pallas kernels: 13.6 us -> 11.1 us  [the longest x1 6.12 us: attend(): pl.pallas_call(functools.partial(first_kernel, scale), in_specs=[smem] *...]
    reshape x0 -> x1, local copies, waits for them, and re-layouts: none -> 1.6 us  [shards(): allowed = allowed.reshape(2 * CHIPS, CHIPS, 2, 2)]
    unnamed x18 -> x20, local copies, waits for them, and re-layouts: 2 us -> 3.32 us
  transfers between devices with their start and end apart: 18 -> 18, of which waited for: 3 -> 0; matrix products, arithmetic and copies ran while one was open for 23% -> 30% of each run, Pallas kernels for 0% -> 4%
where the time goes in v6:
time: 135 us; the launch traced here: 136 us
  starting transfers between devices  38.5 us (29%)
  local copies, waits for them, and re-layouts  29.7 us (22%)
  blocking collectives  24.6 us (18%)
  Pallas kernels  17.8 us (13%)
  other arithmetic  13.2 us (10%)
  between operations  6.69 us (5%)
  matrix products  5.94 us (4%)
    all_to_all x1, blocking collectives, exchange(): lax.all_to_all(block, TOKENS_AXES, split_axis=0, concat_axis=0, tiled=True)  24.6 us
    gather x4, local copies, waits for them, and re-layouts, shards(): jnp.take(w_heads, w_order, axis=0, mode='clip')  19.6 us
    ppermute x9, starting transfers between devices, swap(): return lax.ppermute(block, 'c', [(0, 1), (1, 0)])  17.3 us
    ppermute x8, starting transfers between devices, along_y(): lax.ppermute(block, 'y', [(i, (i + step) % PLANES) for i in range(PLANES)])  12.7 us
    all_to_all x1, starting transfers between devices, exchange(): lax.all_to_all(block, TOKENS_AXES, split_axis=0, concat_axis=0, tiled=True)  8.44 us
    pallas_call x1, Pallas kernels, attend(): pl.pallas_call(functools.partial(first_kernel, scale), in_specs=[smem] *...  6.12 us
    dot_general x8, matrix products, project(): return jnp.dot(both, weight, preferred_element_type=jnp.float32)  5.56 us
    pallas_call x1, Pallas kernels, attend(): pl.pallas_call(functools.partial(second_kernel, scale), in_specs=[smem] *...  4.96 us
  transfers between devices with their start and end apart: 18, of which 0 were waited for; matrix products, arithmetic and copies ran while one was open for 30% of the time, Pallas kernels for 4%

profile of v6, /device:TPU:1, one launch (start us, length us, event | category | flops | bytes accessed | tf_op | source)
XLA Modules:
  0.0 136.5 jit_solution(6189667306374616456)
XLA Ops:
  0.0 2.1 %fusion.68 = (s32[40,64]{1,0:T(8,128)S(1)}, s32[40]{0:T(128)S(1)}) fusion(s32[40,64,64]{2,1,0:T(8,128)} %param.13), kind=kLoop, calls=%fused_computation.185 | loop fusion | flops 325080 | bytes 665760 | tf_op jit(solution)/shard_map/reduce_sum | solution.py:247
  4.1 4.5 %shard_map.73 = bf16[16,768,128]{2,1,0:T(8,128)(2,1)} custom-call(s32[17]{0:T(128)} %pad_add_fusion.heads, bf16[512,5120]{1,0:T(8,128)(2,1)} %q_ref.1, bf16[512,5120]{1,0:T(8,128)(2,1)} %k_ref.1, bf16[512,5120]{1,0:T(8,128)(2,1)} %v_ref.1), custom_call_target="tpu_custom_call" | custom-call | tf_op jit(solution)/shard_map/pallas_call | solution.py:87
  8.6 8.4 %all-to-all-start = ((bf16[16,768,128]{2,1,0:T(8,128)(2,1)}), bf16[16,768,128]{2,1,0:T(8,128)(2,1)S(1)}, u32[]{:S(2)}, u32[]{:S(2)}) async-start(bf16[16,768,128]{2,1,0:T(8,128)(2,1)} %shard_map.73), calls=%async_computation | async-start | bytes 6291456 | tf_op jit(solution)/shard_map/all_to_all | solution.py:232
  22.1 1.6 %reshape.408 = s32[32,16,2,2]{3,2,1,0:T(2,128)} reshape(s32[16,1,2,64]{3,2,1,0:T(2,128)S(1)} %constant_dynamic-slice_fusion.3) | data formatting | bytes 16384 | tf_op jit(solution)/shard_map/reshape | solution.py:276
  24.9 3.1 %fusion.69 = (s32[32]{0:T(128)S(1)}, s32[32,16,1,2]{3,2,1,0:T(1,128)S(1)}, s32[32]{0:T(128)S(1)}, s32[32,16,1,2]{3,2,1,0:T(1,128)}) fusion(s32[32,16,2,2]{3,2,1,0:T(2,128)} %reshape.408, s32[]{:T(128)S(6)} %select_n.227, s32[]{:T(128)S(6)} %select_n.214), kind=kLoop, calls=%fused_computation.186 | loop fusion | flops 1984 | bytes 16648 | tf_op jit(solution)/shard_map/reduce_sum | solution.py:189
  39.5 5.0 %gather_fusion.1 = bf16[10,128,640]{2,1,0:T(8,128)(2,1)} fusion(bf16[40,128,640]{2,1,0:T(8,128)(2,1)} %bitcast.80, s32[1024]{0:T(1024)S(1)} %get-tuple-element.104), kind=kCustom, calls=%fused_computation.1 | custom fusion | bytes 3276840 | tf_op jit(solution)/shard_map/jit(_take)/gather | solution.py:275
  44.5 4.9 %gather_fusion.2 = bf16[10,128,640]{2,1,0:T(8,128)(2,1)} fusion(bf16[40,128,640]{2,1,0:T(8,128)(2,1)} %bitcast.81, s32[1024]{0:T(1024)S(1)} %get-tuple-element.103), kind=kCustom, calls=%fused_computation.2 | custom fusion | bytes 3276840 | tf_op jit(solution)/shard_map/jit(_take)/gather | solution.py:275
  49.3 4.9 %gather_fusion.3 = bf16[10,128,640]{2,1,0:T(8,128)(2,1)} fusion(bf16[40,128,640]{2,1,0:T(8,128)(2,1)} %bitcast.82, s32[1024]{0:T(1024)S(1)} %get-tuple-element.102), kind=kCustom, calls=%fused_computation.3 | custom fusion | bytes 3276840 | tf_op jit(solution)/shard_map/jit(_take)/gather | solution.py:275
  54.2 4.9 %gather_fusion.4 = bf16[10,128,640]{2,1,0:T(8,128)(2,1)} fusion(bf16[40,128,640]{2,1,0:T(8,128)(2,1)} %bitcast.83, s32[1024]{0:T(1024)S(1)} %get-tuple-element.101), kind=kCustom, calls=%fused_computation.4 | custom fusion | bytes 3276840 | tf_op jit(solution)/shard_map/jit(_take)/gather | solution.py:275
  59.1 1.4 %collective-permute-start = (bf16[16,6,128,128]{3,2,1,0:T(8,128)(2,1)S(1)}, bf16[16,6,128,128]{3,2,1,0:T(8,128)(2,1)S(1)}, u32[]{:S(2)}, u32[]{:S(2)}) collective-permute-start(bf16[16,6,128,128]{3,2,1,0:T(8,128)(2,1)S(1)} %bitcast.72), channel_id=1, source_target_pairs={{0,1},{1,0},{2,3},{3,2},{4,5},{5,4},{6,7},{7,6},{8,9},{9,8},{10,11... | collective-permute-start | bytes 9437192 | tf_op jit(solution)/shard_map/ppermute | solution.py:240
  60.5 6.1 %shard_map.74 = (f32[32,128,128]{2,1,0:T(8,128)S(1)}, f32[32,1,128]{2,1,0:T(1,128)S(1)}, f32[32,1,128]{2,1,0:T(1,128)S(1)}) custom-call(s32[1]{0:T(128)} %bitcast.12.meta, s32[256]{0:T(256)S(1)} %broadcast_minimum_fusion.1.q_of, s32[1024]{0:T(1024)S(1)} %convert_element_type.102.k_of, s32[256]{0:T(256)S(1)} %get-tuple-element.37.valid_of, ...), custom_call_target="tpu_custom_call" | custom-call | flops 4000000000 | bytes 8388608 | tf_op jit(solution)/shard_map/pallas_call | solution.py:170
  66.7 5.0 %shard_map.75 = bf16[32,128,128]{2,1,0:T(8,128)(2,1)S(1)} custom-call(s32[1]{0:T(128)} %bitcast.20.meta, s32[256]{0:T(256)S(1)} %broadcast_minimum_fusion.q_of, s32[1024]{0:T(1024)S(1)} %convert_element_type.108.k_of, s32[256]{0:T(256)S(1)} %get-tuple-element.32.valid_of, bf16[16,6,128,128]{3,2,1,0:T(8,128)(2,1)S(1)} %bitcast.74, ...), custom_call_target="tpu_custom_call" | custom-call | flops 4000000000 | bytes 8388608 | tf_op jit(solution)/shard_map/pallas_call | solution.py:177
  71.7 24.6 %all_to_all.10.got_ref = bf16[16,2,128,128]{3,2,1,0:T(8,128)(2,1)} all-to-all(bf16[16,2,128,128]{3,2,1,0:T(8,128)(2,1)S(1)} %bitcast.75), channel_id=1, replica_groups=mesh['x'=4,'z'=4,'y'=4,'c'=2] {'x','z'}, dimensions={0} | all-to-all | bytes 2097152 | tf_op jit(solution)/shard_map/all_to_all | solution.py:232
  96.3 2.2 %shard_map.76 = (bf16[128,1280]{1,0:T(8,128)(2,1)}, bf16[128,1280]{1,0:T(8,128)(2,1)}) custom-call(s32[20]{0:T(128)} %reshape.353.source, bf16[16,2,128,128]{3,2,1,0:T(8,128)(2,1)} %all_to_all.10.got_ref), custom_call_target="tpu_custom_call" | custom-call | tf_op jit(solution)/shard_map/pallas_call | solution.py:223
  99.2 2.1 %collective-permute-start.12 = (bf16[128,1280]{1,0:T(8,128)(2,1)}, bf16[128,1280]{1,0:T(8,128)(2,1)S(1)}, u32[]{:S(2)}, u32[]{:S(2)}) collective-permute-start(bf16[128,1280]{1,0:T(8,128)(2,1)} %get-tuple-element.47), channel_id=1, source_target_pairs={{0,6},{2,0},{4,2},{6,4},{1,7},{3,1},{5,3},{7,5},{8,14},{10,8},{12,... | collective-permute-start | bytes 983048 | tf_op jit(solution)/shard_map/ppermute | solution.py:236
  101.2 2.5 %collective-permute-start.2 = (bf16[128,1280]{1,0:T(8,128)(2,1)}, bf16[128,1280]{1,0:T(8,128)(2,1)S(1)}, u32[]{:S(2)}, u32[]{:S(2)}) collective-permute-start(bf16[128,1280]{1,0:T(8,128)(2,1)} %get-tuple-element.41), channel_id=1, source_target_pairs={{0,2},{2,4},{4,6},{6,0},{1,3},{3,5},{5,7},{7,1},{8,10},{10,12},{12... | collective-permute-start | bytes 983048 | tf_op jit(solution)/shard_map/ppermute | solution.py:236
  104.3 3.0 %collective-permute-start.9 = (bf16[128,1280]{1,0:T(8,128)(2,1)}, bf16[128,1280]{1,0:T(8,128)(2,1)S(1)}, u32[]{:S(2)}, u32[]{:S(2)}) collective-permute-start(bf16[128,1280]{1,0:T(8,128)(2,1)} %get-tuple-element.47), channel_id=1, source_target_pairs={{0,1},{1,0},{2,3},{3,2},{4,5},{5,4},{6,7},{7,6},{8,9},{9,8},{10,11... | collective-permute-start | bytes 983048 | tf_op jit(solution)/shard_map/ppermute | solution.py:240
  107.3 5.6 %collective-permute-start.1 = (bf16[128,1280]{1,0:T(8,128)(2,1)}, bf16[128,1280]{1,0:T(8,128)(2,1)S(1)}, u32[]{:S(2)}, u32[]{:S(2)}) collective-permute-start(bf16[128,1280]{1,0:T(8,128)(2,1)} %get-tuple-element.41), channel_id=1, source_target_pairs={{0,1},{1,0},{2,3},{3,2},{4,5},{5,4},{6,7},{7,6},{8,9},{9,8},{10,11... | collective-permute-start | bytes 983048 | tf_op jit(solution)/shard_map/ppermute | solution.py:240
  113.0 1.9 %collective-permute-start.14 = (bf16[128,640]{1,0:T(8,128)(2,1)S(1)}, bf16[128,640]{1,0:T(8,128)(2,1)S(1)}, u32[]{:S(2)}, u32[]{:S(2)}) collective-permute-start(bf16[128,640]{1,0:T(8,128)(2,1)S(1)} %slice.98), channel_id=1, source_target_pairs={{0,2},{2,4},{4,6},{6,0},{1,3},{3,5},{5,7},{7,1},{8,10},{10,12},{12... | collective-permute-start | bytes 491528 | tf_op jit(solution)/shard_map/ppermute | solution.py:236
  115.0 2.2 %collective-permute-start.15 = (bf16[128,640]{1,0:T(8,128)(2,1)S(1)}, bf16[128,640]{1,0:T(8,128)(2,1)S(1)}, u32[]{:S(2)}, u32[]{:S(2)}) collective-permute-start(bf16[128,640]{1,0:T(8,128)(2,1)S(1)} %slice.99), channel_id=1, source_target_pairs={{0,6},{2,0},{4,2},{6,4},{1,7},{3,1},{5,3},{7,5},{8,14},{10,8},{12,... | collective-permute-start | bytes 491528 | tf_op jit(solution)/shard_map/ppermute | solution.py:236
  117.6 2.5 %collective-permute-start.7 = (bf16[128,640]{1,0:T(8,128)(2,1)S(1)}, bf16[128,640]{1,0:T(8,128)(2,1)S(1)}, u32[]{:S(2)}, u32[]{:S(2)}) collective-permute-start(bf16[128,640]{1,0:T(8,128)(2,1)S(1)} %slice.91), channel_id=1, source_target_pairs={{0,6},{2,0},{4,2},{6,4},{1,7},{3,1},{5,3},{7,5},{8,14},{10,8},{12,... | collective-permute-start | bytes 491528 | tf_op jit(solution)/shard_map/ppermute | solution.py:236
  120.8 4.7 %collective-permute-start.11 = (bf16[128,1280]{1,0:T(8,128)(2,1)S(1)}, bf16[128,1280]{1,0:T(8,128)(2,1)S(1)}, u32[]{:S(2)}, u32[]{:S(2)}) collective-permute-start(bf16[128,1280]{1,0:T(8,128)(2,1)S(1)} %collective-permute-done.10), channel_id=1, source_target_pairs={{0,1},{1,0},{2,3},{3,2},{4,5},{5,4},{6,7},{7,6},{8,9},{9,8},{10,11... | collective-permute-start | bytes 983048 | tf_op jit(solution)/shard_map/ppermute | solution.py:240
  126.3 1.6 %collective-permute-start.3 = (bf16[128,1280]{1,0:T(8,128)(2,1)S(1)}, bf16[128,1280]{1,0:T(8,128)(2,1)S(1)}, u32[]{:S(2)}, u32[]{:S(2)}) collective-permute-start(bf16[128,1280]{1,0:T(8,128)(2,1)S(1)} %collective-permute-done.2), channel_id=1, source_target_pairs={{0,1},{1,0},{2,3},{3,2},{4,5},{5,4},{6,7},{7,6},{8,9},{9,8},{10,11... | collective-permute-start | bytes 983048 | tf_op jit(solution)/shard_map/ppermute | solution.py:240
  132.8 1.2 copy-done.2
  (135 shorter events, 23.8 us)
Async XLA Ops:
  8.6 50.5 %all-to-all-start = ((bf16[16,768,128]{2,1,0:T(8,128)(2,1)}), bf16[16,768,128]{2,1,0:T(8,128)(2,1)S(1)}, u32[]{:S(2)}, u32[]{:S(2)}) async-start(bf16[16,768,128]{2,1,0:T(8,128)(2,1)} %shard_map.73), calls=%async_computation | async-start | bytes 6291456 | tf_op jit(solution)/shard_map/all_to_all | solution.py:232
  59.1 7.5 %collective-permute-start = (bf16[16,6,128,128]{3,2,1,0:T(8,128)(2,1)S(1)}, bf16[16,6,128,128]{3,2,1,0:T(8,128)(2,1)S(1)}, u32[]{:S(2)}, u32[]{:S(2)}) collective-permute-start(bf16[16,6,128,128]{3,2,1,0:T(8,128)(2,1)S(1)} %bitcast.72), channel_id=1, source_target_pairs={{0,1},{1,0},{2,3},{3,2},{4,5},{5,4},{6,7},{7,6},{8,9},{9,8},{10,11... | collective-permute-start | bytes 9437192 | tf_op jit(solution)/shard_map/ppermute | solution.py:240
  71.6 41.3 %copy-start.4 = (bf16[512,640]{1,0:T(8,128)(2,1)S(1)}, bf16[512,640]{1,0:T(8,128)(2,1)}, u32[]{:S(2)}) copy-start(bf16[512,640]{1,0:T(8,128)(2,1)} %param.7) | copy-start | bytes 1966084
  98.5 8.8 %collective-permute-start.10 = (bf16[128,1280]{1,0:T(8,128)(2,1)}, bf16[128,1280]{1,0:T(8,128)(2,1)S(1)}, u32[]{:S(2)}, u32[]{:S(2)}) collective-permute-start(bf16[128,1280]{1,0:T(8,128)(2,1)} %get-tuple-element.47), channel_id=1, source_target_pairs={{0,2},{2,4},{4,6},{6,0},{1,3},{3,5},{5,7},{7,1},{8,10},{10,12},{12... | collective-permute-start | bytes 983048 | tf_op jit(solution)/shard_map/ppermute | solution.py:236
  99.2 13.9 %collective-permute-start.12 = (bf16[128,1280]{1,0:T(8,128)(2,1)}, bf16[128,1280]{1,0:T(8,128)(2,1)S(1)}, u32[]{:S(2)}, u32[]{:S(2)}) collective-permute-start(bf16[128,1280]{1,0:T(8,128)(2,1)} %get-tuple-element.47), channel_id=1, source_target_pairs={{0,6},{2,0},{4,2},{6,4},{1,7},{3,1},{5,3},{7,5},{8,14},{10,8},{12,... | collective-permute-start | bytes 983048 | tf_op jit(solution)/shard_map/ppermute | solution.py:236
  101.2 13.8 %collective-permute-start.2 = (bf16[128,1280]{1,0:T(8,128)(2,1)}, bf16[128,1280]{1,0:T(8,128)(2,1)S(1)}, u32[]{:S(2)}, u32[]{:S(2)}) collective-permute-start(bf16[128,1280]{1,0:T(8,128)(2,1)} %get-tuple-element.41), channel_id=1, source_target_pairs={{0,2},{2,4},{4,6},{6,0},{1,3},{3,5},{5,7},{7,1},{8,10},{10,12},{12... | collective-permute-start | bytes 983048 | tf_op jit(solution)/shard_map/ppermute | solution.py:236
  103.7 13.6 %collective-permute-start.4 = (bf16[128,1280]{1,0:T(8,128)(2,1)}, bf16[128,1280]{1,0:T(8,128)(2,1)S(1)}, u32[]{:S(2)}, u32[]{:S(2)}) collective-permute-start(bf16[128,1280]{1,0:T(8,128)(2,1)} %get-tuple-element.41), channel_id=1, source_target_pairs={{0,6},{2,0},{4,2},{6,4},{1,7},{3,1},{5,3},{7,5},{8,14},{10,8},{12,... | collective-permute-start | bytes 983048 | tf_op jit(solution)/shard_map/ppermute | solution.py:236
  104.3 13.3 %collective-permute-start.9 = (bf16[128,1280]{1,0:T(8,128)(2,1)}, bf16[128,1280]{1,0:T(8,128)(2,1)S(1)}, u32[]{:S(2)}, u32[]{:S(2)}) collective-permute-start(bf16[128,1280]{1,0:T(8,128)(2,1)} %get-tuple-element.47), channel_id=1, source_target_pairs={{0,1},{1,0},{2,3},{3,2},{4,5},{5,4},{6,7},{7,6},{8,9},{9,8},{10,11... | collective-permute-start | bytes 983048 | tf_op jit(solution)/shard_map/ppermute | solution.py:240
  107.3 13.5 %collective-permute-start.1 = (bf16[128,1280]{1,0:T(8,128)(2,1)}, bf16[128,1280]{1,0:T(8,128)(2,1)S(1)}, u32[]{:S(2)}, u32[]{:S(2)}) collective-permute-start(bf16[128,1280]{1,0:T(8,128)(2,1)} %get-tuple-element.41), channel_id=1, source_target_pairs={{0,1},{1,0},{2,3},{3,2},{4,5},{5,4},{6,7},{7,6},{8,9},{9,8},{10,11... | collective-permute-start | bytes 983048 | tf_op jit(solution)/shard_map/ppermute | solution.py:240
  112.9 7.2 %copy-start.3 = (bf16[10,128,640]{2,1,0:T(8,128)(2,1)S(1)}, bf16[10,128,640]{2,1,0:T(8,128)(2,1)}, u32[]{:S(2)}) copy-start(bf16[10,128,640]{2,1,0:T(8,128)(2,1)} %gather_fusion.1) | copy-start | bytes 4915204
  112.9 7.2 %copy-start.7 = (bf16[128,1280]{1,0:T(8,128)(2,1)S(1)}, bf16[128,1280]{1,0:T(8,128)(2,1)}, u32[]{:S(2)}) copy-start(bf16[128,1280]{1,0:T(8,128)(2,1)} %get-tuple-element.47) | copy-start | bytes 983044
  113.0 13.1 %collective-permute-start.14 = (bf16[128,640]{1,0:T(8,128)(2,1)S(1)}, bf16[128,640]{1,0:T(8,128)(2,1)S(1)}, u32[]{:S(2)}, u32[]{:S(2)}) collective-permute-start(bf16[128,640]{1,0:T(8,128)(2,1)S(1)} %slice.98), channel_id=1, source_target_pairs={{0,2},{2,4},{4,6},{6,0},{1,3},{3,5},{5,7},{7,1},{8,10},{10,12},{12... | collective-permute-start | bytes 491528 | tf_op jit(solution)/shard_map/ppermute | solution.py:236
  115.0 12.9 %collective-permute-start.15 = (bf16[128,640]{1,0:T(8,128)(2,1)S(1)}, bf16[128,640]{1,0:T(8,128)(2,1)S(1)}, u32[]{:S(2)}, u32[]{:S(2)}) collective-permute-start(bf16[128,640]{1,0:T(8,128)(2,1)S(1)} %slice.99), channel_id=1, source_target_pairs={{0,6},{2,0},{4,2},{6,4},{1,7},{3,1},{5,3},{7,5},{8,14},{10,8},{12,... | collective-permute-start | bytes 491528 | tf_op jit(solution)/shard_map/ppermute | solution.py:236
  117.3 9.1 %collective-permute-start.6 = (bf16[128,640]{1,0:T(8,128)(2,1)S(1)}, bf16[128,640]{1,0:T(8,128)(2,1)S(1)}, u32[]{:S(2)}, u32[]{:S(2)}) collective-permute-start(bf16[128,640]{1,0:T(8,128)(2,1)S(1)} %slice.90), channel_id=1, source_target_pairs={{0,2},{2,4},{4,6},{6,0},{1,3},{3,5},{5,7},{7,1},{8,10},{10,12},{12... | collective-permute-start | bytes 491528 | tf_op jit(solution)/shard_map/ppermute | solution.py:236
  117.5 8.0 %copy-start.6 = (bf16[128,1280]{1,0:T(8,128)(2,1)S(1)}, bf16[128,1280]{1,0:T(8,128)(2,1)}, u32[]{:S(2)}) copy-start(bf16[128,1280]{1,0:T(8,128)(2,1)} %get-tuple-element.41) | copy-start | bytes 983044
  117.6 10.5 %collective-permute-start.7 = (bf16[128,640]{1,0:T(8,128)(2,1)S(1)}, bf16[128,640]{1,0:T(8,128)(2,1)S(1)}, u32[]{:S(2)}, u32[]{:S(2)}) collective-permute-start(bf16[128,640]{1,0:T(8,128)(2,1)S(1)} %slice.91), channel_id=1, source_target_pairs={{0,6},{2,0},{4,2},{6,4},{1,7},{3,1},{5,3},{7,5},{8,14},{10,8},{12,... | collective-permute-start | bytes 491528 | tf_op jit(solution)/shard_map/ppermute | solution.py:236
  120.8 8.2 %copy-start.1 = (bf16[10,128,640]{2,1,0:T(8,128)(2,1)S(1)}, bf16[10,128,640]{2,1,0:T(8,128)(2,1)}, u32[]{:S(2)}) copy-start(bf16[10,128,640]{2,1,0:T(8,128)(2,1)} %gather_fusion.2) | copy-start | bytes 4915204
  120.8 7.8 %collective-permute-start.11 = (bf16[128,1280]{1,0:T(8,128)(2,1)S(1)}, bf16[128,1280]{1,0:T(8,128)(2,1)S(1)}, u32[]{:S(2)}, u32[]{:S(2)}) collective-permute-start(bf16[128,1280]{1,0:T(8,128)(2,1)S(1)} %collective-permute-done.10), channel_id=1, source_target_pairs={{0,1},{1,0},{2,3},{3,2},{4,5},{5,4},{6,7},{7,6},{8,9},{9,8},{10,11... | collective-permute-start | bytes 983048 | tf_op jit(solution)/shard_map/ppermute | solution.py:240
  126.2 4.2 %collective-permute-start.13 = (bf16[128,1280]{1,0:T(8,128)(2,1)S(1)}, bf16[128,1280]{1,0:T(8,128)(2,1)S(1)}, u32[]{:S(2)}, u32[]{:S(2)}) collective-permute-start(bf16[128,1280]{1,0:T(8,128)(2,1)S(1)} %collective-permute-done.12), channel_id=1, source_target_pairs={{0,1},{1,0},{2,3},{3,2},{4,5},{5,4},{6,7},{7,6},{8,9},{9,8},{10,11... | collective-permute-start | bytes 983048 | tf_op jit(solution)/shard_map/ppermute | solution.py:240
  126.3 3.4 %collective-permute-start.3 = (bf16[128,1280]{1,0:T(8,128)(2,1)S(1)}, bf16[128,1280]{1,0:T(8,128)(2,1)S(1)}, u32[]{:S(2)}, u32[]{:S(2)}) collective-permute-start(bf16[128,1280]{1,0:T(8,128)(2,1)S(1)} %collective-permute-done.2), channel_id=1, source_target_pairs={{0,1},{1,0},{2,3},{3,2},{4,5},{5,4},{6,7},{7,6},{8,9},{9,8},{10,11... | collective-permute-start | bytes 983048 | tf_op jit(solution)/shard_map/ppermute | solution.py:240
  127.9 3.9 %collective-permute-start.5 = (bf16[128,1280]{1,0:T(8,128)(2,1)S(1)}, bf16[128,1280]{1,0:T(8,128)(2,1)S(1)}, u32[]{:S(2)}, u32[]{:S(2)}) collective-permute-start(bf16[128,1280]{1,0:T(8,128)(2,1)S(1)} %collective-permute-done.4), channel_id=1, source_target_pairs={{0,1},{1,0},{2,3},{3,2},{4,5},{5,4},{6,7},{7,6},{8,9},{9,8},{10,11... | collective-permute-start | bytes 983048 | tf_op jit(solution)/shard_map/ppermute | solution.py:240
  128.1 4.7 %collective-permute-start.16 = (bf16[128,1280]{1,0:T(8,128)(2,1)S(1)}, bf16[128,1280]{1,0:T(8,128)(2,1)S(1)}, u32[]{:S(2)}, u32[]{:S(2)}) collective-permute-start(bf16[128,1280]{1,0:T(8,128)(2,1)S(1)} %constant_dynamic-update-slice_fusion.2), channel_id=1, source_target_pairs={{0,1},{1,0},{2,3},{3,2},{4,5},{5,4},{6,7},{7,6},{8,9},{9,8},{10,11... | collective-permute-start | bytes 983048 | tf_op jit(solution)/shard_map/ppermute | solution.py:240
  128.7 6.1 %collective-permute-start.8 = (bf16[128,1280]{1,0:T(8,128)(2,1)S(1)}, bf16[128,1280]{1,0:T(8,128)(2,1)S(1)}, u32[]{:S(2)}, u32[]{:S(2)}) collective-permute-start(bf16[128,1280]{1,0:T(8,128)(2,1)S(1)} %constant_dynamic-update-slice_fusion), channel_id=1, source_target_pairs={{0,1},{1,0},{2,3},{3,2},{4,5},{5,4},{6,7},{7,6},{8,9},{9,8},{10,11... | collective-permute-start | bytes 983048 | tf_op jit(solution)/shard_map/ppermute | solution.py:240
  129.7 1.4 %copy-start = (bf16[10,128,640]{2,1,0:T(8,128)(2,1)S(1)}, bf16[10,128,640]{2,1,0:T(8,128)(2,1)}, u32[]{:S(2)}) copy-start(bf16[10,128,640]{2,1,0:T(8,128)(2,1)} %gather_fusion.3) | copy-start | bytes 4915204
  (2 other events, 2.2 us)

commit v7 on v6

--- a/solution.py
+++ b/solution.py
@@ -150,7 +150,7 @@
 
     def finish(t, _):
         inverse = 1.0 / jnp.maximum(sum_s[t], 1e-30)
-        out_ref[t] = (acc_s[t] * inverse).astype(jnp.bfloat16)
+        out_ref[t // 2, t % 2] = (acc_s[t] * inverse).astype(jnp.bfloat16)
         return 0
 
     lax.fori_loop(0, 2 * CHIPS, finish, 0)
@@ -178,7 +178,7 @@
         functools.partial(second_kernel, scale),
         in_specs=[smem] * 4 + [vmem] * 5,
         out_specs=vmem,
-        out_shape=jax.ShapeDtypeStruct((tiles, TILE, TILE), jnp.bfloat16),
+        out_shape=jax.ShapeDtypeStruct((CHIPS, 2, TILE, TILE), jnp.bfloat16),
         scratch_shapes=[pltpu.VMEM(*shape) for shape in shapes],
         **options,
     )(*lists, own, other, *state)
@@ -212,10 +212,10 @@
     return steps[None], q_of, k_of.astype(jnp.int32).reshape(-1), valid
 
 
-def select_kernel(source, got_ref, *out_refs):
-    for sub, out_ref in enumerate(out_refs):
+def select_kernel(source, got_ref, out_ref):
+    for sub in range(2):
         for i in range(PLANE_HEADS):
-            out_ref[:, pl.ds(i * TILE, TILE)] = got_ref[source[2 * i + sub], sub].T
+            out_ref[pl.ds(sub * TILE, TILE), pl.ds(i * TILE, TILE)] = got_ref[source[2 * i + sub], sub].T
 
 
 def select(source, got):
@@ -223,9 +223,42 @@
     return pl.pallas_call(
         select_kernel,
         in_specs=[pl.BlockSpec(memory_space=pltpu.SMEM), vmem],
-        out_specs=[vmem] * 2,
-        out_shape=[jax.ShapeDtypeStruct((TILE, PLANE_HEADS * TILE), jnp.bfloat16)] * 2,
+        out_specs=vmem,
+        out_shape=jax.ShapeDtypeStruct((HALF, PLANE_HEADS * TILE), jnp.bfloat16),
     )(source, got)
+
+
+def gather_kernel(heads, w_ref, *rest):
+    out_refs, (held, sem_in, sem_out) = rest[:PLANES], rest[PLANES:]
+    loads, stores = [], []
+    for n in range(HEADS):
+        rows = pl.ds(pl.multiple_of(heads[n] * TILE, TILE), TILE)
+        loads.append(pltpu.make_async_copy(w_ref.at[rows], held.at[n], sem_in.at[n]))
+        loads[n].start()
+    for n in range(HEADS):
+        loads[n].wait()
+        part = out_refs[n // PLANE_HEADS].at[pl.ds(n % PLANE_HEADS * TILE, TILE)]
+        stores.append(pltpu.make_async_copy(held.at[n], part, sem_out.at[n]))
+        stores[n].start()
+    for store in stores:
+        store.wait()
+
+
+def gather(w_out, heads):
+    cols = w_out.shape[1]
+    hbm = pl.BlockSpec(memory_space=pl.ANY)
+    return pl.pallas_call(
+        gather_kernel,
+        in_specs=[pl.BlockSpec(memory_space=pltpu.SMEM), hbm],
+        out_specs=[hbm] * PLANES,
+        out_shape=[jax.ShapeDtypeStruct((PLANE_HEADS * TILE, cols), w_out.dtype)] * PLANES,
+        scratch_shapes=[
+            pltpu.VMEM((HEADS, TILE, cols), w_out.dtype),
+            pltpu.SemaphoreType.DMA((HEADS,)),
+            pltpu.SemaphoreType.DMA((HEADS,)),
+        ],
+        compiler_params=pltpu.CompilerParams(vmem_limit_bytes=56 * 2**20),
+    )(heads, w_out)
 
 
 def exchange(block):
@@ -268,11 +301,10 @@
     allowed = lax.dynamic_index_in_dim(allowed.reshape(CHIPS, 2, 2, 4 * CHIPS), core, 1, keepdims=False)
     source = lax.dynamic_slice_in_dim(owner, 2 * chip, 2, 1).reshape(-1)
 
-    w_heads = w_out.reshape(HEADS, TILE, w_out.shape[1])
-    weights = []
-    for ahead in (0, 3, 1, 2):
-        w_order = lax.dynamic_slice_in_dim(head_at, (plane + ahead) % PLANES * PLANE_HEADS, PLANE_HEADS)
-        weights.append(jnp.take(w_heads, w_order, axis=0, mode="clip").reshape(PLANE_HEADS * TILE, -1))
+    w_order = jnp.concatenate(
+        [lax.dynamic_slice_in_dim(head_at, (plane + k) % PLANES * PLANE_HEADS, PLANE_HEADS) for k in (0, 3, 1, 2)]
+    )
+    weights = gather(w_out, w_order)
     allowed = allowed.reshape(2 * CHIPS, CHIPS, 2, 2)
     lists = [
         item_lists(lax.dynamic_index_in_dim(allowed, c, 2, keepdims=False).reshape(2 * CHIPS, 2 * CHIPS), mine_tiles)
@@ -286,23 +318,19 @@
         return jnp.dot(both, weight, preferred_element_type=jnp.float32)
 
     def by_rows(total):
-        mine, theirs = total[:TILE], total[TILE:]
-        return jnp.where(core == 0, mine, theirs), jnp.where(core == 0, theirs, mine)
+        mine, theirs = total[:HALF], total[HALF:]
+        return jnp.concatenate([jnp.where(core == 0, mine, theirs), jnp.where(core == 0, theirs, mine)], axis=0)
 
     attended = attend(lists[1], got, got_other, attend(lists[0], got))
-    own_rows = select(source, exchange(attended.reshape(CHIPS, 2, TILE, TILE)))
-
-    residual = residual_in.astype(jnp.float32).reshape(2, 2, TILE, -1)
+    own = select(source, exchange(attended))
+    below, above = along_y(own, 1), along_y(own, 3)
     width = PLANE_HEADS * TILE // 2
-    halves = []
-    for sub, own in enumerate(own_rows):
-        below, above = along_y(own, 1), along_y(own, 3)
-        far_low, far_high = along_y(below[:, :width], 1), along_y(above[:, width:], 3)
-        total = project(own, weights[0]) + project(below, weights[1]) + project(above, weights[2])
-        near = lax.optimization_barrier([residual[c, sub] + gate_scale * rows for c, rows in enumerate(by_rows(total))])
-        far = project(jnp.concatenate([far_low, far_high], axis=1), weights[3])
-        halves.append([(near[c] + gate_scale * rows).astype(jnp.bfloat16) for c, rows in enumerate(by_rows(far))])
-    return jnp.concatenate([halves[0][0], halves[1][0], halves[0][1], halves[1][1]], axis=0)
+    far_low, far_high = along_y(below[:, :width], 1), along_y(above[:, width:], 3)
+    total = project(own, weights[0]) + project(below, weights[1]) + project(above, weights[2])
+    base = residual_in.astype(jnp.float32) + gate_scale * by_rows(total)
+    base, far_low, far_high = lax.optimization_barrier((base, far_low, far_high))
+    far = project(far_low, weights[3][:width]) + project(far_high, weights[3][width:])
+    return (base + gate_scale * by_rows(far)).astype(jnp.bfloat16)
 
 
 def solution(mesh):

time: 135 us -> 135 us (level); the launches traced: 136 us -> 135 us
  waiting for transfers between devices: 0.05 us -> 25 us
  local copies, waits for them, and re-layouts: 29.7 us -> 9.03 us
  starting transfers between devices: 38.5 us -> 24.4 us
  Pallas kernels: 17.8 us -> 27.9 us
  blocking collectives: 24.6 us -> 20 us
  matrix products: 5.94 us -> 8.22 us
    gather x4 -> x0, local copies, waits for them, and re-layouts: 19.6 us -> none  [shards(): jnp.take(w_heads, w_order, axis=0, mode='clip')]
    ppermute x8 -> x4, waiting for transfers between devices: 0.02 us -> 13 us  [along_y(): lax.ppermute(block, 'y', [(i, (i + step) % PLANES) for i in range(PLANES)])]
    all_to_all x1, waiting for transfers between devices: 0.01 us -> 10.8 us  [exchange(): lax.all_to_all(block, TOKENS_AXES, split_axis=0, concat_axis=0, tiled=True)]
    ppermute x9 -> x6, starting transfers between devices: 17.3 us -> 9.69 us  [swap(): return lax.ppermute(block, 'c', [(0, 1), (1, 0)])]
    pallas_call x0 -> x1, Pallas kernels: none -> 6.58 us  [gather(): pl.pallas_call(gather_kernel, in_specs=[pl.BlockSpec(memory_space=pltpu.S...]
    ppermute x8 -> x4, starting transfers between devices: 12.7 us -> 6.31 us  [along_y(): lax.ppermute(block, 'y', [(i, (i + step) % PLANES) for i in range(PLANES)])]
    all_to_all x1, blocking collectives: 24.6 us -> 20 us  [exchange(): lax.all_to_all(block, TOKENS_AXES, split_axis=0, concat_axis=0, tiled=True)]
    dot_general x8 -> x5, matrix products: 5.56 us -> 7.84 us  [project(): return jnp.dot(both, weight, preferred_element_type=jnp.float32)]
  transfers between devices with their start and end apart: 18 -> 11, of which waited for: 0 -> 4; matrix products, arithmetic and copies ran while one was open for 30% -> 18% of each run, Pallas kernels for 4% -> 11%
where the time goes in v7:
time: 135 us
  Pallas kernels  27.9 us (21%)
  waiting for transfers between devices  25 us (19%)
  starting transfers between devices  24.4 us (18%)
  blocking collectives  20 us (15%)
  other arithmetic  13.7 us (10%)
  local copies, waits for them, and re-layouts  9.03 us (7%)
  matrix products  8.22 us (6%)
  between operations  6.51 us (5%)
    all_to_all x1, blocking collectives, exchange(): lax.all_to_all(block, TOKENS_AXES, split_axis=0, concat_axis=0, tiled=True)  20 us
    ppermute x4, waiting for transfers between devices, along_y(): lax.ppermute(block, 'y', [(i, (i + step) % PLANES) for i in range(PLANES)])  13 us
    all_to_all x1, waiting for transfers between devices, exchange(): lax.all_to_all(block, TOKENS_AXES, split_axis=0, concat_axis=0, tiled=True)  10.8 us
    ppermute x6, starting transfers between devices, swap(): return lax.ppermute(block, 'c', [(0, 1), (1, 0)])  9.69 us
    all_to_all x1, starting transfers between devices, exchange(): lax.all_to_all(block, TOKENS_AXES, split_axis=0, concat_axis=0, tiled=True)  8.44 us
    pallas_call x1, Pallas kernels, attend(): pl.pallas_call(functools.partial(first_kernel, scale), in_specs=[smem] *...  7.89 us
    dot_general x5, matrix products, project(): return jnp.dot(both, weight, preferred_element_type=jnp.float32)  7.84 us
    pallas_call x1, Pallas kernels, attend(): pl.pallas_call(functools.partial(second_kernel, scale), in_specs=[smem] *...  6.61 us
  transfers between devices with their start and end apart: 11, of which 4 were waited for; matrix products, arithmetic and copies ran while one was open for 18% of the time, Pallas kernels for 11%

profile of v7, /device:TPU:1, one launch (start us, length us, event | category | flops | bytes accessed | tf_op | source)
XLA Modules:
  0.0 134.8 jit_solution(17586770034655216719)
XLA Ops:
  0.0 2.1 %fusion.55 = (s32[40,64]{1,0:T(8,128)S(1)}, s32[40]{0:T(128)S(1)}) fusion(s32[40,64,64]{2,1,0:T(8,128)} %param.13), kind=kLoop, calls=%fused_computation.157 | loop fusion | flops 325080 | bytes 665760 | tf_op jit(solution)/shard_map/reduce_sum | solution.py:280
  4.1 4.6 %shard_map.73 = bf16[16,768,128]{2,1,0:T(8,128)(2,1)} custom-call(s32[17]{0:T(128)} %pad_add_fusion.heads, bf16[512,5120]{1,0:T(8,128)(2,1)} %q_ref.1, bf16[512,5120]{1,0:T(8,128)(2,1)} %k_ref.1, bf16[512,5120]{1,0:T(8,128)(2,1)} %v_ref.1), custom_call_target="tpu_custom_call" | custom-call | tf_op jit(solution)/shard_map/pallas_call | solution.py:87
  8.6 8.4 %all-to-all-start = ((bf16[16,768,128]{2,1,0:T(8,128)(2,1)}), bf16[16,768,128]{2,1,0:T(8,128)(2,1)S(1)}, u32[]{:S(2)}, u32[]{:S(2)}) async-start(bf16[16,768,128]{2,1,0:T(8,128)(2,1)} %shard_map.73), calls=%async_computation | async-start | bytes 6291456 | tf_op jit(solution)/shard_map/all_to_all | solution.py:265
  23.3 1.6 %reshape.338 = s32[32,16,2,2]{3,2,1,0:T(2,128)} reshape(s32[16,1,2,64]{3,2,1,0:T(2,128)S(1)} %constant_dynamic-slice_fusion.3) | data formatting | bytes 16384 | tf_op jit(solution)/shard_map/reshape | solution.py:308
  25.4 3.1 %fusion.56 = (s32[32]{0:T(128)S(1)}, s32[32,16,1,2]{3,2,1,0:T(1,128)}, s32[32]{0:T(128)S(1)}, s32[32,16,1,2]{3,2,1,0:T(1,128)S(1)}) fusion(s32[32,16,2,2]{3,2,1,0:T(2,128)} %reshape.338, s32[]{:T(128)S(6)} %select_n.211, s32[]{:T(128)S(6)} %select_n.198), kind=kLoop, calls=%fused_computation.158 | loop fusion | flops 1984 | bytes 16648 | tf_op jit(solution)/shard_map/reduce_sum | solution.py:189
  35.3 1.2 multiply_reduce_fusion
  37.2 1.2 compare_select_fusion.2
  40.0 6.6 %shard_map.74 = (bf16[1280,640]{1,0:T(8,128)(2,1)}, bf16[1280,640]{1,0:T(8,128)(2,1)}, bf16[1280,640]{1,0:T(8,128)(2,1)}, bf16[1280,640]{1,0:T(8,128)(2,1)}) custom-call(s32[40]{0:T(128)} %pad_add_fusion.1.heads, bf16[5120,640]{1,0:T(8,128)(2,1)} %w_ref.1), custom_call_target="tpu_custom_call" | custom-call | tf_op jit(solution)/shard_map/pallas_call | solution.py:250
  46.6 10.8 %all-to-all-done = bf16[16,768,128]{2,1,0:T(8,128)(2,1)S(1)} async-done(((bf16[16,768,128]{2,1,0:T(8,128)(2,1)}), bf16[16,768,128]{2,1,0:T(8,128)(2,1)S(1)}, u32[]{:S(2)}, u32[]{:S(2)}) %all-to-all-start) | async-done | bytes 3145760 | tf_op jit(solution)/shard_map/all_to_all | solution.py:265
  57.4 3.0 %collective-permute-start = (bf16[16,6,128,128]{3,2,1,0:T(8,128)(2,1)S(1)}, bf16[16,6,128,128]{3,2,1,0:T(8,128)(2,1)S(1)}, u32[]{:S(2)}, u32[]{:S(2)}) collective-permute-start(bf16[16,6,128,128]{3,2,1,0:T(8,128)(2,1)S(1)} %bitcast.43), channel_id=1, source_target_pairs={{0,1},{1,0},{2,3},{3,2},{4,5},{5,4},{6,7},{7,6},{8,9},{9,8},{10,11... | collective-permute-start | bytes 9437192 | tf_op jit(solution)/shard_map/ppermute | solution.py:273
  60.4 7.9 %shard_map.75 = (f32[32,128,128]{2,1,0:T(8,128)S(1)}, f32[32,1,128]{2,1,0:T(1,128)S(1)}, f32[32,1,128]{2,1,0:T(1,128)S(1)}) custom-call(s32[1]{0:T(128)} %bitcast.10.meta, s32[256]{0:T(256)S(1)} %broadcast_minimum_fusion.1.q_of, s32[1024]{0:T(1024)S(1)} %convert_element_type.96.k_of, s32[256]{0:T(256)S(1)} %get-tuple-element.42.valid_of, ...), custom_call_target="tpu_custom_call" | custom-call | flops 4000000000 | bytes 8388608 | tf_op jit(solution)/shard_map/pallas_call | solution.py:170
  68.3 6.6 %shard_map.76 = bf16[16,2,128,128]{3,2,1,0:T(8,128)(2,1)S(1)} custom-call(s32[1]{0:T(128)} %bitcast.18.meta, s32[256]{0:T(256)S(1)} %broadcast_minimum_fusion.q_of, s32[1024]{0:T(1024)S(1)} %convert_element_type.102.k_of, s32[256]{0:T(256)S(1)} %get-tuple-element.37.valid_of, bf16[16,6,128,128]{3,2,1,0:T(8,128)(2,1)S(1)} %bitcast.45, ...), custom_call_target="tpu_custom_call" | custom-call | flops 4000000000 | bytes 8388608 | tf_op jit(solution)/shard_map/pallas_call | solution.py:177
  75.0 20.0 %all_to_all.10.got_ref = bf16[16,2,128,128]{3,2,1,0:T(8,128)(2,1)} all-to-all(bf16[16,2,128,128]{3,2,1,0:T(8,128)(2,1)S(1)} %shard_map.76), channel_id=1, replica_groups=mesh['x'=4,'z'=4,'y'=4,'c'=2] {'x','z'}, dimensions={0} | all-to-all | bytes 2097152 | tf_op jit(solution)/shard_map/all_to_all | solution.py:265
  94.9 2.3 %shard_map.77 = bf16[256,1280]{1,0:T(8,128)(2,1)} custom-call(s32[20]{0:T(128)} %reshape.327.source, bf16[16,2,128,128]{3,2,1,0:T(8,128)(2,1)} %all_to_all.10.got_ref), custom_call_target="tpu_custom_call" | custom-call | tf_op jit(solution)/shard_map/pallas_call | solution.py:223
  97.9 2.9 %collective-permute-start.4 = (bf16[256,1280]{1,0:T(8,128)(2,1)}, bf16[256,1280]{1,0:T(8,128)(2,1)S(1)}, u32[]{:S(2)}, u32[]{:S(2)}) collective-permute-start(bf16[256,1280]{1,0:T(8,128)(2,1)} %shard_map.77), channel_id=1, source_target_pairs={{0,6},{2,0},{4,2},{6,4},{1,7},{3,1},{5,3},{7,5},{8,14},{10,8},{12,... | collective-permute-start | bytes 1966088 | tf_op jit(solution)/shard_map/ppermute | solution.py:269
  100.8 2.6 %collective-permute-start.1 = (bf16[256,1280]{1,0:T(8,128)(2,1)}, bf16[256,1280]{1,0:T(8,128)(2,1)S(1)}, u32[]{:S(2)}, u32[]{:S(2)}) collective-permute-start(bf16[256,1280]{1,0:T(8,128)(2,1)} %shard_map.77), channel_id=1, source_target_pairs={{0,1},{1,0},{2,3},{3,2},{4,5},{5,4},{6,7},{7,6},{8,9},{9,8},{10,11... | collective-permute-start | bytes 1966088 | tf_op jit(solution)/shard_map/ppermute | solution.py:273
  103.4 10.4 %collective-permute-done.2 = bf16[256,1280]{1,0:T(8,128)(2,1)S(1)} collective-permute-done((bf16[256,1280]{1,0:T(8,128)(2,1)}, bf16[256,1280]{1,0:T(8,128)(2,1)S(1)}, u32[]{:S(2)}, u32[]{:S(2)}) %collective-permute-start.2) | collective-permute-done | bytes 655392 | tf_op jit(solution)/shard_map/ppermute | solution.py:269
  113.8 3.0 %collective-permute-start.3 = (bf16[256,1280]{1,0:T(8,128)(2,1)S(1)}, bf16[256,1280]{1,0:T(8,128)(2,1)}, u32[]{:S(2)}, u32[]{:S(2)}) collective-permute-start(bf16[256,1280]{1,0:T(8,128)(2,1)S(1)} %collective-permute-done.2), channel_id=1, source_target_pairs={{0,1},{1,0},{2,3},{3,2},{4,5},{5,4},{6,7},{7,6},{8,9},{9,8},{10,11... | collective-permute-start | bytes 1966088 | tf_op jit(solution)/shard_map/ppermute | solution.py:273
  116.8 2.7 %collective-permute-start.7 = (bf16[256,640]{1,0:T(8,128)(2,1)S(1)}, bf16[256,640]{1,0:T(8,128)(2,1)S(1)}, u32[]{:S(2)}, u32[]{:S(2)}) collective-permute-start(bf16[256,640]{1,0:T(8,128)(2,1)S(1)} %slice.49), channel_id=1, source_target_pairs={{0,6},{2,0},{4,2},{6,4},{1,7},{3,1},{5,3},{7,5},{8,14},{10,8},{12,... | collective-permute-start | bytes 983048 | tf_op jit(solution)/shard_map/ppermute | solution.py:269
  119.6 2.7 %fusion = f32[512,640]{1,0:T(8,128)S(1)} fusion(bf16[1280,640]{1,0:T(8,128)(2,1)} %get-tuple-element.46, bf16[256,1280]{1,0:T(8,128)(2,1)S(1)} %collective-permute-done.1, bf16[256,1280]{1,0:T(8,128)(2,1)S(1)} %copy-done), kind=kOutput, calls=%fused_computation.4 | convolution fusion | flops 841482240 | bytes 4259840 | tf_op jit(solution)/shard_map/dot_general | solution.py:318
  122.4 2.4 %convolution_add_fusion.2 = f32[512,640]{1,0:T(8,128)S(1)} fusion(f32[512,640]{1,0:T(8,128)S(1)} %fusion, bf16[1280,640]{1,0:T(8,128)(2,1)S(1)} %copy-done.5, bf16[256,1280]{1,0:T(8,128)(2,1)} %collective-permute-done.3, bf16[256,1280]{1,0:T(8,128)(2,1)S(1)} %collective-permute-done.2), kind=kOutput, calls=%fused_computation.3 | convolution fusion | flops 841809920 | bytes 5570560 | tf_op jit(solution)/shard_map/dot_general | solution.py:318
  124.8 1.2 convolution_add_fusion.1
  127.2 2.6 %collective-permute-done.6 = bf16[256,640]{1,0:T(8,128)(2,1)S(1)} collective-permute-done((bf16[256,640]{1,0:T(8,128)(2,1)S(1)}, bf16[256,640]{1,0:T(8,128)(2,1)S(1)}, u32[]{:S(2)}, u32[]{:S(2)}) %collective-permute-start.6) | collective-permute-done | bytes 327712 | tf_op jit(solution)/shard_map/ppermute | solution.py:269
  130.9 1.3 collective-permute-done.9
  (104 shorter events, 17.3 us)
Async XLA Ops:
  8.6 48.8 %all-to-all-start = ((bf16[16,768,128]{2,1,0:T(8,128)(2,1)}), bf16[16,768,128]{2,1,0:T(8,128)(2,1)S(1)}, u32[]{:S(2)}, u32[]{:S(2)}) async-start(bf16[16,768,128]{2,1,0:T(8,128)(2,1)} %shard_map.73), calls=%async_computation | async-start | bytes 6291456 | tf_op jit(solution)/shard_map/all_to_all | solution.py:265
  57.4 10.9 %collective-permute-start = (bf16[16,6,128,128]{3,2,1,0:T(8,128)(2,1)S(1)}, bf16[16,6,128,128]{3,2,1,0:T(8,128)(2,1)S(1)}, u32[]{:S(2)}, u32[]{:S(2)}) collective-permute-start(bf16[16,6,128,128]{3,2,1,0:T(8,128)(2,1)S(1)} %bitcast.43), channel_id=1, source_target_pairs={{0,1},{1,0},{2,3},{3,2},{4,5},{5,4},{6,7},{7,6},{8,9},{9,8},{10,11... | collective-permute-start | bytes 9437192 | tf_op jit(solution)/shard_map/ppermute | solution.py:273
  97.2 22.4 %copy-start = (bf16[256,1280]{1,0:T(8,128)(2,1)S(1)}, bf16[256,1280]{1,0:T(8,128)(2,1)}, u32[]{:S(2)}) copy-start(bf16[256,1280]{1,0:T(8,128)(2,1)} %shard_map.77) | copy-start | bytes 1966084
  97.2 16.6 %collective-permute-start.2 = (bf16[256,1280]{1,0:T(8,128)(2,1)}, bf16[256,1280]{1,0:T(8,128)(2,1)S(1)}, u32[]{:S(2)}, u32[]{:S(2)}) collective-permute-start(bf16[256,1280]{1,0:T(8,128)(2,1)} %shard_map.77), channel_id=1, source_target_pairs={{0,2},{2,4},{4,6},{6,0},{1,3},{3,5},{5,7},{7,1},{8,10},{10,12},{12... | collective-permute-start | bytes 1966088 | tf_op jit(solution)/shard_map/ppermute | solution.py:269
  97.9 18.9 %collective-permute-start.4 = (bf16[256,1280]{1,0:T(8,128)(2,1)}, bf16[256,1280]{1,0:T(8,128)(2,1)S(1)}, u32[]{:S(2)}, u32[]{:S(2)}) collective-permute-start(bf16[256,1280]{1,0:T(8,128)(2,1)} %shard_map.77), channel_id=1, source_target_pairs={{0,6},{2,0},{4,2},{6,4},{1,7},{3,1},{5,3},{7,5},{8,14},{10,8},{12,... | collective-permute-start | bytes 1966088 | tf_op jit(solution)/shard_map/ppermute | solution.py:269
  100.8 18.8 %collective-permute-start.1 = (bf16[256,1280]{1,0:T(8,128)(2,1)}, bf16[256,1280]{1,0:T(8,128)(2,1)S(1)}, u32[]{:S(2)}, u32[]{:S(2)}) collective-permute-start(bf16[256,1280]{1,0:T(8,128)(2,1)} %shard_map.77), channel_id=1, source_target_pairs={{0,1},{1,0},{2,3},{3,2},{4,5},{5,4},{6,7},{7,6},{8,9},{9,8},{10,11... | collective-permute-start | bytes 1966088 | tf_op jit(solution)/shard_map/ppermute | solution.py:273
  113.8 8.5 %collective-permute-start.3 = (bf16[256,1280]{1,0:T(8,128)(2,1)S(1)}, bf16[256,1280]{1,0:T(8,128)(2,1)}, u32[]{:S(2)}, u32[]{:S(2)}) collective-permute-start(bf16[256,1280]{1,0:T(8,128)(2,1)S(1)} %collective-permute-done.2), channel_id=1, source_target_pairs={{0,1},{1,0},{2,3},{3,2},{4,5},{5,4},{6,7},{7,6},{8,9},{9,8},{10,11... | collective-permute-start | bytes 1966088 | tf_op jit(solution)/shard_map/ppermute | solution.py:273
  116.8 8.0 %collective-permute-start.5 = (bf16[256,1280]{1,0:T(8,128)(2,1)S(1)}, bf16[256,1280]{1,0:T(8,128)(2,1)S(1)}, u32[]{:S(2)}, u32[]{:S(2)}) collective-permute-start(bf16[256,1280]{1,0:T(8,128)(2,1)S(1)} %collective-permute-done.4), channel_id=1, source_target_pairs={{0,1},{1,0},{2,3},{3,2},{4,5},{5,4},{6,7},{7,6},{8,9},{9,8},{10,11... | collective-permute-start | bytes 1966088 | tf_op jit(solution)/shard_map/ppermute | solution.py:273
  116.8 10.4 %collective-permute-start.7 = (bf16[256,640]{1,0:T(8,128)(2,1)S(1)}, bf16[256,640]{1,0:T(8,128)(2,1)S(1)}, u32[]{:S(2)}, u32[]{:S(2)}) collective-permute-start(bf16[256,640]{1,0:T(8,128)(2,1)S(1)} %slice.49), channel_id=1, source_target_pairs={{0,6},{2,0},{4,2},{6,4},{1,7},{3,1},{5,3},{7,5},{8,14},{10,8},{12,... | collective-permute-start | bytes 983048 | tf_op jit(solution)/shard_map/ppermute | solution.py:269
  119.5 2.9 %copy-start.5 = (bf16[1280,640]{1,0:T(8,128)(2,1)S(1)}, bf16[1280,640]{1,0:T(8,128)(2,1)}, u32[]{:S(2)}) copy-start(bf16[1280,640]{1,0:T(8,128)(2,1)} %get-tuple-element.47) | copy-start | bytes 4915204
  119.5 10.3 %collective-permute-start.6 = (bf16[256,640]{1,0:T(8,128)(2,1)S(1)}, bf16[256,640]{1,0:T(8,128)(2,1)S(1)}, u32[]{:S(2)}, u32[]{:S(2)}) collective-permute-start(bf16[256,640]{1,0:T(8,128)(2,1)S(1)} %slice.48), channel_id=1, source_target_pairs={{0,2},{2,4},{4,6},{6,0},{1,3},{3,5},{5,7},{7,1},{8,10},{10,12},{12... | collective-permute-start | bytes 983048 | tf_op jit(solution)/shard_map/ppermute | solution.py:269
  122.3 2.5 %copy-start.4 = (bf16[1280,640]{1,0:T(8,128)(2,1)S(1)}, bf16[1280,640]{1,0:T(8,128)(2,1)}, u32[]{:S(2)}) copy-start(bf16[1280,640]{1,0:T(8,128)(2,1)} %get-tuple-element.48) | copy-start | bytes 4915204
  126.0 1.1 copy-start.1
  126.0 1.1 copy-start.3
  127.1 5.1 %copy-start.2 = (bf16[1280,640]{1,0:T(8,128)(2,1)S(1)}, bf16[1280,640]{1,0:T(8,128)(2,1)}, u32[]{:S(2)}) copy-start(bf16[1280,640]{1,0:T(8,128)(2,1)} %get-tuple-element.51) | copy-start | bytes 4915204
  129.8 2.4 %collective-permute-start.9 = (bf16[256,640]{1,0:T(8,128)(2,1)S(1)}, bf16[256,640]{1,0:T(8,128)(2,1)S(1)}, u32[]{:S(2)}, u32[]{:S(2)}) collective-permute-start(bf16[256,640]{1,0:T(8,128)(2,1)S(1)} %collective-permute-done.7), channel_id=1, source_target_pairs={{0,1},{1,0},{2,3},{3,2},{4,5},{5,4},{6,7},{7,6},{8,9},{9,8},{10,11... | collective-permute-start | bytes 983048 | tf_op jit(solution)/shard_map/ppermute | solution.py:273
  130.9 2.0 %collective-permute-start.8 = (bf16[256,640]{1,0:T(8,128)(2,1)S(1)}, bf16[256,640]{1,0:T(8,128)(2,1)S(1)}, u32[]{:S(2)}, u32[]{:S(2)}) collective-permute-start(bf16[256,640]{1,0:T(8,128)(2,1)S(1)} %collective-permute-done.6), channel_id=1, source_target_pairs={{0,1},{1,0},{2,3},{3,2},{4,5},{5,4},{6,7},{7,6},{8,9},{9,8},{10,11... | collective-permute-start | bytes 983048 | tf_op jit(solution)/shard_map/ppermute | solution.py:273

commit v8 on v7

--- a/solution.py
+++ b/solution.py
@@ -12,6 +12,7 @@
 HEADS = 40
 PLANES = 4
 PLANE_HEADS = HEADS // PLANES
+PART_HEADS = PLANE_HEADS // 2
 CHIPS = 16
 HALF = 256
 GROUP = 4
@@ -212,10 +213,14 @@
     return steps[None], q_of, k_of.astype(jnp.int32).reshape(-1), valid
 
 
-def select_kernel(source, got_ref, out_ref):
-    for sub in range(2):
-        for i in range(PLANE_HEADS):
-            out_ref[pl.ds(sub * TILE, TILE), pl.ds(i * TILE, TILE)] = got_ref[source[2 * i + sub], sub].T
+def select_kernel(source, got_ref, out_ref, low_ref, high_ref):
+    for i in range(PLANE_HEADS):
+        part_ref, at = (low_ref, i) if i < PART_HEADS else (high_ref, i - PART_HEADS)
+        for sub in range(2):
+            rows = pl.ds(sub * TILE, TILE)
+            tile = got_ref[source[2 * i + sub], sub].T
+            out_ref[rows, pl.ds(i * TILE, TILE)] = tile
+            part_ref[rows, pl.ds(at * TILE, TILE)] = tile
 
 
 def select(source, got):
@@ -223,35 +228,39 @@
     return pl.pallas_call(
         select_kernel,
         in_specs=[pl.BlockSpec(memory_space=pltpu.SMEM), vmem],
-        out_specs=vmem,
-        out_shape=jax.ShapeDtypeStruct((HALF, PLANE_HEADS * TILE), jnp.bfloat16),
+        out_specs=[vmem] * 3,
+        out_shape=[
+            jax.ShapeDtypeStruct((HALF, heads * TILE), jnp.bfloat16) for heads in (PLANE_HEADS, PART_HEADS, PART_HEADS)
+        ],
     )(source, got)
 
 
-def gather_kernel(heads, w_ref, *rest):
-    out_refs, (held, sem_in, sem_out) = rest[:PLANES], rest[PLANES:]
+def gather_kernel(counts, heads, w_ref, *rest):
+    out_refs, (held, sem_in, sem_out) = rest[: len(counts)], rest[len(counts) :]
     loads, stores = [], []
     for n in range(HEADS):
         rows = pl.ds(pl.multiple_of(heads[n] * TILE, TILE), TILE)
         loads.append(pltpu.make_async_copy(w_ref.at[rows], held.at[n], sem_in.at[n]))
         loads[n].start()
-    for n in range(HEADS):
-        loads[n].wait()
-        part = out_refs[n // PLANE_HEADS].at[pl.ds(n % PLANE_HEADS * TILE, TILE)]
-        stores.append(pltpu.make_async_copy(held.at[n], part, sem_out.at[n]))
-        stores[n].start()
+    n = 0
+    for out_ref, count in zip(out_refs, counts):
+        for at in range(count):
+            loads[n].wait()
+            stores.append(pltpu.make_async_copy(held.at[n], out_ref.at[pl.ds(at * TILE, TILE)], sem_out.at[n]))
+            stores[n].start()
+            n += 1
     for store in stores:
         store.wait()
 
 
-def gather(w_out, heads):
+def gather(w_out, heads, counts):
     cols = w_out.shape[1]
     hbm = pl.BlockSpec(memory_space=pl.ANY)
     return pl.pallas_call(
-        gather_kernel,
+        functools.partial(gather_kernel, counts),
         in_specs=[pl.BlockSpec(memory_space=pltpu.SMEM), hbm],
-        out_specs=[hbm] * PLANES,
-        out_shape=[jax.ShapeDtypeStruct((PLANE_HEADS * TILE, cols), w_out.dtype)] * PLANES,
+        out_specs=[hbm] * len(counts),
+        out_shape=[jax.ShapeDtypeStruct((count * TILE, cols), w_out.dtype) for count in counts],
         scratch_shapes=[
             pltpu.VMEM((HEADS, TILE, cols), w_out.dtype),
             pltpu.SemaphoreType.DMA((HEADS,)),
@@ -304,7 +313,7 @@
     w_order = jnp.concatenate(
         [lax.dynamic_slice_in_dim(head_at, (plane + k) % PLANES * PLANE_HEADS, PLANE_HEADS) for k in (0, 3, 1, 2)]
     )
-    weights = gather(w_out, w_order)
+    weights = gather(w_out, w_order, (PLANE_HEADS,) + (PART_HEADS,) * 6)
     allowed = allowed.reshape(2 * CHIPS, CHIPS, 2, 2)
     lists = [
         item_lists(lax.dynamic_index_in_dim(allowed, c, 2, keepdims=False).reshape(2 * CHIPS, 2 * CHIPS), mine_tiles)
@@ -313,23 +322,28 @@
     got, lists, source, weights = lax.optimization_barrier((got, lists, source, weights))
     got_other = swap(got)
 
+    def product(block, other, weight):
+        return jnp.dot(jnp.concatenate([block, other], axis=0), weight, preferred_element_type=jnp.float32)
+
     def project(block, weight):
-        both = jnp.concatenate([block, swap(block)], axis=0)
-        return jnp.dot(both, weight, preferred_element_type=jnp.float32)
+        return product(block, swap(block), weight)
 
     def by_rows(total):
         mine, theirs = total[:HALF], total[HALF:]
         return jnp.concatenate([jnp.where(core == 0, mine, theirs), jnp.where(core == 0, theirs, mine)], axis=0)
 
     attended = attend(lists[1], got, got_other, attend(lists[0], got))
-    own = select(source, exchange(attended))
-    below, above = along_y(own, 1), along_y(own, 3)
-    width = PLANE_HEADS * TILE // 2
-    far_low, far_high = along_y(below[:, :width], 1), along_y(above[:, width:], 3)
-    total = project(own, weights[0]) + project(below, weights[1]) + project(above, weights[2])
+    own, low, high = select(source, exchange(attended))
+    below_low, above_high = along_y(low, 1), along_y(high, 3)
+    own_other, low, high = lax.optimization_barrier((swap(own), low, high))
+    below_high, above_low = along_y(high, 1), along_y(low, 3)
+    far_low, far_high = along_y(below_low, 1), along_y(above_high, 3)
+    total = product(own, own_other, weights[0])
+    for block, weight in zip((below_low, above_high, below_high, above_low), (weights[1], weights[4], weights[2], weights[3])):
+        total = total + project(block, weight)
     base = residual_in.astype(jnp.float32) + gate_scale * by_rows(total)
     base, far_low, far_high = lax.optimization_barrier((base, far_low, far_high))
-    far = project(far_low, weights[3][:width]) + project(far_high, weights[3][width:])
+    far = project(far_low, weights[5]) + project(far_high, weights[6])
     return (base + gate_scale * by_rows(far)).astype(jnp.bfloat16)
 
 

time: 135 us -> 135 us (level)
  starting transfers between devices: 24.4 us -> 27.3 us
  waiting for transfers between devices: 25 us -> 22.2 us
  Pallas kernels: 27.9 us -> 26.2 us
    ppermute x4 -> x6, starting transfers between devices: 6.31 us -> 9.57 us  [along_y(): lax.ppermute(block, 'y', [(i, (i + step) % PLANES) for i in range(PLANES)])]
    ppermute x4 -> x6, waiting for transfers between devices: 13 us -> 10.1 us  [along_y(): lax.ppermute(block, 'y', [(i, (i + step) % PLANES) for i in range(PLANES)])]
    pallas_call x1, Pallas kernels: 7.89 us -> 6.11 us  [attend(): pl.pallas_call(functools.partial(first_kernel, scale), in_specs=[smem] *...]
    dot_general x5 -> x7, matrix products: 7.84 us -> 7.03 us  [product(): jnp.dot(jnp.concatenate([block, other], axis=0), weight, preferred_elemen...]
    unnamed x14 -> x20, local copies, waits for them, and re-layouts: 2.32 us -> 2.74 us
    ppermute x6 -> x8, starting transfers between devices: 9.69 us -> 9.28 us  [swap(): return lax.ppermute(block, 'c', [(0, 1), (1, 0)])]
  transfers between devices with their start and end apart: 11 -> 15, of which waited for: 4 -> 5; matrix products, arithmetic and copies ran while one was open for 18% -> 17% of each run, Pallas kernels for 11% -> 10%
where the time goes in v8:
time: 135 us; the launch traced here: 133 us
  starting transfers between devices  27.3 us (20%)
  Pallas kernels  26.2 us (19%)
  waiting for transfers between devices  22.2 us (16%)
  blocking collectives  20.7 us (15%)
  other arithmetic  13.7 us (10%)
  local copies, waits for them, and re-layouts  9.4 us (7%)
  matrix products  7.41 us (5%)
  between operations  6.56 us (5%)
    all_to_all x1, blocking collectives, exchange(): lax.all_to_all(block, TOKENS_AXES, split_axis=0, concat_axis=0, tiled=True)  20.7 us
    all_to_all x1, waiting for transfers between devices, exchange(): lax.all_to_all(block, TOKENS_AXES, split_axis=0, concat_axis=0, tiled=True)  10.8 us
    ppermute x6, waiting for transfers between devices, along_y(): lax.ppermute(block, 'y', [(i, (i + step) % PLANES) for i in range(PLANES)])  10.1 us
    ppermute x6, starting transfers between devices, along_y(): lax.ppermute(block, 'y', [(i, (i + step) % PLANES) for i in range(PLANES)])  9.57 us
    ppermute x8, starting transfers between devices, swap(): return lax.ppermute(block, 'c', [(0, 1), (1, 0)])  9.28 us
    all_to_all x1, starting transfers between devices, exchange(): lax.all_to_all(block, TOKENS_AXES, split_axis=0, concat_axis=0, tiled=True)  8.44 us
    dot_general x7, matrix products, product(): jnp.dot(jnp.concatenate([block, other], axis=0), weight, preferred_elemen...  7.03 us
    pallas_call x1, Pallas kernels, attend(): pl.pallas_call(functools.partial(second_kernel, scale), in_specs=[smem] *...  6.61 us
  transfers between devices with their start and end apart: 15, of which 5 were waited for; matrix products, arithmetic and copies ran while one was open for 17% of the time, Pallas kernels for 10%

profile of v8, /device:TPU:1, one launch (start us, length us, event | category | flops | bytes accessed | tf_op | source)
XLA Modules:
  0.0 133.5 jit_solution(4523237028198282868)
XLA Ops:
  0.0 2.1 %fusion.65 = (s32[40,64]{1,0:T(8,128)S(1)}, s32[40]{0:T(128)S(1)}) fusion(s32[40,64,64]{2,1,0:T(8,128)} %param.13), kind=kLoop, calls=%fused_computation.167 | loop fusion | flops 325080 | bytes 665760 | tf_op jit(solution)/shard_map/reduce_sum | solution.py:289
  4.1 4.5 %shard_map.73 = bf16[16,768,128]{2,1,0:T(8,128)(2,1)} custom-call(s32[17]{0:T(128)} %pad_add_fusion.heads, bf16[512,5120]{1,0:T(8,128)(2,1)} %q_ref.1, bf16[512,5120]{1,0:T(8,128)(2,1)} %k_ref.1, bf16[512,5120]{1,0:T(8,128)(2,1)} %v_ref.1), custom_call_target="tpu_custom_call" | custom-call | tf_op jit(solution)/shard_map/pallas_call | solution.py:88
  8.5 8.4 %all-to-all-start = ((bf16[16,768,128]{2,1,0:T(8,128)(2,1)}), bf16[16,768,128]{2,1,0:T(8,128)(2,1)S(1)}, u32[]{:S(2)}, u32[]{:S(2)}) async-start(bf16[16,768,128]{2,1,0:T(8,128)(2,1)} %shard_map.73), calls=%async_computation | async-start | bytes 6291456 | tf_op jit(solution)/shard_map/all_to_all | solution.py:274
  23.2 1.6 %reshape.338 = s32[32,16,2,2]{3,2,1,0:T(2,128)} reshape(s32[16,1,2,64]{3,2,1,0:T(2,128)S(1)} %constant_dynamic-slice_fusion.3) | data formatting | bytes 16384 | tf_op jit(solution)/shard_map/reshape | solution.py:317
  25.3 3.1 %fusion.66 = (s32[32]{0:T(128)S(1)}, s32[32,16,1,2]{3,2,1,0:T(1,128)}, s32[32]{0:T(128)S(1)}, s32[32,16,1,2]{3,2,1,0:T(1,128)S(1)}) fusion(s32[32,16,2,2]{3,2,1,0:T(2,128)} %reshape.338, s32[]{:T(128)S(6)} %select_n.211, s32[]{:T(128)S(6)} %select_n.198), kind=kLoop, calls=%fused_computation.168 | loop fusion | flops 1984 | bytes 16648 | tf_op jit(solution)/shard_map/reduce_sum | solution.py:190
  32.4 1.1 copy.45
  35.2 1.2 multiply_reduce_fusion
  37.1 1.2 compare_select_fusion.2
  40.0 6.6 %shard_map.74 = (bf16[1280,640]{1,0:T(8,128)(2,1)}, bf16[640,640]{1,0:T(8,128)(2,1)}, bf16[640,640]{1,0:T(8,128)(2,1)}, bf16[640,640]{1,0:T(8,128)(2,1)}, bf16[6...) custom-call(s32[40]{0:T(128)} %pad_add_fusion.1.heads, bf16[5120,640]{1,0:T(8,128)(2,1)} %w_ref.1), custom_call_target="tpu_custom_call" | custom-call | tf_op jit(solution)/shard_map/pallas_call | solution.py:259
  46.6 10.8 %all-to-all-done = bf16[16,768,128]{2,1,0:T(8,128)(2,1)S(1)} async-done(((bf16[16,768,128]{2,1,0:T(8,128)(2,1)}), bf16[16,768,128]{2,1,0:T(8,128)(2,1)S(1)}, u32[]{:S(2)}, u32[]{:S(2)}) %all-to-all-start) | async-done | bytes 3145760 | tf_op jit(solution)/shard_map/all_to_all | solution.py:274
  57.4 3.5 %collective-permute-start = (bf16[16,6,128,128]{3,2,1,0:T(8,128)(2,1)S(1)}, bf16[16,6,128,128]{3,2,1,0:T(8,128)(2,1)S(1)}, u32[]{:S(2)}, u32[]{:S(2)}) collective-permute-start(bf16[16,6,128,128]{3,2,1,0:T(8,128)(2,1)S(1)} %bitcast.47), channel_id=1, source_target_pairs={{0,1},{1,0},{2,3},{3,2},{4,5},{5,4},{6,7},{7,6},{8,9},{9,8},{10,11... | collective-permute-start | bytes 9437192 | tf_op jit(solution)/shard_map/ppermute | solution.py:282
  60.9 6.1 %shard_map.75 = (f32[32,128,128]{2,1,0:T(8,128)S(1)}, f32[32,1,128]{2,1,0:T(1,128)S(1)}, f32[32,1,128]{2,1,0:T(1,128)S(1)}) custom-call(s32[1]{0:T(128)} %bitcast.10.meta, s32[256]{0:T(256)S(1)} %broadcast_minimum_fusion.1.q_of, s32[1024]{0:T(1024)S(1)} %convert_element_type.96.k_of, s32[256]{0:T(256)S(1)} %get-tuple-element.57.valid_of, ...), custom_call_target="tpu_custom_call" | custom-call | flops 4000000000 | bytes 8388608 | tf_op jit(solution)/shard_map/pallas_call | solution.py:171
  67.0 6.6 %shard_map.76 = bf16[16,2,128,128]{3,2,1,0:T(8,128)(2,1)S(1)} custom-call(s32[1]{0:T(128)} %bitcast.18.meta, s32[256]{0:T(256)S(1)} %broadcast_minimum_fusion.q_of, s32[1024]{0:T(1024)S(1)} %convert_element_type.102.k_of, s32[256]{0:T(256)S(1)} %get-tuple-element.52.valid_of, bf16[16,6,128,128]{3,2,1,0:T(8,128)(2,1)S(1)} %bitcast.49, ...), custom_call_target="tpu_custom_call" | custom-call | flops 4000000000 | bytes 8388608 | tf_op jit(solution)/shard_map/pallas_call | solution.py:178
  73.6 20.7 %all_to_all.10.got_ref = bf16[16,2,128,128]{3,2,1,0:T(8,128)(2,1)} all-to-all(bf16[16,2,128,128]{3,2,1,0:T(8,128)(2,1)S(1)} %shard_map.76), channel_id=1, replica_groups=mesh['x'=4,'z'=4,'y'=4,'c'=2] {'x','z'}, dimensions={0} | all-to-all | bytes 2097152 | tf_op jit(solution)/shard_map/all_to_all | solution.py:274
  94.4 2.4 %shard_map.77 = (bf16[256,1280]{1,0:T(8,128)(2,1)}, bf16[256,640]{1,0:T(8,128)(2,1)}, bf16[256,640]{1,0:T(8,128)(2,1)}) custom-call(s32[20]{0:T(128)} %reshape.327.source, bf16[16,2,128,128]{3,2,1,0:T(8,128)(2,1)} %all_to_all.10.got_ref), custom_call_target="tpu_custom_call" | custom-call | tf_op jit(solution)/shard_map/pallas_call | solution.py:228
  96.8 2.3 %collective-permute-start.1 = (bf16[256,1280]{1,0:T(8,128)(2,1)}, bf16[256,1280]{1,0:T(8,128)(2,1)}, u32[]{:S(2)}, u32[]{:S(2)}) collective-permute-start(bf16[256,1280]{1,0:T(8,128)(2,1)} %get-tuple-element.61), channel_id=1, source_target_pairs={{0,1},{1,0},{2,3},{3,2},{4,5},{5,4},{6,7},{7,6},{8,9},{9,8},{10,11... | collective-permute-start | bytes 1966088 | tf_op jit(solution)/shard_map/ppermute | solution.py:282
  99.1 3.2 %collective-permute-start.2 = (bf16[256,640]{1,0:T(8,128)(2,1)}, bf16[256,640]{1,0:T(8,128)(2,1)S(1)}, u32[]{:S(2)}, u32[]{:S(2)}) collective-permute-start(bf16[256,640]{1,0:T(8,128)(2,1)} %get-tuple-element.70), channel_id=1, source_target_pairs={{0,2},{2,4},{4,6},{6,0},{1,3},{3,5},{5,7},{7,1},{8,10},{10,12},{12... | collective-permute-start | bytes 983048 | tf_op jit(solution)/shard_map/ppermute | solution.py:278
  103.2 1.1 collective-permute-start.6
  104.3 7.1 %collective-permute-done.2 = bf16[256,640]{1,0:T(8,128)(2,1)S(1)} collective-permute-done((bf16[256,640]{1,0:T(8,128)(2,1)}, bf16[256,640]{1,0:T(8,128)(2,1)S(1)}, u32[]{:S(2)}, u32[]{:S(2)}) %collective-permute-start.2) | collective-permute-done | bytes 327712 | tf_op jit(solution)/shard_map/ppermute | solution.py:278
  112.2 1.7 %collective-permute-start.8 = (bf16[256,640]{1,0:T(8,128)(2,1)}, bf16[256,640]{1,0:T(8,128)(2,1)S(1)}, u32[]{:S(2)}, u32[]{:S(2)}) collective-permute-start(bf16[256,640]{1,0:T(8,128)(2,1)} %get-tuple-element.70), channel_id=1, source_target_pairs={{0,6},{2,0},{4,2},{6,4},{1,7},{3,1},{5,3},{7,5},{8,14},{10,8},{12,... | collective-permute-start | bytes 983048 | tf_op jit(solution)/shard_map/ppermute | solution.py:278
  113.9 2.7 %collective-permute-start.11 = (bf16[256,640]{1,0:T(8,128)(2,1)S(1)}, bf16[256,640]{1,0:T(8,128)(2,1)S(1)}, u32[]{:S(2)}, u32[]{:S(2)}) collective-permute-start(bf16[256,640]{1,0:T(8,128)(2,1)S(1)} %collective-permute-done.4), channel_id=1, source_target_pairs={{0,6},{2,0},{4,2},{6,4},{1,7},{3,1},{5,3},{7,5},{8,14},{10,8},{12,... | collective-permute-start | bytes 983048 | tf_op jit(solution)/shard_map/ppermute | solution.py:278
  116.6 1.9 %collective-permute-done.6 = bf16[256,640]{1,0:T(8,128)(2,1)S(1)} collective-permute-done((bf16[256,640]{1,0:T(8,128)(2,1)}, bf16[256,640]{1,0:T(8,128)(2,1)S(1)}, u32[]{:S(2)}, u32[]{:S(2)}) %collective-permute-start.6) | collective-permute-done | bytes 327712 | tf_op jit(solution)/shard_map/ppermute | solution.py:278
  119.2 2.5 %fusion.2 = f32[512,640]{1,0:T(8,128)S(1)} fusion(bf16[1280,640]{1,0:T(8,128)(2,1)S(1)} %copy-done.8, bf16[256,1280]{1,0:T(8,128)(2,1)} %collective-permute-done.1, bf16[256,1280]{1,0:T(8,128)(2,1)} %get-tuple-element.61), kind=kOutput, calls=%fused_computation.6 | convolution fusion | flops 841482240 | bytes 4259840 | tf_op jit(solution)/shard_map/dot_general | solution.py:326
  129.6 1.3 collective-permute-done.13
  (118 shorter events, 23.2 us)
Async XLA Ops:
  8.5 48.9 %all-to-all-start = ((bf16[16,768,128]{2,1,0:T(8,128)(2,1)}), bf16[16,768,128]{2,1,0:T(8,128)(2,1)S(1)}, u32[]{:S(2)}, u32[]{:S(2)}) async-start(bf16[16,768,128]{2,1,0:T(8,128)(2,1)} %shard_map.73), calls=%async_computation | async-start | bytes 6291456 | tf_op jit(solution)/shard_map/all_to_all | solution.py:274
  57.4 9.6 %collective-permute-start = (bf16[16,6,128,128]{3,2,1,0:T(8,128)(2,1)S(1)}, bf16[16,6,128,128]{3,2,1,0:T(8,128)(2,1)S(1)}, u32[]{:S(2)}, u32[]{:S(2)}) collective-permute-start(bf16[16,6,128,128]{3,2,1,0:T(8,128)(2,1)S(1)} %bitcast.47), channel_id=1, source_target_pairs={{0,1},{1,0},{2,3},{3,2},{4,5},{5,4},{6,7},{7,6},{8,9},{9,8},{10,11... | collective-permute-start | bytes 9437192 | tf_op jit(solution)/shard_map/ppermute | solution.py:282
  73.6 45.6 %copy-start.8 = (bf16[1280,640]{1,0:T(8,128)(2,1)S(1)}, bf16[1280,640]{1,0:T(8,128)(2,1)}, u32[]{:S(2)}) copy-start(bf16[1280,640]{1,0:T(8,128)(2,1)} %get-tuple-element.65) | copy-start | bytes 4915204
  96.8 6.4 %collective-permute-start.1 = (bf16[256,1280]{1,0:T(8,128)(2,1)}, bf16[256,1280]{1,0:T(8,128)(2,1)}, u32[]{:S(2)}, u32[]{:S(2)}) collective-permute-start(bf16[256,1280]{1,0:T(8,128)(2,1)} %get-tuple-element.61), channel_id=1, source_target_pairs={{0,1},{1,0},{2,3},{3,2},{4,5},{5,4},{6,7},{7,6},{8,9},{9,8},{10,11... | collective-permute-start | bytes 1966088 | tf_op jit(solution)/shard_map/ppermute | solution.py:282
  99.1 12.4 %collective-permute-start.2 = (bf16[256,640]{1,0:T(8,128)(2,1)}, bf16[256,640]{1,0:T(8,128)(2,1)S(1)}, u32[]{:S(2)}, u32[]{:S(2)}) collective-permute-start(bf16[256,640]{1,0:T(8,128)(2,1)} %get-tuple-element.70), channel_id=1, source_target_pairs={{0,2},{2,4},{4,6},{6,0},{1,3},{3,5},{5,7},{7,1},{8,10},{10,12},{12... | collective-permute-start | bytes 983048 | tf_op jit(solution)/shard_map/ppermute | solution.py:278
  102.2 11.6 %collective-permute-start.4 = (bf16[256,640]{1,0:T(8,128)(2,1)}, bf16[256,640]{1,0:T(8,128)(2,1)S(1)}, u32[]{:S(2)}, u32[]{:S(2)}) collective-permute-start(bf16[256,640]{1,0:T(8,128)(2,1)} %get-tuple-element.68), channel_id=1, source_target_pairs={{0,6},{2,0},{4,2},{6,4},{1,7},{3,1},{5,3},{7,5},{8,14},{10,8},{12,... | collective-permute-start | bytes 983048 | tf_op jit(solution)/shard_map/ppermute | solution.py:278
  103.2 15.3 %collective-permute-start.6 = (bf16[256,640]{1,0:T(8,128)(2,1)}, bf16[256,640]{1,0:T(8,128)(2,1)S(1)}, u32[]{:S(2)}, u32[]{:S(2)}) collective-permute-start(bf16[256,640]{1,0:T(8,128)(2,1)} %get-tuple-element.68), channel_id=1, source_target_pairs={{0,2},{2,4},{4,6},{6,0},{1,3},{3,5},{5,7},{7,1},{8,10},{10,12},{12... | collective-permute-start | bytes 983048 | tf_op jit(solution)/shard_map/ppermute | solution.py:278
  111.5 10.3 %collective-permute-start.3 = (bf16[256,640]{1,0:T(8,128)(2,1)S(1)}, bf16[256,640]{1,0:T(8,128)(2,1)S(1)}, u32[]{:S(2)}, u32[]{:S(2)}) collective-permute-start(bf16[256,640]{1,0:T(8,128)(2,1)S(1)} %collective-permute-done.2), channel_id=1, source_target_pairs={{0,1},{1,0},{2,3},{3,2},{4,5},{5,4},{6,7},{7,6},{8,9},{9,8},{10,11... | collective-permute-start | bytes 983048 | tf_op jit(solution)/shard_map/ppermute | solution.py:282
  112.2 9.6 %collective-permute-start.8 = (bf16[256,640]{1,0:T(8,128)(2,1)}, bf16[256,640]{1,0:T(8,128)(2,1)S(1)}, u32[]{:S(2)}, u32[]{:S(2)}) collective-permute-start(bf16[256,640]{1,0:T(8,128)(2,1)} %get-tuple-element.70), channel_id=1, source_target_pairs={{0,6},{2,0},{4,2},{6,4},{1,7},{3,1},{5,3},{7,5},{8,14},{10,8},{12,... | collective-permute-start | bytes 983048 | tf_op jit(solution)/shard_map/ppermute | solution.py:278
  113.9 9.1 %copy-start.5 = (bf16[640,640]{1,0:T(8,128)(2,1)S(1)}, bf16[640,640]{1,0:T(8,128)(2,1)}, u32[]{:S(2)}) copy-start(bf16[640,640]{1,0:T(8,128)(2,1)} %get-tuple-element.66) | copy-start | bytes 2457604
  113.9 13.9 %collective-permute-start.10 = (bf16[256,640]{1,0:T(8,128)(2,1)S(1)}, bf16[256,640]{1,0:T(8,128)(2,1)S(1)}, u32[]{:S(2)}, u32[]{:S(2)}) collective-permute-start(bf16[256,640]{1,0:T(8,128)(2,1)S(1)} %collective-permute-done.2), channel_id=1, source_target_pairs={{0,2},{2,4},{4,6},{6,0},{1,3},{3,5},{5,7},{7,1},{8,10},{10,12},{12... | collective-permute-start | bytes 983048 | tf_op jit(solution)/shard_map/ppermute | solution.py:278
  113.9 14.9 %collective-permute-start.11 = (bf16[256,640]{1,0:T(8,128)(2,1)S(1)}, bf16[256,640]{1,0:T(8,128)(2,1)S(1)}, u32[]{:S(2)}, u32[]{:S(2)}) collective-permute-start(bf16[256,640]{1,0:T(8,128)(2,1)S(1)} %collective-permute-done.4), channel_id=1, source_target_pairs={{0,6},{2,0},{4,2},{6,4},{1,7},{3,1},{5,3},{7,5},{8,14},{10,8},{12,... | collective-permute-start | bytes 983048 | tf_op jit(solution)/shard_map/ppermute | solution.py:278
  118.5 5.2 %collective-permute-start.7 = (bf16[256,640]{1,0:T(8,128)(2,1)S(1)}, bf16[256,640]{1,0:T(8,128)(2,1)S(1)}, u32[]{:S(2)}, u32[]{:S(2)}) collective-permute-start(bf16[256,640]{1,0:T(8,128)(2,1)S(1)} %collective-permute-done.6), channel_id=1, source_target_pairs={{0,1},{1,0},{2,3},{3,2},{4,5},{5,4},{6,7},{7,6},{8,9},{9,8},{10,11... | collective-permute-start | bytes 983048 | tf_op jit(solution)/shard_map/ppermute | solution.py:282
  121.7 2.0 %copy-start.3 = (bf16[640,640]{1,0:T(8,128)(2,1)S(1)}, bf16[640,640]{1,0:T(8,128)(2,1)}, u32[]{:S(2)}) copy-start(bf16[640,640]{1,0:T(8,128)(2,1)} %get-tuple-element.69) | copy-start | bytes 2457604
  121.7 3.9 %collective-permute-start.5 = (bf16[256,640]{1,0:T(8,128)(2,1)S(1)}, bf16[256,640]{1,0:T(8,128)(2,1)S(1)}, u32[]{:S(2)}, u32[]{:S(2)}) collective-permute-start(bf16[256,640]{1,0:T(8,128)(2,1)S(1)} %collective-permute-done.4), channel_id=1, source_target_pairs={{0,1},{1,0},{2,3},{3,2},{4,5},{5,4},{6,7},{7,6},{8,9},{9,8},{10,11... | collective-permute-start | bytes 983048 | tf_op jit(solution)/shard_map/ppermute | solution.py:282
  121.8 2.7 %collective-permute-start.9 = (bf16[256,640]{1,0:T(8,128)(2,1)S(1)}, bf16[256,640]{1,0:T(8,128)(2,1)S(1)}, u32[]{:S(2)}, u32[]{:S(2)}) collective-permute-start(bf16[256,640]{1,0:T(8,128)(2,1)S(1)} %collective-permute-done.8), channel_id=1, source_target_pairs={{0,1},{1,0},{2,3},{3,2},{4,5},{5,4},{6,7},{7,6},{8,9},{9,8},{10,11... | collective-permute-start | bytes 983048 | tf_op jit(solution)/shard_map/ppermute | solution.py:282
  123.7 1.1 copy-start.2
  124.5 1.2 copy-start
  126.5 1.1 copy-start.6
  126.5 1.1 copy-start.7
  127.6 3.2 %copy-start.1 = (bf16[640,640]{1,0:T(8,128)(2,1)S(1)}, bf16[640,640]{1,0:T(8,128)(2,1)}, u32[]{:S(2)}) copy-start(bf16[640,640]{1,0:T(8,128)(2,1)} %get-tuple-element.76) | copy-start | bytes 2457604
  127.7 3.9 %copy-start.4 = (bf16[640,640]{1,0:T(8,128)(2,1)S(1)}, bf16[640,640]{1,0:T(8,128)(2,1)}, u32[]{:S(2)}) copy-start(bf16[640,640]{1,0:T(8,128)(2,1)} %get-tuple-element.74) | copy-start | bytes 2457604
  128.8 2.0 %collective-permute-start.13 = (bf16[256,640]{1,0:T(8,128)(2,1)S(1)}, bf16[256,640]{1,0:T(8,128)(2,1)S(1)}, u32[]{:S(2)}, u32[]{:S(2)}) collective-permute-start(bf16[256,640]{1,0:T(8,128)(2,1)S(1)} %collective-permute-done.11), channel_id=1, source_target_pairs={{0,1},{1,0},{2,3},{3,2},{4,5},{5,4},{6,7},{7,6},{8,9},{9,8},{10,11... | collective-permute-start | bytes 983048 | tf_op jit(solution)/shard_map/ppermute | solution.py:282
  129.6 2.0 %collective-permute-start.12 = (bf16[256,640]{1,0:T(8,128)(2,1)S(1)}, bf16[256,640]{1,0:T(8,128)(2,1)S(1)}, u32[]{:S(2)}, u32[]{:S(2)}) collective-permute-start(bf16[256,640]{1,0:T(8,128)(2,1)S(1)} %collective-permute-done.10), channel_id=1, source_target_pairs={{0,1},{1,0},{2,3},{3,2},{4,5},{5,4},{6,7},{7,6},{8,9},{9,8},{10,11... | collective-permute-start | bytes 983048 | tf_op jit(solution)/shard_map/ppermute | solution.py:282

commit v9 on v8

--- a/solution.py
+++ b/solution.py
@@ -48,36 +48,26 @@
     return chips, first
 
 
-def pack_kernel(heads, q_ref, k_ref, v_ref, out_ref, held, turned, sem_in, sem_out):
-    start = pl.multiple_of(heads[CHIPS] * HALF, HALF)
-    rows = pl.ds(start, HALF)
-    loads, stores = [], []
+def pack_kernel(heads, q_ref, k_ref, v_ref, out_ref, held, values, sem_v, sem_kq, sem_out):
+    rows = pl.ds(pl.multiple_of(heads[CHIPS] * HALF, HALF), HALF)
+    cols = [pl.ds(pl.multiple_of(heads[t] * TILE, TILE), TILE) for t in range(CHIPS)]
+    first = [pltpu.make_async_copy(v_ref.at[rows, cols[t]], values.at[t], sem_v.at[t]) for t in range(CHIPS)]
+    others = [
+        pltpu.make_async_copy(ref.at[rows, cols[t]], held.at[t, pl.ds(at * HALF, HALF)], sem_kq.at[t, at // 2])
+        for t in range(CHIPS)
+        for ref, at in ((k_ref, 0), (q_ref, 2))
+    ]
+    for load in first + others:
+        load.start()
+    stores = []
     for t in range(CHIPS):
-        cols = pl.ds(pl.multiple_of(heads[t] * TILE, TILE), TILE)
-        loads.append(
-            [
-                pltpu.make_async_copy(k_ref.at[rows, cols], held.at[t, pl.ds(0, HALF)], sem_in.at[t, 0]),
-                pltpu.make_async_copy(v_ref.at[rows, cols], held.at[t, pl.ds(HALF, HALF)], sem_in.at[t, 1]),
-                pltpu.make_async_copy(q_ref.at[rows, cols], held.at[t, pl.ds(2 * HALF, HALF)], sem_in.at[t, 2]),
-            ]
-        )
-        for load in loads[-1]:
-            load.start()
-    for t in range(CHIPS):
-        for load in loads[t]:
+        first[t].wait()
+        for sub in range(2):
+            held[t, pl.ds(HALF + sub * TILE, TILE), :] = values[t, pl.ds(sub * TILE, TILE), :].T
+        for load in others[2 * t : 2 * t + 2]:
             load.wait()
-        for sub in range(2):
-            part = pl.ds(sub * TILE, TILE)
-            turned[t, part, :] = held[t, pl.ds(HALF + sub * TILE, TILE), :].T
-        stores += [
-            pltpu.make_async_copy(held.at[t, pl.ds(0, HALF)], out_ref.at[t, pl.ds(0, HALF)], sem_out.at[t, 0]),
-            pltpu.make_async_copy(turned.at[t], out_ref.at[t, pl.ds(HALF, HALF)], sem_out.at[t, 1]),
-            pltpu.make_async_copy(
-                held.at[t, pl.ds(2 * HALF, HALF)], out_ref.at[t, pl.ds(2 * HALF, HALF)], sem_out.at[t, 2]
-            ),
-        ]
-        for store in stores[-3:]:
-            store.start()
+        stores.append(pltpu.make_async_copy(held.at[t], out_ref.at[t], sem_out.at[t]))
+        stores[t].start()
     for store in stores:
         store.wait()
 
@@ -93,8 +83,9 @@
         scratch_shapes=[
             pltpu.VMEM((CHIPS, 3 * HALF, TILE), jnp.bfloat16),
             pltpu.VMEM((CHIPS, HALF, TILE), jnp.bfloat16),
-            pltpu.SemaphoreType.DMA((CHIPS, 3)),
-            pltpu.SemaphoreType.DMA((CHIPS, 3)),
+            pltpu.SemaphoreType.DMA((CHIPS,)),
+            pltpu.SemaphoreType.DMA((CHIPS, 2)),
+            pltpu.SemaphoreType.DMA((CHIPS,)),
         ],
         compiler_params=pltpu.CompilerParams(vmem_limit_bytes=60 * 2**20),
     )(scalars, queries, keys, values)
@@ -335,11 +326,13 @@
     attended = attend(lists[1], got, got_other, attend(lists[0], got))
     own, low, high = select(source, exchange(attended))
     below_low, above_high = along_y(low, 1), along_y(high, 3)
-    own_other, low, high = lax.optimization_barrier((swap(own), low, high))
-    below_high, above_low = along_y(high, 1), along_y(low, 3)
+    below_high = along_y(high, 1)
+    own_other = swap(own)
+    above_low = along_y(low, 3)
     far_low, far_high = along_y(below_low, 1), along_y(above_high, 3)
     total = product(own, own_other, weights[0])
-    for block, weight in zip((below_low, above_high, below_high, above_low), (weights[1], weights[4], weights[2], weights[3])):
+    near = ((below_high, weights[2]), (above_low, weights[3]), (below_low, weights[1]), (above_high, weights[4]))
+    for block, weight in near:
         total = total + project(block, weight)
     base = residual_in.astype(jnp.float32) + gate_scale * by_rows(total)
     base, far_low, far_high = lax.optimization_barrier((base, far_low, far_high))

time: 135 us -> 138 us (1.022)
  waiting for transfers between devices: 22.2 us -> 24.6 us
  starting transfers between devices: 27.3 us -> 25.1 us
  Pallas kernels: 26.2 us -> 28.2 us
    ppermute x6, starting transfers between devices: 9.57 us -> 6.62 us  [along_y(): lax.ppermute(block, 'y', [(i, (i + step) % PLANES) for i in range(PLANES)])]
    ppermute x6, waiting for transfers between devices: 10.1 us -> 12.6 us  [along_y(): lax.ppermute(block, 'y', [(i, (i + step) % PLANES) for i in range(PLANES)])]
    pallas_call x1, Pallas kernels: 6.11 us -> 7.89 us  [attend(): pl.pallas_call(functools.partial(first_kernel, scale), in_specs=[smem] *...]
  transfers between devices with their start and end apart: 15 -> 15, of which waited for: 5 -> 6; matrix products, arithmetic and copies ran while one was open for 17% -> 17% of each run, Pallas kernels for 10% -> 11%
where the time goes in v9:
time: 138 us; the launch traced here: 136 us
  Pallas kernels  28.2 us (20%)
  starting transfers between devices  25.1 us (18%)
  waiting for transfers between devices  24.6 us (18%)
  blocking collectives  20.9 us (15%)
  other arithmetic  13.7 us (10%)
  local copies, waits for them, and re-layouts  9.38 us (7%)
  matrix products  7.41 us (5%)
  between operations  6.54 us (5%)
    all_to_all x1, blocking collectives, exchange(): lax.all_to_all(block, TOKENS_AXES, split_axis=0, concat_axis=0, tiled=True)  20.9 us
    ppermute x6, waiting for transfers between devices, along_y(): lax.ppermute(block, 'y', [(i, (i + step) % PLANES) for i in range(PLANES)])  12.6 us
    all_to_all x1, waiting for transfers between devices, exchange(): lax.all_to_all(block, TOKENS_AXES, split_axis=0, concat_axis=0, tiled=True)  10.8 us
    ppermute x8, starting transfers between devices, swap(): return lax.ppermute(block, 'c', [(0, 1), (1, 0)])  10 us
    all_to_all x1, starting transfers between devices, exchange(): lax.all_to_all(block, TOKENS_AXES, split_axis=0, concat_axis=0, tiled=True)  8.44 us
    pallas_call x1, Pallas kernels, attend(): pl.pallas_call(functools.partial(first_kernel, scale), in_specs=[smem] *...  7.89 us
    dot_general x7, matrix products, product(): jnp.dot(jnp.concatenate([block, other], axis=0), weight, preferred_elemen...  7.03 us
    ppermute x6, starting transfers between devices, along_y(): lax.ppermute(block, 'y', [(i, (i + step) % PLANES) for i in range(PLANES)])  6.62 us
  transfers between devices with their start and end apart: 15, of which 6 were waited for; matrix products, arithmetic and copies ran while one was open for 17% of the time, Pallas kernels for 11%

profile of v9, /device:TPU:1, one launch (start us, length us, event | category | flops | bytes accessed | tf_op | source)
XLA Modules:
  0.0 135.8 jit_solution(6442933761559788684)
XLA Ops:
  0.0 2.1 %fusion.65 = (s32[40,64]{1,0:T(8,128)S(1)}, s32[40]{0:T(128)S(1)}) fusion(s32[40,64,64]{2,1,0:T(8,128)} %param.13), kind=kLoop, calls=%fused_computation.167 | loop fusion | flops 325080 | bytes 665760 | tf_op jit(solution)/shard_map/reduce_sum | solution.py:280
  4.1 4.6 %shard_map.73 = bf16[16,768,128]{2,1,0:T(8,128)(2,1)} custom-call(s32[17]{0:T(128)} %pad_add_fusion.heads, bf16[512,5120]{1,0:T(8,128)(2,1)} %q_ref.1, bf16[512,5120]{1,0:T(8,128)(2,1)} %k_ref.1, bf16[512,5120]{1,0:T(8,128)(2,1)} %v_ref.1), custom_call_target="tpu_custom_call" | custom-call | tf_op jit(solution)/shard_map/pallas_call | solution.py:78
  8.7 8.4 %all-to-all-start = ((bf16[16,768,128]{2,1,0:T(8,128)(2,1)}), bf16[16,768,128]{2,1,0:T(8,128)(2,1)S(1)}, u32[]{:S(2)}, u32[]{:S(2)}) async-start(bf16[16,768,128]{2,1,0:T(8,128)(2,1)} %shard_map.73), calls=%async_computation | async-start | bytes 6291456 | tf_op jit(solution)/shard_map/all_to_all | solution.py:265
  23.3 1.6 %reshape.338 = s32[32,16,2,2]{3,2,1,0:T(2,128)} reshape(s32[16,1,2,64]{3,2,1,0:T(2,128)S(1)} %constant_dynamic-slice_fusion.3) | data formatting | bytes 16384 | tf_op jit(solution)/shard_map/reshape | solution.py:308
  25.5 3.1 %fusion.66 = (s32[32]{0:T(128)S(1)}, s32[32,16,1,2]{3,2,1,0:T(1,128)}, s32[32]{0:T(128)S(1)}, s32[32,16,1,2]{3,2,1,0:T(1,128)S(1)}) fusion(s32[32,16,2,2]{3,2,1,0:T(2,128)} %reshape.338, s32[]{:T(128)S(6)} %select_n.211, s32[]{:T(128)S(6)} %select_n.198), kind=kLoop, calls=%fused_computation.168 | loop fusion | flops 1984 | bytes 16648 | tf_op jit(solution)/shard_map/reduce_sum | solution.py:181
  37.3 1.2 compare_select_fusion.2
  40.1 6.6 %shard_map.74 = (bf16[1280,640]{1,0:T(8,128)(2,1)}, bf16[640,640]{1,0:T(8,128)(2,1)}, bf16[640,640]{1,0:T(8,128)(2,1)}, bf16[640,640]{1,0:T(8,128)(2,1)}, bf16[6...) custom-call(s32[40]{0:T(128)} %pad_add_fusion.1.heads, bf16[5120,640]{1,0:T(8,128)(2,1)} %w_ref.1), custom_call_target="tpu_custom_call" | custom-call | tf_op jit(solution)/shard_map/pallas_call | solution.py:250
  46.7 10.8 %all-to-all-done = bf16[16,768,128]{2,1,0:T(8,128)(2,1)S(1)} async-done(((bf16[16,768,128]{2,1,0:T(8,128)(2,1)}), bf16[16,768,128]{2,1,0:T(8,128)(2,1)S(1)}, u32[]{:S(2)}, u32[]{:S(2)}) %all-to-all-start) | async-done | bytes 3145760 | tf_op jit(solution)/shard_map/all_to_all | solution.py:265
  57.5 2.9 %collective-permute-start = (bf16[16,6,128,128]{3,2,1,0:T(8,128)(2,1)S(1)}, bf16[16,6,128,128]{3,2,1,0:T(8,128)(2,1)S(1)}, u32[]{:S(2)}, u32[]{:S(2)}) collective-permute-start(bf16[16,6,128,128]{3,2,1,0:T(8,128)(2,1)S(1)} %bitcast.47), channel_id=1, source_target_pairs={{0,1},{1,0},{2,3},{3,2},{4,5},{5,4},{6,7},{7,6},{8,9},{9,8},{10,11... | collective-permute-start | bytes 9437192 | tf_op jit(solution)/shard_map/ppermute | solution.py:273
  60.5 7.9 %shard_map.75 = (f32[32,128,128]{2,1,0:T(8,128)S(1)}, f32[32,1,128]{2,1,0:T(1,128)S(1)}, f32[32,1,128]{2,1,0:T(1,128)S(1)}) custom-call(s32[1]{0:T(128)} %bitcast.10.meta, s32[256]{0:T(256)S(1)} %broadcast_minimum_fusion.1.q_of, s32[1024]{0:T(1024)S(1)} %convert_element_type.96.k_of, s32[256]{0:T(256)S(1)} %get-tuple-element.54.valid_of, ...), custom_call_target="tpu_custom_call" | custom-call | flops 4000000000 | bytes 8388608 | tf_op jit(solution)/shard_map/pallas_call | solution.py:162
  68.4 6.6 %shard_map.76 = bf16[16,2,128,128]{3,2,1,0:T(8,128)(2,1)S(1)} custom-call(s32[1]{0:T(128)} %bitcast.18.meta, s32[256]{0:T(256)S(1)} %broadcast_minimum_fusion.q_of, s32[1024]{0:T(1024)S(1)} %convert_element_type.102.k_of, s32[256]{0:T(256)S(1)} %get-tuple-element.49.valid_of, bf16[16,6,128,128]{3,2,1,0:T(8,128)(2,1)S(1)} %bitcast.49, ...), custom_call_target="tpu_custom_call" | custom-call | flops 4000000000 | bytes 8388608 | tf_op jit(solution)/shard_map/pallas_call | solution.py:169
  75.0 20.9 %all_to_all.10.got_ref = bf16[16,2,128,128]{3,2,1,0:T(8,128)(2,1)} all-to-all(bf16[16,2,128,128]{3,2,1,0:T(8,128)(2,1)S(1)} %shard_map.76), channel_id=1, replica_groups=mesh['x'=4,'z'=4,'y'=4,'c'=2] {'x','z'}, dimensions={0} | all-to-all | bytes 2097152 | tf_op jit(solution)/shard_map/all_to_all | solution.py:265
  95.9 2.4 %shard_map.77 = (bf16[256,1280]{1,0:T(8,128)(2,1)}, bf16[256,640]{1,0:T(8,128)(2,1)}, bf16[256,640]{1,0:T(8,128)(2,1)}) custom-call(s32[20]{0:T(128)} %reshape.327.source, bf16[16,2,128,128]{3,2,1,0:T(8,128)(2,1)} %all_to_all.10.got_ref), custom_call_target="tpu_custom_call" | custom-call | tf_op jit(solution)/shard_map/pallas_call | solution.py:219
  98.3 2.3 %collective-permute-start.1 = (bf16[256,1280]{1,0:T(8,128)(2,1)}, bf16[256,1280]{1,0:T(8,128)(2,1)}, u32[]{:S(2)}, u32[]{:S(2)}) collective-permute-start(bf16[256,1280]{1,0:T(8,128)(2,1)} %get-tuple-element.58), channel_id=1, source_target_pairs={{0,1},{1,0},{2,3},{3,2},{4,5},{5,4},{6,7},{7,6},{8,9},{9,8},{10,11... | collective-permute-start | bytes 1966088 | tf_op jit(solution)/shard_map/ppermute | solution.py:273
  100.6 2.4 %collective-permute-start.8 = (bf16[256,640]{1,0:T(8,128)(2,1)}, bf16[256,640]{1,0:T(8,128)(2,1)S(1)}, u32[]{:S(2)}, u32[]{:S(2)}) collective-permute-start(bf16[256,640]{1,0:T(8,128)(2,1)} %get-tuple-element.60), channel_id=1, source_target_pairs={{0,6},{2,0},{4,2},{6,4},{1,7},{3,1},{5,3},{7,5},{8,14},{10,8},{12,... | collective-permute-start | bytes 983048 | tf_op jit(solution)/shard_map/ppermute | solution.py:269
  103.1 2.7 %collective-permute-start.4 = (bf16[256,640]{1,0:T(8,128)(2,1)}, bf16[256,640]{1,0:T(8,128)(2,1)S(1)}, u32[]{:S(2)}, u32[]{:S(2)}) collective-permute-start(bf16[256,640]{1,0:T(8,128)(2,1)} %get-tuple-element.62), channel_id=1, source_target_pairs={{0,6},{2,0},{4,2},{6,4},{1,7},{3,1},{5,3},{7,5},{8,14},{10,8},{12,... | collective-permute-start | bytes 983048 | tf_op jit(solution)/shard_map/ppermute | solution.py:269
  105.8 4.7 %collective-permute-done.8 = bf16[256,640]{1,0:T(8,128)(2,1)S(1)} collective-permute-done((bf16[256,640]{1,0:T(8,128)(2,1)}, bf16[256,640]{1,0:T(8,128)(2,1)S(1)}, u32[]{:S(2)}, u32[]{:S(2)}) %collective-permute-start.8) | collective-permute-done | bytes 327712 | tf_op jit(solution)/shard_map/ppermute | solution.py:269
  111.7 1.8 %collective-permute-done.6 = bf16[256,640]{1,0:T(8,128)(2,1)S(1)} collective-permute-done((bf16[256,640]{1,0:T(8,128)(2,1)}, bf16[256,640]{1,0:T(8,128)(2,1)S(1)}, u32[]{:S(2)}, u32[]{:S(2)}) %collective-permute-start.6) | collective-permute-done | bytes 327712 | tf_op jit(solution)/shard_map/ppermute | solution.py:269
  113.5 1.5 %collective-permute-start.11 = (bf16[256,640]{1,0:T(8,128)(2,1)S(1)}, bf16[256,640]{1,0:T(8,128)(2,1)S(1)}, u32[]{:S(2)}, u32[]{:S(2)}) collective-permute-start(bf16[256,640]{1,0:T(8,128)(2,1)S(1)} %collective-permute-done.8), channel_id=1, source_target_pairs={{0,6},{2,0},{4,2},{6,4},{1,7},{3,1},{5,3},{7,5},{8,14},{10,8},{12,... | collective-permute-start | bytes 983048 | tf_op jit(solution)/shard_map/ppermute | solution.py:269
  115.4 2.5 %fusion.2 = f32[512,640]{1,0:T(8,128)S(1)} fusion(bf16[1280,640]{1,0:T(8,128)(2,1)S(1)} %copy-done.8, bf16[256,1280]{1,0:T(8,128)(2,1)} %collective-permute-done.1, bf16[256,1280]{1,0:T(8,128)(2,1)} %get-tuple-element.58), kind=kOutput, calls=%fused_computation.6 | convolution fusion | flops 841482240 | bytes 4259840 | tf_op jit(solution)/shard_map/dot_general | solution.py:317
  117.8 2.7 %collective-permute-done.2 = bf16[256,640]{1,0:T(8,128)(2,1)S(1)} collective-permute-done((bf16[256,640]{1,0:T(8,128)(2,1)}, bf16[256,640]{1,0:T(8,128)(2,1)S(1)}, u32[]{:S(2)}, u32[]{:S(2)}) %collective-permute-start.2) | collective-permute-done | bytes 327712 | tf_op jit(solution)/shard_map/ppermute | solution.py:269
  126.5 3.3 %collective-permute-done.10 = bf16[256,640]{1,0:T(8,128)(2,1)S(1)} collective-permute-done((bf16[256,640]{1,0:T(8,128)(2,1)S(1)}, bf16[256,640]{1,0:T(8,128)(2,1)S(1)}, u32[]{:S(2)}, u32[]{:S(2)}) %collective-permute-start.10) | collective-permute-done | bytes 327712 | tf_op jit(solution)/shard_map/ppermute | solution.py:269
  129.8 2.0 %collective-permute-start.13 = (bf16[256,640]{1,0:T(8,128)(2,1)S(1)}, bf16[256,640]{1,0:T(8,128)(2,1)S(1)}, u32[]{:S(2)}, u32[]{:S(2)}) collective-permute-start(bf16[256,640]{1,0:T(8,128)(2,1)S(1)} %collective-permute-done.11), channel_id=1, source_target_pairs={{0,1},{1,0},{2,3},{3,2},{4,5},{5,4},{6,7},{7,6},{8,9},{9,8},{10,11... | collective-permute-start | bytes 983048 | tf_op jit(solution)/shard_map/ppermute | solution.py:273
  131.9 1.3 collective-permute-done.13
  (118 shorter events, 22.7 us)
Async XLA Ops:
  8.7 48.8 %all-to-all-start = ((bf16[16,768,128]{2,1,0:T(8,128)(2,1)}), bf16[16,768,128]{2,1,0:T(8,128)(2,1)S(1)}, u32[]{:S(2)}, u32[]{:S(2)}) async-start(bf16[16,768,128]{2,1,0:T(8,128)(2,1)} %shard_map.73), calls=%async_computation | async-start | bytes 6291456 | tf_op jit(solution)/shard_map/all_to_all | solution.py:265
  57.5 10.9 %collective-permute-start = (bf16[16,6,128,128]{3,2,1,0:T(8,128)(2,1)S(1)}, bf16[16,6,128,128]{3,2,1,0:T(8,128)(2,1)S(1)}, u32[]{:S(2)}, u32[]{:S(2)}) collective-permute-start(bf16[16,6,128,128]{3,2,1,0:T(8,128)(2,1)S(1)} %bitcast.47), channel_id=1, source_target_pairs={{0,1},{1,0},{2,3},{3,2},{4,5},{5,4},{6,7},{7,6},{8,9},{9,8},{10,11... | collective-permute-start | bytes 9437192 | tf_op jit(solution)/shard_map/ppermute | solution.py:273
  75.0 40.4 %copy-start.8 = (bf16[1280,640]{1,0:T(8,128)(2,1)S(1)}, bf16[1280,640]{1,0:T(8,128)(2,1)}, u32[]{:S(2)}) copy-start(bf16[1280,640]{1,0:T(8,128)(2,1)} %get-tuple-element.59) | copy-start | bytes 4915204
  98.3 16.7 %collective-permute-start.1 = (bf16[256,1280]{1,0:T(8,128)(2,1)}, bf16[256,1280]{1,0:T(8,128)(2,1)}, u32[]{:S(2)}, u32[]{:S(2)}) collective-permute-start(bf16[256,1280]{1,0:T(8,128)(2,1)} %get-tuple-element.58), channel_id=1, source_target_pairs={{0,1},{1,0},{2,3},{3,2},{4,5},{5,4},{6,7},{7,6},{8,9},{9,8},{10,11... | collective-permute-start | bytes 1966088 | tf_op jit(solution)/shard_map/ppermute | solution.py:273
  100.6 9.9 %collective-permute-start.8 = (bf16[256,640]{1,0:T(8,128)(2,1)}, bf16[256,640]{1,0:T(8,128)(2,1)S(1)}, u32[]{:S(2)}, u32[]{:S(2)}) collective-permute-start(bf16[256,640]{1,0:T(8,128)(2,1)} %get-tuple-element.60), channel_id=1, source_target_pairs={{0,6},{2,0},{4,2},{6,4},{1,7},{3,1},{5,3},{7,5},{8,14},{10,8},{12,... | collective-permute-start | bytes 983048 | tf_op jit(solution)/shard_map/ppermute | solution.py:269
  103.1 10.4 %collective-permute-start.6 = (bf16[256,640]{1,0:T(8,128)(2,1)}, bf16[256,640]{1,0:T(8,128)(2,1)S(1)}, u32[]{:S(2)}, u32[]{:S(2)}) collective-permute-start(bf16[256,640]{1,0:T(8,128)(2,1)} %get-tuple-element.62), channel_id=1, source_target_pairs={{0,2},{2,4},{4,6},{6,0},{1,3},{3,5},{5,7},{7,1},{8,10},{10,12},{12... | collective-permute-start | bytes 983048 | tf_op jit(solution)/shard_map/ppermute | solution.py:269
  103.1 17.5 %collective-permute-start.2 = (bf16[256,640]{1,0:T(8,128)(2,1)}, bf16[256,640]{1,0:T(8,128)(2,1)S(1)}, u32[]{:S(2)}, u32[]{:S(2)}) collective-permute-start(bf16[256,640]{1,0:T(8,128)(2,1)} %get-tuple-element.60), channel_id=1, source_target_pairs={{0,2},{2,4},{4,6},{6,0},{1,3},{3,5},{5,7},{7,1},{8,10},{10,12},{12... | collective-permute-start | bytes 983048 | tf_op jit(solution)/shard_map/ppermute | solution.py:269
  103.1 17.5 %collective-permute-start.4 = (bf16[256,640]{1,0:T(8,128)(2,1)}, bf16[256,640]{1,0:T(8,128)(2,1)S(1)}, u32[]{:S(2)}, u32[]{:S(2)}) collective-permute-start(bf16[256,640]{1,0:T(8,128)(2,1)} %get-tuple-element.62), channel_id=1, source_target_pairs={{0,6},{2,0},{4,2},{6,4},{1,7},{3,1},{5,3},{7,5},{8,14},{10,8},{12,... | collective-permute-start | bytes 983048 | tf_op jit(solution)/shard_map/ppermute | solution.py:269
  110.5 11.1 %collective-permute-start.9 = (bf16[256,640]{1,0:T(8,128)(2,1)S(1)}, bf16[256,640]{1,0:T(8,128)(2,1)S(1)}, u32[]{:S(2)}, u32[]{:S(2)}) collective-permute-start(bf16[256,640]{1,0:T(8,128)(2,1)S(1)} %collective-permute-done.8), channel_id=1, source_target_pairs={{0,1},{1,0},{2,3},{3,2},{4,5},{5,4},{6,7},{7,6},{8,9},{9,8},{10,11... | collective-permute-start | bytes 983048 | tf_op jit(solution)/shard_map/ppermute | solution.py:273
  111.7 10.1 %copy-start.3 = (bf16[640,640]{1,0:T(8,128)(2,1)S(1)}, bf16[640,640]{1,0:T(8,128)(2,1)}, u32[]{:S(2)}) copy-start(bf16[640,640]{1,0:T(8,128)(2,1)} %get-tuple-element.65) | copy-start | bytes 2457604
  113.5 13.0 %collective-permute-start.11 = (bf16[256,640]{1,0:T(8,128)(2,1)S(1)}, bf16[256,640]{1,0:T(8,128)(2,1)S(1)}, u32[]{:S(2)}, u32[]{:S(2)}) collective-permute-start(bf16[256,640]{1,0:T(8,128)(2,1)S(1)} %collective-permute-done.8), channel_id=1, source_target_pairs={{0,6},{2,0},{4,2},{6,4},{1,7},{3,1},{5,3},{7,5},{8,14},{10,8},{12,... | collective-permute-start | bytes 983048 | tf_op jit(solution)/shard_map/ppermute | solution.py:269
  115.0 7.5 %collective-permute-start.7 = (bf16[256,640]{1,0:T(8,128)(2,1)S(1)}, bf16[256,640]{1,0:T(8,128)(2,1)S(1)}, u32[]{:S(2)}, u32[]{:S(2)}) collective-permute-start(bf16[256,640]{1,0:T(8,128)(2,1)S(1)} %collective-permute-done.6), channel_id=1, source_target_pairs={{0,1},{1,0},{2,3},{3,2},{4,5},{5,4},{6,7},{7,6},{8,9},{9,8},{10,11... | collective-permute-start | bytes 983048 | tf_op jit(solution)/shard_map/ppermute | solution.py:273
  117.8 4.7 %copy-start.2 = (bf16[640,640]{1,0:T(8,128)(2,1)S(1)}, bf16[640,640]{1,0:T(8,128)(2,1)}, u32[]{:S(2)}) copy-start(bf16[640,640]{1,0:T(8,128)(2,1)} %get-tuple-element.64) | copy-start | bytes 2457604
  120.5 9.3 %collective-permute-start.10 = (bf16[256,640]{1,0:T(8,128)(2,1)S(1)}, bf16[256,640]{1,0:T(8,128)(2,1)S(1)}, u32[]{:S(2)}, u32[]{:S(2)}) collective-permute-start(bf16[256,640]{1,0:T(8,128)(2,1)S(1)} %collective-permute-done.6), channel_id=1, source_target_pairs={{0,2},{2,4},{4,6},{6,0},{1,3},{3,5},{5,7},{7,1},{8,10},{10,12},{12... | collective-permute-start | bytes 983048 | tf_op jit(solution)/shard_map/ppermute | solution.py:269
  120.5 2.8 %collective-permute-start.3 = (bf16[256,640]{1,0:T(8,128)(2,1)S(1)}, bf16[256,640]{1,0:T(8,128)(2,1)S(1)}, u32[]{:S(2)}, u32[]{:S(2)}) collective-permute-start(bf16[256,640]{1,0:T(8,128)(2,1)S(1)} %collective-permute-done.2), channel_id=1, source_target_pairs={{0,1},{1,0},{2,3},{3,2},{4,5},{5,4},{6,7},{7,6},{8,9},{9,8},{10,11... | collective-permute-start | bytes 983048 | tf_op jit(solution)/shard_map/ppermute | solution.py:273
  121.6 2.8 %collective-permute-start.5 = (bf16[256,640]{1,0:T(8,128)(2,1)S(1)}, bf16[256,640]{1,0:T(8,128)(2,1)S(1)}, u32[]{:S(2)}, u32[]{:S(2)}) collective-permute-start(bf16[256,640]{1,0:T(8,128)(2,1)S(1)} %collective-permute-done.4), channel_id=1, source_target_pairs={{0,1},{1,0},{2,3},{3,2},{4,5},{5,4},{6,7},{7,6},{8,9},{9,8},{10,11... | collective-permute-start | bytes 983048 | tf_op jit(solution)/shard_map/ppermute | solution.py:273
  122.5 1.1 copy-start.5
  123.3 1.2 copy-start
  125.3 1.1 copy-start.6
  125.3 1.1 copy-start.7
  126.4 6.7 %copy-start.1 = (bf16[640,640]{1,0:T(8,128)(2,1)S(1)}, bf16[640,640]{1,0:T(8,128)(2,1)}, u32[]{:S(2)}) copy-start(bf16[640,640]{1,0:T(8,128)(2,1)} %get-tuple-element.70) | copy-start | bytes 2457604
  126.5 7.4 %copy-start.4 = (bf16[640,640]{1,0:T(8,128)(2,1)S(1)}, bf16[640,640]{1,0:T(8,128)(2,1)}, u32[]{:S(2)}) copy-start(bf16[640,640]{1,0:T(8,128)(2,1)} %get-tuple-element.68) | copy-start | bytes 2457604
  129.8 3.3 %collective-permute-start.13 = (bf16[256,640]{1,0:T(8,128)(2,1)S(1)}, bf16[256,640]{1,0:T(8,128)(2,1)S(1)}, u32[]{:S(2)}, u32[]{:S(2)}) collective-permute-start(bf16[256,640]{1,0:T(8,128)(2,1)S(1)} %collective-permute-done.11), channel_id=1, source_target_pairs={{0,1},{1,0},{2,3},{3,2},{4,5},{5,4},{6,7},{7,6},{8,9},{9,8},{10,11... | collective-permute-start | bytes 983048 | tf_op jit(solution)/shard_map/ppermute | solution.py:273
  131.9 2.0 %collective-permute-start.12 = (bf16[256,640]{1,0:T(8,128)(2,1)S(1)}, bf16[256,640]{1,0:T(8,128)(2,1)S(1)}, u32[]{:S(2)}, u32[]{:S(2)}) collective-permute-start(bf16[256,640]{1,0:T(8,128)(2,1)S(1)} %collective-permute-done.10), channel_id=1, source_target_pairs={{0,1},{1,0},{2,3},{3,2},{4,5},{5,4},{6,7},{7,6},{8,9},{9,8},{10,11... | collective-permute-start | bytes 983048 | tf_op jit(solution)/shard_map/ppermute | solution.py:273

commit v10 on v9

--- a/solution.py
+++ b/solution.py
@@ -326,18 +326,24 @@
     attended = attend(lists[1], got, got_other, attend(lists[0], got))
     own, low, high = select(source, exchange(attended))
     below_low, above_high = along_y(low, 1), along_y(high, 3)
-    below_high = along_y(high, 1)
-    own_other = swap(own)
-    above_low = along_y(low, 3)
+    own_other, low, high = lax.optimization_barrier((swap(own), low, high))
+    below_high, above_low = along_y(high, 1), along_y(low, 3)
     far_low, far_high = along_y(below_low, 1), along_y(above_high, 3)
     total = product(own, own_other, weights[0])
-    near = ((below_high, weights[2]), (above_low, weights[3]), (below_low, weights[1]), (above_high, weights[4]))
-    for block, weight in near:
+    for block, weight in zip((below_low, above_high, below_high, above_low), (weights[1], weights[4], weights[2], weights[3])):
         total = total + project(block, weight)
     base = residual_in.astype(jnp.float32) + gate_scale * by_rows(total)
     base, far_low, far_high = lax.optimization_barrier((base, far_low, far_high))
-    far = project(far_low, weights[5]) + project(far_high, weights[6])
-    return (base + gate_scale * by_rows(far)).astype(jnp.bfloat16)
+
+    def far_product(low, high):
+        low = jnp.dot(low, weights[5], preferred_element_type=jnp.float32)
+        return low + jnp.dot(high, weights[6], preferred_element_type=jnp.float32)
+
+    mine, other_low, other_high = lax.optimization_barrier(
+        (far_product(far_low, far_high), swap(far_low), swap(far_high))
+    )
+    theirs = far_product(other_low, other_high)
+    return (base + gate_scale * by_rows(jnp.concatenate([mine, theirs], axis=0))).astype(jnp.bfloat16)
 
 
 def solution(mesh):

time: 138 us -> 137 us (level); the launches traced: 136 us -> 137 us
  matrix products: 7.41 us -> 11.3 us
  starting transfers between devices: 25.1 us -> 22.9 us
  waiting for transfers between devices: 24.6 us -> 22.5 us
  blocking collectives: 20.9 us -> 22.4 us
    dot_general x7 -> x5, matrix products: 7.03 us -> 9.04 us  [product(): jnp.dot(jnp.concatenate([block, other], axis=0), weight, preferred_elemen...]
    dot_general x0 -> x4, matrix products: none -> 1.84 us  [the longest x2 0.92 us: far_product(): low = jnp.dot(low, weights[5], preferred_element_type=jnp.float32)]
    all_to_all x1, blocking collectives: 20.9 us -> 22.4 us  [exchange(): lax.all_to_all(block, TOKENS_AXES, split_axis=0, concat_axis=0, tiled=True)]
  transfers between devices with their start and end apart: 15 -> 15, of which waited for: 6 -> 4; matrix products, arithmetic and copies ran while one was open for 17% -> 20% of each run, Pallas kernels for 11% -> 11%
where the time goes in v10:
time: 137 us
  Pallas kernels  28.1 us (21%)
  starting transfers between devices  22.9 us (17%)
  waiting for transfers between devices  22.5 us (16%)
  blocking collectives  22.4 us (16%)
  other arithmetic  13.7 us (10%)
  matrix products  11.3 us (8%)
  local copies, waits for them, and re-layouts  9.34 us (7%)
  between operations  6.59 us (5%)
    all_to_all x1, blocking collectives, exchange(): lax.all_to_all(block, TOKENS_AXES, split_axis=0, concat_axis=0, tiled=True)  22.4 us
    ppermute x6, waiting for transfers between devices, along_y(): lax.ppermute(block, 'y', [(i, (i + step) % PLANES) for i in range(PLANES)])  11.4 us
    all_to_all x1, waiting for transfers between devices, exchange(): lax.all_to_all(block, TOKENS_AXES, split_axis=0, concat_axis=0, tiled=True)  10.8 us
    ppermute x8, starting transfers between devices, swap(): return lax.ppermute(block, 'c', [(0, 1), (1, 0)])  9.07 us
    dot_general x5, matrix products, product(): jnp.dot(jnp.concatenate([block, other], axis=0), weight, preferred_elemen...  9.04 us
    all_to_all x1, starting transfers between devices, exchange(): lax.all_to_all(block, TOKENS_AXES, split_axis=0, concat_axis=0, tiled=True)  8.44 us
    pallas_call x1, Pallas kernels, attend(): pl.pallas_call(functools.partial(first_kernel, scale), in_specs=[smem] *...  7.9 us
    pallas_call x1, Pallas kernels, attend(): pl.pallas_call(functools.partial(second_kernel, scale), in_specs=[smem] *...  6.61 us
  transfers between devices with their start and end apart: 15, of which 4 were waited for; matrix products, arithmetic and copies ran while one was open for 20% of the time, Pallas kernels for 11%

profile of v10, /device:TPU:1, one launch (start us, length us, event | category | flops | bytes accessed | tf_op | source)
XLA Modules:
  0.0 136.7 jit_solution(2703796850600840294)
XLA Ops:
  0.0 2.1 %fusion.56 = (s32[40,64]{1,0:T(8,128)S(1)}, s32[40]{0:T(128)S(1)}) fusion(s32[40,64,64]{2,1,0:T(8,128)} %param.13), kind=kLoop, calls=%fused_computation.159 | loop fusion | flops 325080 | bytes 665760 | tf_op jit(solution)/shard_map/reduce_sum | solution.py:280
  4.1 4.6 %shard_map.73 = bf16[16,768,128]{2,1,0:T(8,128)(2,1)} custom-call(s32[17]{0:T(128)} %pad_add_fusion.heads, bf16[512,5120]{1,0:T(8,128)(2,1)} %q_ref.1, bf16[512,5120]{1,0:T(8,128)(2,1)} %k_ref.1, bf16[512,5120]{1,0:T(8,128)(2,1)} %v_ref.1), custom_call_target="tpu_custom_call" | custom-call | tf_op jit(solution)/shard_map/pallas_call | solution.py:78
  8.6 8.4 %all-to-all-start = ((bf16[16,768,128]{2,1,0:T(8,128)(2,1)}), bf16[16,768,128]{2,1,0:T(8,128)(2,1)S(1)}, u32[]{:S(2)}, u32[]{:S(2)}) async-start(bf16[16,768,128]{2,1,0:T(8,128)(2,1)} %shard_map.73), calls=%async_computation | async-start | bytes 6291456 | tf_op jit(solution)/shard_map/all_to_all | solution.py:265
  23.3 1.6 %reshape.338 = s32[32,16,2,2]{3,2,1,0:T(2,128)} reshape(s32[16,1,2,64]{3,2,1,0:T(2,128)S(1)} %constant_dynamic-slice_fusion.3) | data formatting | bytes 16384 | tf_op jit(solution)/shard_map/reshape | solution.py:308
  25.4 3.1 %fusion.57 = (s32[32]{0:T(128)S(1)}, s32[32,16,1,2]{3,2,1,0:T(1,128)}, s32[32]{0:T(128)S(1)}, s32[32,16,1,2]{3,2,1,0:T(1,128)S(1)}) fusion(s32[32,16,2,2]{3,2,1,0:T(2,128)} %reshape.338, s32[]{:T(128)S(6)} %select_n.211, s32[]{:T(128)S(6)} %select_n.198), kind=kLoop, calls=%fused_computation.160 | loop fusion | flops 1984 | bytes 16648 | tf_op jit(solution)/shard_map/reduce_sum | solution.py:181
  37.2 1.2 compare_select_fusion.2
  40.1 6.6 %shard_map.74 = (bf16[1280,640]{1,0:T(8,128)(2,1)}, bf16[640,640]{1,0:T(8,128)(2,1)}, bf16[640,640]{1,0:T(8,128)(2,1)}, bf16[640,640]{1,0:T(8,128)(2,1)}, bf16[6...) custom-call(s32[40]{0:T(128)} %pad_add_fusion.1.heads, bf16[5120,640]{1,0:T(8,128)(2,1)} %w_ref.1), custom_call_target="tpu_custom_call" | custom-call | tf_op jit(solution)/shard_map/pallas_call | solution.py:250
  46.7 10.8 %all-to-all-done = bf16[16,768,128]{2,1,0:T(8,128)(2,1)S(1)} async-done(((bf16[16,768,128]{2,1,0:T(8,128)(2,1)}), bf16[16,768,128]{2,1,0:T(8,128)(2,1)S(1)}, u32[]{:S(2)}, u32[]{:S(2)}) %all-to-all-start) | async-done | bytes 3145760 | tf_op jit(solution)/shard_map/all_to_all | solution.py:265
  57.5 2.9 %collective-permute-start = (bf16[16,6,128,128]{3,2,1,0:T(8,128)(2,1)S(1)}, bf16[16,6,128,128]{3,2,1,0:T(8,128)(2,1)S(1)}, u32[]{:S(2)}, u32[]{:S(2)}) collective-permute-start(bf16[16,6,128,128]{3,2,1,0:T(8,128)(2,1)S(1)} %bitcast.53), channel_id=1, source_target_pairs={{0,1},{1,0},{2,3},{3,2},{4,5},{5,4},{6,7},{7,6},{8,9},{9,8},{10,11... | collective-permute-start | bytes 9437192 | tf_op jit(solution)/shard_map/ppermute | solution.py:273
  60.4 7.9 %shard_map.75 = (f32[32,128,128]{2,1,0:T(8,128)S(1)}, f32[32,1,128]{2,1,0:T(1,128)S(1)}, f32[32,1,128]{2,1,0:T(1,128)S(1)}) custom-call(s32[1]{0:T(128)} %bitcast.10.meta, s32[256]{0:T(256)S(1)} %broadcast_minimum_fusion.1.q_of, s32[1024]{0:T(1024)S(1)} %convert_element_type.96.k_of, s32[256]{0:T(256)S(1)} %get-tuple-element.60.valid_of, ...), custom_call_target="tpu_custom_call" | custom-call | flops 4000000000 | bytes 8388608 | tf_op jit(solution)/shard_map/pallas_call | solution.py:162
  68.3 6.6 %shard_map.76 = bf16[16,2,128,128]{3,2,1,0:T(8,128)(2,1)S(1)} custom-call(s32[1]{0:T(128)} %bitcast.18.meta, s32[256]{0:T(256)S(1)} %broadcast_minimum_fusion.q_of, s32[1024]{0:T(1024)S(1)} %convert_element_type.102.k_of, s32[256]{0:T(256)S(1)} %get-tuple-element.55.valid_of, bf16[16,6,128,128]{3,2,1,0:T(8,128)(2,1)S(1)} %bitcast.55, ...), custom_call_target="tpu_custom_call" | custom-call | flops 4000000000 | bytes 8388608 | tf_op jit(solution)/shard_map/pallas_call | solution.py:169
  74.9 22.4 %all_to_all.10.got_ref = bf16[16,2,128,128]{3,2,1,0:T(8,128)(2,1)} all-to-all(bf16[16,2,128,128]{3,2,1,0:T(8,128)(2,1)S(1)} %shard_map.76), channel_id=1, replica_groups=mesh['x'=4,'z'=4,'y'=4,'c'=2] {'x','z'}, dimensions={0} | all-to-all | bytes 2097152 | tf_op jit(solution)/shard_map/all_to_all | solution.py:265
  97.3 2.4 %shard_map.77 = (bf16[256,1280]{1,0:T(8,128)(2,1)}, bf16[256,640]{1,0:T(8,128)(2,1)}, bf16[256,640]{1,0:T(8,128)(2,1)}) custom-call(s32[20]{0:T(128)} %reshape.327.source, bf16[16,2,128,128]{3,2,1,0:T(8,128)(2,1)} %all_to_all.10.got_ref), custom_call_target="tpu_custom_call" | custom-call | tf_op jit(solution)/shard_map/pallas_call | solution.py:219
  99.8 2.3 %collective-permute-start.1 = (bf16[256,1280]{1,0:T(8,128)(2,1)}, bf16[256,1280]{1,0:T(8,128)(2,1)S(1)}, u32[]{:S(2)}, u32[]{:S(2)}) collective-permute-start(bf16[256,1280]{1,0:T(8,128)(2,1)} %get-tuple-element.64), channel_id=1, source_target_pairs={{0,1},{1,0},{2,3},{3,2},{4,5},{5,4},{6,7},{7,6},{8,9},{9,8},{10,11... | collective-permute-start | bytes 1966088 | tf_op jit(solution)/shard_map/ppermute | solution.py:273
  102.8 1.9 %collective-permute-start.4 = (bf16[256,640]{1,0:T(8,128)(2,1)}, bf16[256,640]{1,0:T(8,128)(2,1)S(1)}, u32[]{:S(2)}, u32[]{:S(2)}) collective-permute-start(bf16[256,640]{1,0:T(8,128)(2,1)} %get-tuple-element.71), channel_id=1, source_target_pairs={{0,6},{2,0},{4,2},{6,4},{1,7},{3,1},{5,3},{7,5},{8,14},{10,8},{12,... | collective-permute-start | bytes 983048 | tf_op jit(solution)/shard_map/ppermute | solution.py:269
  104.8 8.2 %collective-permute-done.2 = bf16[256,640]{1,0:T(8,128)(2,1)} collective-permute-done((bf16[256,640]{1,0:T(8,128)(2,1)}, bf16[256,640]{1,0:T(8,128)(2,1)}, u32[]{:S(2)}, u32[]{:S(2)}) %collective-permute-start.2) | collective-permute-done | bytes 327712 | tf_op jit(solution)/shard_map/ppermute | solution.py:269
  112.9 1.2 collective-permute-start.3
  114.1 1.5 %collective-permute-start.10 = (bf16[256,640]{1,0:T(8,128)(2,1)}, bf16[256,640]{1,0:T(8,128)(2,1)S(1)}, u32[]{:S(2)}, u32[]{:S(2)}) collective-permute-start(bf16[256,640]{1,0:T(8,128)(2,1)} %collective-permute-done.2), channel_id=1, source_target_pairs={{0,2},{2,4},{4,6},{6,0},{1,3},{3,5},{5,7},{7,1},{8,10},{10,12},{12... | collective-permute-start | bytes 983048 | tf_op jit(solution)/shard_map/ppermute | solution.py:269
  115.6 1.2 collective-permute-start.11
  116.8 3.2 %collective-permute-done.6 = bf16[256,640]{1,0:T(8,128)(2,1)} collective-permute-done((bf16[256,640]{1,0:T(8,128)(2,1)}, bf16[256,640]{1,0:T(8,128)(2,1)}, u32[]{:S(2)}, u32[]{:S(2)}) %collective-permute-start.6) | collective-permute-done | bytes 327712 | tf_op jit(solution)/shard_map/ppermute | solution.py:269
  121.1 2.8 %fusion.2 = f32[512,640]{1,0:T(8,128)S(1)} fusion(bf16[1280,640]{1,0:T(8,128)(2,1)} %get-tuple-element.68, bf16[256,1280]{1,0:T(8,128)(2,1)S(1)} %collective-permute-done.1, bf16[256,1280]{1,0:T(8,128)(2,1)} %get-tuple-element.64), kind=kOutput, calls=%fused_computation.5 | convolution fusion | flops 841482240 | bytes 4259840 | tf_op jit(solution)/shard_map/dot_general | solution.py:317
  124.9 1.8 %convolution_add_fusion.1 = f32[512,640]{1,0:T(8,128)S(1)} fusion(f32[512,640]{1,0:T(8,128)S(1)} %fusion.2, bf16[640,640]{1,0:T(8,128)(2,1)S(1)} %copy-done.5, bf16[256,640]{1,0:T(8,128)(2,1)} %collective-permute-done.3, bf16[256,640]{1,0:T(8,128)(2,1)} %collective-permute-done.2), kind=kOutput, calls=%fused_computation.3 | convolution fusion | flops 421068800 | bytes 4096000 | tf_op jit(solution)/shard_map/dot_general | solution.py:317
  126.8 1.8 %fusion.15 = f32[512,640]{1,0:T(8,128)S(1)} fusion(bf16[640,640]{1,0:T(8,128)(2,1)S(1)} %copy-done.4, bf16[256,640]{1,0:T(8,128)(2,1)S(1)} %collective-permute-done.7, bf16[256,640]{1,0:T(8,128)(2,1)} %collective-permute-done.6), kind=kOutput, calls=%fused_computation.22 | convolution fusion | flops 420741120 | bytes 2785280 | tf_op jit(solution)/shard_map/dot_general | solution.py:317
  128.6 1.8 %fusion.19 = f32[512,640]{1,0:T(8,128)S(1)} fusion(bf16[640,640]{1,0:T(8,128)(2,1)S(1)} %copy-done.3, bf16[256,640]{1,0:T(8,128)(2,1)S(1)} %collective-permute-done.9, bf16[256,640]{1,0:T(8,128)(2,1)} %collective-permute-done.8), kind=kOutput, calls=%fused_computation.26 | convolution fusion | flops 420741120 | bytes 2785280 | tf_op jit(solution)/shard_map/dot_general | solution.py:317
  (118 shorter events, 21.8 us)
Async XLA Ops:
  8.6 48.9 %all-to-all-start = ((bf16[16,768,128]{2,1,0:T(8,128)(2,1)}), bf16[16,768,128]{2,1,0:T(8,128)(2,1)S(1)}, u32[]{:S(2)}, u32[]{:S(2)}) async-start(bf16[16,768,128]{2,1,0:T(8,128)(2,1)} %shard_map.73), calls=%async_computation | async-start | bytes 6291456 | tf_op jit(solution)/shard_map/all_to_all | solution.py:265
  57.5 10.8 %collective-permute-start = (bf16[16,6,128,128]{3,2,1,0:T(8,128)(2,1)S(1)}, bf16[16,6,128,128]{3,2,1,0:T(8,128)(2,1)S(1)}, u32[]{:S(2)}, u32[]{:S(2)}) collective-permute-start(bf16[16,6,128,128]{3,2,1,0:T(8,128)(2,1)S(1)} %bitcast.53), channel_id=1, source_target_pairs={{0,1},{1,0},{2,3},{3,2},{4,5},{5,4},{6,7},{7,6},{8,9},{9,8},{10,11... | collective-permute-start | bytes 9437192 | tf_op jit(solution)/shard_map/ppermute | solution.py:273
  99.8 5.0 %collective-permute-start.1 = (bf16[256,1280]{1,0:T(8,128)(2,1)}, bf16[256,1280]{1,0:T(8,128)(2,1)S(1)}, u32[]{:S(2)}, u32[]{:S(2)}) collective-permute-start(bf16[256,1280]{1,0:T(8,128)(2,1)} %get-tuple-element.64), channel_id=1, source_target_pairs={{0,1},{1,0},{2,3},{3,2},{4,5},{5,4},{6,7},{7,6},{8,9},{9,8},{10,11... | collective-permute-start | bytes 1966088 | tf_op jit(solution)/shard_map/ppermute | solution.py:273
  102.1 10.9 %collective-permute-start.2 = (bf16[256,640]{1,0:T(8,128)(2,1)}, bf16[256,640]{1,0:T(8,128)(2,1)}, u32[]{:S(2)}, u32[]{:S(2)}) collective-permute-start(bf16[256,640]{1,0:T(8,128)(2,1)} %get-tuple-element.73), channel_id=1, source_target_pairs={{0,2},{2,4},{4,6},{6,0},{1,3},{3,5},{5,7},{7,1},{8,10},{10,12},{12... | collective-permute-start | bytes 983048 | tf_op jit(solution)/shard_map/ppermute | solution.py:269
  102.8 12.8 %collective-permute-start.4 = (bf16[256,640]{1,0:T(8,128)(2,1)}, bf16[256,640]{1,0:T(8,128)(2,1)S(1)}, u32[]{:S(2)}, u32[]{:S(2)}) collective-permute-start(bf16[256,640]{1,0:T(8,128)(2,1)} %get-tuple-element.71), channel_id=1, source_target_pairs={{0,6},{2,0},{4,2},{6,4},{1,7},{3,1},{5,3},{7,5},{8,14},{10,8},{12,... | collective-permute-start | bytes 983048 | tf_op jit(solution)/shard_map/ppermute | solution.py:269
  104.8 15.2 %collective-permute-start.6 = (bf16[256,640]{1,0:T(8,128)(2,1)}, bf16[256,640]{1,0:T(8,128)(2,1)}, u32[]{:S(2)}, u32[]{:S(2)}) collective-permute-start(bf16[256,640]{1,0:T(8,128)(2,1)} %get-tuple-element.71), channel_id=1, source_target_pairs={{0,2},{2,4},{4,6},{6,0},{1,3},{3,5},{5,7},{7,1},{8,10},{10,12},{12... | collective-permute-start | bytes 983048 | tf_op jit(solution)/shard_map/ppermute | solution.py:269
  112.9 11.0 %collective-permute-start.3 = (bf16[256,640]{1,0:T(8,128)(2,1)}, bf16[256,640]{1,0:T(8,128)(2,1)}, u32[]{:S(2)}, u32[]{:S(2)}) collective-permute-start(bf16[256,640]{1,0:T(8,128)(2,1)} %collective-permute-done.2), channel_id=1, source_target_pairs={{0,1},{1,0},{2,3},{3,2},{4,5},{5,4},{6,7},{7,6},{8,9},{9,8},{10,11... | collective-permute-start | bytes 983048 | tf_op jit(solution)/shard_map/ppermute | solution.py:273
  114.1 10.0 %collective-permute-start.8 = (bf16[256,640]{1,0:T(8,128)(2,1)}, bf16[256,640]{1,0:T(8,128)(2,1)}, u32[]{:S(2)}, u32[]{:S(2)}) collective-permute-start(bf16[256,640]{1,0:T(8,128)(2,1)} %get-tuple-element.73), channel_id=1, source_target_pairs={{0,6},{2,0},{4,2},{6,4},{1,7},{3,1},{5,3},{7,5},{8,14},{10,8},{12,... | collective-permute-start | bytes 983048 | tf_op jit(solution)/shard_map/ppermute | solution.py:269
  114.1 10.8 %copy-start.5 = (bf16[640,640]{1,0:T(8,128)(2,1)S(1)}, bf16[640,640]{1,0:T(8,128)(2,1)}, u32[]{:S(2)}) copy-start(bf16[640,640]{1,0:T(8,128)(2,1)} %get-tuple-element.69) | copy-start | bytes 2457604
  114.1 18.4 %collective-permute-start.10 = (bf16[256,640]{1,0:T(8,128)(2,1)}, bf16[256,640]{1,0:T(8,128)(2,1)S(1)}, u32[]{:S(2)}, u32[]{:S(2)}) collective-permute-start(bf16[256,640]{1,0:T(8,128)(2,1)} %collective-permute-done.2), channel_id=1, source_target_pairs={{0,2},{2,4},{4,6},{6,0},{1,3},{3,5},{5,7},{7,1},{8,10},{10,12},{12... | collective-permute-start | bytes 983048 | tf_op jit(solution)/shard_map/ppermute | solution.py:269
  115.6 17.0 %collective-permute-start.11 = (bf16[256,640]{1,0:T(8,128)(2,1)S(1)}, bf16[256,640]{1,0:T(8,128)(2,1)S(1)}, u32[]{:S(2)}, u32[]{:S(2)}) collective-permute-start(bf16[256,640]{1,0:T(8,128)(2,1)S(1)} %collective-permute-done.4), channel_id=1, source_target_pairs={{0,6},{2,0},{4,2},{6,4},{1,7},{3,1},{5,3},{7,5},{8,14},{10,8},{12,... | collective-permute-start | bytes 983048 | tf_op jit(solution)/shard_map/ppermute | solution.py:269
  120.0 6.8 %collective-permute-start.7 = (bf16[256,640]{1,0:T(8,128)(2,1)}, bf16[256,640]{1,0:T(8,128)(2,1)S(1)}, u32[]{:S(2)}, u32[]{:S(2)}) collective-permute-start(bf16[256,640]{1,0:T(8,128)(2,1)} %collective-permute-done.6), channel_id=1, source_target_pairs={{0,1},{1,0},{2,3},{3,2},{4,5},{5,4},{6,7},{7,6},{8,9},{9,8},{10,11... | collective-permute-start | bytes 983048 | tf_op jit(solution)/shard_map/ppermute | solution.py:273
  124.0 2.8 %copy-start.4 = (bf16[640,640]{1,0:T(8,128)(2,1)S(1)}, bf16[640,640]{1,0:T(8,128)(2,1)}, u32[]{:S(2)}) copy-start(bf16[640,640]{1,0:T(8,128)(2,1)} %get-tuple-element.72) | copy-start | bytes 2457604
  124.0 6.5 %collective-permute-start.5 = (bf16[256,640]{1,0:T(8,128)(2,1)S(1)}, bf16[256,640]{1,0:T(8,128)(2,1)S(1)}, u32[]{:S(2)}, u32[]{:S(2)}) collective-permute-start(bf16[256,640]{1,0:T(8,128)(2,1)S(1)} %collective-permute-done.4), channel_id=1, source_target_pairs={{0,1},{1,0},{2,3},{3,2},{4,5},{5,4},{6,7},{7,6},{8,9},{9,8},{10,11... | collective-permute-start | bytes 983048 | tf_op jit(solution)/shard_map/ppermute | solution.py:273
  124.1 4.5 %collective-permute-start.9 = (bf16[256,640]{1,0:T(8,128)(2,1)}, bf16[256,640]{1,0:T(8,128)(2,1)S(1)}, u32[]{:S(2)}, u32[]{:S(2)}) collective-permute-start(bf16[256,640]{1,0:T(8,128)(2,1)} %collective-permute-done.8), channel_id=1, source_target_pairs={{0,1},{1,0},{2,3},{3,2},{4,5},{5,4},{6,7},{7,6},{8,9},{9,8},{10,11... | collective-permute-start | bytes 983048 | tf_op jit(solution)/shard_map/ppermute | solution.py:273
  126.8 1.9 %copy-start.3 = (bf16[640,640]{1,0:T(8,128)(2,1)S(1)}, bf16[640,640]{1,0:T(8,128)(2,1)}, u32[]{:S(2)}) copy-start(bf16[640,640]{1,0:T(8,128)(2,1)} %get-tuple-element.74) | copy-start | bytes 2457604
  128.6 1.8 %copy-start.2 = (bf16[640,640]{1,0:T(8,128)(2,1)S(1)}, bf16[640,640]{1,0:T(8,128)(2,1)}, u32[]{:S(2)}) copy-start(bf16[640,640]{1,0:T(8,128)(2,1)} %get-tuple-element.70) | copy-start | bytes 2457604
  131.3 1.1 copy-start.6
  131.3 1.1 copy-start.7
  132.4 1.1 copy-start
  132.5 1.4 %copy-start.1 = (bf16[640,640]{1,0:T(8,128)(2,1)S(1)}, bf16[640,640]{1,0:T(8,128)(2,1)}, u32[]{:S(2)}) copy-start(bf16[640,640]{1,0:T(8,128)(2,1)} %get-tuple-element.77) | copy-start | bytes 2457604
  132.6 1.9 %collective-permute-start.12 = (bf16[256,640]{1,0:T(8,128)(2,1)S(1)}, bf16[256,640]{1,0:T(8,128)(2,1)S(1)}, u32[]{:S(2)}, u32[]{:S(2)}) collective-permute-start(bf16[256,640]{1,0:T(8,128)(2,1)S(1)} %collective-permute-done.10), channel_id=1, source_target_pairs={{0,1},{1,0},{2,3},{3,2},{4,5},{5,4},{6,7},{7,6},{8,9},{9,8},{10,11... | collective-permute-start | bytes 983048 | tf_op jit(solution)/shard_map/ppermute | solution.py:273
  132.7 2.1 %collective-permute-start.13 = (bf16[256,640]{1,0:T(8,128)(2,1)S(1)}, bf16[256,640]{1,0:T(8,128)(2,1)S(1)}, u32[]{:S(2)}, u32[]{:S(2)}) collective-permute-start(bf16[256,640]{1,0:T(8,128)(2,1)S(1)} %collective-permute-done.11), channel_id=1, source_target_pairs={{0,1},{1,0},{2,3},{3,2},{4,5},{5,4},{6,7},{7,6},{8,9},{9,8},{10,11... | collective-permute-start | bytes 983048 | tf_op jit(solution)/shard_map/ppermute | solution.py:273

commit v11 on v9

--- a/solution.py
+++ b/solution.py
@@ -48,8 +48,8 @@
     return chips, first
 
 
-def pack_kernel(heads, q_ref, k_ref, v_ref, out_ref, held, values, sem_v, sem_kq, sem_out):
-    rows = pl.ds(pl.multiple_of(heads[CHIPS] * HALF, HALF), HALF)
+def pack_kernel(heads, core, q_ref, k_ref, v_ref, out_ref, held, values, sem_v, sem_kq, sem_out):
+    rows = pl.ds(pl.multiple_of(core[0] * HALF, HALF), HALF)
     cols = [pl.ds(pl.multiple_of(heads[t] * TILE, TILE), TILE) for t in range(CHIPS)]
     first = [pltpu.make_async_copy(v_ref.at[rows, cols[t]], values.at[t], sem_v.at[t]) for t in range(CHIPS)]
     others = [
@@ -73,11 +73,11 @@
 
 
 def pack(queries, keys, values, chip_heads, core):
-    scalars = jnp.concatenate([chip_heads, core[None]]).astype(jnp.int32)
+    smem = pl.BlockSpec(memory_space=pltpu.SMEM)
     hbm = pl.BlockSpec(memory_space=pl.ANY)
     return pl.pallas_call(
         pack_kernel,
-        in_specs=[pl.BlockSpec(memory_space=pltpu.SMEM)] + [hbm] * 3,
+        in_specs=[smem] * 2 + [hbm] * 3,
         out_specs=hbm,
         out_shape=jax.ShapeDtypeStruct((CHIPS, 6 * TILE, TILE), jnp.bfloat16),
         scratch_shapes=[
@@ -88,7 +88,7 @@
             pltpu.SemaphoreType.DMA((CHIPS,)),
         ],
         compiler_params=pltpu.CompilerParams(vmem_limit_bytes=60 * 2**20),
-    )(scalars, queries, keys, values)
+    )(chip_heads.astype(jnp.int32), core.reshape(1).astype(jnp.int32), queries, keys, values)
 
 
 def attend_items(scale, meta, q_of, k_of, valid_of, query_ref, key_ref, acc_ref, max_ref, sum_ref):
@@ -326,13 +326,11 @@
     attended = attend(lists[1], got, got_other, attend(lists[0], got))
     own, low, high = select(source, exchange(attended))
     below_low, above_high = along_y(low, 1), along_y(high, 3)
-    below_high = along_y(high, 1)
-    own_other = swap(own)
-    above_low = along_y(low, 3)
+    own_other, low, high = lax.optimization_barrier((swap(own), low, high))
+    below_high, above_low = along_y(high, 1), along_y(low, 3)
     far_low, far_high = along_y(below_low, 1), along_y(above_high, 3)
     total = product(own, own_other, weights[0])
-    near = ((below_high, weights[2]), (above_low, weights[3]), (below_low, weights[1]), (above_high, weights[4]))
-    for block, weight in near:
+    for block, weight in zip((below_low, above_high, below_high, above_low), (weights[1], weights[4], weights[2], weights[3])):
         total = total + project(block, weight)
     base = residual_in.astype(jnp.float32) + gate_scale * by_rows(total)
     base, far_low, far_high = lax.optimization_barrier((base, far_low, far_high))

time: 138 us -> 136 us (0.986); the launches traced: 136 us -> 136 us
  matrix products: 7.41 us -> 10.8 us
  waiting for transfers between devices: 24.6 us -> 22 us
  blocking collectives: 20.9 us -> 23.3 us
  Pallas kernels: 28.2 us -> 26.2 us
  starting transfers between devices: 25.1 us -> 23.6 us
    dot_general x7, matrix products: 7.03 us -> 10.5 us  [product(): jnp.dot(jnp.concatenate([block, other], axis=0), weight, preferred_elemen...]
    ppermute x6, waiting for transfers between devices: 12.6 us -> 10.1 us  [along_y(): lax.ppermute(block, 'y', [(i, (i + step) % PLANES) for i in range(PLANES)])]
    all_to_all x1, blocking collectives: 20.9 us -> 23.3 us  [exchange(): lax.all_to_all(block, TOKENS_AXES, split_axis=0, concat_axis=0, tiled=True)]
    pallas_call x1, Pallas kernels: 7.89 us -> 6.12 us  [attend(): pl.pallas_call(functools.partial(first_kernel, scale), in_specs=[smem] *...]
    ppermute x8, starting transfers between devices: 10 us -> 8.55 us  [swap(): return lax.ppermute(block, 'c', [(0, 1), (1, 0)])]
    unnamed x20 -> x22, local copies, waits for them, and re-layouts: 2.72 us -> 2.95 us
  transfers between devices with their start and end apart: 15 -> 15, of which waited for: 6 -> 4; matrix products, arithmetic and copies ran while one was open for 17% -> 20% of each run, Pallas kernels for 11% -> 9%
where the time goes in v11:
time: 136 us
  Pallas kernels  26.2 us (19%)
  starting transfers between devices  23.6 us (17%)
  blocking collectives  23.3 us (17%)
  waiting for transfers between devices  22 us (16%)
  other arithmetic  13.6 us (10%)
  matrix products  10.8 us (8%)
  local copies, waits for them, and re-layouts  9.6 us (7%)
  between operations  6.6 us (5%)
    all_to_all x1, blocking collectives, exchange(): lax.all_to_all(block, TOKENS_AXES, split_axis=0, concat_axis=0, tiled=True)  23.3 us
    all_to_all x1, waiting for transfers between devices, exchange(): lax.all_to_all(block, TOKENS_AXES, split_axis=0, concat_axis=0, tiled=True)  10.7 us
    dot_general x7, matrix products, product(): jnp.dot(jnp.concatenate([block, other], axis=0), weight, preferred_elemen...  10.5 us
    ppermute x6, waiting for transfers between devices, along_y(): lax.ppermute(block, 'y', [(i, (i + step) % PLANES) for i in range(PLANES)])  10.1 us
    ppermute x8, starting transfers between devices, swap(): return lax.ppermute(block, 'c', [(0, 1), (1, 0)])  8.55 us
    all_to_all x1, starting transfers between devices, exchange(): lax.all_to_all(block, TOKENS_AXES, split_axis=0, concat_axis=0, tiled=True)  8.44 us
    pallas_call x1, Pallas kernels, attend(): pl.pallas_call(functools.partial(second_kernel, scale), in_specs=[smem] *...  6.61 us
    ppermute x6, starting transfers between devices, along_y(): lax.ppermute(block, 'y', [(i, (i + step) % PLANES) for i in range(PLANES)])  6.59 us
  transfers between devices with their start and end apart: 15, of which 4 were waited for; matrix products, arithmetic and copies ran while one was open for 20% of the time, Pallas kernels for 9%

profile of v11, /device:TPU:1, one launch (start us, length us, event | category | flops | bytes accessed | tf_op | source)
XLA Modules:
  0.0 135.8 jit_solution(4164945365407174259)
XLA Ops:
  0.0 2.1 %fusion.65 = (s32[40,64]{1,0:T(8,128)S(1)}, s32[40]{0:T(128)S(1)}) fusion(s32[40,64,64]{2,1,0:T(8,128)} %param.13), kind=kLoop, calls=%fused_computation.166 | loop fusion | flops 325080 | bytes 665760 | tf_op jit(solution)/shard_map/reduce_sum | solution.py:280
  4.0 4.5 %shard_map.73 = bf16[16,768,128]{2,1,0:T(8,128)(2,1)} custom-call(s32[16]{0:T(128)} %select_reduce_fusion.13.heads, s32[1]{0:T(128)} %bitcast.core, bf16[512,5120]{1,0:T(8,128)(2,1)} %q_ref.1, bf16[512,5120]{1,0:T(8,128)(2,1)} %k_ref.1, bf16[512,5120]{1,0:T(8,128)(2,1)} %v_ref.1), custom_call_target="tpu_custom_call" | custom-call | tf_op jit(solution)/shard_map/pallas_call | solution.py:78
  8.5 8.4 %all-to-all-start = ((bf16[16,768,128]{2,1,0:T(8,128)(2,1)}), bf16[16,768,128]{2,1,0:T(8,128)(2,1)S(1)}, u32[]{:S(2)}, u32[]{:S(2)}) async-start(bf16[16,768,128]{2,1,0:T(8,128)(2,1)} %shard_map.73), calls=%async_computation | async-start | bytes 6291456 | tf_op jit(solution)/shard_map/all_to_all | solution.py:265
  23.1 1.6 %reshape.342 = s32[32,16,2,2]{3,2,1,0:T(2,128)} reshape(s32[16,1,2,64]{3,2,1,0:T(2,128)S(1)} %constant_dynamic-slice_fusion.3) | data formatting | bytes 16384 | tf_op jit(solution)/shard_map/reshape | solution.py:308
  25.3 3.1 %fusion.66 = (s32[32]{0:T(128)S(1)}, s32[32,16,1,2]{3,2,1,0:T(1,128)}, s32[32]{0:T(128)S(1)}, s32[32,16,1,2]{3,2,1,0:T(1,128)S(1)}) fusion(s32[32,16,2,2]{3,2,1,0:T(2,128)} %reshape.342, s32[]{:T(128)S(6)} %select_n.211, s32[]{:T(128)S(6)} %select_n.198), kind=kLoop, calls=%fused_computation.167 | loop fusion | flops 1984 | bytes 16648 | tf_op jit(solution)/shard_map/reduce_sum | solution.py:181
  37.1 1.2 compare_select_fusion.2
  39.9 6.6 %shard_map.74 = (bf16[1280,640]{1,0:T(8,128)(2,1)}, bf16[640,640]{1,0:T(8,128)(2,1)}, bf16[640,640]{1,0:T(8,128)(2,1)}, bf16[640,640]{1,0:T(8,128)(2,1)}, bf16[6...) custom-call(s32[40]{0:T(128)} %pad_add_fusion.heads, bf16[5120,640]{1,0:T(8,128)(2,1)} %w_ref.1), custom_call_target="tpu_custom_call" | custom-call | tf_op jit(solution)/shard_map/pallas_call | solution.py:250
  46.5 10.7 %all-to-all-done = bf16[16,768,128]{2,1,0:T(8,128)(2,1)S(1)} async-done(((bf16[16,768,128]{2,1,0:T(8,128)(2,1)}), bf16[16,768,128]{2,1,0:T(8,128)(2,1)S(1)}, u32[]{:S(2)}, u32[]{:S(2)}) %all-to-all-start) | async-done | bytes 3145760 | tf_op jit(solution)/shard_map/all_to_all | solution.py:265
  57.2 3.1 %collective-permute-start = (bf16[16,6,128,128]{3,2,1,0:T(8,128)(2,1)S(1)}, bf16[16,6,128,128]{3,2,1,0:T(8,128)(2,1)S(1)}, u32[]{:S(2)}, u32[]{:S(2)}) collective-permute-start(bf16[16,6,128,128]{3,2,1,0:T(8,128)(2,1)S(1)} %bitcast.47), channel_id=1, source_target_pairs={{0,1},{1,0},{2,3},{3,2},{4,5},{5,4},{6,7},{7,6},{8,9},{9,8},{10,11... | collective-permute-start | bytes 9437192 | tf_op jit(solution)/shard_map/ppermute | solution.py:273
  60.3 6.1 %shard_map.75 = (f32[32,128,128]{2,1,0:T(8,128)S(1)}, f32[32,1,128]{2,1,0:T(1,128)S(1)}, f32[32,1,128]{2,1,0:T(1,128)S(1)}) custom-call(s32[1]{0:T(128)} %bitcast.10.meta, s32[256]{0:T(256)S(1)} %broadcast_minimum_fusion.1.q_of, s32[1024]{0:T(1024)S(1)} %convert_element_type.96.k_of, s32[256]{0:T(256)S(1)} %get-tuple-element.57.valid_of, ...), custom_call_target="tpu_custom_call" | custom-call | flops 4000000000 | bytes 8388608 | tf_op jit(solution)/shard_map/pallas_call | solution.py:162
  66.4 6.6 %shard_map.76 = bf16[16,2,128,128]{3,2,1,0:T(8,128)(2,1)S(1)} custom-call(s32[1]{0:T(128)} %bitcast.18.meta, s32[256]{0:T(256)S(1)} %broadcast_minimum_fusion.q_of, s32[1024]{0:T(1024)S(1)} %convert_element_type.102.k_of, s32[256]{0:T(256)S(1)} %get-tuple-element.52.valid_of, bf16[16,6,128,128]{3,2,1,0:T(8,128)(2,1)S(1)} %bitcast.49, ...), custom_call_target="tpu_custom_call" | custom-call | flops 4000000000 | bytes 8388608 | tf_op jit(solution)/shard_map/pallas_call | solution.py:169
  73.1 23.3 %all_to_all.10.got_ref = bf16[16,2,128,128]{3,2,1,0:T(8,128)(2,1)} all-to-all(bf16[16,2,128,128]{3,2,1,0:T(8,128)(2,1)S(1)} %shard_map.76), channel_id=1, replica_groups=mesh['x'=4,'z'=4,'y'=4,'c'=2] {'x','z'}, dimensions={0} | all-to-all | bytes 2097152 | tf_op jit(solution)/shard_map/all_to_all | solution.py:265
  96.4 2.4 %shard_map.77 = (bf16[256,1280]{1,0:T(8,128)(2,1)}, bf16[256,640]{1,0:T(8,128)(2,1)}, bf16[256,640]{1,0:T(8,128)(2,1)}) custom-call(s32[20]{0:T(128)} %reshape.331.source, bf16[16,2,128,128]{3,2,1,0:T(8,128)(2,1)} %all_to_all.10.got_ref), custom_call_target="tpu_custom_call" | custom-call | tf_op jit(solution)/shard_map/pallas_call | solution.py:219
  98.8 2.3 %collective-permute-start.1 = (bf16[256,1280]{1,0:T(8,128)(2,1)}, bf16[256,1280]{1,0:T(8,128)(2,1)S(1)}, u32[]{:S(2)}, u32[]{:S(2)}) collective-permute-start(bf16[256,1280]{1,0:T(8,128)(2,1)} %get-tuple-element.61), channel_id=1, source_target_pairs={{0,1},{1,0},{2,3},{3,2},{4,5},{5,4},{6,7},{7,6},{8,9},{9,8},{10,11... | collective-permute-start | bytes 1966088 | tf_op jit(solution)/shard_map/ppermute | solution.py:273
  101.1 1.8 %collective-permute-start.2 = (bf16[256,640]{1,0:T(8,128)(2,1)}, bf16[256,640]{1,0:T(8,128)(2,1)S(1)}, u32[]{:S(2)}, u32[]{:S(2)}) collective-permute-start(bf16[256,640]{1,0:T(8,128)(2,1)} %get-tuple-element.70), channel_id=1, source_target_pairs={{0,2},{2,4},{4,6},{6,0},{1,3},{3,5},{5,7},{7,1},{8,10},{10,12},{12... | collective-permute-start | bytes 983048 | tf_op jit(solution)/shard_map/ppermute | solution.py:269
  104.9 7.0 %collective-permute-done.2 = bf16[256,640]{1,0:T(8,128)(2,1)S(1)} collective-permute-done((bf16[256,640]{1,0:T(8,128)(2,1)}, bf16[256,640]{1,0:T(8,128)(2,1)S(1)}, u32[]{:S(2)}, u32[]{:S(2)}) %collective-permute-start.2) | collective-permute-done | bytes 327712 | tf_op jit(solution)/shard_map/ppermute | solution.py:269
  111.9 1.2 collective-permute-start.3
  113.2 1.3 collective-permute-start.10
  114.5 1.4 collective-permute-start.11
  115.9 3.1 %collective-permute-done.6 = bf16[256,640]{1,0:T(8,128)(2,1)} collective-permute-done((bf16[256,640]{1,0:T(8,128)(2,1)}, bf16[256,640]{1,0:T(8,128)(2,1)}, u32[]{:S(2)}, u32[]{:S(2)}) %collective-permute-start.6) | collective-permute-done | bytes 327712 | tf_op jit(solution)/shard_map/ppermute | solution.py:269
  120.2 2.8 %fusion.2 = f32[512,640]{1,0:T(8,128)S(1)} fusion(bf16[1280,640]{1,0:T(8,128)(2,1)} %get-tuple-element.65, bf16[256,1280]{1,0:T(8,128)(2,1)S(1)} %collective-permute-done.1, bf16[256,1280]{1,0:T(8,128)(2,1)} %get-tuple-element.61), kind=kOutput, calls=%fused_computation.6 | convolution fusion | flops 841482240 | bytes 4259840 | tf_op jit(solution)/shard_map/dot_general | solution.py:317
  123.9 1.7 %convolution_add_fusion.2 = f32[512,640]{1,0:T(8,128)S(1)} fusion(f32[512,640]{1,0:T(8,128)S(1)} %fusion.2, bf16[640,640]{1,0:T(8,128)(2,1)S(1)} %copy-done.5, bf16[256,640]{1,0:T(8,128)(2,1)} %copy-done.7, bf16[256,640]{1,0:T(8,128)(2,1)S(1)} %collective-permute-done.2), kind=kOutput, calls=%fused_computation.4 | convolution fusion | flops 421068800 | bytes 4096000 | tf_op jit(solution)/shard_map/dot_general | solution.py:317
  125.6 1.8 %fusion.15 = f32[512,640]{1,0:T(8,128)S(1)} fusion(bf16[640,640]{1,0:T(8,128)(2,1)S(1)} %copy-done.3, bf16[256,640]{1,0:T(8,128)(2,1)S(1)} %collective-permute-done.7, bf16[256,640]{1,0:T(8,128)(2,1)} %collective-permute-done.6), kind=kOutput, calls=%fused_computation.21 | convolution fusion | flops 420741120 | bytes 2785280 | tf_op jit(solution)/shard_map/dot_general | solution.py:317
  127.5 1.8 %fusion.19 = f32[512,640]{1,0:T(8,128)S(1)} fusion(bf16[640,640]{1,0:T(8,128)(2,1)S(1)} %copy-done.2, bf16[256,640]{1,0:T(8,128)(2,1)S(1)} %collective-permute-done.9, bf16[256,640]{1,0:T(8,128)(2,1)} %collective-permute-done.8), kind=kOutput, calls=%fused_computation.25 | convolution fusion | flops 420741120 | bytes 2785280 | tf_op jit(solution)/shard_map/dot_general | solution.py:317
  (119 shorter events, 23.2 us)
Async XLA Ops:
  8.5 8.5 %copy-start.9 = (s32[16]{0:T(128)S(1)}, s32[16]{0:T(128)}, u32[]{:S(2)}) copy-start(s32[16]{0:T(128)} %select_reduce_fusion.13.heads) | copy-start | bytes 196
  8.5 48.7 %all-to-all-start = ((bf16[16,768,128]{2,1,0:T(8,128)(2,1)}), bf16[16,768,128]{2,1,0:T(8,128)(2,1)S(1)}, u32[]{:S(2)}, u32[]{:S(2)}) async-start(bf16[16,768,128]{2,1,0:T(8,128)(2,1)} %shard_map.73), calls=%async_computation | async-start | bytes 6291456 | tf_op jit(solution)/shard_map/all_to_all | solution.py:265
  57.2 9.2 %collective-permute-start = (bf16[16,6,128,128]{3,2,1,0:T(8,128)(2,1)S(1)}, bf16[16,6,128,128]{3,2,1,0:T(8,128)(2,1)S(1)}, u32[]{:S(2)}, u32[]{:S(2)}) collective-permute-start(bf16[16,6,128,128]{3,2,1,0:T(8,128)(2,1)S(1)} %bitcast.47), channel_id=1, source_target_pairs={{0,1},{1,0},{2,3},{3,2},{4,5},{5,4},{6,7},{7,6},{8,9},{9,8},{10,11... | collective-permute-start | bytes 9437192 | tf_op jit(solution)/shard_map/ppermute | solution.py:273
  98.8 5.0 %collective-permute-start.1 = (bf16[256,1280]{1,0:T(8,128)(2,1)}, bf16[256,1280]{1,0:T(8,128)(2,1)S(1)}, u32[]{:S(2)}, u32[]{:S(2)}) collective-permute-start(bf16[256,1280]{1,0:T(8,128)(2,1)} %get-tuple-element.61), channel_id=1, source_target_pairs={{0,1},{1,0},{2,3},{3,2},{4,5},{5,4},{6,7},{7,6},{8,9},{9,8},{10,11... | collective-permute-start | bytes 1966088 | tf_op jit(solution)/shard_map/ppermute | solution.py:273
  101.1 10.8 %collective-permute-start.2 = (bf16[256,640]{1,0:T(8,128)(2,1)}, bf16[256,640]{1,0:T(8,128)(2,1)S(1)}, u32[]{:S(2)}, u32[]{:S(2)}) collective-permute-start(bf16[256,640]{1,0:T(8,128)(2,1)} %get-tuple-element.70), channel_id=1, source_target_pairs={{0,2},{2,4},{4,6},{6,0},{1,3},{3,5},{5,7},{7,1},{8,10},{10,12},{12... | collective-permute-start | bytes 983048 | tf_op jit(solution)/shard_map/ppermute | solution.py:269
  102.9 11.6 %collective-permute-start.4 = (bf16[256,640]{1,0:T(8,128)(2,1)}, bf16[256,640]{1,0:T(8,128)(2,1)S(1)}, u32[]{:S(2)}, u32[]{:S(2)}) collective-permute-start(bf16[256,640]{1,0:T(8,128)(2,1)} %get-tuple-element.68), channel_id=1, source_target_pairs={{0,6},{2,0},{4,2},{6,4},{1,7},{3,1},{5,3},{7,5},{8,14},{10,8},{12,... | collective-permute-start | bytes 983048 | tf_op jit(solution)/shard_map/ppermute | solution.py:269
  103.8 15.2 %collective-permute-start.6 = (bf16[256,640]{1,0:T(8,128)(2,1)}, bf16[256,640]{1,0:T(8,128)(2,1)}, u32[]{:S(2)}, u32[]{:S(2)}) collective-permute-start(bf16[256,640]{1,0:T(8,128)(2,1)} %get-tuple-element.68), channel_id=1, source_target_pairs={{0,2},{2,4},{4,6},{6,0},{1,3},{3,5},{5,7},{7,1},{8,10},{10,12},{12... | collective-permute-start | bytes 983048 | tf_op jit(solution)/shard_map/ppermute | solution.py:269
  111.9 11.1 %collective-permute-start.3 = (bf16[256,640]{1,0:T(8,128)(2,1)S(1)}, bf16[256,640]{1,0:T(8,128)(2,1)S(1)}, u32[]{:S(2)}, u32[]{:S(2)}) collective-permute-start(bf16[256,640]{1,0:T(8,128)(2,1)S(1)} %collective-permute-done.2), channel_id=1, source_target_pairs={{0,1},{1,0},{2,3},{3,2},{4,5},{5,4},{6,7},{7,6},{8,9},{9,8},{10,11... | collective-permute-start | bytes 983048 | tf_op jit(solution)/shard_map/ppermute | solution.py:273
  113.0 10.1 %collective-permute-start.8 = (bf16[256,640]{1,0:T(8,128)(2,1)}, bf16[256,640]{1,0:T(8,128)(2,1)}, u32[]{:S(2)}, u32[]{:S(2)}) collective-permute-start(bf16[256,640]{1,0:T(8,128)(2,1)} %get-tuple-element.70), channel_id=1, source_target_pairs={{0,6},{2,0},{4,2},{6,4},{1,7},{3,1},{5,3},{7,5},{8,14},{10,8},{12,... | collective-permute-start | bytes 983048 | tf_op jit(solution)/shard_map/ppermute | solution.py:269
  113.2 10.7 %copy-start.5 = (bf16[640,640]{1,0:T(8,128)(2,1)S(1)}, bf16[640,640]{1,0:T(8,128)(2,1)}, u32[]{:S(2)}) copy-start(bf16[640,640]{1,0:T(8,128)(2,1)} %get-tuple-element.66) | copy-start | bytes 2457604
  113.2 18.2 %collective-permute-start.10 = (bf16[256,640]{1,0:T(8,128)(2,1)S(1)}, bf16[256,640]{1,0:T(8,128)(2,1)S(1)}, u32[]{:S(2)}, u32[]{:S(2)}) collective-permute-start(bf16[256,640]{1,0:T(8,128)(2,1)S(1)} %collective-permute-done.2), channel_id=1, source_target_pairs={{0,2},{2,4},{4,6},{6,0},{1,3},{3,5},{5,7},{7,1},{8,10},{10,12},{12... | collective-permute-start | bytes 983048 | tf_op jit(solution)/shard_map/ppermute | solution.py:269
  114.5 16.9 %collective-permute-start.11 = (bf16[256,640]{1,0:T(8,128)(2,1)S(1)}, bf16[256,640]{1,0:T(8,128)(2,1)S(1)}, u32[]{:S(2)}, u32[]{:S(2)}) collective-permute-start(bf16[256,640]{1,0:T(8,128)(2,1)S(1)} %collective-permute-done.4), channel_id=1, source_target_pairs={{0,6},{2,0},{4,2},{6,4},{1,7},{3,1},{5,3},{7,5},{8,14},{10,8},{12,... | collective-permute-start | bytes 983048 | tf_op jit(solution)/shard_map/ppermute | solution.py:269
  119.0 6.6 %collective-permute-start.7 = (bf16[256,640]{1,0:T(8,128)(2,1)}, bf16[256,640]{1,0:T(8,128)(2,1)S(1)}, u32[]{:S(2)}, u32[]{:S(2)}) collective-permute-start(bf16[256,640]{1,0:T(8,128)(2,1)} %collective-permute-done.6), channel_id=1, source_target_pairs={{0,1},{1,0},{2,3},{3,2},{4,5},{5,4},{6,7},{7,6},{8,9},{9,8},{10,11... | collective-permute-start | bytes 983048 | tf_op jit(solution)/shard_map/ppermute | solution.py:273
  123.0 2.6 %copy-start.3 = (bf16[640,640]{1,0:T(8,128)(2,1)S(1)}, bf16[640,640]{1,0:T(8,128)(2,1)}, u32[]{:S(2)}) copy-start(bf16[640,640]{1,0:T(8,128)(2,1)} %get-tuple-element.69) | copy-start | bytes 2457604
  123.0 6.3 %collective-permute-start.5 = (bf16[256,640]{1,0:T(8,128)(2,1)S(1)}, bf16[256,640]{1,0:T(8,128)(2,1)S(1)}, u32[]{:S(2)}, u32[]{:S(2)}) collective-permute-start(bf16[256,640]{1,0:T(8,128)(2,1)S(1)} %collective-permute-done.4), channel_id=1, source_target_pairs={{0,1},{1,0},{2,3},{3,2},{4,5},{5,4},{6,7},{7,6},{8,9},{9,8},{10,11... | collective-permute-start | bytes 983048 | tf_op jit(solution)/shard_map/ppermute | solution.py:273
  123.7 3.7 %collective-permute-start.9 = (bf16[256,640]{1,0:T(8,128)(2,1)}, bf16[256,640]{1,0:T(8,128)(2,1)S(1)}, u32[]{:S(2)}, u32[]{:S(2)}) collective-permute-start(bf16[256,640]{1,0:T(8,128)(2,1)} %collective-permute-done.8), channel_id=1, source_target_pairs={{0,1},{1,0},{2,3},{3,2},{4,5},{5,4},{6,7},{7,6},{8,9},{9,8},{10,11... | collective-permute-start | bytes 983048 | tf_op jit(solution)/shard_map/ppermute | solution.py:273
  125.6 1.9 %copy-start.2 = (bf16[640,640]{1,0:T(8,128)(2,1)S(1)}, bf16[640,640]{1,0:T(8,128)(2,1)}, u32[]{:S(2)}) copy-start(bf16[640,640]{1,0:T(8,128)(2,1)} %get-tuple-element.71) | copy-start | bytes 2457604
  127.4 1.8 %copy-start = (bf16[640,640]{1,0:T(8,128)(2,1)S(1)}, bf16[640,640]{1,0:T(8,128)(2,1)}, u32[]{:S(2)}) copy-start(bf16[640,640]{1,0:T(8,128)(2,1)} %get-tuple-element.67) | copy-start | bytes 2457604
  130.1 1.1 copy-start.6
  130.1 1.1 copy-start.8
  131.2 1.9 %copy-start.1 = (bf16[640,640]{1,0:T(8,128)(2,1)S(1)}, bf16[640,640]{1,0:T(8,128)(2,1)}, u32[]{:S(2)}) copy-start(bf16[640,640]{1,0:T(8,128)(2,1)} %get-tuple-element.76) | copy-start | bytes 2457604
  131.4 2.5 %copy-start.4 = (bf16[640,640]{1,0:T(8,128)(2,1)S(1)}, bf16[640,640]{1,0:T(8,128)(2,1)}, u32[]{:S(2)}) copy-start(bf16[640,640]{1,0:T(8,128)(2,1)} %get-tuple-element.74) | copy-start | bytes 2457604
  131.4 1.7 %collective-permute-start.13 = (bf16[256,640]{1,0:T(8,128)(2,1)S(1)}, bf16[256,640]{1,0:T(8,128)(2,1)S(1)}, u32[]{:S(2)}, u32[]{:S(2)}) collective-permute-start(bf16[256,640]{1,0:T(8,128)(2,1)S(1)} %collective-permute-done.11), channel_id=1, source_target_pairs={{0,1},{1,0},{2,3},{3,2},{4,5},{5,4},{6,7},{7,6},{8,9},{9,8},{10,11... | collective-permute-start | bytes 983048 | tf_op jit(solution)/shard_map/ppermute | solution.py:273
  131.9 2.0 %collective-permute-start.12 = (bf16[256,640]{1,0:T(8,128)(2,1)S(1)}, bf16[256,640]{1,0:T(8,128)(2,1)S(1)}, u32[]{:S(2)}, u32[]{:S(2)}) collective-permute-start(bf16[256,640]{1,0:T(8,128)(2,1)S(1)} %collective-permute-done.10), channel_id=1, source_target_pairs={{0,1},{1,0},{2,3},{3,2},{4,5},{5,4},{6,7},{7,6},{8,9},{9,8},{10,11... | collective-permute-start | bytes 983048 | tf_op jit(solution)/shard_map/ppermute | solution.py:273
  (1 other events, 0.7 us)

commit v12 on v9

--- a/solution.py
+++ b/solution.py
@@ -326,13 +326,11 @@
     attended = attend(lists[1], got, got_other, attend(lists[0], got))
     own, low, high = select(source, exchange(attended))
     below_low, above_high = along_y(low, 1), along_y(high, 3)
-    below_high = along_y(high, 1)
-    own_other = swap(own)
-    above_low = along_y(low, 3)
+    own_other, low, high = lax.optimization_barrier((swap(own), low, high))
+    below_high, above_low = along_y(high, 1), along_y(low, 3)
     far_low, far_high = along_y(below_low, 1), along_y(above_high, 3)
     total = product(own, own_other, weights[0])
-    near = ((below_high, weights[2]), (above_low, weights[3]), (below_low, weights[1]), (above_high, weights[4]))
-    for block, weight in near:
+    for block, weight in zip((below_low, above_high, below_high, above_low), (weights[1], weights[4], weights[2], weights[3])):
         total = total + project(block, weight)
     base = residual_in.astype(jnp.float32) + gate_scale * by_rows(total)
     base, far_low, far_high = lax.optimization_barrier((base, far_low, far_high))

time: 138 us -> 135 us (0.978); the launches traced: 136 us -> 136 us
  Pallas kernels: 28.2 us -> 29.9 us
    pallas_call x1, Pallas kernels: 6.61 us -> 8.39 us  [attend(): pl.pallas_call(functools.partial(second_kernel, scale), in_specs=[smem] *...]
  transfers between devices with their start and end apart: 15 -> 15, of which waited for: 6 -> 5; matrix products, arithmetic and copies ran while one was open for 17% -> 17% of each run, Pallas kernels for 11% -> 11%
where the time goes in v12:
time: 135 us; the launch traced here: 136 us
  Pallas kernels  29.9 us (22%)
  waiting for transfers between devices  23.9 us (18%)
  starting transfers between devices  23.8 us (18%)
  blocking collectives  20.9 us (15%)
  other arithmetic  13.7 us (10%)
  local copies, waits for them, and re-layouts  9.4 us (7%)
  matrix products  7.4 us (5%)
  between operations  6.56 us (5%)
    all_to_all x1, blocking collectives, exchange(): lax.all_to_all(block, TOKENS_AXES, split_axis=0, concat_axis=0, tiled=True)  20.9 us
    ppermute x6, waiting for transfers between devices, along_y(): lax.ppermute(block, 'y', [(i, (i + step) % PLANES) for i in range(PLANES)])  11.9 us
    all_to_all x1, waiting for transfers between devices, exchange(): lax.all_to_all(block, TOKENS_AXES, split_axis=0, concat_axis=0, tiled=True)  10.8 us
    ppermute x8, starting transfers between devices, swap(): return lax.ppermute(block, 'c', [(0, 1), (1, 0)])  9.6 us
    all_to_all x1, starting transfers between devices, exchange(): lax.all_to_all(block, TOKENS_AXES, split_axis=0, concat_axis=0, tiled=True)  8.44 us
    pallas_call x1, Pallas kernels, attend(): pl.pallas_call(functools.partial(second_kernel, scale), in_specs=[smem] *...  8.39 us
    pallas_call x1, Pallas kernels, attend(): pl.pallas_call(functools.partial(first_kernel, scale), in_specs=[smem] *...  7.89 us
    dot_general x7, matrix products, product(): jnp.dot(jnp.concatenate([block, other], axis=0), weight, preferred_elemen...  7.02 us
  transfers between devices with their start and end apart: 15, of which 5 were waited for; matrix products, arithmetic and copies ran while one was open for 17% of the time, Pallas kernels for 11%

profile of v12, /device:TPU:1, one launch (start us, length us, event | category | flops | bytes accessed | tf_op | source)
XLA Modules:
  0.0 135.5 jit_solution(13504919618941818204)
XLA Ops:
  0.0 2.1 %fusion.65 = (s32[40,64]{1,0:T(8,128)S(1)}, s32[40]{0:T(128)S(1)}) fusion(s32[40,64,64]{2,1,0:T(8,128)} %param.13), kind=kLoop, calls=%fused_computation.167 | loop fusion | flops 325080 | bytes 665760 | tf_op jit(solution)/shard_map/reduce_sum | solution.py:280
  4.1 4.5 %shard_map.73 = bf16[16,768,128]{2,1,0:T(8,128)(2,1)} custom-call(s32[17]{0:T(128)} %pad_add_fusion.heads, bf16[512,5120]{1,0:T(8,128)(2,1)} %q_ref.1, bf16[512,5120]{1,0:T(8,128)(2,1)} %k_ref.1, bf16[512,5120]{1,0:T(8,128)(2,1)} %v_ref.1), custom_call_target="tpu_custom_call" | custom-call | tf_op jit(solution)/shard_map/pallas_call | solution.py:78
  8.6 8.4 %all-to-all-start = ((bf16[16,768,128]{2,1,0:T(8,128)(2,1)}), bf16[16,768,128]{2,1,0:T(8,128)(2,1)S(1)}, u32[]{:S(2)}, u32[]{:S(2)}) async-start(bf16[16,768,128]{2,1,0:T(8,128)(2,1)} %shard_map.73), calls=%async_computation | async-start | bytes 6291456 | tf_op jit(solution)/shard_map/all_to_all | solution.py:265
  23.2 1.6 %reshape.338 = s32[32,16,2,2]{3,2,1,0:T(2,128)} reshape(s32[16,1,2,64]{3,2,1,0:T(2,128)S(1)} %constant_dynamic-slice_fusion.3) | data formatting | bytes 16384 | tf_op jit(solution)/shard_map/reshape | solution.py:308
  25.4 3.1 %fusion.66 = (s32[32]{0:T(128)S(1)}, s32[32,16,1,2]{3,2,1,0:T(1,128)}, s32[32]{0:T(128)S(1)}, s32[32,16,1,2]{3,2,1,0:T(1,128)S(1)}) fusion(s32[32,16,2,2]{3,2,1,0:T(2,128)} %reshape.338, s32[]{:T(128)S(6)} %select_n.211, s32[]{:T(128)S(6)} %select_n.198), kind=kLoop, calls=%fused_computation.168 | loop fusion | flops 1984 | bytes 16648 | tf_op jit(solution)/shard_map/reduce_sum | solution.py:181
  35.3 1.2 multiply_reduce_fusion
  37.2 1.2 compare_select_fusion.2
  40.0 6.6 %shard_map.74 = (bf16[1280,640]{1,0:T(8,128)(2,1)}, bf16[640,640]{1,0:T(8,128)(2,1)}, bf16[640,640]{1,0:T(8,128)(2,1)}, bf16[640,640]{1,0:T(8,128)(2,1)}, bf16[6...) custom-call(s32[40]{0:T(128)} %pad_add_fusion.1.heads, bf16[5120,640]{1,0:T(8,128)(2,1)} %w_ref.1), custom_call_target="tpu_custom_call" | custom-call | tf_op jit(solution)/shard_map/pallas_call | solution.py:250
  46.7 10.8 %all-to-all-done = bf16[16,768,128]{2,1,0:T(8,128)(2,1)S(1)} async-done(((bf16[16,768,128]{2,1,0:T(8,128)(2,1)}), bf16[16,768,128]{2,1,0:T(8,128)(2,1)S(1)}, u32[]{:S(2)}, u32[]{:S(2)}) %all-to-all-start) | async-done | bytes 3145760 | tf_op jit(solution)/shard_map/all_to_all | solution.py:265
  57.4 3.0 %collective-permute-start = (bf16[16,6,128,128]{3,2,1,0:T(8,128)(2,1)S(1)}, bf16[16,6,128,128]{3,2,1,0:T(8,128)(2,1)S(1)}, u32[]{:S(2)}, u32[]{:S(2)}) collective-permute-start(bf16[16,6,128,128]{3,2,1,0:T(8,128)(2,1)S(1)} %bitcast.47), channel_id=1, source_target_pairs={{0,1},{1,0},{2,3},{3,2},{4,5},{5,4},{6,7},{7,6},{8,9},{9,8},{10,11... | collective-permute-start | bytes 9437192 | tf_op jit(solution)/shard_map/ppermute | solution.py:273
  60.4 7.9 %shard_map.75 = (f32[32,128,128]{2,1,0:T(8,128)S(1)}, f32[32,1,128]{2,1,0:T(1,128)S(1)}, f32[32,1,128]{2,1,0:T(1,128)S(1)}) custom-call(s32[1]{0:T(128)} %bitcast.10.meta, s32[256]{0:T(256)S(1)} %broadcast_minimum_fusion.1.q_of, s32[1024]{0:T(1024)S(1)} %convert_element_type.96.k_of, s32[256]{0:T(256)S(1)} %get-tuple-element.57.valid_of, ...), custom_call_target="tpu_custom_call" | custom-call | flops 4000000000 | bytes 8388608 | tf_op jit(solution)/shard_map/pallas_call | solution.py:162
  68.3 8.4 %shard_map.76 = bf16[16,2,128,128]{3,2,1,0:T(8,128)(2,1)S(1)} custom-call(s32[1]{0:T(128)} %bitcast.18.meta, s32[256]{0:T(256)S(1)} %broadcast_minimum_fusion.q_of, s32[1024]{0:T(1024)S(1)} %convert_element_type.102.k_of, s32[256]{0:T(256)S(1)} %get-tuple-element.52.valid_of, bf16[16,6,128,128]{3,2,1,0:T(8,128)(2,1)S(1)} %bitcast.49, ...), custom_call_target="tpu_custom_call" | custom-call | flops 4000000000 | bytes 8388608 | tf_op jit(solution)/shard_map/pallas_call | solution.py:169
  76.7 20.9 %all_to_all.10.got_ref = bf16[16,2,128,128]{3,2,1,0:T(8,128)(2,1)} all-to-all(bf16[16,2,128,128]{3,2,1,0:T(8,128)(2,1)S(1)} %shard_map.76), channel_id=1, replica_groups=mesh['x'=4,'z'=4,'y'=4,'c'=2] {'x','z'}, dimensions={0} | all-to-all | bytes 2097152 | tf_op jit(solution)/shard_map/all_to_all | solution.py:265
  97.6 2.4 %shard_map.77 = (bf16[256,1280]{1,0:T(8,128)(2,1)}, bf16[256,640]{1,0:T(8,128)(2,1)}, bf16[256,640]{1,0:T(8,128)(2,1)}) custom-call(s32[20]{0:T(128)} %reshape.327.source, bf16[16,2,128,128]{3,2,1,0:T(8,128)(2,1)} %all_to_all.10.got_ref), custom_call_target="tpu_custom_call" | custom-call | tf_op jit(solution)/shard_map/pallas_call | solution.py:219
  100.0 2.3 %collective-permute-start.1 = (bf16[256,1280]{1,0:T(8,128)(2,1)}, bf16[256,1280]{1,0:T(8,128)(2,1)}, u32[]{:S(2)}, u32[]{:S(2)}) collective-permute-start(bf16[256,1280]{1,0:T(8,128)(2,1)} %get-tuple-element.61), channel_id=1, source_target_pairs={{0,1},{1,0},{2,3},{3,2},{4,5},{5,4},{6,7},{7,6},{8,9},{9,8},{10,11... | collective-permute-start | bytes 1966088 | tf_op jit(solution)/shard_map/ppermute | solution.py:273
  103.3 1.7 %collective-permute-start.4 = (bf16[256,640]{1,0:T(8,128)(2,1)}, bf16[256,640]{1,0:T(8,128)(2,1)S(1)}, u32[]{:S(2)}, u32[]{:S(2)}) collective-permute-start(bf16[256,640]{1,0:T(8,128)(2,1)} %get-tuple-element.68), channel_id=1, source_target_pairs={{0,6},{2,0},{4,2},{6,4},{1,7},{3,1},{5,3},{7,5},{8,14},{10,8},{12,... | collective-permute-start | bytes 983048 | tf_op jit(solution)/shard_map/ppermute | solution.py:269
  105.4 7.7 %collective-permute-done.2 = bf16[256,640]{1,0:T(8,128)(2,1)S(1)} collective-permute-done((bf16[256,640]{1,0:T(8,128)(2,1)}, bf16[256,640]{1,0:T(8,128)(2,1)S(1)}, u32[]{:S(2)}, u32[]{:S(2)}) %collective-permute-start.2) | collective-permute-done | bytes 327712 | tf_op jit(solution)/shard_map/ppermute | solution.py:269
  113.1 1.2 collective-permute-start.3
  114.3 1.4 %collective-permute-start.10 = (bf16[256,640]{1,0:T(8,128)(2,1)S(1)}, bf16[256,640]{1,0:T(8,128)(2,1)S(1)}, u32[]{:S(2)}, u32[]{:S(2)}) collective-permute-start(bf16[256,640]{1,0:T(8,128)(2,1)S(1)} %collective-permute-done.2), channel_id=1, source_target_pairs={{0,2},{2,4},{4,6},{6,0},{1,3},{3,5},{5,7},{7,1},{8,10},{10,12},{12... | collective-permute-start | bytes 983048 | tf_op jit(solution)/shard_map/ppermute | solution.py:269
  115.8 1.3 collective-permute-start.11
  117.0 3.1 %collective-permute-done.6 = bf16[256,640]{1,0:T(8,128)(2,1)S(1)} collective-permute-done((bf16[256,640]{1,0:T(8,128)(2,1)}, bf16[256,640]{1,0:T(8,128)(2,1)S(1)}, u32[]{:S(2)}, u32[]{:S(2)}) %collective-permute-start.6) | collective-permute-done | bytes 327712 | tf_op jit(solution)/shard_map/ppermute | solution.py:269
  120.1 1.2 collective-permute-start.7
  121.3 2.5 %fusion.2 = f32[512,640]{1,0:T(8,128)S(1)} fusion(bf16[1280,640]{1,0:T(8,128)(2,1)S(1)} %copy-done.8, bf16[256,1280]{1,0:T(8,128)(2,1)} %collective-permute-done.1, bf16[256,1280]{1,0:T(8,128)(2,1)} %get-tuple-element.61), kind=kOutput, calls=%fused_computation.6 | convolution fusion | flops 841482240 | bytes 4259840 | tf_op jit(solution)/shard_map/dot_general | solution.py:317
  131.7 1.3 collective-permute-done.13
  (118 shorter events, 23.2 us)
Async XLA Ops:
  8.6 48.8 %all-to-all-start = ((bf16[16,768,128]{2,1,0:T(8,128)(2,1)}), bf16[16,768,128]{2,1,0:T(8,128)(2,1)S(1)}, u32[]{:S(2)}, u32[]{:S(2)}) async-start(bf16[16,768,128]{2,1,0:T(8,128)(2,1)} %shard_map.73), calls=%async_computation | async-start | bytes 6291456 | tf_op jit(solution)/shard_map/all_to_all | solution.py:265
  57.4 10.9 %collective-permute-start = (bf16[16,6,128,128]{3,2,1,0:T(8,128)(2,1)S(1)}, bf16[16,6,128,128]{3,2,1,0:T(8,128)(2,1)S(1)}, u32[]{:S(2)}, u32[]{:S(2)}) collective-permute-start(bf16[16,6,128,128]{3,2,1,0:T(8,128)(2,1)S(1)} %bitcast.47), channel_id=1, source_target_pairs={{0,1},{1,0},{2,3},{3,2},{4,5},{5,4},{6,7},{7,6},{8,9},{9,8},{10,11... | collective-permute-start | bytes 9437192 | tf_op jit(solution)/shard_map/ppermute | solution.py:273
  76.7 44.6 %copy-start.8 = (bf16[1280,640]{1,0:T(8,128)(2,1)S(1)}, bf16[1280,640]{1,0:T(8,128)(2,1)}, u32[]{:S(2)}) copy-start(bf16[1280,640]{1,0:T(8,128)(2,1)} %get-tuple-element.65) | copy-start | bytes 4915204
  100.0 5.0 %collective-permute-start.1 = (bf16[256,1280]{1,0:T(8,128)(2,1)}, bf16[256,1280]{1,0:T(8,128)(2,1)}, u32[]{:S(2)}, u32[]{:S(2)}) collective-permute-start(bf16[256,1280]{1,0:T(8,128)(2,1)} %get-tuple-element.61), channel_id=1, source_target_pairs={{0,1},{1,0},{2,3},{3,2},{4,5},{5,4},{6,7},{7,6},{8,9},{9,8},{10,11... | collective-permute-start | bytes 1966088 | tf_op jit(solution)/shard_map/ppermute | solution.py:273
  102.4 10.8 %collective-permute-start.2 = (bf16[256,640]{1,0:T(8,128)(2,1)}, bf16[256,640]{1,0:T(8,128)(2,1)S(1)}, u32[]{:S(2)}, u32[]{:S(2)}) collective-permute-start(bf16[256,640]{1,0:T(8,128)(2,1)} %get-tuple-element.70), channel_id=1, source_target_pairs={{0,2},{2,4},{4,6},{6,0},{1,3},{3,5},{5,7},{7,1},{8,10},{10,12},{12... | collective-permute-start | bytes 983048 | tf_op jit(solution)/shard_map/ppermute | solution.py:269
  103.3 12.4 %collective-permute-start.4 = (bf16[256,640]{1,0:T(8,128)(2,1)}, bf16[256,640]{1,0:T(8,128)(2,1)S(1)}, u32[]{:S(2)}, u32[]{:S(2)}) collective-permute-start(bf16[256,640]{1,0:T(8,128)(2,1)} %get-tuple-element.68), channel_id=1, source_target_pairs={{0,6},{2,0},{4,2},{6,4},{1,7},{3,1},{5,3},{7,5},{8,14},{10,8},{12,... | collective-permute-start | bytes 983048 | tf_op jit(solution)/shard_map/ppermute | solution.py:269
  105.0 15.1 %collective-permute-start.6 = (bf16[256,640]{1,0:T(8,128)(2,1)}, bf16[256,640]{1,0:T(8,128)(2,1)S(1)}, u32[]{:S(2)}, u32[]{:S(2)}) collective-permute-start(bf16[256,640]{1,0:T(8,128)(2,1)} %get-tuple-element.68), channel_id=1, source_target_pairs={{0,2},{2,4},{4,6},{6,0},{1,3},{3,5},{5,7},{7,1},{8,10},{10,12},{12... | collective-permute-start | bytes 983048 | tf_op jit(solution)/shard_map/ppermute | solution.py:269
  113.1 10.7 %collective-permute-start.3 = (bf16[256,640]{1,0:T(8,128)(2,1)S(1)}, bf16[256,640]{1,0:T(8,128)(2,1)S(1)}, u32[]{:S(2)}, u32[]{:S(2)}) collective-permute-start(bf16[256,640]{1,0:T(8,128)(2,1)S(1)} %collective-permute-done.2), channel_id=1, source_target_pairs={{0,1},{1,0},{2,3},{3,2},{4,5},{5,4},{6,7},{7,6},{8,9},{9,8},{10,11... | collective-permute-start | bytes 983048 | tf_op jit(solution)/shard_map/ppermute | solution.py:273
  114.3 9.6 %collective-permute-start.8 = (bf16[256,640]{1,0:T(8,128)(2,1)}, bf16[256,640]{1,0:T(8,128)(2,1)S(1)}, u32[]{:S(2)}, u32[]{:S(2)}) collective-permute-start(bf16[256,640]{1,0:T(8,128)(2,1)} %get-tuple-element.70), channel_id=1, source_target_pairs={{0,6},{2,0},{4,2},{6,4},{1,7},{3,1},{5,3},{7,5},{8,14},{10,8},{12,... | collective-permute-start | bytes 983048 | tf_op jit(solution)/shard_map/ppermute | solution.py:269
  114.3 10.7 %copy-start.5 = (bf16[640,640]{1,0:T(8,128)(2,1)S(1)}, bf16[640,640]{1,0:T(8,128)(2,1)}, u32[]{:S(2)}) copy-start(bf16[640,640]{1,0:T(8,128)(2,1)} %get-tuple-element.66) | copy-start | bytes 2457604
  114.3 15.5 %collective-permute-start.10 = (bf16[256,640]{1,0:T(8,128)(2,1)S(1)}, bf16[256,640]{1,0:T(8,128)(2,1)S(1)}, u32[]{:S(2)}, u32[]{:S(2)}) collective-permute-start(bf16[256,640]{1,0:T(8,128)(2,1)S(1)} %collective-permute-done.2), channel_id=1, source_target_pairs={{0,2},{2,4},{4,6},{6,0},{1,3},{3,5},{5,7},{7,1},{8,10},{10,12},{12... | collective-permute-start | bytes 983048 | tf_op jit(solution)/shard_map/ppermute | solution.py:269
  115.8 15.1 %collective-permute-start.11 = (bf16[256,640]{1,0:T(8,128)(2,1)S(1)}, bf16[256,640]{1,0:T(8,128)(2,1)S(1)}, u32[]{:S(2)}, u32[]{:S(2)}) collective-permute-start(bf16[256,640]{1,0:T(8,128)(2,1)S(1)} %collective-permute-done.4), channel_id=1, source_target_pairs={{0,6},{2,0},{4,2},{6,4},{1,7},{3,1},{5,3},{7,5},{8,14},{10,8},{12,... | collective-permute-start | bytes 983048 | tf_op jit(solution)/shard_map/ppermute | solution.py:269
  120.1 5.7 %collective-permute-start.7 = (bf16[256,640]{1,0:T(8,128)(2,1)S(1)}, bf16[256,640]{1,0:T(8,128)(2,1)S(1)}, u32[]{:S(2)}, u32[]{:S(2)}) collective-permute-start(bf16[256,640]{1,0:T(8,128)(2,1)S(1)} %collective-permute-done.6), channel_id=1, source_target_pairs={{0,1},{1,0},{2,3},{3,2},{4,5},{5,4},{6,7},{7,6},{8,9},{9,8},{10,11... | collective-permute-start | bytes 983048 | tf_op jit(solution)/shard_map/ppermute | solution.py:273
  123.8 2.0 %copy-start.3 = (bf16[640,640]{1,0:T(8,128)(2,1)S(1)}, bf16[640,640]{1,0:T(8,128)(2,1)}, u32[]{:S(2)}) copy-start(bf16[640,640]{1,0:T(8,128)(2,1)} %get-tuple-element.69) | copy-start | bytes 2457604
  123.8 3.9 %collective-permute-start.5 = (bf16[256,640]{1,0:T(8,128)(2,1)S(1)}, bf16[256,640]{1,0:T(8,128)(2,1)S(1)}, u32[]{:S(2)}, u32[]{:S(2)}) collective-permute-start(bf16[256,640]{1,0:T(8,128)(2,1)S(1)} %collective-permute-done.4), channel_id=1, source_target_pairs={{0,1},{1,0},{2,3},{3,2},{4,5},{5,4},{6,7},{7,6},{8,9},{9,8},{10,11... | collective-permute-start | bytes 983048 | tf_op jit(solution)/shard_map/ppermute | solution.py:273
  123.9 2.7 %collective-permute-start.9 = (bf16[256,640]{1,0:T(8,128)(2,1)S(1)}, bf16[256,640]{1,0:T(8,128)(2,1)S(1)}, u32[]{:S(2)}, u32[]{:S(2)}) collective-permute-start(bf16[256,640]{1,0:T(8,128)(2,1)S(1)} %collective-permute-done.8), channel_id=1, source_target_pairs={{0,1},{1,0},{2,3},{3,2},{4,5},{5,4},{6,7},{7,6},{8,9},{9,8},{10,11... | collective-permute-start | bytes 983048 | tf_op jit(solution)/shard_map/ppermute | solution.py:273
  125.8 1.1 copy-start.2
  126.6 1.2 copy-start
  128.6 1.1 copy-start.6
  128.6 1.1 copy-start.7
  129.7 3.2 %copy-start.1 = (bf16[640,640]{1,0:T(8,128)(2,1)S(1)}, bf16[640,640]{1,0:T(8,128)(2,1)}, u32[]{:S(2)}) copy-start(bf16[640,640]{1,0:T(8,128)(2,1)} %get-tuple-element.76) | copy-start | bytes 2457604
  129.8 3.9 %copy-start.4 = (bf16[640,640]{1,0:T(8,128)(2,1)S(1)}, bf16[640,640]{1,0:T(8,128)(2,1)}, u32[]{:S(2)}) copy-start(bf16[640,640]{1,0:T(8,128)(2,1)} %get-tuple-element.74) | copy-start | bytes 2457604
  130.9 2.0 %collective-permute-start.13 = (bf16[256,640]{1,0:T(8,128)(2,1)S(1)}, bf16[256,640]{1,0:T(8,128)(2,1)S(1)}, u32[]{:S(2)}, u32[]{:S(2)}) collective-permute-start(bf16[256,640]{1,0:T(8,128)(2,1)S(1)} %collective-permute-done.11), channel_id=1, source_target_pairs={{0,1},{1,0},{2,3},{3,2},{4,5},{5,4},{6,7},{7,6},{8,9},{9,8},{10,11... | collective-permute-start | bytes 983048 | tf_op jit(solution)/shard_map/ppermute | solution.py:273
  131.6 2.0 %collective-permute-start.12 = (bf16[256,640]{1,0:T(8,128)(2,1)S(1)}, bf16[256,640]{1,0:T(8,128)(2,1)S(1)}, u32[]{:S(2)}, u32[]{:S(2)}) collective-permute-start(bf16[256,640]{1,0:T(8,128)(2,1)S(1)} %collective-permute-done.10), channel_id=1, source_target_pairs={{0,1},{1,0},{2,3},{3,2},{4,5},{5,4},{6,7},{7,6},{8,9},{9,8},{10,11... | collective-permute-start | bytes 983048 | tf_op jit(solution)/shard_map/ppermute | solution.py:273
